TPU v7x, 32 devices: a whole 2x2x4 slice. The times are simulated.
32 devices in a mesh: occ: 2 (over core), row: 4 (over y, x), col: 4 (over z).
Axes of the slice: x: 2, y: 2, z: 4, core: 2. Of those that a mesh axis runs over, the one named last changes fastest.
Arguments:
- bra_factor: bfloat16 [3072, 2, 4096], P(('occ', 'col'), None, 'row'), may hold values from -0.5 to 0.5
- ket_factor: bfloat16 [3072, 2, 4096], P(('occ', 'row'), None, 'col'), may hold values from -0.5 to 0.5
- occ_energy: float32 [2], replicated, may hold values from -2 to -0.5
- virt_energy: float32 [4096], replicated, may hold values from 0.2 to 3
Outputs:
- amplitudes: bfloat16 [2, 2, 4096, 4096], P(None, None, 'row', 'col')
- gamma: float32 [3072, 2, 4096], P(('occ', 'col'), None, 'row')
All inputs are finite; a program needn't handle non-finite values.
Results may differ from a plain program's by a relative error of at most 0.002.
Values may be sent and summed in bfloat16 or wider, within the bound.
No kernel may reach another device: no remote copies, remote signals or barrier semaphores. Data moves between devices by JAX's collectives and lax.ppermute only.
A program may use at most 128 MiB of HBM per device.

v0:
```python
import functools

import jax
import jax.numpy as jnp
from jax import lax
from jax.experimental import pallas as pl
from jax.experimental.pallas import tpu as pltpu
from jax.sharding import PartitionSpec as P


def make_amplitudes(coulomb, occ_energy, virt_first, virt_second):
    denominator = (
        occ_energy[:, None, None, None]
        + occ_energy[None, :, None, None]
        - virt_first[None, None, :, None]
        - virt_second[None, None, None, :]
    )
    return ((2.0 * coulomb - jnp.transpose(coulomb, (1, 0, 2, 3))) / denominator).astype(
        jnp.bfloat16
    )


def general(bra_factor, ket_factor, occ_energy, virt_energy):
    a_width = bra_factor.shape[2]
    b_width = ket_factor.shape[2]
    ket_whole = lax.all_gather(ket_factor, "row", axis=0, tiled=True)
    row_index = lax.axis_index("row")
    col_index = lax.axis_index("col")
    virt_first = lax.dynamic_slice_in_dim(virt_energy, row_index * a_width, a_width, 0)
    virt_second = lax.dynamic_slice_in_dim(virt_energy, col_index * b_width, b_width, 0)
    partial_sum = jnp.einsum(
        "qia,qjb->ijab",
        lax.all_gather(bra_factor, "col", axis=0, tiled=True),
        ket_whole,
        preferred_element_type=jnp.float32,
    )
    batch_count = lax.axis_size("occ")
    pad_rows = (batch_count - a_width % batch_count) % batch_count
    padded = jnp.pad(partial_sum, ((0, 0), (0, 0), (0, pad_rows), (0, 0)))
    share_sum = lax.psum_scatter(padded, "occ", scatter_dimension=2, tiled=True)
    share_len = share_sum.shape[2]
    energy_padded = jnp.pad(virt_first, (0, pad_rows), constant_values=1.0)
    energy_share = lax.dynamic_slice_in_dim(
        energy_padded, lax.axis_index("occ") * share_len, share_len, 0
    )
    share_amps = make_amplitudes(share_sum, occ_energy, energy_share, virt_second)
    collected = lax.all_gather(share_amps, "occ", axis=2, tiled=True)
    amplitudes = collected[:, :, :a_width, :]
    gamma = lax.psum_scatter(
        jnp.einsum("ijab,qjb->qia", amplitudes, ket_whole, preferred_element_type=jnp.float32),
        "col",
        scatter_dimension=0,
        tiled=True,
    )
    return (amplitudes, gamma)


CHUNKS = 4
TOGETHER = 2
GROUPS = 4


def chunk_kernel(pieces, chunk, *refs):
    refs = list(refs)
    take = lambda count: [refs.pop(0) for _ in range(count)]
    ket = take(1 if chunk else 2 * len(pieces))
    (bra,) = take(1)
    ups, downs = take(3), take(3)
    occ_ref, virt_ref = take(2)
    if chunk:
        take(2)
    whole_ref, half_ref, own_ref, pair_ref, far_ref, send_ref = take(6)
    if not chunk:
        (ket_all,) = take(1)
    kv, bv, bt, t2, amps, ket_sem, bra_sem, out_sem = refs
    width = bra.shape[3]
    span = ket[0].shape[1] // 2
    half = half_ref.shape[2]
    part = span // GROUPS
    batch = bra.shape[2]
    here_row, here_col = lax.axis_index("row"), lax.axis_index("col")
    me = lax.axis_index("occ")
    pair = lax.bitwise_xor(here_col, 1)
    low = here_col < 2
    middle = jnp.logical_or(here_col == 1, here_col == 2)

    def bra_copies(source, home, slot):
        return [
            pltpu.make_async_copy(
                source.at[q, i],
                bv.at[home, pl.ds(q * batch, batch), pl.ds(i * width, width)],
                bra_sem.at[slot, q, i],
            )
            for q in range(2)
            for i in range(2)
        ]

    def fetch(condition, source, home, slot):
        @pl.when(condition)
        def _():
            for copy in bra_copies(source, home, slot):
                copy.start()

    for copy in bra_copies(bra, here_col, 0):
        copy.start()
    place = chunk % TOGETHER
    for d in range(1, 4):
        home = lax.rem(here_col + 4 - d, 4)
        fetch(here_col >= d, ups[d - 1].at[place], home, d)
        fetch(here_col < d, downs[3 - d].at[place], home, d)

    copies = [[] for _ in range(GROUPS)]
    for group in range(GROUPS):
        for j in range(2):
            columns = pl.ds(j * span + group * part, part)
            if chunk:
                moves = [(ket[0], 0, 8 * batch, 0)]
            else:
                moves = []
                for n in range(2 * len(pieces)):
                    q, index = divmod(n, len(pieces))
                    offset, begin, rows = pieces[index]
                    home = lax.bitwise_xor(here_row, offset) * (2 * batch) + q * batch + begin
                    moves.append((ket[n], pl.multiple_of(home, 16), rows, n))
            for source, home, rows, n in moves:
                copy = pltpu.make_async_copy(
                    source.at[:, columns],
                    kv.at[pl.ds(home, rows), columns],
                    ket_sem.at[group, n, j],
                )
                copy.start()
                copies[group].append(copy)
    for slot in range(4):
        for copy in bra_copies(bra, slot, slot):
            copy.wait()
    first_at = here_row * (2 * half) + me * half + chunk * width
    first = virt_ref[:, pl.ds(pl.multiple_of(first_at, 128), width)]
    first = jnp.broadcast_to(first, (width, width)).T[:, :1]
    for d in range(4):
        bt[:, d * 2 * batch : (d + 1) * 2 * batch] = bv[d].T
    for group in range(GROUPS):
        for copy in copies[group]:
            copy.wait()
        tile = [
            jnp.dot(
                bt[...],
                kv[:, j * span + group * part : j * span + (group + 1) * part],
                preferred_element_type=jnp.float32,
            )
            for j in range(2)
        ]
        second_at = pl.multiple_of(here_col * span + group * part, 128)
        second = virt_ref[:, pl.ds(second_at, part)]
        for i in range(2):
            for j in range(2):
                direct = tile[j][i * width : (i + 1) * width, :]
                exchange = tile[i][j * width : (j + 1) * width, :]
                denominator = ((occ_ref[i] + occ_ref[j]) - first) - second
                block = ((2.0 * direct - exchange) / denominator).astype(jnp.bfloat16)
                amps[i, j, :, group * part : (group + 1) * part] = block
                t2[
                    i * width : (i + 1) * width,
                    j * span + group * part : j * span + (group + 1) * part,
                ] = block
    at = pl.multiple_of(me * half + chunk * width, 16)
    outs = [pltpu.make_async_copy(kv, ket_all, out_sem.at[2])] if not chunk else []
    outs += [
        pltpu.make_async_copy(amps, whole_ref.at[:, :, pl.ds(at, width), :], out_sem.at[0]),
        pltpu.make_async_copy(
            amps, half_ref.at[:, :, pl.ds(chunk * width, width), :], out_sem.at[1]
        ),
    ]
    for copy in outs:
        copy.start()

    def share_of(home):
        rows = pl.ds(pl.multiple_of(home * (2 * batch), 16), 2 * batch)
        return lax.dot_general(
            kv[rows, :],
            t2[...],
            (((1,), (1,)), ((), ())),
            preferred_element_type=jnp.float32,
        )

    for n in range(2):
        share = share_of(jnp.where(low, 2 + n, n))
        far_ref[n] = share
        send_ref[n] = share.astype(jnp.bfloat16)
    pair_ref[...] = share_of(pair)
    own_ref[...] = share_of(here_col)
    for copy in outs:
        copy.wait()


def run_chunk(chunk, ket, pieces, bras, energies, held):
    _, _, batch, width = bras[0].shape
    span = ket[0].shape[1] // 2
    half = width * CHUNKS
    total = 8 * batch
    flops = 2 * 2 * total * 2 * width * 2 * span
    ins = [*ket, *bras]
    any_space = pl.BlockSpec(memory_space=pl.ANY)
    in_vmem = pl.BlockSpec(memory_space=pltpu.VMEM)
    in_hbm = pl.BlockSpec(memory_space=pltpu.HBM)
    return pl.pallas_call(
        functools.partial(chunk_kernel, pieces, chunk),
        out_shape=(
            jax.ShapeDtypeStruct((2, 2, 2 * half, span), jnp.bfloat16),
            jax.ShapeDtypeStruct((2, 2, half, span), jnp.bfloat16),
            jax.ShapeDtypeStruct((2 * batch, 2 * width), jnp.float32),
            jax.ShapeDtypeStruct((2 * batch, 2 * width), jnp.float32),
            jax.ShapeDtypeStruct((2, 2 * batch, 2 * width), jnp.float32),
            jax.ShapeDtypeStruct((2, 2 * batch, 2 * width), jnp.bfloat16),
        )
        + (() if chunk else (jax.ShapeDtypeStruct((total, 2 * span), jnp.bfloat16),)),
        in_specs=[in_hbm if chunk else any_space] * len(ket)
        + [any_space] * len(bras)
        + [pl.BlockSpec(memory_space=pltpu.SMEM), in_vmem]
        + [any_space] * len(held),
        out_specs=(any_space, any_space, in_vmem, in_vmem, in_vmem, in_vmem)
        + (() if chunk else (in_hbm,)),
        scratch_shapes=[
            pltpu.VMEM((total, 2 * span), jnp.bfloat16),
            pltpu.VMEM((4, 2 * batch, 2 * width), jnp.bfloat16),
            pltpu.VMEM((2 * width, total), jnp.bfloat16),
            pltpu.VMEM((2 * width, 2 * span), jnp.bfloat16),
            pltpu.VMEM((2, 2, width, span), jnp.bfloat16),
            pltpu.SemaphoreType.DMA((GROUPS, 2 * len(pieces), 2)),
            pltpu.SemaphoreType.DMA((4, 2, 2)),
            pltpu.SemaphoreType.DMA((3,)),
        ],
        input_output_aliases={len(ins) + 2 + n: n for n in range(len(held))},
        compiler_params=pltpu.CompilerParams(vmem_limit_bytes=30 * 2**20),
        cost_estimate=pl.CostEstimate(
            flops=flops, bytes_accessed=total * 2 * span * 2, transcendentals=0
        ),
    )(*ins, *energies, *held)


def pick_kernel(bra, kept_out, given_out):
    _, _, _, width = kept_out.shape
    span = bra.shape[1] // 2
    me = lax.axis_index("occ")
    for side, out in ((1 - me, given_out), (me, kept_out)):
        for k in range(CHUNKS):
            for i in range(2):
                home = i * span + side * (span // 2) + k * width
                out[k, i] = bra[:, pl.ds(pl.multiple_of(home, 128), width)]


def pick(bra):
    batch, columns = bra.shape
    part = jax.ShapeDtypeStruct((CHUNKS, 2, batch, columns // 4 // CHUNKS), bra.dtype)
    return pl.pallas_call(
        pick_kernel,
        out_shape=(part, part),
        compiler_params=pltpu.CompilerParams(vmem_limit_bytes=16 * 2**20),
        cost_estimate=pl.CostEstimate(
            flops=0, bytes_accessed=4 * bra.size, transcendentals=0
        ),
    )(bra)


def close_kernel(*refs):
    other, _, *totals = refs[: 2 + 2 * CHUNKS]
    amps, gamma, amp_buffer, gamma_buffer, sems, gamma_sems = refs[2 + 2 * CHUNKS :]
    half = other.shape[2]
    me = lax.axis_index("occ")
    batch, _, columns = gamma.shape
    width = columns // 2 // CHUNKS
    at = pl.multiple_of((1 - me) * half, 16)
    blocks = [(i, j) for i in range(2) for j in range(2)]
    reads = [
        pltpu.make_async_copy(other.at[i, j], amp_buffer.at[i, j], sems.at[0, i, j])
        for i, j in blocks
    ]
    writes = [
        pltpu.make_async_copy(
            amp_buffer.at[i, j], amps.at[i, j, pl.ds(at, half), :], sems.at[1, i, j]
        )
        for i, j in blocks
    ]
    for copy in reads:
        copy.start()
    for n in range(2 * CHUNKS):
        side, k = divmod(n, CHUNKS)
        home = jnp.where(me == side, 0, columns // 2) + k * width
        for i in range(2):
            gamma_buffer[n, :, i, :] = totals[n][:batch, i * width : (i + 1) * width]
        writes.append(
            pltpu.make_async_copy(
                gamma_buffer.at[n],
                gamma.at[:, :, pl.ds(pl.multiple_of(home, 128), width)],
                gamma_sems.at[n],
            )
        )
        if n < len(blocks):
            reads[n].wait()
            writes[n].start()
        writes[-1].start()
    for copy in writes:
        copy.wait()


def close(other, whole, kept, received):
    batch, double = received[0].shape
    any_space = pl.BlockSpec(memory_space=pl.ANY)
    in_vmem = pl.BlockSpec(memory_space=pltpu.VMEM)
    return pl.pallas_call(
        close_kernel,
        out_shape=(
            jax.ShapeDtypeStruct(whole.shape, whole.dtype),
            jax.ShapeDtypeStruct((batch, 2, CHUNKS * double), jnp.float32),
        ),
        in_specs=[any_space, any_space] + [in_vmem] * (2 * CHUNKS),
        out_specs=(any_space, any_space),
        scratch_shapes=[
            pltpu.VMEM(other.shape, other.dtype),
            pltpu.VMEM((2 * CHUNKS, batch, 2, double // 2), jnp.float32),
            pltpu.SemaphoreType.DMA((2, 2, 2)),
            pltpu.SemaphoreType.DMA((2 * CHUNKS,)),
        ],
        input_output_aliases={1: 0},
        compiler_params=pltpu.CompilerParams(vmem_limit_bytes=48 * 2**20),
        cost_estimate=pl.CostEstimate(
            flops=0, bytes_accessed=4 * other.size + 16 * batch * double * CHUNKS, transcendentals=0
        ),
    )(other, whole, *kept, *received)


def swap(x):
    return lax.ppermute(x, "occ", [(0, 1), (1, 0)])


def planar(x, offset):
    return lax.ppermute(x, "row", [(r, r ^ offset) for r in range(4)])


def hop_up(x, first):
    return lax.ppermute(x, "col", [(c, c + 1) for c in range(first, 3)])


def hop_down(x, first):
    return lax.ppermute(x, "col", [(3 - c, 2 - c) for c in range(first, 3)])


def pairs(x):
    return lax.ppermute(x, "col", [(0, 1), (1, 0), (2, 3), (3, 2)])


def across(x):
    return lax.ppermute(x, "col", [(1, 2), (2, 1)])


def outward(x):
    return lax.ppermute(x, "col", [(1, 0), (2, 3)])


def inward(x):
    return lax.ppermute(x, "col", [(0, 1), (3, 2)])


def tie(*arrays):
    return lax.optimization_barrier(arrays)


def planned(bra_factor, ket_factor, occ_energy, virt_energy):
    batch, _, a_width = bra_factor.shape
    b_width = ket_factor.shape[2]
    half = a_width // 2
    width = half // CHUNKS
    me, row_index, col_index = (lax.axis_index(name) for name in ("occ", "row", "col"))

    bra_kept, bra_given = pick(bra_factor.reshape(batch, 2 * a_width))
    ket_own = ket_factor.reshape(batch, 2 * b_width)
    bra = jnp.stack([bra_kept, swap(bra_given)], axis=1)
    ket_x = planar(ket_own, 1)
    ket_y = planar(ket_own, 2)
    cut = batch // 2
    pieces = ((0, 0, batch), (1, 0, batch), (2, 0, batch), (3, 0, cut), (3, cut, batch - cut))

    blocks = [bra[:TOGETHER], bra[TOGETHER:]]
    ups, downs = [[hop_up(blocks[0], 0)], []], [[hop_down(blocks[0], 0)], []]
    ket_swapped = swap(ket_own)
    ups[0].append(hop_up(ups[0][0], 1))
    downs[0].append(hop_down(downs[0][0], 1))
    ket_x, ket_y, ups[0][1], downs[0][1], ket_swapped = tie(
        ket_x, ket_y, ups[0][1], downs[0][1], ket_swapped
    )
    part_x, part_y, late_x, late_y = tie(ket_x[:cut], ket_y[cut:], ket_x, ket_y)
    ket_far_y, ket_far_x = planar(part_x, 2), planar(part_y, 1)
    ups[0].append(hop_up(ups[0][1], 2))
    downs[0].append(hop_down(downs[0][1], 2))
    mine = [ket_own, ket_x, ket_y]
    ket = [ket_swapped, swap(late_x), swap(late_y)]
    ups[0][2], downs[0][2], *far_pieces = tie(ups[0][2], downs[0][2], ket_far_y, ket_far_x)
    ket = mine + far_pieces + ket + [swap(piece) for piece in far_pieces]
    ups[0][2], downs[0][2], block = tie(ups[0][2], downs[0][2], blocks[1])
    ups[1].append(hop_up(block, 0))
    downs[1].append(hop_down(block, 0))
    energies = (occ_energy, virt_energy[None, :])

    def up_cast(x):
        return x.astype(jnp.float32)

    near = lax.bitwise_and(col_index, 1)
    held = ()
    own, pair, far, one, two, three, kept, received = ({} for _ in range(8))

    def cross(k):
        two[k] = across((far[k] + up_cast(one[k])).astype(jnp.bfloat16))

    def exchange(k):
        theirs = lax.dynamic_index_in_dim(two[k], 1 - near, 0, keepdims=False)
        three[k] = pairs((pair[k] + up_cast(theirs)).astype(jnp.bfloat16))

    def finish(k):
        ours = lax.dynamic_index_in_dim(two[k], near, 0, keepdims=False)
        total = own[k] + up_cast(ours) + up_cast(three[k])
        kept[k] = total[:batch]
        received[k] = swap(total[batch:])

    for tick in range(CHUNKS + 3):
        if tick < CHUNKS:
            k = tick
            group = k // TOGETHER
            arrived = [bra[k], *ups[group], *downs[group]]
            if k >= 2:
                one[k - 2], arrived[0] = tie(one[k - 2], arrived[0])
            if k >= 3:
                exchange(k - 3)
                three[k - 3], arrived[0] = tie(three[k - 3], arrived[0])
            results = run_chunk(k, ket, pieces, arrived, energies, held)
            held = results[:2]
            own[k], pair[k], far[k], send = results[2:6]
            if k == 0:
                ket = [results[6]]
            one[k] = inward(send)
            if k < 2:
                own[k], up, down = tie(own[k], ups[1][k], downs[1][k])
                ups[1].append(hop_up(up, k + 1))
                downs[1].append(hop_down(down, k + 1))
            if k == 1:
                far[0], own[1] = tie(far[0], own[1])
        if 1 <= tick <= CHUNKS:
            cross(tick - 1)
    last = CHUNKS - 1
    one[last], two[1] = tie(one[last], two[1])
    for k in range(1, CHUNKS):
        exchange(k)
    for k in range(CHUNKS):
        finish(k)
    every = range(CHUNKS)
    return close(swap(held[1]), held[0], [kept[k] for k in every], [received[k] for k in every])


def solution(mesh):
    sizes = mesh.shape

    def on_device(bra_factor, ket_factor, occ_energy, virt_energy):
        fits = (
            sizes["occ"] == 2
            and sizes["row"] == 4
            and sizes["col"] == 4
            and bra_factor.shape[2] % (256 * CHUNKS) == 0
            and ket_factor.shape[2] % 512 == 0
            and bra_factor.shape[0] % 128 == 0
        )
        body = planned if fits else general
        return body(bra_factor, ket_factor, occ_energy, virt_energy)

    placed = (P(("occ", "col"), None, "row"), P(("occ", "row"), None, "col"), P(), P())
    return jax.shard_map(
        on_device,
        mesh=mesh,
        in_specs=placed,
        out_specs=(P(None, None, "row", "col"), P(("occ", "col"), None, "row")),
        check_vma=False,
    )
```

profile of v0, /device:TPU:0, one launch (start us, length us, event | category | flops | bytes accessed | tf_op | source)
XLA Modules:
  0.0 253.5 jit_solution(677794486247693686)
XLA Ops:
  0.6 1.8 copy.14
  2.9 0.5 collective-permute-start.2
  3.4 0.5 copy-done.25
  4.3 0.5 collective-permute-start.7
  4.9 2.6 %collective-permute-start.1 = (bf16[384,2048]{1,0:T(8,128)(2,1)S(1)}, bf16[384,2048]{1,0:T(8,128)(2,1)S(1)}, u32[]{:S(2)}, u32[]{:S(2)}) collective-permute-start(bf16[384,2048]{1,0:T(8,128)(2,1)S(1)} %bitcast.43), channel_id=1, source_target_pairs={{0,8},{4,12},{8,0},{12,4},{1,9},{5,13},{9,1},{13,5},{2,10},{6,14},... | collective-permute-start | bytes 4718600 | tf_op jit(solution)/shard_map/ppermute | solution.py:336
  7.6 1.3 collective-permute-start.5
  8.9 1.6 collective-permute-start
  10.5 4.6 %collective-permute-start.3 = (bf16[2,2,2,384,128]{4,3,2,1,0:T(8,128)(2,1)S(1)}, bf16[2,2,2,384,128]{4,3,2,1,0:T(8,128)(2,1)S(1)}, u32[]{:S(2)}, u32[]{:S(2)}) collective-permute-start(bf16[2,2,2,384,128]{4,3,2,1,0:T(8,128)(2,1)S(1)} %get-tuple-element.119), channel_id=1, source_target_pairs={{0,1},{1,2},{2,3},{4,5},{5,6},{6,7},{8,9},{9,10},{10,11},{12,13},{... | collective-permute-start | bytes 2359304 | tf_op jit(solution)/shard_map/ppermute | solution.py:340
  15.0 14.1 %collective-permute-done.5.refs_14_.refs_5_ = bf16[2,2,2,384,128]{4,3,2,1,0:T(8,128)(2,1)S(1)} collective-permute-done((bf16[2,2,2,384,128]{4,3,2,1,0:T(8,128)(2,1)S(1)}, bf16[2,2,2,384,128]{4,3,2,1,0:T(8,128)(2,1)S(1)}, u32[]{:S(2)}, u32[]{:S(2)}) %collective-permute-start.5) | collective-permute-done | bytes 786464 | tf_op jit(solution)/shard_map/ppermute | solution.py:344
  29.1 1.3 collective-permute-start.6
  30.4 1.2 collective-permute-done.3.refs_11_.refs_2_
  31.6 0.7 collective-permute-start.4
  32.3 10.2 %collective-permute-done.1.refs_2_ = bf16[384,2048]{1,0:T(8,128)(2,1)S(1)} collective-permute-done((bf16[384,2048]{1,0:T(8,128)(2,1)S(1)}, bf16[384,2048]{1,0:T(8,128)(2,1)S(1)}, u32[]{:S(2)}, u32[]{:S(2)}) %collective-permute-start.1) | collective-permute-done | bytes 1572896 | tf_op jit(solution)/shard_map/ppermute | solution.py:336
  42.4 3.0 %collective-permute-done.refs_1_ = bf16[384,2048]{1,0:T(8,128)(2,1)S(1)} collective-permute-done((bf16[384,2048]{1,0:T(8,128)(2,1)S(1)}, bf16[384,2048]{1,0:T(8,128)(2,1)S(1)}, u32[]{:S(2)}, u32[]{:S(2)}) %collective-permute-start) | collective-permute-done | bytes 1572896 | tf_op jit(solution)/shard_map/ppermute | solution.py:336
  45.4 4.3 %collective-permute-done.6.refs_15_.refs_6_ = bf16[2,2,2,384,128]{4,3,2,1,0:T(8,128)(2,1)S(1)} collective-permute-done((bf16[2,2,2,384,128]{4,3,2,1,0:T(8,128)(2,1)S(1)}, bf16[2,2,2,384,128]{4,3,2,1,0:T(8,128)(2,1)S(1)}, u32[]{:S(2)}, u32[]{:S(2)}) %collective-permute-start.6) | collective-permute-done | bytes 786464 | tf_op jit(solution)/shard_map/ppermute | solution.py:344
  49.9 0.8 collective-permute-start.10
  50.7 1.5 collective-permute-start.11
  52.2 0.7 collective-permute-start.8
  52.9 1.3 collective-permute-start.9
  54.3 13.6 %collective-permute-done.10.refs_3_ = bf16[192,2048]{1,0:T(8,128)(2,1)S(1)} collective-permute-done((bf16[192,2048]{1,0:T(8,128)(2,1)S(1)}, bf16[192,2048]{1,0:T(8,128)(2,1)S(1)}, u32[]{:S(2)}, u32[]{:S(2)}) %collective-permute-start.10) | collective-permute-done | bytes 786464 | tf_op jit(solution)/shard_map/ppermute | solution.py:336
  68.3 4.0 %collective-permute-done.9.refs_16_.refs_7_ = bf16[2,2,2,384,128]{4,3,2,1,0:T(8,128)(2,1)S(1)} collective-permute-done((bf16[2,2,2,384,128]{4,3,2,1,0:T(8,128)(2,1)S(1)}, bf16[2,2,2,384,128]{4,3,2,1,0:T(8,128)(2,1)S(1)}, u32[]{:S(2)}, u32[]{:S(2)}) %collective-permute-start.9) | collective-permute-done | bytes 786464 | tf_op jit(solution)/shard_map/ppermute | solution.py:344
  72.2 0.5 collective-permute-start.15
  72.8 1.4 collective-permute-start.17
  74.5 4.3 %collective-permute-start.16 = (bf16[2,2,2,384,128]{4,3,2,1,0:T(8,128)(2,1)S(1)}, bf16[2,2,2,384,128]{4,3,2,1,0:T(8,128)(2,1)S(1)}, u32[]{:S(2)}, u32[]{:S(2)}) collective-permute-start(bf16[2,2,2,384,128]{4,3,2,1,0:T(8,128)(2,1)S(1)} %get-tuple-element.82), channel_id=1, source_target_pairs={{0,1},{1,2},{2,3},{4,5},{5,6},{6,7},{8,9},{9,10},{10,11},{12,13},{... | collective-permute-start | bytes 2359304 | tf_op jit(solution)/shard_map/ppermute | solution.py:340
  78.8 0.9 fusion.16
  79.7 14.1 %shard_map.60 = (bf16[2,2,1024,1024]{3,2,1,0:T(8,128)(2,1)}, bf16[2,2,512,1024]{3,2,1,0:T(8,128)(2,1)}, f32[768,256]{1,0:T(8,128)S(1)}, f32[768,256]{1,0:T(8,128...) custom-call(bf16[384,2048]{1,0:T(8,128)(2,1)S(1)} %bitcast.45, ...), custom_call_target="tpu_custom_call" | custom-call | flops 6442450944 | bytes 12582912 | tf_op jit(solution)/shard_map/pallas_call | solution.py:205
  94.2 1.2 collective-permute-done.16.refs_2_
  95.4 0.7 collective-permute-start.18
  96.1 1.3 collective-permute-start.19
  97.4 7.5 %collective-permute-start.20 = (bf16[2,768,256]{2,1,0:T(8,128)(2,1)S(1)}, bf16[2,768,256]{2,1,0:T(8,128)(2,1)S(1)}, u32[]{:S(2)}, u32[]{:S(2)}) collective-permute-start(bf16[2,768,256]{2,1,0:T(8,128)(2,1)S(1)} %get-tuple-element.87), channel_id=1, source_target_pairs={{0,1},{3,2},{4,5},{7,6},{8,9},{11,10},{12,13},{15,14},{16,17},{19,... | collective-permute-start | bytes 2359304 | tf_op jit(solution)/shard_map/ppermute | solution.py:360
  104.9 12.0 %shard_map.61 = (bf16[2,2,1024,1024]{3,2,1,0:T(8,128)(2,1)}, bf16[2,2,512,1024]{3,2,1,0:T(8,128)(2,1)}, f32[768,256]{1,0:T(8,128)S(1)}, f32[768,256]{1,0:T(8,128...) custom-call(bf16[3072,2048]{1,0:T(8,128)(2,1)} %get-tuple-element.75, ...), custom_call_target="tpu_custom_call", output_to_operand_aliasing={{0}: (10, {}), {1}: (11, {})} | custom-call | flops 6442450944 | bytes 12582912 | tf_op jit(solution)/shard_map/pallas_call | solution.py:205
  117.0 2.2 collective-permute-start.23
  119.2 0.5 collective-permute-done.19.refs_6_
  119.7 3.2 %collective-permute-done.20 = bf16[2,768,256]{2,1,0:T(8,128)(2,1)S(1)} collective-permute-done((bf16[2,768,256]{2,1,0:T(8,128)(2,1)S(1)}, bf16[2,768,256]{2,1,0:T(8,128)(2,1)S(1)}, u32[]{:S(2)}, u32[]{:S(2)}) %collective-permute-start.20) | collective-permute-done | bytes 786464 | tf_op jit(solution)/shard_map/ppermute | solution.py:360
  122.8 1.1 add_convert_fusion.3
  123.9 1.6 collective-permute-start.21
  125.5 1.6 collective-permute-start.24
  127.1 1.3 collective-permute-start.25
  128.4 9.4 %collective-permute-done.23 = bf16[2,768,256]{2,1,0:T(8,128)(2,1)} collective-permute-done((bf16[2,768,256]{2,1,0:T(8,128)(2,1)}, bf16[2,768,256]{2,1,0:T(8,128)(2,1)}, u32[]{:S(2)}, u32[]{:S(2)}) %collective-permute-start.23) | collective-permute-done | bytes 786464 | tf_op jit(solution)/shard_map/ppermute | solution.py:360
  137.8 1.3 fusion.9
  139.1 6.4 %collective-permute-start.22 = (bf16[768,256]{1,0:T(8,128)(2,1)S(1)}, bf16[768,256]{1,0:T(8,128)(2,1)S(1)}, u32[]{:S(2)}, u32[]{:S(2)}) collective-permute-start(bf16[768,256]{1,0:T(8,128)(2,1)S(1)} %fusion.9), channel_id=1, source_target_pairs={{0,1},{1,0},{2,3},{3,2},{4,5},{5,4},{6,7},{7,6},{8,9},{9,8},{10,11... | collective-permute-start | bytes 1179656 | tf_op jit(solution)/shard_map/ppermute | solution.py:348
  145.6 4.9 %collective-permute-done.25.refs_7_ = bf16[2,2,2,384,128]{4,3,2,1,0:T(8,128)(2,1)} collective-permute-done((bf16[2,2,2,384,128]{4,3,2,1,0:T(8,128)(2,1)S(1)}, bf16[2,2,2,384,128]{4,3,2,1,0:T(8,128)(2,1)}, u32[]{:S(2)}, u32[]{:S(2)}) %collective-permute-start.25) | collective-permute-done | bytes 786464 | tf_op jit(solution)/shard_map/ppermute | solution.py:344
  150.5 12.0 %shard_map.62 = (bf16[2,2,1024,1024]{3,2,1,0:T(8,128)(2,1)}, bf16[2,2,512,1024]{3,2,1,0:T(8,128)(2,1)}, f32[768,256]{1,0:T(8,128)S(1)}, f32[768,256]{1,0:T(8,128...) custom-call(bf16[3072,2048]{1,0:T(8,128)(2,1)} %get-tuple-element.75, ...), custom_call_target="tpu_custom_call", output_to_operand_aliasing={{0}: (10, {}), {1}: (11, {})} | custom-call | flops 6442450944 | bytes 12582912 | tf_op jit(solution)/shard_map/pallas_call | solution.py:205
  162.5 1.2 copy-done.4
  163.7 0.9 copy-done.13
  164.6 0.9 copy-done.20
  165.5 2.3 collective-permute-start.30
  167.8 0.8 copy-done.26
  168.5 13.2 %shard_map.63 = (bf16[2,2,1024,1024]{3,2,1,0:T(8,128)(2,1)}, bf16[2,2,512,1024]{3,2,1,0:T(8,128)(2,1)}, f32[768,256]{1,0:T(8,128)S(1)}, f32[768,256]{1,0:T(8,128...) custom-call(bf16[3072,2048]{1,0:T(8,128)(2,1)} %get-tuple-element.75, ...), custom_call_target="tpu_custom_call", output_to_operand_aliasing={{0}: (10, {}), {1}: (11, {})} | custom-call | flops 6442450944 | bytes 12582912 | tf_op jit(solution)/shard_map/pallas_call | solution.py:205
  181.8 2.9 %add_convert_fusion.2 = bf16[2,768,256]{2,1,0:T(8,128)(2,1)} fusion(f32[2,768,256]{2,1,0:T(8,128)S(1)} %copy-done.1, bf16[2,768,256]{2,1,0:T(8,128)(2,1)} %collective-permute-done.23), kind=kLoop, calls=%fused_computation.12 | loop fusion | flops 1179648 | bytes 3145728 | tf_op jit(solution)/shard_map/convert_element_type | solution.py:411
  184.7 0.8 collective-permute-start.28
  185.6 2.5 collective-permute-start.27
  188.1 1.1 fusion.8
  189.2 1.4 add_convert_fusion.1
  190.6 0.8 collective-permute-start.31
  191.5 12.9 %collective-permute-done.27 = bf16[2,768,256]{2,1,0:T(8,128)(2,1)} collective-permute-done((bf16[2,768,256]{2,1,0:T(8,128)(2,1)}, bf16[2,768,256]{2,1,0:T(8,128)(2,1)}, u32[]{:S(2)}, u32[]{:S(2)}) %collective-permute-start.27) | collective-permute-done | bytes 786464 | tf_op jit(solution)/shard_map/ppermute | solution.py:360
  204.4 2.5 %collective-permute-start.29 = (bf16[768,256]{1,0:T(8,128)(2,1)S(1)}, bf16[768,256]{1,0:T(8,128)(2,1)S(1)}, u32[]{:S(2)}, u32[]{:S(2)}) collective-permute-start(bf16[768,256]{1,0:T(8,128)(2,1)S(1)} %fusion.6), channel_id=1, source_target_pairs={{0,1},{1,0},{2,3},{3,2},{4,5},{5,4},{6,7},{7,6},{8,9},{9,8},{10,11... | collective-permute-start | bytes 1179656 | tf_op jit(solution)/shard_map/ppermute | solution.py:348
  207.0 1.3 add_convert_fusion
  208.4 0.8 collective-permute-start.33
  209.6 13.3 %collective-permute-start.32 = (bf16[768,256]{1,0:T(8,128)(2,1)S(1)}, bf16[768,256]{1,0:T(8,128)(2,1)S(1)}, u32[]{:S(2)}, u32[]{:S(2)}) collective-permute-start(bf16[768,256]{1,0:T(8,128)(2,1)S(1)} %fusion.4), channel_id=1, source_target_pairs={{0,1},{1,0},{2,3},{3,2},{4,5},{5,4},{6,7},{7,6},{8,9},{9,8},{10,11... | collective-permute-start | bytes 1179656 | tf_op jit(solution)/shard_map/ppermute | solution.py:348
  223.3 15.4 %collective-permute-start.34 = (bf16[768,256]{1,0:T(8,128)(2,1)S(1)}, bf16[768,256]{1,0:T(8,128)(2,1)S(1)}, u32[]{:S(2)}, u32[]{:S(2)}) collective-permute-start(bf16[768,256]{1,0:T(8,128)(2,1)S(1)} %fusion.2), channel_id=1, source_target_pairs={{0,1},{1,0},{2,3},{3,2},{4,5},{5,4},{6,7},{7,6},{8,9},{9,8},{10,11... | collective-permute-start | bytes 1179656 | tf_op jit(solution)/shard_map/ppermute | solution.py:348
  238.9 8.0 %collective-permute-done.34 = bf16[768,256]{1,0:T(8,128)(2,1)S(1)} collective-permute-done((bf16[768,256]{1,0:T(8,128)(2,1)S(1)}, bf16[768,256]{1,0:T(8,128)(2,1)S(1)}, u32[]{:S(2)}, u32[]{:S(2)}) %collective-permute-start.34) | collective-permute-done | bytes 393248 | tf_op jit(solution)/shard_map/ppermute | solution.py:348
  247.2 1.7 collective-permute-done.38.refs_9_
  248.9 4.3 %shard_map.64 = (bf16[2,2,1024,1024]{3,2,1,0:T(8,128)(2,1)}, f32[384,2,1024]{2,1,0:T(2,128)}) custom-call(bf16[2,2,512,1024]{3,2,1,0:T(8,128)(2,1)} %collective-permute-done.26.refs_0_, bf16[2,2,1024,1024]{3,2,1,0:T(8,128)(2,1)} %get-tuple-element.99.refs_1_, f32[384,256]{1,0:T(8,128)S(1)} %get-tuple-element.127.refs_2_, ...), custom_call_target="tpu_custom_call", output_to_operand_aliasing={{0}: (1, {})} | custom-call | bytes 14680064 | tf_op jit(solution)/shard_map/pallas_call | solution.py:309
  (98 shorter events, 3.8 us)
Async XLA Ops:
  2.5 1.4 copy-start.25
  2.9 4.5 %collective-permute-start.2 = (bf16[4,2,384,128]{3,2,1,0:T(8,128)(2,1)S(1)}, bf16[4,2,384,128]{3,2,1,0:T(8,128)(2,1)S(1)}, u32[]{:S(2)}, u32[]{:S(2)}) collective-permute-start(bf16[4,2,384,128]{3,2,1,0:T(8,128)(2,1)S(1)} %get-tuple-element.59), channel_id=1, source_target_pairs={{0,16},{16,0},{1,17},{17,1},{2,18},{18,2},{3,19},{19,3},{4,20},{20... | collective-permute-start | bytes 2359304 | tf_op jit(solution)/shard_map/ppermute | solution.py:332
  4.3 27.9 %collective-permute-start.7 = (bf16[384,2048]{1,0:T(8,128)(2,1)S(1)}, bf16[384,2048]{1,0:T(8,128)(2,1)S(1)}, u32[]{:S(2)}, u32[]{:S(2)}) collective-permute-start(bf16[384,2048]{1,0:T(8,128)(2,1)S(1)} %bitcast.42), channel_id=1, source_target_pairs={{0,16},{16,0},{1,17},{17,1},{2,18},{18,2},{3,19},{19,3},{4,20},{20... | collective-permute-start | bytes 4718600 | tf_op jit(solution)/shard_map/ppermute | solution.py:332
  4.9 37.6 %collective-permute-start.1 = (bf16[384,2048]{1,0:T(8,128)(2,1)S(1)}, bf16[384,2048]{1,0:T(8,128)(2,1)S(1)}, u32[]{:S(2)}, u32[]{:S(2)}) collective-permute-start(bf16[384,2048]{1,0:T(8,128)(2,1)S(1)} %bitcast.43), channel_id=1, source_target_pairs={{0,8},{4,12},{8,0},{12,4},{1,9},{5,13},{9,1},{13,5},{2,10},{6,14},... | collective-permute-start | bytes 4718600 | tf_op jit(solution)/shard_map/ppermute | solution.py:336
  7.6 21.5 %collective-permute-start.5 = (bf16[2,2,2,384,128]{4,3,2,1,0:T(8,128)(2,1)S(1)}, bf16[2,2,2,384,128]{4,3,2,1,0:T(8,128)(2,1)S(1)}, u32[]{:S(2)}, u32[]{:S(2)}) collective-permute-start(bf16[2,2,2,384,128]{4,3,2,1,0:T(8,128)(2,1)S(1)} %get-tuple-element.119), channel_id=1, source_target_pairs={{3,2},{2,1},{1,0},{7,6},{6,5},{5,4},{11,10},{10,9},{9,8},{15,14},{... | collective-permute-start | bytes 2359304 | tf_op jit(solution)/shard_map/ppermute | solution.py:344
  8.9 36.5 %collective-permute-start = (bf16[384,2048]{1,0:T(8,128)(2,1)S(1)}, bf16[384,2048]{1,0:T(8,128)(2,1)S(1)}, u32[]{:S(2)}, u32[]{:S(2)}) collective-permute-start(bf16[384,2048]{1,0:T(8,128)(2,1)S(1)} %bitcast.44), channel_id=1, source_target_pairs={{0,4},{4,0},{8,12},{12,8},{1,5},{5,1},{9,13},{13,9},{2,6},{6,2},{1... | collective-permute-start | bytes 4718600 | tf_op jit(solution)/shard_map/ppermute | solution.py:336
  10.5 21.1 %collective-permute-start.3 = (bf16[2,2,2,384,128]{4,3,2,1,0:T(8,128)(2,1)S(1)}, bf16[2,2,2,384,128]{4,3,2,1,0:T(8,128)(2,1)S(1)}, u32[]{:S(2)}, u32[]{:S(2)}) collective-permute-start(bf16[2,2,2,384,128]{4,3,2,1,0:T(8,128)(2,1)S(1)} %get-tuple-element.119), channel_id=1, source_target_pairs={{0,1},{1,2},{2,3},{4,5},{5,6},{6,7},{8,9},{9,10},{10,11},{12,13},{... | collective-permute-start | bytes 2359304 | tf_op jit(solution)/shard_map/ppermute | solution.py:340
  29.1 20.7 %collective-permute-start.6 = (bf16[2,2,2,384,128]{4,3,2,1,0:T(8,128)(2,1)S(1)}, bf16[2,2,2,384,128]{4,3,2,1,0:T(8,128)(2,1)S(1)}, u32[]{:S(2)}, u32[]{:S(2)}) collective-permute-start(bf16[2,2,2,384,128]{4,3,2,1,0:T(8,128)(2,1)S(1)} %collective-permute-done.5.refs_14_.refs_5_), channel_id=1, source_target_pairs={{2,1},{1,0},{6,5},{5,4},{10,9},{9,8},{14,13},{13,12},{18,17},{17,1... | collective-permute-start | bytes 2359304 | tf_op jit(solution)/shard_map/ppermute | solution.py:344
  31.6 18.2 %collective-permute-start.4 = (bf16[2,2,2,384,128]{4,3,2,1,0:T(8,128)(2,1)S(1)}, bf16[2,2,2,384,128]{4,3,2,1,0:T(8,128)(2,1)S(1)}, u32[]{:S(2)}, u32[]{:S(2)}) collective-permute-start(bf16[2,2,2,384,128]{4,3,2,1,0:T(8,128)(2,1)S(1)} %collective-permute-done.3.refs_11_.refs_2_), channel_id=1, source_target_pairs={{1,2},{2,3},{5,6},{6,7},{9,10},{10,11},{13,14},{14,15},{17,18},{18... | collective-permute-start | bytes 2359304 | tf_op jit(solution)/shard_map/ppermute | solution.py:340
  49.9 17.9 %collective-permute-start.10 = (bf16[192,2048]{1,0:T(8,128)(2,1)S(1)}, bf16[192,2048]{1,0:T(8,128)(2,1)S(1)}, u32[]{:S(2)}, u32[]{:S(2)}) collective-permute-start(bf16[192,2048]{1,0:T(8,128)(2,1)S(1)} %slice.49), channel_id=1, source_target_pairs={{0,8},{4,12},{8,0},{12,4},{1,9},{5,13},{9,1},{13,5},{2,10},{6,14},... | collective-permute-start | bytes 2359304 | tf_op jit(solution)/shard_map/ppermute | solution.py:336
  50.7 17.6 %collective-permute-start.11 = (bf16[192,2048]{1,0:T(8,128)(2,1)S(1)}, bf16[192,2048]{1,0:T(8,128)(2,1)S(1)}, u32[]{:S(2)}, u32[]{:S(2)}) collective-permute-start(bf16[192,2048]{1,0:T(8,128)(2,1)S(1)} %slice.50), channel_id=1, source_target_pairs={{0,4},{4,0},{8,12},{12,8},{1,5},{5,1},{9,13},{13,9},{2,6},{6,2},{1... | collective-permute-start | bytes 2359304 | tf_op jit(solution)/shard_map/ppermute | solution.py:336
  52.2 16.1 %collective-permute-start.8 = (bf16[2,2,2,384,128]{4,3,2,1,0:T(8,128)(2,1)S(1)}, bf16[2,2,2,384,128]{4,3,2,1,0:T(8,128)(2,1)S(1)}, u32[]{:S(2)}, u32[]{:S(2)}) collective-permute-start(bf16[2,2,2,384,128]{4,3,2,1,0:T(8,128)(2,1)S(1)} %collective-permute-done.4.refs_12_.refs_3_), channel_id=1, source_target_pairs={{2,3},{6,7},{10,11},{14,15},{18,19},{22,23},{26,27},{30,31}} | collective-permute-start | bytes 2359304 | tf_op jit(solution)/shard_map/ppermute | solution.py:340
  52.9 19.3 %collective-permute-start.9 = (bf16[2,2,2,384,128]{4,3,2,1,0:T(8,128)(2,1)S(1)}, bf16[2,2,2,384,128]{4,3,2,1,0:T(8,128)(2,1)S(1)}, u32[]{:S(2)}, u32[]{:S(2)}) collective-permute-start(bf16[2,2,2,384,128]{4,3,2,1,0:T(8,128)(2,1)S(1)} %collective-permute-done.6.refs_15_.refs_6_), channel_id=1, source_target_pairs={{1,0},{5,4},{9,8},{13,12},{17,16},{21,20},{25,24},{29,28}} | collective-permute-start | bytes 2359304 | tf_op jit(solution)/shard_map/ppermute | solution.py:344
  54.2 25.5 %collective-permute-start.12 = (bf16[384,2048]{1,0:T(8,128)(2,1)S(1)}, bf16[384,2048]{1,0:T(8,128)(2,1)S(1)}, u32[]{:S(2)}, u32[]{:S(2)}) collective-permute-start(bf16[384,2048]{1,0:T(8,128)(2,1)S(1)} %collective-permute-done.refs_1_), channel_id=1, source_target_pairs={{0,16},{16,0},{1,17},{17,1},{2,18},{18,2},{3,19},{19,3},{4,20},{20... | collective-permute-start | bytes 4718600 | tf_op jit(solution)/shard_map/ppermute | solution.py:332
  67.8 11.8 %collective-permute-start.13 = (bf16[384,2048]{1,0:T(8,128)(2,1)S(1)}, bf16[384,2048]{1,0:T(8,128)(2,1)S(1)}, u32[]{:S(2)}, u32[]{:S(2)}) collective-permute-start(bf16[384,2048]{1,0:T(8,128)(2,1)S(1)} %collective-permute-done.1.refs_2_), channel_id=1, source_target_pairs={{0,16},{16,0},{1,17},{17,1},{2,18},{18,2},{3,19},{19,3},{4,20},{20... | collective-permute-start | bytes 4718600 | tf_op jit(solution)/shard_map/ppermute | solution.py:332
  72.2 2.3 collective-permute-start.14
  72.2 7.4 %collective-permute-start.15 = (bf16[192,2048]{1,0:T(8,128)(2,1)S(1)}, bf16[192,2048]{1,0:T(8,128)(2,1)S(1)}, u32[]{:S(2)}, u32[]{:S(2)}) collective-permute-start(bf16[192,2048]{1,0:T(8,128)(2,1)S(1)} %collective-permute-done.11.refs_4_), channel_id=1, source_target_pairs={{0,16},{16,0},{1,17},{17,1},{2,18},{18,2},{3,19},{19,3},{4,20},{20... | collective-permute-start | bytes 2359304 | tf_op jit(solution)/shard_map/ppermute | solution.py:332
  72.8 6.9 %copy-start.22 = (f32[4096]{0:T(1024)S(1)}, f32[4096]{0:T(1024)}, u32[]{:S(2)}) copy-start(f32[4096]{0:T(1024)} %param.7) | copy-start | bytes 49156
  72.8 6.9 %copy-start.23 = (f32[2]{0:T(128)S(1)}, f32[2]{0:T(128)}, u32[]{:S(2)}) copy-start(f32[2]{0:T(128)} %refs_8_.5) | copy-start | bytes 28
  72.8 21.5 %collective-permute-start.17 = (bf16[2,2,2,384,128]{4,3,2,1,0:T(8,128)(2,1)S(1)}, bf16[2,2,2,384,128]{4,3,2,1,0:T(8,128)(2,1)S(1)}, u32[]{:S(2)}, u32[]{:S(2)}) collective-permute-start(bf16[2,2,2,384,128]{4,3,2,1,0:T(8,128)(2,1)S(1)} %get-tuple-element.82), channel_id=1, source_target_pairs={{3,2},{2,1},{1,0},{7,6},{6,5},{5,4},{11,10},{10,9},{9,8},{15,14},{... | collective-permute-start | bytes 2359304 | tf_op jit(solution)/shard_map/ppermute | solution.py:344
  74.5 20.9 %collective-permute-start.16 = (bf16[2,2,2,384,128]{4,3,2,1,0:T(8,128)(2,1)S(1)}, bf16[2,2,2,384,128]{4,3,2,1,0:T(8,128)(2,1)S(1)}, u32[]{:S(2)}, u32[]{:S(2)}) collective-permute-start(bf16[2,2,2,384,128]{4,3,2,1,0:T(8,128)(2,1)S(1)} %get-tuple-element.82), channel_id=1, source_target_pairs={{0,1},{1,2},{2,3},{4,5},{5,6},{6,7},{8,9},{9,10},{10,11},{12,13},{... | collective-permute-start | bytes 2359304 | tf_op jit(solution)/shard_map/ppermute | solution.py:340
  93.8 23.1 %copy-start.9 = (f32[768,256]{1,0:T(8,128)}, f32[768,256]{1,0:T(8,128)S(1)}, u32[]{:S(2)}) copy-start(f32[768,256]{1,0:T(8,128)S(1)} %get-tuple-element.100) | copy-start | bytes 2359300
  93.8 23.1 %copy-start.19 = (f32[768,256]{1,0:T(8,128)}, f32[768,256]{1,0:T(8,128)S(1)}, u32[]{:S(2)}) copy-start(f32[768,256]{1,0:T(8,128)S(1)} %get-tuple-element.76) | copy-start | bytes 2359300
  95.4 23.8 %collective-permute-start.18 = (bf16[2,2,2,384,128]{4,3,2,1,0:T(8,128)(2,1)S(1)}, bf16[2,2,2,384,128]{4,3,2,1,0:T(8,128)(2,1)S(1)}, u32[]{:S(2)}, u32[]{:S(2)}) collective-permute-start(bf16[2,2,2,384,128]{4,3,2,1,0:T(8,128)(2,1)S(1)} %collective-permute-done.16.refs_2_), channel_id=1, source_target_pairs={{1,2},{2,3},{5,6},{6,7},{9,10},{10,11},{13,14},{14,15},{17,18},{18... | collective-permute-start | bytes 2359304 | tf_op jit(solution)/shard_map/ppermute | solution.py:340
  96.1 23.5 %collective-permute-start.19 = (bf16[2,2,2,384,128]{4,3,2,1,0:T(8,128)(2,1)S(1)}, bf16[2,2,2,384,128]{4,3,2,1,0:T(8,128)(2,1)S(1)}, u32[]{:S(2)}, u32[]{:S(2)}) collective-permute-start(bf16[2,2,2,384,128]{4,3,2,1,0:T(8,128)(2,1)S(1)} %collective-permute-done.17.refs_5_), channel_id=1, source_target_pairs={{2,1},{1,0},{6,5},{5,4},{10,9},{9,8},{14,13},{13,12},{18,17},{17,1... | collective-permute-start | bytes 2359304 | tf_op jit(solution)/shard_map/ppermute | solution.py:344
  97.4 25.4 %collective-permute-start.20 = (bf16[2,768,256]{2,1,0:T(8,128)(2,1)S(1)}, bf16[2,768,256]{2,1,0:T(8,128)(2,1)S(1)}, u32[]{:S(2)}, u32[]{:S(2)}) collective-permute-start(bf16[2,768,256]{2,1,0:T(8,128)(2,1)S(1)} %get-tuple-element.87), channel_id=1, source_target_pairs={{0,1},{3,2},{4,5},{7,6},{8,9},{11,10},{12,13},{15,14},{16,17},{19,... | collective-permute-start | bytes 2359304 | tf_op jit(solution)/shard_map/ppermute | solution.py:360
  117.0 7.0 %copy-start = (f32[2,768,256]{2,1,0:T(8,128)}, f32[2,768,256]{2,1,0:T(8,128)S(1)}, u32[]{:S(2)}) copy-start(f32[2,768,256]{2,1,0:T(8,128)S(1)} %get-tuple-element.104) | copy-start | bytes 4718596
  117.0 7.0 %copy-start.7 = (f32[768,256]{1,0:T(8,128)}, f32[768,256]{1,0:T(8,128)S(1)}, u32[]{:S(2)}) copy-start(f32[768,256]{1,0:T(8,128)S(1)} %get-tuple-element.102) | copy-start | bytes 2359300
  117.0 6.9 %copy-start.15 = (f32[768,256]{1,0:T(8,128)}, f32[768,256]{1,0:T(8,128)S(1)}, u32[]{:S(2)}) copy-start(f32[768,256]{1,0:T(8,128)S(1)} %get-tuple-element.106) | copy-start | bytes 2359300
  117.0 20.8 %collective-permute-start.23 = (bf16[2,768,256]{2,1,0:T(8,128)(2,1)}, bf16[2,768,256]{2,1,0:T(8,128)(2,1)}, u32[]{:S(2)}, u32[]{:S(2)}) collective-permute-start(bf16[2,768,256]{2,1,0:T(8,128)(2,1)} %get-tuple-element.88), channel_id=1, source_target_pairs={{0,1},{3,2},{4,5},{7,6},{8,9},{11,10},{12,13},{15,14},{16,17},{19,... | collective-permute-start | bytes 2359304 | tf_op jit(solution)/shard_map/ppermute | solution.py:360
  123.9 13.9 %collective-permute-start.21 = (bf16[2,768,256]{2,1,0:T(8,128)(2,1)}, bf16[2,768,256]{2,1,0:T(8,128)(2,1)}, u32[]{:S(2)}, u32[]{:S(2)}) collective-permute-start(bf16[2,768,256]{2,1,0:T(8,128)(2,1)} %add_convert_fusion.3), channel_id=1, source_target_pairs={{1,2},{2,1},{5,6},{6,5},{9,10},{10,9},{13,14},{14,13},{17,18},{18,... | collective-permute-start | bytes 2359304 | tf_op jit(solution)/shard_map/ppermute | solution.py:352
  125.5 20.0 %collective-permute-start.24 = (bf16[2,2,2,384,128]{4,3,2,1,0:T(8,128)(2,1)S(1)}, bf16[2,2,2,384,128]{4,3,2,1,0:T(8,128)(2,1)}, u32[]{:S(2)}, u32[]{:S(2)}) collective-permute-start(bf16[2,2,2,384,128]{4,3,2,1,0:T(8,128)(2,1)S(1)} %collective-permute-done.18.refs_3_), channel_id=1, source_target_pairs={{2,3},{6,7},{10,11},{14,15},{18,19},{22,23},{26,27},{30,31}} | collective-permute-start | bytes 2359304 | tf_op jit(solution)/shard_map/ppermute | solution.py:340
  127.1 23.4 %collective-permute-start.25 = (bf16[2,2,2,384,128]{4,3,2,1,0:T(8,128)(2,1)S(1)}, bf16[2,2,2,384,128]{4,3,2,1,0:T(8,128)(2,1)}, u32[]{:S(2)}, u32[]{:S(2)}) collective-permute-start(bf16[2,2,2,384,128]{4,3,2,1,0:T(8,128)(2,1)S(1)} %collective-permute-done.19.refs_6_), channel_id=1, source_target_pairs={{1,0},{5,4},{9,8},{13,12},{17,16},{21,20},{25,24},{29,28}} | collective-permute-start | bytes 2359304 | tf_op jit(solution)/shard_map/ppermute | solution.py:344
  128.4 22.1 %copy-start.6 = (bf16[2,2,384,128]{3,2,1,0:T(8,128)(2,1)S(1)}, bf16[2,2,384,128]{3,2,1,0:T(8,128)(2,1)}, u32[]{:S(2)}) copy-start(bf16[2,2,384,128]{3,2,1,0:T(8,128)(2,1)} %get-tuple-element.93.refs_1_) | copy-start | bytes 1179652
  128.4 22.1 %copy-start.24 = (f32[2]{0:T(128)S(1)}, f32[2]{0:T(128)}, u32[]{:S(2)}) copy-start(f32[2]{0:T(128)} %refs_8_.5) | copy-start | bytes 28
  139.1 28.6 %collective-permute-start.22 = (bf16[768,256]{1,0:T(8,128)(2,1)S(1)}, bf16[768,256]{1,0:T(8,128)(2,1)S(1)}, u32[]{:S(2)}, u32[]{:S(2)}) collective-permute-start(bf16[768,256]{1,0:T(8,128)(2,1)S(1)} %fusion.9), channel_id=1, source_target_pairs={{0,1},{1,0},{2,3},{3,2},{4,5},{5,4},{6,7},{7,6},{8,9},{9,8},{10,11... | collective-permute-start | bytes 1179656 | tf_op jit(solution)/shard_map/ppermute | solution.py:348
  162.5 1.2 copy-start.4
  165.5 23.7 %collective-permute-start.30 = (bf16[2,768,256]{2,1,0:T(8,128)(2,1)}, bf16[2,768,256]{2,1,0:T(8,128)(2,1)}, u32[]{:S(2)}, u32[]{:S(2)}) collective-permute-start(bf16[2,768,256]{2,1,0:T(8,128)(2,1)} %get-tuple-element.109), channel_id=1, source_target_pairs={{0,1},{3,2},{4,5},{7,6},{8,9},{11,10},{12,13},{15,14},{16,17},{19,... | collective-permute-start | bytes 2359304 | tf_op jit(solution)/shard_map/ppermute | solution.py:360
  168.5 13.3 %copy-start.1 = (f32[2,768,256]{2,1,0:T(8,128)S(1)}, f32[2,768,256]{2,1,0:T(8,128)}, u32[]{:S(2)}) copy-start(f32[2,768,256]{2,1,0:T(8,128)} %copy-done) | copy-start | bytes 4718596
  181.7 3.0 %copy-start.2 = (f32[2,768,256]{2,1,0:T(8,128)}, f32[2,768,256]{2,1,0:T(8,128)S(1)}, u32[]{:S(2)}) copy-start(f32[2,768,256]{2,1,0:T(8,128)S(1)} %get-tuple-element.112) | copy-start | bytes 4718596
  181.7 3.0 %copy-start.11 = (f32[768,256]{1,0:T(8,128)}, f32[768,256]{1,0:T(8,128)S(1)}, u32[]{:S(2)}) copy-start(f32[768,256]{1,0:T(8,128)S(1)} %get-tuple-element.111) | copy-start | bytes 2359300
  181.7 3.0 %copy-start.17 = (f32[768,256]{1,0:T(8,128)}, f32[768,256]{1,0:T(8,128)S(1)}, u32[]{:S(2)}) copy-start(f32[768,256]{1,0:T(8,128)S(1)} %get-tuple-element.113) | copy-start | bytes 2359300
  181.7 67.2 %collective-permute-start.26 = (bf16[2,2,512,1024]{3,2,1,0:T(8,128)(2,1)}, bf16[2,2,512,1024]{3,2,1,0:T(8,128)(2,1)}, u32[]{:S(2)}, u32[]{:S(2)}) collective-permute-start(bf16[2,2,512,1024]{3,2,1,0:T(8,128)(2,1)} %get-tuple-element.98), channel_id=1, source_target_pairs={{0,16},{16,0},{1,17},{17,1},{2,18},{18,2},{3,19},{19,3},{4,20},{20... | collective-permute-start | bytes 12582920 | tf_op jit(solution)/shard_map/ppermute | solution.py:332
  181.8 6.3 %copy-start.10 = (f32[768,256]{1,0:T(8,128)S(1)}, f32[768,256]{1,0:T(8,128)}, u32[]{:S(2)}) copy-start(f32[768,256]{1,0:T(8,128)} %copy-done.9) | copy-start | bytes 2359300
  181.8 6.3 %copy-start.27 = (bf16[768,256]{1,0:T(8,128)(2,1)S(1)}, bf16[768,256]{1,0:T(8,128)(2,1)}, u32[]{:S(2)}) copy-start(bf16[768,256]{1,0:T(8,128)(2,1)} %copy-done.26) | copy-start | bytes 1179652
  184.7 4.5 %copy-start.5 = (f32[2,768,256]{2,1,0:T(8,128)S(1)}, f32[2,768,256]{2,1,0:T(8,128)}, u32[]{:S(2)}) copy-start(f32[2,768,256]{2,1,0:T(8,128)} %copy-done.4) | copy-start | bytes 4718596
  184.7 6.8 %collective-permute-start.28 = (bf16[2,768,256]{2,1,0:T(8,128)(2,1)}, bf16[2,768,256]{2,1,0:T(8,128)(2,1)S(1)}, u32[]{:S(2)}, u32[]{:S(2)}) collective-permute-start(bf16[2,768,256]{2,1,0:T(8,128)(2,1)} %add_convert_fusion.2), channel_id=1, source_target_pairs={{1,2},{2,1},{5,6},{6,5},{9,10},{10,9},{13,14},{14,13},{17,18},{18,... | collective-permute-start | bytes 2359304 | tf_op jit(solution)/shard_map/ppermute | solution.py:352
  185.6 18.8 %collective-permute-start.27 = (bf16[2,768,256]{2,1,0:T(8,128)(2,1)}, bf16[2,768,256]{2,1,0:T(8,128)(2,1)}, u32[]{:S(2)}, u32[]{:S(2)}) collective-permute-start(bf16[2,768,256]{2,1,0:T(8,128)(2,1)} %get-tuple-element.103), channel_id=1, source_target_pairs={{0,1},{3,2},{4,5},{7,6},{8,9},{11,10},{12,13},{15,14},{16,17},{19,... | collective-permute-start | bytes 2359304 | tf_op jit(solution)/shard_map/ppermute | solution.py:360
  189.2 15.1 %copy-start.16 = (f32[768,256]{1,0:T(8,128)S(1)}, f32[768,256]{1,0:T(8,128)}, u32[]{:S(2)}) copy-start(f32[768,256]{1,0:T(8,128)} %copy-done.15) | copy-start | bytes 2359300
  190.6 16.4 %copy-start.3 = (f32[2,768,256]{2,1,0:T(8,128)S(1)}, f32[2,768,256]{2,1,0:T(8,128)}, u32[]{:S(2)}) copy-start(f32[2,768,256]{2,1,0:T(8,128)} %copy-done.2) | copy-start | bytes 4718596
  190.6 18.7 %collective-permute-start.31 = (bf16[2,768,256]{2,1,0:T(8,128)(2,1)S(1)}, bf16[2,768,256]{2,1,0:T(8,128)(2,1)S(1)}, u32[]{:S(2)}, u32[]{:S(2)}) collective-permute-start(bf16[2,768,256]{2,1,0:T(8,128)(2,1)S(1)} %add_convert_fusion.1), channel_id=1, source_target_pairs={{1,2},{2,1},{5,6},{6,5},{9,10},{10,9},{13,14},{14,13},{17,18},{18,... | collective-permute-start | bytes 2359304 | tf_op jit(solution)/shard_map/ppermute | solution.py:352
  204.4 18.5 %collective-permute-start.29 = (bf16[768,256]{1,0:T(8,128)(2,1)S(1)}, bf16[768,256]{1,0:T(8,128)(2,1)S(1)}, u32[]{:S(2)}, u32[]{:S(2)}) collective-permute-start(bf16[768,256]{1,0:T(8,128)(2,1)S(1)} %fusion.6), channel_id=1, source_target_pairs={{0,1},{1,0},{2,3},{3,2},{4,5},{5,4},{6,7},{7,6},{8,9},{9,8},{10,11... | collective-permute-start | bytes 1179656 | tf_op jit(solution)/shard_map/ppermute | solution.py:348
  208.3 1.1 copy-start.21
  208.4 14.6 %copy-start.8 = (f32[768,256]{1,0:T(8,128)S(1)}, f32[768,256]{1,0:T(8,128)}, u32[]{:S(2)}) copy-start(f32[768,256]{1,0:T(8,128)} %copy-done.7) | copy-start | bytes 2359300
  208.4 14.8 %collective-permute-start.33 = (bf16[2,768,256]{2,1,0:T(8,128)(2,1)S(1)}, bf16[2,768,256]{2,1,0:T(8,128)(2,1)S(1)}, u32[]{:S(2)}, u32[]{:S(2)}) collective-permute-start(bf16[2,768,256]{2,1,0:T(8,128)(2,1)S(1)} %add_convert_fusion), channel_id=1, source_target_pairs={{1,2},{2,1},{5,6},{6,5},{9,10},{10,9},{13,14},{14,13},{17,18},{18,... | collective-permute-start | bytes 2359304 | tf_op jit(solution)/shard_map/ppermute | solution.py:352
  209.3 37.9 %collective-permute-start.35 = (f32[384,256]{1,0:T(8,128)S(1)}, f32[384,256]{1,0:T(8,128)S(1)}, u32[]{:S(2)}, u32[]{:S(2)}) collective-permute-start(f32[384,256]{1,0:T(8,128)S(1)} %get-tuple-element.126), channel_id=1, source_target_pairs={{0,16},{16,0},{1,17},{17,1},{2,18},{18,2},{3,19},{19,3},{4,20},{20... | collective-permute-start | bytes 1179656 | tf_op jit(solution)/shard_map/ppermute | solution.py:332
  209.6 13.6 %copy-start.18 = (f32[768,256]{1,0:T(8,128)S(1)}, f32[768,256]{1,0:T(8,128)}, u32[]{:S(2)}) copy-start(f32[768,256]{1,0:T(8,128)} %copy-done.17) | copy-start | bytes 2359300
  209.6 29.1 %collective-permute-start.32 = (bf16[768,256]{1,0:T(8,128)(2,1)S(1)}, bf16[768,256]{1,0:T(8,128)(2,1)S(1)}, u32[]{:S(2)}, u32[]{:S(2)}) collective-permute-start(bf16[768,256]{1,0:T(8,128)(2,1)S(1)} %fusion.4), channel_id=1, source_target_pairs={{0,1},{1,0},{2,3},{3,2},{4,5},{5,4},{6,7},{7,6},{8,9},{9,8},{10,11... | collective-permute-start | bytes 1179656 | tf_op jit(solution)/shard_map/ppermute | solution.py:348
  223.0 15.6 %copy-start.14 = (f32[768,256]{1,0:T(8,128)S(1)}, f32[768,256]{1,0:T(8,128)}, u32[]{:S(2)}) copy-start(f32[768,256]{1,0:T(8,128)} %copy-done.13) | copy-start | bytes 2359300
  223.1 24.1 %collective-permute-start.36 = (f32[384,256]{1,0:T(8,128)S(1)}, f32[384,256]{1,0:T(8,128)S(1)}, u32[]{:S(2)}, u32[]{:S(2)}) collective-permute-start(f32[384,256]{1,0:T(8,128)S(1)} %get-tuple-element.124), channel_id=1, source_target_pairs={{0,16},{16,0},{1,17},{17,1},{2,18},{18,2},{3,19},{19,3},{4,20},{20... | collective-permute-start | bytes 1179656 | tf_op jit(solution)/shard_map/ppermute | solution.py:332
  223.3 23.6 %collective-permute-start.34 = (bf16[768,256]{1,0:T(8,128)(2,1)S(1)}, bf16[768,256]{1,0:T(8,128)(2,1)S(1)}, u32[]{:S(2)}, u32[]{:S(2)}) collective-permute-start(bf16[768,256]{1,0:T(8,128)(2,1)S(1)} %fusion.2), channel_id=1, source_target_pairs={{0,1},{1,0},{2,3},{3,2},{4,5},{5,4},{6,7},{7,6},{8,9},{9,8},{10,11... | collective-permute-start | bytes 1179656 | tf_op jit(solution)/shard_map/ppermute | solution.py:348
  238.7 8.3 %copy-start.12 = (f32[768,256]{1,0:T(8,128)S(1)}, f32[768,256]{1,0:T(8,128)}, u32[]{:S(2)}) copy-start(f32[768,256]{1,0:T(8,128)} %copy-done.11) | copy-start | bytes 2359300
  238.8 8.4 %collective-permute-start.37 = (f32[384,256]{1,0:T(8,128)S(1)}, f32[384,256]{1,0:T(8,128)S(1)}, u32[]{:S(2)}, u32[]{:S(2)}) collective-permute-start(f32[384,256]{1,0:T(8,128)S(1)} %get-tuple-element.122), channel_id=1, source_target_pairs={{0,16},{16,0},{1,17},{17,1},{2,18},{18,2},{3,19},{19,3},{4,20},{20... | collective-permute-start | bytes 1179656 | tf_op jit(solution)/shard_map/ppermute | solution.py:332
  247.1 1.8 collective-permute-start.38
  (3 other events, 2.5 us)
where the time goes:
time: 258 us; the launch traced here: 254 us
  waiting for transfers between devices  93.2 us (36%)
  starting transfers between devices  85 us (33%)
  Pallas kernels  56.1 us (22%)
  other arithmetic  10.7 us (4%)
  local copies, waits for them, and re-layouts  6.99 us (3%)
    pallas_call x4, Pallas kernels, run_chunk(): pl.pallas_call(functools.partial(chunk_kernel, pieces, chunk), out_shape=...  51.3 us
    ppermute x4, starting transfers between devices, pairs(): return lax.ppermute(x, 'col', [(0, 1), (1, 0), (2, 3), (3, 2)])  37.7 us
    ppermute x6, waiting for transfers between devices, hop_down(): return lax.ppermute(x, 'col', [(3 - c, 2 - c) for c in range(first, 3)])  28.2 us
    ppermute x4, waiting for transfers between devices, planar(): return lax.ppermute(x, 'row', [(r, r ^ offset) for r in range(4)])  27.1 us
    ppermute x4, waiting for transfers between devices, inward(): return lax.ppermute(x, 'col', [(0, 1), (3, 2)])  25.5 us
    ppermute x4, starting transfers between devices, inward(): return lax.ppermute(x, 'col', [(0, 1), (3, 2)])  14.4 us
    ppermute x6, starting transfers between devices, hop_up(): return lax.ppermute(x, 'col', [(c, c + 1) for c in range(first, 3)])  12.5 us
    ppermute x4, waiting for transfers between devices, pairs(): return lax.ppermute(x, 'col', [(0, 1), (1, 0), (2, 3), (3, 2)])  8.04 us
  transfers between devices with their start and end apart: 39, of which 18 were waited for; matrix products, arithmetic and copies ran while one was open for 4% of the time, Pallas kernels for 20%

commit v1 on v0

v1 whole, which is shorter than its diff:
```python
import functools

import jax
import jax.numpy as jnp
from jax import lax
from jax.experimental import pallas as pl
from jax.experimental.pallas import tpu as pltpu
from jax.sharding import PartitionSpec as P


def make_amplitudes(coulomb, occ_energy, virt_first, virt_second):
    denominator = (
        occ_energy[:, None, None, None]
        + occ_energy[None, :, None, None]
        - virt_first[None, None, :, None]
        - virt_second[None, None, None, :]
    )
    return ((2.0 * coulomb - jnp.transpose(coulomb, (1, 0, 2, 3))) / denominator).astype(
        jnp.bfloat16
    )


def general(bra_factor, ket_factor, occ_energy, virt_energy):
    a_width = bra_factor.shape[2]
    b_width = ket_factor.shape[2]
    ket_whole = lax.all_gather(ket_factor, "row", axis=0, tiled=True)
    row_index = lax.axis_index("row")
    col_index = lax.axis_index("col")
    virt_first = lax.dynamic_slice_in_dim(virt_energy, row_index * a_width, a_width, 0)
    virt_second = lax.dynamic_slice_in_dim(virt_energy, col_index * b_width, b_width, 0)
    partial_sum = jnp.einsum(
        "qia,qjb->ijab",
        lax.all_gather(bra_factor, "col", axis=0, tiled=True),
        ket_whole,
        preferred_element_type=jnp.float32,
    )
    batch_count = lax.axis_size("occ")
    pad_rows = (batch_count - a_width % batch_count) % batch_count
    padded = jnp.pad(partial_sum, ((0, 0), (0, 0), (0, pad_rows), (0, 0)))
    share_sum = lax.psum_scatter(padded, "occ", scatter_dimension=2, tiled=True)
    share_len = share_sum.shape[2]
    energy_padded = jnp.pad(virt_first, (0, pad_rows), constant_values=1.0)
    energy_share = lax.dynamic_slice_in_dim(
        energy_padded, lax.axis_index("occ") * share_len, share_len, 0
    )
    share_amps = make_amplitudes(share_sum, occ_energy, energy_share, virt_second)
    collected = lax.all_gather(share_amps, "occ", axis=2, tiled=True)
    amplitudes = collected[:, :, :a_width, :]
    gamma = lax.psum_scatter(
        jnp.einsum("ijab,qjb->qia", amplitudes, ket_whole, preferred_element_type=jnp.float32),
        "col",
        scatter_dimension=0,
        tiled=True,
    )
    return (amplitudes, gamma)


GROUPS = 2
SLICES = 4


def group_kernel(pieces, group, *refs):
    refs = list(refs)
    take = lambda count: [refs.pop(0) for _ in range(count)]
    ket = take(1 if group else 2 * len(pieces))
    (bra,) = take(1)
    ups, downs = take(3), take(3)
    occ_ref, virt_ref = take(2)
    other, _ = take(2) if group else (None, None)
    whole_ref, half_ref = take(2)
    own_ref, pair_ref, far_ref, send_ref = (take(2) for _ in range(4))
    (ket_all,) = (None,) if group else take(1)
    kv, bv, bt, t2, amps, given, ket_sem, bra_sem, out_sem = refs
    batch, width = bra.shape[2:]
    span = ket[0].shape[1] // 2
    half = whole_ref.shape[2] // 2
    part = span // SLICES
    here_row, here_col = lax.axis_index("row"), lax.axis_index("col")
    me = lax.axis_index("occ")
    pair = lax.bitwise_xor(here_col, 1)
    low = here_col < 2

    def bra_copies(source, home, slot):
        return [
            pltpu.make_async_copy(
                source.at[q, i],
                bv.at[home, pl.ds(q * batch, batch), pl.ds(i * width, width)],
                bra_sem.at[slot, q, i],
            )
            for q in range(2)
            for i in range(2)
        ]

    def fetch(condition, source, home, slot):
        @pl.when(condition)
        def _():
            for copy in bra_copies(source, home, slot):
                copy.start()

    for copy in bra_copies(bra, here_col, 0):
        copy.start()
    for d in range(1, 4):
        home = lax.rem(here_col + 4 - d, 4)
        fetch(here_col >= d, ups[d - 1], home, d)
        fetch(here_col < d, downs[3 - d], home, d)

    copies = [[] for _ in range(SLICES)]
    for n in range(SLICES):
        for j in range(2):
            columns = pl.ds(j * span + n * part, part)
            if group:
                moves = [(ket[0], 0, 8 * batch, 0)]
            else:
                moves = []
                for index, source in enumerate(ket):
                    q, place = divmod(index, len(pieces))
                    offset, begin, rows = pieces[place]
                    home = lax.bitwise_xor(here_row, offset) * (2 * batch) + q * batch + begin
                    moves.append((source, pl.multiple_of(home, 16), rows, index))
            for source, home, rows, index in moves:
                copy = pltpu.make_async_copy(
                    source.at[:, columns],
                    kv.at[pl.ds(home, rows), columns],
                    ket_sem.at[n, index, j],
                )
                copy.start()
                copies[n].append(copy)
    if group:
        given_in = pltpu.make_async_copy(other, given, out_sem.at[2])
        given_in.start()
    for slot in range(4):
        for copy in bra_copies(bra, slot, slot):
            copy.wait()
    first_at = here_row * (2 * half) + me * half + group * width
    first = virt_ref[:, pl.ds(pl.multiple_of(first_at, 128), width)]
    first = jnp.broadcast_to(first, (width, width)).T[:, :1]
    for d in range(4):
        bt[:, d * 2 * batch : (d + 1) * 2 * batch] = bv[d].T
    for n in range(SLICES):
        for copy in copies[n]:
            copy.wait()
        tile = [
            jnp.dot(
                bt[...],
                kv[:, j * span + n * part : j * span + (n + 1) * part],
                preferred_element_type=jnp.float32,
            )
            for j in range(2)
        ]
        second_at = pl.multiple_of(here_col * span + n * part, 128)
        second = virt_ref[:, pl.ds(second_at, part)]
        for i in range(2):
            for j in range(2):
                direct = tile[j][i * width : (i + 1) * width, :]
                exchange = tile[i][j * width : (j + 1) * width, :]
                denominator = ((occ_ref[i] + occ_ref[j]) - first) - second
                block = ((2.0 * direct - exchange) / denominator).astype(jnp.bfloat16)
                amps[i, j, :, n * part : (n + 1) * part] = block
                t2[
                    i * width : (i + 1) * width,
                    j * span + n * part : j * span + (n + 1) * part,
                ] = block
    at = pl.multiple_of(me * half + group * width, 16)
    outs = [
        pltpu.make_async_copy(amps, whole_ref.at[:, :, pl.ds(at, width), :], out_sem.at[0]),
        pltpu.make_async_copy(amps, half_ref, out_sem.at[1]),
    ]
    if group:
        given_in.wait()
        at = pl.multiple_of((1 - me) * half, 16)
        outs.append(
            pltpu.make_async_copy(given, whole_ref.at[:, :, pl.ds(at, width), :], out_sem.at[2])
        )
    else:
        outs.append(pltpu.make_async_copy(kv, ket_all, out_sem.at[2]))
    for copy in outs:
        copy.start()

    def share_of(home):
        rows = pl.ds(pl.multiple_of(home * (2 * batch), 16), 2 * batch)
        return lax.dot_general(
            kv[rows, :],
            t2[...],
            (((1,), (1,)), ((), ())),
            preferred_element_type=jnp.float32,
        )

    for n in range(2):
        share = share_of(jnp.where(low, 2 + n, n))
        for q in range(2):
            far_ref[q][n] = share[q * batch : (q + 1) * batch]
            send_ref[q][n] = share[q * batch : (q + 1) * batch].astype(jnp.bfloat16)
    for out, home in ((pair_ref, pair), (own_ref, here_col)):
        share = share_of(home)
        for q in range(2):
            out[q][...] = share[q * batch : (q + 1) * batch]
    for copy in outs:
        copy.wait()


def run_group(group, ket, pieces, bras, energies, held):
    _, _, batch, width = bras[0].shape
    span = ket[0].shape[1] // 2
    half = width * GROUPS
    total = 8 * batch
    flops = 2 * 2 * total * 2 * width * 2 * span
    any_space = pl.BlockSpec(memory_space=pl.ANY)
    in_vmem = pl.BlockSpec(memory_space=pltpu.VMEM)
    in_hbm = pl.BlockSpec(memory_space=pltpu.HBM)
    ahead = len(ket) + len(bras) + 2
    block = jax.ShapeDtypeStruct((batch, 2 * width), jnp.float32)
    far = jax.ShapeDtypeStruct((2, batch, 2 * width), jnp.float32)
    send = jax.ShapeDtypeStruct((2, batch, 2 * width), jnp.bfloat16)
    results = pl.pallas_call(
        functools.partial(group_kernel, pieces, group),
        out_shape=(
            jax.ShapeDtypeStruct((2, 2, 2 * half, span), jnp.bfloat16),
            jax.ShapeDtypeStruct((2, 2, width, span), jnp.bfloat16),
        )
        + (block,) * 4
        + (far,) * 2
        + (send,) * 2
        + (() if group else (jax.ShapeDtypeStruct((total, 2 * span), jnp.bfloat16),)),
        in_specs=[in_hbm if group else any_space] * len(ket)
        + [any_space] * len(bras)
        + [pl.BlockSpec(memory_space=pltpu.SMEM), in_vmem]
        + [any_space] * len(held),
        out_specs=(any_space, any_space) + (in_vmem,) * 8 + (() if group else (in_hbm,)),
        scratch_shapes=[
            pltpu.VMEM((total, 2 * span), jnp.bfloat16),
            pltpu.VMEM((4, 2 * batch, 2 * width), jnp.bfloat16),
            pltpu.VMEM((2 * width, total), jnp.bfloat16),
            pltpu.VMEM((2 * width, 2 * span), jnp.bfloat16),
            pltpu.VMEM((2, 2, width, span), jnp.bfloat16),
            pltpu.VMEM((2, 2, width, span), jnp.bfloat16),
            pltpu.SemaphoreType.DMA((SLICES, 2 * len(pieces), 2)),
            pltpu.SemaphoreType.DMA((4, 2, 2)),
            pltpu.SemaphoreType.DMA((3,)),
        ],
        input_output_aliases={ahead + 1: 0} if held else {},
        compiler_params=pltpu.CompilerParams(vmem_limit_bytes=44 * 2**20),
        cost_estimate=pl.CostEstimate(
            flops=flops, bytes_accessed=total * 2 * span * 2, transcendentals=0
        ),
    )(*ket, *bras, *energies, *held)
    return results[:2], *(results[n : n + 2] for n in (2, 4, 6, 8)), results[10:]


def pick_kernel(bra, kept_out, given_out):
    width = kept_out.shape[3]
    span = bra.shape[1] // 2
    me = lax.axis_index("occ")
    for side, out in ((1 - me, given_out), (me, kept_out)):
        for g in range(GROUPS):
            for i in range(2):
                home = i * span + side * (span // 2) + g * width
                out[g, i] = bra[:, pl.ds(pl.multiple_of(home, 128), width)]


def pick(bra):
    batch, columns = bra.shape
    part = jax.ShapeDtypeStruct((GROUPS, 2, batch, columns // 4 // GROUPS), bra.dtype)
    return pl.pallas_call(
        pick_kernel,
        out_shape=(part, part),
        compiler_params=pltpu.CompilerParams(vmem_limit_bytes=16 * 2**20),
        cost_estimate=pl.CostEstimate(
            flops=0, bytes_accessed=4 * bra.size, transcendentals=0
        ),
    )(bra)


def close_kernel(*refs):
    other, _, *totals = refs[: 2 + 2 * GROUPS]
    amps, gamma, amp_buffer, gamma_buffer, sems, gamma_sems = refs[2 + 2 * GROUPS :]
    width = other.shape[2]
    half = width * GROUPS
    me = lax.axis_index("occ")
    at = pl.multiple_of((1 - me) * half + half - width, 16)
    blocks = [(i, j) for i in range(2) for j in range(2)]
    reads = [
        pltpu.make_async_copy(other.at[i, j], amp_buffer.at[i, j], sems.at[0, i, j])
        for i, j in blocks
    ]
    writes = [
        pltpu.make_async_copy(
            amp_buffer.at[i, j], amps.at[i, j, pl.ds(at, width), :], sems.at[1, i, j]
        )
        for i, j in blocks
    ]
    for copy in reads:
        copy.start()
    for n in range(2 * GROUPS):
        side, g = divmod(n, GROUPS)
        home = jnp.where(me == side, 0, half) + g * width
        for i in range(2):
            gamma_buffer[n, :, i, :] = totals[n][:, i * width : (i + 1) * width]
        writes.append(
            pltpu.make_async_copy(
                gamma_buffer.at[n],
                gamma.at[:, :, pl.ds(pl.multiple_of(home, 128), width)],
                gamma_sems.at[n],
            )
        )
        reads[n].wait()
        writes[n].start()
        writes[-1].start()
    for copy in writes:
        copy.wait()


def close(other, whole, kept, received):
    batch, double = received[0].shape
    any_space = pl.BlockSpec(memory_space=pl.ANY)
    in_vmem = pl.BlockSpec(memory_space=pltpu.VMEM)
    return pl.pallas_call(
        close_kernel,
        out_shape=(
            jax.ShapeDtypeStruct(whole.shape, whole.dtype),
            jax.ShapeDtypeStruct((batch, 2, GROUPS * double), jnp.float32),
        ),
        in_specs=[any_space, any_space] + [in_vmem] * (2 * GROUPS),
        out_specs=(any_space, any_space),
        scratch_shapes=[
            pltpu.VMEM(other.shape, other.dtype),
            pltpu.VMEM((2 * GROUPS, batch, 2, double // 2), jnp.float32),
            pltpu.SemaphoreType.DMA((2, 2, 2)),
            pltpu.SemaphoreType.DMA((2 * GROUPS,)),
        ],
        input_output_aliases={1: 0},
        compiler_params=pltpu.CompilerParams(vmem_limit_bytes=48 * 2**20),
        cost_estimate=pl.CostEstimate(
            flops=0, bytes_accessed=4 * other.size + 16 * batch * double * GROUPS, transcendentals=0
        ),
    )(other, whole, *kept, *received)


def swap(x):
    return lax.ppermute(x, "occ", [(0, 1), (1, 0)])


def planar(x, offset):
    return lax.ppermute(x, "row", [(r, r ^ offset) for r in range(4)])


def hop_up(x, first):
    return lax.ppermute(x, "col", [(c, c + 1) for c in range(first, 3)])


def hop_down(x, first):
    return lax.ppermute(x, "col", [(3 - c, 2 - c) for c in range(first, 3)])


def pairs(x):
    return lax.ppermute(x, "col", [(0, 1), (1, 0), (2, 3), (3, 2)])


def across(x):
    return lax.ppermute(x, "col", [(1, 2), (2, 1)])


def outward(x):
    return lax.ppermute(x, "col", [(1, 0), (2, 3)])


def inward(x):
    return lax.ppermute(x, "col", [(0, 1), (3, 2)])


def tie(*arrays):
    return lax.optimization_barrier(arrays)


def planned(bra_factor, ket_factor, occ_energy, virt_energy):
    batch, _, a_width = bra_factor.shape
    b_width = ket_factor.shape[2]

    bra_kept, bra_given = pick(bra_factor.reshape(batch, 2 * a_width))
    ket_own = ket_factor.reshape(batch, 2 * b_width)
    bra = jnp.stack([bra_kept, swap(bra_given)], axis=1)
    ket_x = planar(ket_own, 1)
    ket_y = planar(ket_own, 2)
    cut = batch // 2
    pieces = ((0, 0, batch), (1, 0, batch), (2, 0, batch), (3, 0, cut), (3, cut, batch - cut))

    ups, downs = [[hop_up(bra[0], 0)], []], [[hop_down(bra[0], 0)], []]
    ket_swapped = swap(ket_own)
    ups[0].append(hop_up(ups[0][0], 1))
    downs[0].append(hop_down(downs[0][0], 1))
    ket_x, ket_y, ups[0][1], downs[0][1], ket_swapped = tie(
        ket_x, ket_y, ups[0][1], downs[0][1], ket_swapped
    )
    part_x, part_y, late_x, late_y = tie(ket_x[:cut], ket_y[cut:], ket_x, ket_y)
    far_y, far_x = planar(part_x, 2), planar(part_y, 1)
    late_y, far_y = tie(late_y, far_y)
    ups[0].append(hop_up(ups[0][1], 2))
    downs[0].append(hop_down(downs[0][1], 2))
    straight = [swap(late_x), swap(late_y)]
    ups[0][2], downs[0][2], far_y, far_x = tie(ups[0][2], downs[0][2], far_y, far_x)
    ket = [ket_own, ket_x, ket_y, far_y, far_x, ket_swapped, *straight, swap(far_y), swap(far_x)]
    ups[0][2], downs[0][2], block = tie(ups[0][2], downs[0][2], bra[1])
    ups[1].append(hop_up(block, 0))
    downs[1].append(hop_down(block, 0))
    energies = (occ_energy, virt_energy[None, :])

    def up_cast(x):
        return x.astype(jnp.float32)

    near = lax.bitwise_and(lax.axis_index("col"), 1)

    def cross(far, one):
        return across((far + up_cast(one)).astype(jnp.bfloat16))

    def exchange(pair, two):
        theirs = lax.dynamic_index_in_dim(two, 1 - near, 0, keepdims=False)
        return pairs((pair + up_cast(theirs)).astype(jnp.bfloat16))

    def finish(own, two, three):
        ours = lax.dynamic_index_in_dim(two, near, 0, keepdims=False)
        return own + up_cast(ours) + up_cast(three)

    both = (1, 0)
    arrived = [bra[0], *ups[0], *downs[0]]
    (whole, mine), own0, pair0, far0, send0, (ket_all,) = run_group(
        0, ket, pieces, arrived, energies, ()
    )
    one0 = {q: inward(send0[q]) for q in both}
    own_first, up, down = tie(own0[0], ups[1][0], downs[1][0])
    for hop in (1, 2):
        ups[1].append(hop_up(ups[1][hop - 1] if hop > 1 else up, hop))
        downs[1].append(hop_down(downs[1][hop - 1] if hop > 1 else down, hop))
    other0 = swap(mine)
    two0 = {1: cross(far0[1], one0[1])}
    arrived = [bra[1], *ups[1], *downs[1]]
    two0[1], arrived[0] = tie(two0[1], arrived[0])
    (whole, mine), own1, pair1, far1, send1, _ = run_group(
        1, [ket_all], pieces, arrived, energies, (other0, whole)
    )
    one1 = {q: inward(send1[q]) for q in both}
    other1 = swap(mine)
    two0[0] = cross(far0[0], one0[0])
    two1 = {q: cross(far1[q], one1[q]) for q in both}
    one1[1], two0[0], two0[1] = tie(one1[1], two0[0], two0[1])
    own0 = (own_first, own0[1])
    three0 = {q: exchange(pair0[q], two0[q]) for q in both}
    three1 = {q: exchange(pair1[q], two1[q]) for q in both}
    received = [
        swap(finish(own[1], two[1], three[1]))
        for own, two, three in ((own0, two0, three0), (own1, two1, three1))
    ]
    kept = [
        finish(own[0], two[0], three[0])
        for own, two, three in ((own0, two0, three0), (own1, two1, three1))
    ]
    return close(other1, whole, kept, received)


def solution(mesh):
    sizes = mesh.shape

    def on_device(bra_factor, ket_factor, occ_energy, virt_energy):
        fits = (
            sizes["occ"] == 2
            and sizes["row"] == 4
            and sizes["col"] == 4
            and bra_factor.shape[2] % (256 * GROUPS) == 0
            and ket_factor.shape[2] % 512 == 0
            and bra_factor.shape[0] % 128 == 0
        )
        body = planned if fits else general
        return body(bra_factor, ket_factor, occ_energy, virt_energy)

    placed = (P(("occ", "col"), None, "row"), P(("occ", "row"), None, "col"), P(), P())
    return jax.shard_map(
        on_device,
        mesh=mesh,
        in_specs=placed,
        out_specs=(P(None, None, "row", "col"), P(("occ", "col"), None, "row")),
        check_vma=False,
    )
```

time: 258 us -> 244 us (0.946); the launches traced: 254 us -> 243 us
  starting transfers between devices: 85 us -> 55.8 us
  waiting for transfers between devices: 93.2 us -> 121 us
  Pallas kernels: 56.1 us -> 46.1 us
    ppermute x4, starting transfers between devices: 37.7 us -> 10.5 us  [pairs(): return lax.ppermute(x, 'col', [(0, 1), (1, 0), (2, 3), (3, 2)])]
    ppermute x6, waiting for transfers between devices: 28.2 us -> 39.6 us  [hop_down(): return lax.ppermute(x, 'col', [(3 - c, 2 - c) for c in range(first, 3)])]
    ppermute x4, waiting for transfers between devices: 25.5 us -> 36.2 us  [inward(): return lax.ppermute(x, 'col', [(0, 1), (3, 2)])]
    ppermute x4, waiting for transfers between devices: 8.04 us -> 16.9 us  [pairs(): return lax.ppermute(x, 'col', [(0, 1), (1, 0), (2, 3), (3, 2)])]
    pallas_call x4 -> x2, Pallas kernels: 51.3 us -> 43.1 us  [run_group(): pl.pallas_call(functools.partial(group_kernel, pieces, group), out_shape=...]
    unnamed x58 -> x54, local copies, waits for them, and re-layouts: 6.66 us -> 5.99 us
  transfers between devices with their start and end apart: 39 -> 38, of which waited for: 18 -> 17; matrix products, arithmetic and copies ran while one was open for 4% -> 5% of each run, Pallas kernels for 20% -> 18%
where the time goes in v1:
time: 244 us; the launch traced here: 243 us
  waiting for transfers between devices  121 us (50%)
  starting transfers between devices  55.8 us (23%)
  Pallas kernels  46.1 us (19%)
  other arithmetic  12.1 us (5%)
  local copies, waits for them, and re-layouts  6.11 us (3%)
    pallas_call x2, Pallas kernels, run_group(): pl.pallas_call(functools.partial(group_kernel, pieces, group), out_shape=...  43.1 us
    ppermute x6, waiting for transfers between devices, hop_down(): return lax.ppermute(x, 'col', [(3 - c, 2 - c) for c in range(first, 3)])  39.6 us
    ppermute x4, waiting for transfers between devices, inward(): return lax.ppermute(x, 'col', [(0, 1), (3, 2)])  36.2 us
    ppermute x4, waiting for transfers between devices, planar(): return lax.ppermute(x, 'row', [(r, r ^ offset) for r in range(4)])  27.1 us
    ppermute x4, waiting for transfers between devices, pairs(): return lax.ppermute(x, 'col', [(0, 1), (1, 0), (2, 3), (3, 2)])  16.9 us
    ppermute x4, starting transfers between devices, inward(): return lax.ppermute(x, 'col', [(0, 1), (3, 2)])  12.8 us
    ppermute x6, starting transfers between devices, hop_up(): return lax.ppermute(x, 'col', [(c, c + 1) for c in range(first, 3)])  11.5 us
    ppermute x4, starting transfers between devices, pairs(): return lax.ppermute(x, 'col', [(0, 1), (1, 0), (2, 3), (3, 2)])  10.5 us
  transfers between devices with their start and end apart: 38, of which 17 were waited for; matrix products, arithmetic and copies ran while one was open for 5% of the time, Pallas kernels for 18%

profile of v1, /device:TPU:0, one launch (start us, length us, event | category | flops | bytes accessed | tf_op | source)
XLA Modules:
  0.0 243.2 jit_solution(12198487644215288328)
XLA Ops:
  0.6 1.8 copy.9
  2.7 0.5 collective-permute-start.2
  3.2 0.6 copy-done.9
  3.9 0.4 copy.8
  4.4 0.5 collective-permute-start.7
  4.9 2.6 %collective-permute-start.1 = (bf16[384,2048]{1,0:T(8,128)(2,1)S(1)}, bf16[384,2048]{1,0:T(8,128)(2,1)S(1)}, u32[]{:S(2)}, u32[]{:S(2)}) collective-permute-start(bf16[384,2048]{1,0:T(8,128)(2,1)S(1)} %bitcast.42), channel_id=1, source_target_pairs={{0,8},{4,12},{8,0},{12,4},{1,9},{5,13},{9,1},{13,5},{2,10},{6,14},... | collective-permute-start | bytes 4718600 | tf_op jit(solution)/shard_map/ppermute | solution.py:343
  7.6 1.3 collective-permute-start.5
  8.9 1.6 collective-permute-start
  10.5 4.6 %collective-permute-start.3 = (bf16[2,2,384,256]{3,2,1,0:T(8,128)(2,1)S(1)}, bf16[2,2,384,256]{3,2,1,0:T(8,128)(2,1)S(1)}, u32[]{:S(2)}, u32[]{:S(2)}) collective-permute-start(bf16[2,2,384,256]{3,2,1,0:T(8,128)(2,1)S(1)} %get-tuple-element.99.refs_10_), channel_id=1, source_target_pairs={{0,1},{1,2},{2,3},{4,5},{5,6},{6,7},{8,9},{9,10},{10,11},{12,13},{... | collective-permute-start | bytes 2359304 | tf_op jit(solution)/shard_map/ppermute | solution.py:347
  15.1 14.0 %collective-permute-done.5.refs_14_ = bf16[2,2,384,256]{3,2,1,0:T(8,128)(2,1)S(1)} collective-permute-done((bf16[2,2,384,256]{3,2,1,0:T(8,128)(2,1)S(1)}, bf16[2,2,384,256]{3,2,1,0:T(8,128)(2,1)S(1)}, u32[]{:S(2)}, u32[]{:S(2)}) %collective-permute-start.5) | collective-permute-done | bytes 786464 | tf_op jit(solution)/shard_map/ppermute | solution.py:351
  29.1 1.3 collective-permute-start.6
  30.4 1.2 collective-permute-done.3.refs_11_
  31.6 0.7 collective-permute-start.4
  32.3 10.1 %collective-permute-done.1.refs_2_ = bf16[384,2048]{1,0:T(8,128)(2,1)S(1)} collective-permute-done((bf16[384,2048]{1,0:T(8,128)(2,1)S(1)}, bf16[384,2048]{1,0:T(8,128)(2,1)S(1)}, u32[]{:S(2)}, u32[]{:S(2)}) %collective-permute-start.1) | collective-permute-done | bytes 1572896 | tf_op jit(solution)/shard_map/ppermute | solution.py:343
  42.5 3.0 %collective-permute-done.refs_1_ = bf16[384,2048]{1,0:T(8,128)(2,1)S(1)} collective-permute-done((bf16[384,2048]{1,0:T(8,128)(2,1)S(1)}, bf16[384,2048]{1,0:T(8,128)(2,1)S(1)}, u32[]{:S(2)}, u32[]{:S(2)}) %collective-permute-start) | collective-permute-done | bytes 1572896 | tf_op jit(solution)/shard_map/ppermute | solution.py:343
  45.5 4.3 %collective-permute-done.6.refs_15_ = bf16[2,2,384,256]{3,2,1,0:T(8,128)(2,1)S(1)} collective-permute-done((bf16[2,2,384,256]{3,2,1,0:T(8,128)(2,1)S(1)}, bf16[2,2,384,256]{3,2,1,0:T(8,128)(2,1)S(1)}, u32[]{:S(2)}, u32[]{:S(2)}) %collective-permute-start.6) | collective-permute-done | bytes 786464 | tf_op jit(solution)/shard_map/ppermute | solution.py:351
  49.9 0.6 collective-permute-start.10
  50.5 1.5 collective-permute-start.11
  52.0 0.7 collective-permute-start.8
  52.7 1.3 collective-permute-start.9
  54.1 13.7 %collective-permute-done.10.refs_3_ = bf16[192,2048]{1,0:T(8,128)(2,1)S(1)} collective-permute-done((bf16[192,2048]{1,0:T(8,128)(2,1)S(1)}, bf16[192,2048]{1,0:T(8,128)(2,1)S(1)}, u32[]{:S(2)}, u32[]{:S(2)}) %collective-permute-start.10) | collective-permute-done | bytes 786464 | tf_op jit(solution)/shard_map/ppermute | solution.py:343
  68.1 4.0 %collective-permute-done.9.refs_16_ = bf16[2,2,384,256]{3,2,1,0:T(8,128)(2,1)S(1)} collective-permute-done((bf16[2,2,384,256]{3,2,1,0:T(8,128)(2,1)S(1)}, bf16[2,2,384,256]{3,2,1,0:T(8,128)(2,1)S(1)}, u32[]{:S(2)}, u32[]{:S(2)}) %collective-permute-start.9) | collective-permute-done | bytes 786464 | tf_op jit(solution)/shard_map/ppermute | solution.py:351
  72.1 0.5 collective-permute-start.15
  72.6 1.3 collective-permute-start.19
  73.9 0.5 collective-permute-done.14.refs_8_
  74.4 4.1 %collective-permute-start.18 = (bf16[2,2,384,256]{3,2,1,0:T(8,128)(2,1)S(1)}, bf16[2,2,384,256]{3,2,1,0:T(8,128)(2,1)S(1)}, u32[]{:S(2)}, u32[]{:S(2)}) collective-permute-start(bf16[2,2,384,256]{3,2,1,0:T(8,128)(2,1)S(1)} %get-tuple-element.73.refs_1_), channel_id=1, source_target_pairs={{0,1},{1,2},{2,3},{4,5},{5,6},{6,7},{8,9},{9,10},{10,11},{12,13},{... | collective-permute-start | bytes 2359304 | tf_op jit(solution)/shard_map/ppermute | solution.py:347
  78.6 1.1 copy-done.20
  79.7 0.6 copy-done.21
  80.2 22.5 %shard_map.60 = (bf16[2,2,1024,1024]{3,2,1,0:T(8,128)(2,1)}, bf16[2,2,256,1024]{3,2,1,0:T(8,128)(2,1)}, f32[384,512]{1,0:T(8,128)S(1)}, f32[384,512]{1,0:T(8,128...) custom-call(bf16[384,2048]{1,0:T(8,128)(2,1)} %bitcast.44, ...), custom_call_target="tpu_custom_call" | custom-call | flops 12884901888 | bytes 12582912 | tf_op jit(solution)/shard_map/pallas_call | solution.py:214
  102.8 3.0 %collective-permute-start.16 = (bf16[2,384,512]{2,1,0:T(8,128)(2,1)S(1)}, bf16[2,384,512]{2,1,0:T(8,128)(2,1)S(1)}, u32[]{:S(2)}, u32[]{:S(2)}) collective-permute-start(bf16[2,384,512]{2,1,0:T(8,128)(2,1)S(1)} %get-tuple-element.71), channel_id=1, source_target_pairs={{0,1},{3,2},{4,5},{7,6},{8,9},{11,10},{12,13},{15,14},{16,17},{19,... | collective-permute-start | bytes 2359304 | tf_op jit(solution)/shard_map/ppermute | solution.py:367
  105.8 0.7 collective-permute-start.20
  106.5 1.5 collective-permute-start.22
  108.1 15.1 %collective-permute-done.16 = bf16[2,384,512]{2,1,0:T(8,128)(2,1)S(1)} collective-permute-done((bf16[2,384,512]{2,1,0:T(8,128)(2,1)S(1)}, bf16[2,384,512]{2,1,0:T(8,128)(2,1)S(1)}, u32[]{:S(2)}, u32[]{:S(2)}) %collective-permute-start.16) | collective-permute-done | bytes 786464 | tf_op jit(solution)/shard_map/ppermute | solution.py:367
  123.2 1.7 add_convert_fusion.3
  124.9 0.7 collective-permute-start.17
  125.6 0.7 collective-permute-start.21
  126.4 2.2 collective-permute-done.22.refs_6_
  128.5 1.3 collective-permute-start.23
  129.8 5.1 %collective-permute-start.27 = (bf16[2,384,512]{2,1,0:T(8,128)(2,1)S(1)}, bf16[2,384,512]{2,1,0:T(8,128)(2,1)S(1)}, u32[]{:S(2)}, u32[]{:S(2)}) collective-permute-start(bf16[2,384,512]{2,1,0:T(8,128)(2,1)S(1)} %get-tuple-element.84), channel_id=1, source_target_pairs={{0,1},{3,2},{4,5},{7,6},{8,9},{11,10},{12,13},{15,14},{16,17},{19,... | collective-permute-start | bytes 2359304 | tf_op jit(solution)/shard_map/ppermute | solution.py:367
  135.0 15.1 %collective-permute-done.23.refs_7_ = bf16[2,2,384,256]{3,2,1,0:T(8,128)(2,1)S(1)} collective-permute-done((bf16[2,2,384,256]{3,2,1,0:T(8,128)(2,1)S(1)}, bf16[2,2,384,256]{3,2,1,0:T(8,128)(2,1)S(1)}, u32[]{:S(2)}, u32[]{:S(2)}) %collective-permute-start.23) | collective-permute-done | bytes 786464 | tf_op jit(solution)/shard_map/ppermute | solution.py:351
  150.1 1.3 copy-done.18
  151.4 20.6 %shard_map.61 = (bf16[2,2,1024,1024]{3,2,1,0:T(8,128)(2,1)}, bf16[2,2,256,1024]{3,2,1,0:T(8,128)(2,1)}, f32[384,512]{1,0:T(8,128)S(1)}, f32[384,512]{1,0:T(8,128...) custom-call(bf16[3072,2048]{1,0:T(8,128)(2,1)} %get-tuple-element.69, ...), custom_call_target="tpu_custom_call", output_to_operand_aliasing={{0}: (11, {})} | custom-call | flops 12884901888 | bytes 12582912 | tf_op jit(solution)/shard_map/pallas_call | solution.py:214
  172.0 1.5 collective-permute-start.26
  173.5 1.1 add_convert_fusion.2
  174.7 1.6 collective-permute-start.28
  176.3 3.2 %collective-permute-start.30 = (bf16[2,384,512]{2,1,0:T(8,128)(2,1)}, bf16[2,384,512]{2,1,0:T(8,128)(2,1)}, u32[]{:S(2)}, u32[]{:S(2)}) collective-permute-start(bf16[2,384,512]{2,1,0:T(8,128)(2,1)} %get-tuple-element.90), channel_id=1, source_target_pairs={{0,1},{3,2},{4,5},{7,6},{8,9},{11,10},{12,13},{15,14},{16,17},{19,... | collective-permute-start | bytes 2359304 | tf_op jit(solution)/shard_map/ppermute | solution.py:367
  179.4 12.0 %collective-permute-done.26 = bf16[2,384,512]{2,1,0:T(8,128)(2,1)S(1)} collective-permute-done((bf16[2,384,512]{2,1,0:T(8,128)(2,1)S(1)}, bf16[2,384,512]{2,1,0:T(8,128)(2,1)S(1)}, u32[]{:S(2)}, u32[]{:S(2)}) %collective-permute-start.26) | collective-permute-done | bytes 786464 | tf_op jit(solution)/shard_map/ppermute | solution.py:367
  191.5 1.2 add_convert_fusion
  192.6 1.8 collective-permute-start.35
  194.4 1.5 fusion.5
  195.9 3.4 %collective-permute-start.33 = (bf16[384,512]{1,0:T(8,128)(2,1)S(1)}, bf16[384,512]{1,0:T(8,128)(2,1)S(1)}, u32[]{:S(2)}, u32[]{:S(2)}) collective-permute-start(bf16[384,512]{1,0:T(8,128)(2,1)S(1)} %fusion.5), channel_id=1, source_target_pairs={{0,1},{1,0},{2,3},{3,2},{4,5},{5,4},{6,7},{7,6},{8,9},{9,8},{10,11... | collective-permute-start | bytes 1179656 | tf_op jit(solution)/shard_map/ppermute | solution.py:355
  199.4 9.0 %collective-permute-done.30 = bf16[2,384,512]{2,1,0:T(8,128)(2,1)} collective-permute-done((bf16[2,384,512]{2,1,0:T(8,128)(2,1)}, bf16[2,384,512]{2,1,0:T(8,128)(2,1)}, u32[]{:S(2)}, u32[]{:S(2)}) %collective-permute-start.30) | collective-permute-done | bytes 786464 | tf_op jit(solution)/shard_map/ppermute | solution.py:367
  208.4 1.5 add_convert_fusion.1
  209.9 0.8 collective-permute-start.31
  210.8 1.2 fusion.3
  212.0 4.4 %collective-permute-start.36 = (bf16[384,512]{1,0:T(8,128)(2,1)S(1)}, bf16[384,512]{1,0:T(8,128)(2,1)S(1)}, u32[]{:S(2)}, u32[]{:S(2)}) collective-permute-start(bf16[384,512]{1,0:T(8,128)(2,1)S(1)} %fusion.3), channel_id=1, source_target_pairs={{0,1},{1,0},{2,3},{3,2},{4,5},{5,4},{6,7},{7,6},{8,9},{9,8},{10,11... | collective-permute-start | bytes 1179656 | tf_op jit(solution)/shard_map/ppermute | solution.py:355
  216.4 1.1 fusion.9
  217.9 8.1 %collective-permute-done.36 = bf16[384,512]{1,0:T(8,128)(2,1)S(1)} collective-permute-done((bf16[384,512]{1,0:T(8,128)(2,1)S(1)}, bf16[384,512]{1,0:T(8,128)(2,1)S(1)}, u32[]{:S(2)}, u32[]{:S(2)}) %collective-permute-start.36) | collective-permute-done | bytes 393248 | tf_op jit(solution)/shard_map/ppermute | solution.py:355
  226.0 1.1 fusion.4
  227.4 2.6 %collective-permute-start.32 = (bf16[384,512]{1,0:T(8,128)(2,1)S(1)}, bf16[384,512]{1,0:T(8,128)(2,1)S(1)}, u32[]{:S(2)}, u32[]{:S(2)}) collective-permute-start(bf16[384,512]{1,0:T(8,128)(2,1)S(1)} %fusion.7), channel_id=1, source_target_pairs={{0,1},{1,0},{2,3},{3,2},{4,5},{5,4},{6,7},{7,6},{8,9},{9,8},{10,11... | collective-permute-start | bytes 1179656 | tf_op jit(solution)/shard_map/ppermute | solution.py:355
  229.9 2.5 %collective-permute-done.29 = bf16[384,512]{1,0:T(8,128)(2,1)S(1)} collective-permute-done((bf16[384,512]{1,0:T(8,128)(2,1)S(1)}, bf16[384,512]{1,0:T(8,128)(2,1)S(1)}, u32[]{:S(2)}, u32[]{:S(2)}) %collective-permute-start.29) | collective-permute-done | bytes 393248 | tf_op jit(solution)/shard_map/ppermute | solution.py:355
  232.4 1.1 fusion.10.refs_2_
  233.5 6.4 %collective-permute-done.32 = bf16[384,512]{1,0:T(8,128)(2,1)S(1)} collective-permute-done((bf16[384,512]{1,0:T(8,128)(2,1)S(1)}, bf16[384,512]{1,0:T(8,128)(2,1)S(1)}, u32[]{:S(2)}, u32[]{:S(2)}) %collective-permute-start.32) | collective-permute-done | bytes 393248 | tf_op jit(solution)/shard_map/ppermute | solution.py:355
  240.1 2.9 %shard_map.62 = (bf16[2,2,1024,1024]{3,2,1,0:T(8,128)(2,1)}, f32[384,2,1024]{2,1,0:T(2,128)}) custom-call(bf16[2,2,256,1024]{3,2,1,0:T(8,128)(2,1)S(1)} %collective-permute-done.25.refs_0_, bf16[2,2,1024,1024]{3,2,1,0:T(8,128)(2,1)} %get-tuple-element.80.refs_1_, f32[384,512]{1,0:T(8,128)S(1)} %fusion.10.refs_2_, ...), custom_call_target="tpu_custom_call", output_to_operand_aliasing={{0}: (1, {})} | custom-call | bytes 10485760 | tf_op jit(solution)/shard_map/pallas_call | solution.py:316
  (85 shorter events, 1.7 us)
Async XLA Ops:
  2.5 1.4 copy-start.9
  2.7 4.7 %collective-permute-start.2 = (bf16[2,2,384,256]{3,2,1,0:T(8,128)(2,1)S(1)}, bf16[2,2,384,256]{3,2,1,0:T(8,128)(2,1)S(1)}, u32[]{:S(2)}, u32[]{:S(2)}) collective-permute-start(bf16[2,2,384,256]{3,2,1,0:T(8,128)(2,1)S(1)} %get-tuple-element.51), channel_id=1, source_target_pairs={{0,16},{16,0},{1,17},{17,1},{2,18},{18,2},{3,19},{19,3},{4,20},{20... | collective-permute-start | bytes 2359304 | tf_op jit(solution)/shard_map/ppermute | solution.py:339
  4.3 4.6 %copy-start.10 = (bf16[48,8,2,1024]{3,1,2,0:T(8,128)(2,1)}, bf16[48,8,2,1024]{3,1,2,0:T(8,128)(2,1)S(1)}, u32[]{:S(2)}) copy-start(bf16[48,8,2,1024]{3,1,2,0:T(8,128)(2,1)S(1)} %copy.8) | copy-start | bytes 4718596
  4.4 28.0 %collective-permute-start.7 = (bf16[384,2048]{1,0:T(8,128)(2,1)S(1)}, bf16[384,2048]{1,0:T(8,128)(2,1)S(1)}, u32[]{:S(2)}, u32[]{:S(2)}) collective-permute-start(bf16[384,2048]{1,0:T(8,128)(2,1)S(1)} %bitcast.41), channel_id=1, source_target_pairs={{0,16},{16,0},{1,17},{17,1},{2,18},{18,2},{3,19},{19,3},{4,20},{20... | collective-permute-start | bytes 4718600 | tf_op jit(solution)/shard_map/ppermute | solution.py:339
  4.9 37.6 %collective-permute-start.1 = (bf16[384,2048]{1,0:T(8,128)(2,1)S(1)}, bf16[384,2048]{1,0:T(8,128)(2,1)S(1)}, u32[]{:S(2)}, u32[]{:S(2)}) collective-permute-start(bf16[384,2048]{1,0:T(8,128)(2,1)S(1)} %bitcast.42), channel_id=1, source_target_pairs={{0,8},{4,12},{8,0},{12,4},{1,9},{5,13},{9,1},{13,5},{2,10},{6,14},... | collective-permute-start | bytes 4718600 | tf_op jit(solution)/shard_map/ppermute | solution.py:343
  7.6 72.6 %copy-start.7 = (f32[4096]{0:T(1024)S(1)}, f32[4096]{0:T(1024)}, u32[]{:S(2)}) copy-start(f32[4096]{0:T(1024)} %param.7) | copy-start | bytes 49156
  7.6 72.6 %copy-start.8 = (f32[2]{0:T(128)S(1)}, f32[2]{0:T(128)}, u32[]{:S(2)}) copy-start(f32[2]{0:T(128)} %refs_8_.1) | copy-start | bytes 28
  7.6 21.5 %collective-permute-start.5 = (bf16[2,2,384,256]{3,2,1,0:T(8,128)(2,1)S(1)}, bf16[2,2,384,256]{3,2,1,0:T(8,128)(2,1)S(1)}, u32[]{:S(2)}, u32[]{:S(2)}) collective-permute-start(bf16[2,2,384,256]{3,2,1,0:T(8,128)(2,1)S(1)} %get-tuple-element.99.refs_10_), channel_id=1, source_target_pairs={{3,2},{2,1},{1,0},{7,6},{6,5},{5,4},{11,10},{10,9},{9,8},{15,14},{... | collective-permute-start | bytes 2359304 | tf_op jit(solution)/shard_map/ppermute | solution.py:351
  8.9 36.5 %collective-permute-start = (bf16[384,2048]{1,0:T(8,128)(2,1)S(1)}, bf16[384,2048]{1,0:T(8,128)(2,1)S(1)}, u32[]{:S(2)}, u32[]{:S(2)}) collective-permute-start(bf16[384,2048]{1,0:T(8,128)(2,1)S(1)} %bitcast.43), channel_id=1, source_target_pairs={{0,4},{4,0},{8,12},{12,8},{1,5},{5,1},{9,13},{13,9},{2,6},{6,2},{1... | collective-permute-start | bytes 4718600 | tf_op jit(solution)/shard_map/ppermute | solution.py:343
  10.5 21.1 %collective-permute-start.3 = (bf16[2,2,384,256]{3,2,1,0:T(8,128)(2,1)S(1)}, bf16[2,2,384,256]{3,2,1,0:T(8,128)(2,1)S(1)}, u32[]{:S(2)}, u32[]{:S(2)}) collective-permute-start(bf16[2,2,384,256]{3,2,1,0:T(8,128)(2,1)S(1)} %get-tuple-element.99.refs_10_), channel_id=1, source_target_pairs={{0,1},{1,2},{2,3},{4,5},{5,6},{6,7},{8,9},{9,10},{10,11},{12,13},{... | collective-permute-start | bytes 2359304 | tf_op jit(solution)/shard_map/ppermute | solution.py:347
  29.1 49.4 %copy-start.22 = (bf16[2,2,384,256]{3,2,1,0:T(8,128)(2,1)}, bf16[2,2,384,256]{3,2,1,0:T(8,128)(2,1)S(1)}, u32[]{:S(2)}) copy-start(bf16[2,2,384,256]{3,2,1,0:T(8,128)(2,1)S(1)} %collective-permute-done.5.refs_14_) | copy-start | bytes 2359300
  29.1 20.7 %collective-permute-start.6 = (bf16[2,2,384,256]{3,2,1,0:T(8,128)(2,1)S(1)}, bf16[2,2,384,256]{3,2,1,0:T(8,128)(2,1)S(1)}, u32[]{:S(2)}, u32[]{:S(2)}) collective-permute-start(bf16[2,2,384,256]{3,2,1,0:T(8,128)(2,1)S(1)} %collective-permute-done.5.refs_14_), channel_id=1, source_target_pairs={{2,1},{1,0},{6,5},{5,4},{10,9},{9,8},{14,13},{13,12},{18,17},{17,1... | collective-permute-start | bytes 2359304 | tf_op jit(solution)/shard_map/ppermute | solution.py:351
  31.6 18.2 %collective-permute-start.4 = (bf16[2,2,384,256]{3,2,1,0:T(8,128)(2,1)S(1)}, bf16[2,2,384,256]{3,2,1,0:T(8,128)(2,1)S(1)}, u32[]{:S(2)}, u32[]{:S(2)}) collective-permute-start(bf16[2,2,384,256]{3,2,1,0:T(8,128)(2,1)S(1)} %collective-permute-done.3.refs_11_), channel_id=1, source_target_pairs={{1,2},{2,3},{5,6},{6,7},{9,10},{10,11},{13,14},{14,15},{17,18},{18... | collective-permute-start | bytes 2359304 | tf_op jit(solution)/shard_map/ppermute | solution.py:347
  32.3 46.2 %copy-start.19 = (bf16[384,2048]{1,0:T(8,128)(2,1)}, bf16[384,2048]{1,0:T(8,128)(2,1)S(1)}, u32[]{:S(2)}) copy-start(bf16[384,2048]{1,0:T(8,128)(2,1)S(1)} %collective-permute-done.7.refs_5_) | copy-start | bytes 4718596
  42.5 25.4 %copy-start.16 = (bf16[384,2048]{1,0:T(8,128)(2,1)}, bf16[384,2048]{1,0:T(8,128)(2,1)S(1)}, u32[]{:S(2)}) copy-start(bf16[384,2048]{1,0:T(8,128)(2,1)S(1)} %collective-permute-done.1.refs_2_) | copy-start | bytes 4718596
  45.5 8.6 %copy-start.17 = (bf16[384,2048]{1,0:T(8,128)(2,1)}, bf16[384,2048]{1,0:T(8,128)(2,1)S(1)}, u32[]{:S(2)}) copy-start(bf16[384,2048]{1,0:T(8,128)(2,1)S(1)} %collective-permute-done.refs_1_) | copy-start | bytes 4718596
  49.8 28.8 %copy-start.23 = (bf16[2,2,384,256]{3,2,1,0:T(8,128)(2,1)}, bf16[2,2,384,256]{3,2,1,0:T(8,128)(2,1)S(1)}, u32[]{:S(2)}) copy-start(bf16[2,2,384,256]{3,2,1,0:T(8,128)(2,1)S(1)} %collective-permute-done.6.refs_15_) | copy-start | bytes 2359300
  49.9 17.9 %collective-permute-start.10 = (bf16[192,2048]{1,0:T(8,128)(2,1)S(1)}, bf16[192,2048]{1,0:T(8,128)(2,1)S(1)}, u32[]{:S(2)}, u32[]{:S(2)}) collective-permute-start(bf16[192,2048]{1,0:T(8,128)(2,1)S(1)} %slice.16), channel_id=1, source_target_pairs={{0,8},{4,12},{8,0},{12,4},{1,9},{5,13},{9,1},{13,5},{2,10},{6,14},... | collective-permute-start | bytes 2359304 | tf_op jit(solution)/shard_map/ppermute | solution.py:343
  50.5 17.6 %collective-permute-start.11 = (bf16[192,2048]{1,0:T(8,128)(2,1)S(1)}, bf16[192,2048]{1,0:T(8,128)(2,1)S(1)}, u32[]{:S(2)}, u32[]{:S(2)}) collective-permute-start(bf16[192,2048]{1,0:T(8,128)(2,1)S(1)} %slice.17), channel_id=1, source_target_pairs={{0,4},{4,0},{8,12},{12,8},{1,5},{5,1},{9,13},{13,9},{2,6},{6,2},{1... | collective-permute-start | bytes 2359304 | tf_op jit(solution)/shard_map/ppermute | solution.py:343
  52.0 16.1 %collective-permute-start.8 = (bf16[2,2,384,256]{3,2,1,0:T(8,128)(2,1)S(1)}, bf16[2,2,384,256]{3,2,1,0:T(8,128)(2,1)S(1)}, u32[]{:S(2)}, u32[]{:S(2)}) collective-permute-start(bf16[2,2,384,256]{3,2,1,0:T(8,128)(2,1)S(1)} %collective-permute-done.4.refs_12_), channel_id=1, source_target_pairs={{2,3},{6,7},{10,11},{14,15},{18,19},{22,23},{26,27},{30,31}} | collective-permute-start | bytes 2359304 | tf_op jit(solution)/shard_map/ppermute | solution.py:347
  52.7 19.3 %collective-permute-start.9 = (bf16[2,2,384,256]{3,2,1,0:T(8,128)(2,1)S(1)}, bf16[2,2,384,256]{3,2,1,0:T(8,128)(2,1)S(1)}, u32[]{:S(2)}, u32[]{:S(2)}) collective-permute-start(bf16[2,2,384,256]{3,2,1,0:T(8,128)(2,1)S(1)} %collective-permute-done.6.refs_15_), channel_id=1, source_target_pairs={{1,0},{5,4},{9,8},{13,12},{17,16},{21,20},{25,24},{29,28}} | collective-permute-start | bytes 2359304 | tf_op jit(solution)/shard_map/ppermute | solution.py:351
  54.0 24.5 %collective-permute-start.12 = (bf16[384,2048]{1,0:T(8,128)(2,1)S(1)}, bf16[384,2048]{1,0:T(8,128)(2,1)S(1)}, u32[]{:S(2)}, u32[]{:S(2)}) collective-permute-start(bf16[384,2048]{1,0:T(8,128)(2,1)S(1)} %collective-permute-done.refs_1_), channel_id=1, source_target_pairs={{0,16},{16,0},{1,17},{17,1},{2,18},{18,2},{3,19},{19,3},{4,20},{20... | collective-permute-start | bytes 4718600 | tf_op jit(solution)/shard_map/ppermute | solution.py:339
  67.9 10.6 %collective-permute-start.13 = (bf16[384,2048]{1,0:T(8,128)(2,1)S(1)}, bf16[384,2048]{1,0:T(8,128)(2,1)S(1)}, u32[]{:S(2)}, u32[]{:S(2)}) collective-permute-start(bf16[384,2048]{1,0:T(8,128)(2,1)S(1)} %collective-permute-done.1.refs_2_), channel_id=1, source_target_pairs={{0,16},{16,0},{1,17},{17,1},{2,18},{18,2},{3,19},{19,3},{4,20},{20... | collective-permute-start | bytes 4718600 | tf_op jit(solution)/shard_map/ppermute | solution.py:339
  68.1 10.5 %copy-start.24 = (bf16[2,2,384,256]{3,2,1,0:T(8,128)(2,1)}, bf16[2,2,384,256]{3,2,1,0:T(8,128)(2,1)S(1)}, u32[]{:S(2)}) copy-start(bf16[2,2,384,256]{3,2,1,0:T(8,128)(2,1)S(1)} %collective-permute-done.8.refs_13_) | copy-start | bytes 2359300
  72.1 6.5 %copy-start.25 = (bf16[2,2,384,256]{3,2,1,0:T(8,128)(2,1)}, bf16[2,2,384,256]{3,2,1,0:T(8,128)(2,1)S(1)}, u32[]{:S(2)}) copy-start(bf16[2,2,384,256]{3,2,1,0:T(8,128)(2,1)S(1)} %collective-permute-done.9.refs_16_) | copy-start | bytes 2359300
  72.1 2.3 collective-permute-start.14
  72.1 6.4 %collective-permute-start.15 = (bf16[192,2048]{1,0:T(8,128)(2,1)S(1)}, bf16[192,2048]{1,0:T(8,128)(2,1)S(1)}, u32[]{:S(2)}, u32[]{:S(2)}) collective-permute-start(bf16[192,2048]{1,0:T(8,128)(2,1)S(1)} %collective-permute-done.11.refs_4_), channel_id=1, source_target_pairs={{0,16},{16,0},{1,17},{17,1},{2,18},{18,2},{3,19},{19,3},{4,20},{20... | collective-permute-start | bytes 2359304 | tf_op jit(solution)/shard_map/ppermute | solution.py:339
  72.6 33.2 %collective-permute-start.19 = (bf16[2,2,384,256]{3,2,1,0:T(8,128)(2,1)S(1)}, bf16[2,2,384,256]{3,2,1,0:T(8,128)(2,1)S(1)}, u32[]{:S(2)}, u32[]{:S(2)}) collective-permute-start(bf16[2,2,384,256]{3,2,1,0:T(8,128)(2,1)S(1)} %get-tuple-element.73.refs_1_), channel_id=1, source_target_pairs={{3,2},{2,1},{1,0},{7,6},{6,5},{5,4},{11,10},{10,9},{9,8},{15,14},{... | collective-permute-start | bytes 2359304 | tf_op jit(solution)/shard_map/ppermute | solution.py:351
  74.4 31.4 %collective-permute-start.18 = (bf16[2,2,384,256]{3,2,1,0:T(8,128)(2,1)S(1)}, bf16[2,2,384,256]{3,2,1,0:T(8,128)(2,1)S(1)}, u32[]{:S(2)}, u32[]{:S(2)}) collective-permute-start(bf16[2,2,384,256]{3,2,1,0:T(8,128)(2,1)S(1)} %get-tuple-element.73.refs_1_), channel_id=1, source_target_pairs={{0,1},{1,2},{2,3},{4,5},{5,6},{6,7},{8,9},{9,10},{10,11},{12,13},{... | collective-permute-start | bytes 2359304 | tf_op jit(solution)/shard_map/ppermute | solution.py:347
  78.5 1.2 copy-start.20
  78.5 1.7 copy-start.21
  102.7 22.2 %copy-start = (f32[384,512]{1,0:T(8,128)}, f32[384,512]{1,0:T(8,128)S(1)}, u32[]{:S(2)}) copy-start(f32[384,512]{1,0:T(8,128)S(1)} %get-tuple-element.87) | copy-start | bytes 2359300
  102.7 22.2 %copy-start.2 = (f32[384,512]{1,0:T(8,128)}, f32[384,512]{1,0:T(8,128)S(1)}, u32[]{:S(2)}) copy-start(f32[384,512]{1,0:T(8,128)S(1)} %get-tuple-element.94) | copy-start | bytes 2359300
  102.7 47.3 %collective-permute-start.24 = (bf16[2,2,256,1024]{3,2,1,0:T(8,128)(2,1)}, bf16[2,2,256,1024]{3,2,1,0:T(8,128)(2,1)S(1)}, u32[]{:S(2)}, u32[]{:S(2)}) collective-permute-start(bf16[2,2,256,1024]{3,2,1,0:T(8,128)(2,1)} %get-tuple-element.77), channel_id=1, source_target_pairs={{0,16},{16,0},{1,17},{17,1},{2,18},{18,2},{3,19},{19,3},{4,20},{20... | collective-permute-start | bytes 6291464 | tf_op jit(solution)/shard_map/ppermute | solution.py:339
  102.8 20.4 %collective-permute-start.16 = (bf16[2,384,512]{2,1,0:T(8,128)(2,1)S(1)}, bf16[2,384,512]{2,1,0:T(8,128)(2,1)S(1)}, u32[]{:S(2)}, u32[]{:S(2)}) collective-permute-start(bf16[2,384,512]{2,1,0:T(8,128)(2,1)S(1)} %get-tuple-element.71), channel_id=1, source_target_pairs={{0,1},{3,2},{4,5},{7,6},{8,9},{11,10},{12,13},{15,14},{16,17},{19,... | collective-permute-start | bytes 2359304 | tf_op jit(solution)/shard_map/ppermute | solution.py:367
  105.8 19.8 %collective-permute-start.20 = (bf16[2,2,384,256]{3,2,1,0:T(8,128)(2,1)S(1)}, bf16[2,2,384,256]{3,2,1,0:T(8,128)(2,1)S(1)}, u32[]{:S(2)}, u32[]{:S(2)}) collective-permute-start(bf16[2,2,384,256]{3,2,1,0:T(8,128)(2,1)S(1)} %collective-permute-done.18.refs_2_), channel_id=1, source_target_pairs={{1,2},{2,3},{5,6},{6,7},{9,10},{10,11},{13,14},{14,15},{17,18},{18... | collective-permute-start | bytes 2359304 | tf_op jit(solution)/shard_map/ppermute | solution.py:347
  106.5 22.0 %collective-permute-start.22 = (bf16[2,2,384,256]{3,2,1,0:T(8,128)(2,1)S(1)}, bf16[2,2,384,256]{3,2,1,0:T(8,128)(2,1)S(1)}, u32[]{:S(2)}, u32[]{:S(2)}) collective-permute-start(bf16[2,2,384,256]{3,2,1,0:T(8,128)(2,1)S(1)} %collective-permute-done.19.refs_5_), channel_id=1, source_target_pairs={{2,1},{1,0},{6,5},{5,4},{10,9},{9,8},{14,13},{13,12},{18,17},{17,1... | collective-permute-start | bytes 2359304 | tf_op jit(solution)/shard_map/ppermute | solution.py:351
  124.9 10.0 %collective-permute-start.17 = (bf16[2,384,512]{2,1,0:T(8,128)(2,1)S(1)}, bf16[2,384,512]{2,1,0:T(8,128)(2,1)S(1)}, u32[]{:S(2)}, u32[]{:S(2)}) collective-permute-start(bf16[2,384,512]{2,1,0:T(8,128)(2,1)S(1)} %add_convert_fusion.3), channel_id=1, source_target_pairs={{1,2},{2,1},{5,6},{6,5},{9,10},{10,9},{13,14},{14,13},{17,18},{18,... | collective-permute-start | bytes 2359304 | tf_op jit(solution)/shard_map/ppermute | solution.py:359
  125.6 9.3 %collective-permute-start.21 = (bf16[2,2,384,256]{3,2,1,0:T(8,128)(2,1)S(1)}, bf16[2,2,384,256]{3,2,1,0:T(8,128)(2,1)S(1)}, u32[]{:S(2)}, u32[]{:S(2)}) collective-permute-start(bf16[2,2,384,256]{3,2,1,0:T(8,128)(2,1)S(1)} %collective-permute-done.20.refs_3_), channel_id=1, source_target_pairs={{2,3},{6,7},{10,11},{14,15},{18,19},{22,23},{26,27},{30,31}} | collective-permute-start | bytes 2359304 | tf_op jit(solution)/shard_map/ppermute | solution.py:347
  128.5 21.5 %collective-permute-start.23 = (bf16[2,2,384,256]{3,2,1,0:T(8,128)(2,1)S(1)}, bf16[2,2,384,256]{3,2,1,0:T(8,128)(2,1)S(1)}, u32[]{:S(2)}, u32[]{:S(2)}) collective-permute-start(bf16[2,2,384,256]{3,2,1,0:T(8,128)(2,1)S(1)} %collective-permute-done.22.refs_6_), channel_id=1, source_target_pairs={{1,0},{5,4},{9,8},{13,12},{17,16},{21,20},{25,24},{29,28}} | collective-permute-start | bytes 2359304 | tf_op jit(solution)/shard_map/ppermute | solution.py:351
  129.8 43.7 %collective-permute-start.27 = (bf16[2,384,512]{2,1,0:T(8,128)(2,1)S(1)}, bf16[2,384,512]{2,1,0:T(8,128)(2,1)S(1)}, u32[]{:S(2)}, u32[]{:S(2)}) collective-permute-start(bf16[2,384,512]{2,1,0:T(8,128)(2,1)S(1)} %get-tuple-element.84), channel_id=1, source_target_pairs={{0,1},{3,2},{4,5},{7,6},{8,9},{11,10},{12,13},{15,14},{16,17},{19,... | collective-permute-start | bytes 2359304 | tf_op jit(solution)/shard_map/ppermute | solution.py:367
  135.0 15.1 %copy-start.14 = (bf16[2,384,512]{2,1,0:T(8,128)(2,1)}, bf16[2,384,512]{2,1,0:T(8,128)(2,1)S(1)}, u32[]{:S(2)}) copy-start(bf16[2,384,512]{2,1,0:T(8,128)(2,1)S(1)} %collective-permute-done.17) | copy-start | bytes 2359300
  150.0 1.3 copy-start.18
  151.4 22.2 %copy-start.11 = (f32[2,384,512]{2,1,0:T(8,128)S(1)}, f32[2,384,512]{2,1,0:T(8,128)}, u32[]{:S(2)}) copy-start(f32[2,384,512]{2,1,0:T(8,128)} %get-tuple-element.83) | copy-start | bytes 4718596
  172.0 2.7 %copy-start.3 = (f32[384,512]{1,0:T(8,128)}, f32[384,512]{1,0:T(8,128)S(1)}, u32[]{:S(2)}) copy-start(f32[384,512]{1,0:T(8,128)S(1)} %get-tuple-element.91) | copy-start | bytes 2359300
  172.0 2.7 %copy-start.5 = (f32[384,512]{1,0:T(8,128)}, f32[384,512]{1,0:T(8,128)S(1)}, u32[]{:S(2)}) copy-start(f32[384,512]{1,0:T(8,128)S(1)} %get-tuple-element.97) | copy-start | bytes 2359300
  172.0 19.5 %collective-permute-start.26 = (bf16[2,384,512]{2,1,0:T(8,128)(2,1)S(1)}, bf16[2,384,512]{2,1,0:T(8,128)(2,1)S(1)}, u32[]{:S(2)}, u32[]{:S(2)}) collective-permute-start(bf16[2,384,512]{2,1,0:T(8,128)(2,1)S(1)} %get-tuple-element.82), channel_id=1, source_target_pairs={{0,1},{3,2},{4,5},{7,6},{8,9},{11,10},{12,13},{15,14},{16,17},{19,... | collective-permute-start | bytes 2359304 | tf_op jit(solution)/shard_map/ppermute | solution.py:367
  173.5 17.9 %copy-start.13 = (f32[2,384,512]{2,1,0:T(8,128)S(1)}, f32[2,384,512]{2,1,0:T(8,128)}, u32[]{:S(2)}) copy-start(f32[2,384,512]{2,1,0:T(8,128)} %get-tuple-element.96) | copy-start | bytes 4718596
  174.7 19.7 %collective-permute-start.28 = (bf16[2,384,512]{2,1,0:T(8,128)(2,1)}, bf16[2,384,512]{2,1,0:T(8,128)(2,1)}, u32[]{:S(2)}, u32[]{:S(2)}) collective-permute-start(bf16[2,384,512]{2,1,0:T(8,128)(2,1)} %add_convert_fusion.2), channel_id=1, source_target_pairs={{1,2},{2,1},{5,6},{6,5},{9,10},{10,9},{13,14},{14,13},{17,18},{18,... | collective-permute-start | bytes 2359304 | tf_op jit(solution)/shard_map/ppermute | solution.py:359
  176.3 32.1 %collective-permute-start.30 = (bf16[2,384,512]{2,1,0:T(8,128)(2,1)}, bf16[2,384,512]{2,1,0:T(8,128)(2,1)}, u32[]{:S(2)}, u32[]{:S(2)}) collective-permute-start(bf16[2,384,512]{2,1,0:T(8,128)(2,1)} %get-tuple-element.90), channel_id=1, source_target_pairs={{0,1},{3,2},{4,5},{7,6},{8,9},{11,10},{12,13},{15,14},{16,17},{19,... | collective-permute-start | bytes 2359304 | tf_op jit(solution)/shard_map/ppermute | solution.py:367
  192.6 18.1 %collective-permute-start.35 = (bf16[2,384,512]{2,1,0:T(8,128)(2,1)}, bf16[2,384,512]{2,1,0:T(8,128)(2,1)}, u32[]{:S(2)}, u32[]{:S(2)}) collective-permute-start(bf16[2,384,512]{2,1,0:T(8,128)(2,1)} %add_convert_fusion), channel_id=1, source_target_pairs={{1,2},{2,1},{5,6},{6,5},{9,10},{10,9},{13,14},{14,13},{17,18},{18,... | collective-permute-start | bytes 2359304 | tf_op jit(solution)/shard_map/ppermute | solution.py:359
  194.4 14.0 %copy-start.12 = (f32[2,384,512]{2,1,0:T(8,128)S(1)}, f32[2,384,512]{2,1,0:T(8,128)}, u32[]{:S(2)}) copy-start(f32[2,384,512]{2,1,0:T(8,128)} %get-tuple-element.89) | copy-start | bytes 4718596
  194.4 45.6 %collective-permute-start.25 = (bf16[2,2,256,1024]{3,2,1,0:T(8,128)(2,1)}, bf16[2,2,256,1024]{3,2,1,0:T(8,128)(2,1)S(1)}, u32[]{:S(2)}, u32[]{:S(2)}) collective-permute-start(bf16[2,2,256,1024]{3,2,1,0:T(8,128)(2,1)} %get-tuple-element.79), channel_id=1, source_target_pairs={{0,16},{16,0},{1,17},{17,1},{2,18},{18,2},{3,19},{19,3},{4,20},{20... | collective-permute-start | bytes 6291464 | tf_op jit(solution)/shard_map/ppermute | solution.py:339
  195.9 21.7 %collective-permute-start.33 = (bf16[384,512]{1,0:T(8,128)(2,1)S(1)}, bf16[384,512]{1,0:T(8,128)(2,1)S(1)}, u32[]{:S(2)}, u32[]{:S(2)}) collective-permute-start(bf16[384,512]{1,0:T(8,128)(2,1)S(1)} %fusion.5), channel_id=1, source_target_pairs={{0,1},{1,0},{2,3},{3,2},{4,5},{5,4},{6,7},{7,6},{8,9},{9,8},{10,11... | collective-permute-start | bytes 1179656 | tf_op jit(solution)/shard_map/ppermute | solution.py:355
  208.4 2.3 copy-start.6
  209.9 6.5 %copy-start.1 = (f32[384,512]{1,0:T(8,128)S(1)}, f32[384,512]{1,0:T(8,128)}, u32[]{:S(2)}) copy-start(f32[384,512]{1,0:T(8,128)} %copy-done) | copy-start | bytes 2359300
  209.9 17.3 %collective-permute-start.31 = (bf16[2,384,512]{2,1,0:T(8,128)(2,1)S(1)}, bf16[2,384,512]{2,1,0:T(8,128)(2,1)S(1)}, u32[]{:S(2)}, u32[]{:S(2)}) collective-permute-start(bf16[2,384,512]{2,1,0:T(8,128)(2,1)S(1)} %add_convert_fusion.1), channel_id=1, source_target_pairs={{1,2},{2,1},{5,6},{6,5},{9,10},{10,9},{13,14},{14,13},{17,18},{18,... | collective-permute-start | bytes 2359304 | tf_op jit(solution)/shard_map/ppermute | solution.py:359
  210.8 6.9 %copy-start.15 = (bf16[2,384,512]{2,1,0:T(8,128)(2,1)S(1)}, bf16[2,384,512]{2,1,0:T(8,128)(2,1)}, u32[]{:S(2)}) copy-start(bf16[2,384,512]{2,1,0:T(8,128)(2,1)} %copy-done.14) | copy-start | bytes 2359300
  212.0 14.0 %collective-permute-start.36 = (bf16[384,512]{1,0:T(8,128)(2,1)S(1)}, bf16[384,512]{1,0:T(8,128)(2,1)S(1)}, u32[]{:S(2)}, u32[]{:S(2)}) collective-permute-start(bf16[384,512]{1,0:T(8,128)(2,1)S(1)} %fusion.3), channel_id=1, source_target_pairs={{0,1},{1,0},{2,3},{3,2},{4,5},{5,4},{6,7},{7,6},{8,9},{9,8},{10,11... | collective-permute-start | bytes 1179656 | tf_op jit(solution)/shard_map/ppermute | solution.py:355
  217.5 14.8 %collective-permute-start.29 = (bf16[384,512]{1,0:T(8,128)(2,1)S(1)}, bf16[384,512]{1,0:T(8,128)(2,1)S(1)}, u32[]{:S(2)}, u32[]{:S(2)}) collective-permute-start(bf16[384,512]{1,0:T(8,128)(2,1)S(1)} %fusion.9), channel_id=1, source_target_pairs={{0,1},{1,0},{2,3},{3,2},{4,5},{5,4},{6,7},{7,6},{8,9},{9,8},{10,11... | collective-permute-start | bytes 1179656 | tf_op jit(solution)/shard_map/ppermute | solution.py:355
  217.8 9.4 %copy-start.4 = (f32[384,512]{1,0:T(8,128)S(1)}, f32[384,512]{1,0:T(8,128)}, u32[]{:S(2)}) copy-start(f32[384,512]{1,0:T(8,128)} %copy-done.3) | copy-start | bytes 2359300
  217.8 22.3 %collective-permute-start.34 = (f32[384,512]{1,0:T(8,128)S(1)}, f32[384,512]{1,0:T(8,128)S(1)}, u32[]{:S(2)}, u32[]{:S(2)}) collective-permute-start(f32[384,512]{1,0:T(8,128)S(1)} %fusion.6), channel_id=1, source_target_pairs={{0,16},{16,0},{1,17},{17,1},{2,18},{18,2},{3,19},{19,3},{4,20},{20... | collective-permute-start | bytes 2359304 | tf_op jit(solution)/shard_map/ppermute | solution.py:339
  227.1 12.9 %collective-permute-start.37 = (f32[384,512]{1,0:T(8,128)S(1)}, f32[384,512]{1,0:T(8,128)S(1)}, u32[]{:S(2)}, u32[]{:S(2)}) collective-permute-start(f32[384,512]{1,0:T(8,128)S(1)} %fusion.4), channel_id=1, source_target_pairs={{0,16},{16,0},{1,17},{17,1},{2,18},{18,2},{3,19},{19,3},{4,20},{20... | collective-permute-start | bytes 2359304 | tf_op jit(solution)/shard_map/ppermute | solution.py:339
  227.4 12.5 %collective-permute-start.32 = (bf16[384,512]{1,0:T(8,128)(2,1)S(1)}, bf16[384,512]{1,0:T(8,128)(2,1)S(1)}, u32[]{:S(2)}, u32[]{:S(2)}) collective-permute-start(bf16[384,512]{1,0:T(8,128)(2,1)S(1)} %fusion.7), channel_id=1, source_target_pairs={{0,1},{1,0},{2,3},{3,2},{4,5},{5,4},{6,7},{7,6},{8,9},{9,8},{10,11... | collective-permute-start | bytes 1179656 | tf_op jit(solution)/shard_map/ppermute | solution.py:355

commit v2 on v1

--- a/solution.py
+++ b/solution.py
@@ -55,8 +55,20 @@
     return (amplitudes, gamma)
 
 
-GROUPS = 2
+BLOCKS = 2
+GROUPS = 3
 SLICES = 4
+SPLIT = (True, False, True)
+
+
+def parts_of(group, batch):
+    return (slice(batch, 2 * batch), slice(0, batch)) if SPLIT[group] else (slice(0, 2 * batch),)
+
+
+def place_of(group, block):
+    if group == 0:
+        return 0, 0, block
+    return 1, (group - 1) * (block // 2), block // 2
 
 
 def group_kernel(pieces, group, *refs):
@@ -66,12 +78,13 @@
     (bra,) = take(1)
     ups, downs = take(3), take(3)
     occ_ref, virt_ref = take(2)
-    other, _ = take(2) if group else (None, None)
+    aliased = take(2) if group else None
     whole_ref, half_ref = take(2)
-    own_ref, pair_ref, far_ref, send_ref = (take(2) for _ in range(4))
+    own_ref, pair_ref, far_ref, send_ref = (take(1 + SPLIT[group]) for _ in range(4))
     (ket_all,) = (None,) if group else take(1)
     kv, bv, bt, t2, amps, given, ket_sem, bra_sem, out_sem = refs
-    batch, width = bra.shape[2:]
+    batch, block_width = bra.shape[2:]
+    number, start, width = place_of(group, block_width)
     span = ket[0].shape[1] // 2
     half = whole_ref.shape[2] // 2
     part = span // SLICES
@@ -83,7 +96,7 @@
     def bra_copies(source, home, slot):
         return [
             pltpu.make_async_copy(
-                source.at[q, i],
+                source.at[q, i, :, pl.ds(start, width)],
                 bv.at[home, pl.ds(q * batch, batch), pl.ds(i * width, width)],
                 bra_sem.at[slot, q, i],
             )
@@ -125,13 +138,14 @@
                 )
                 copy.start()
                 copies[n].append(copy)
-    if group:
-        given_in = pltpu.make_async_copy(other, given, out_sem.at[2])
+    if group == 1:
+        given_in = pltpu.make_async_copy(aliased[0], given, out_sem.at[2])
         given_in.start()
     for slot in range(4):
         for copy in bra_copies(bra, slot, slot):
             copy.wait()
-    first_at = here_row * (2 * half) + me * half + group * width
+    row_at = number * block_width + start
+    first_at = here_row * (2 * half) + me * half + row_at
     first = virt_ref[:, pl.ds(pl.multiple_of(first_at, 128), width)]
     first = jnp.broadcast_to(first, (width, width)).T[:, :1]
     for d in range(4):
@@ -160,18 +174,20 @@
                     i * width : (i + 1) * width,
                     j * span + n * part : j * span + (n + 1) * part,
                 ] = block
-    at = pl.multiple_of(me * half + group * width, 16)
+    at = pl.multiple_of(me * half + row_at, 16)
     outs = [
         pltpu.make_async_copy(amps, whole_ref.at[:, :, pl.ds(at, width), :], out_sem.at[0]),
-        pltpu.make_async_copy(amps, half_ref, out_sem.at[1]),
+        pltpu.make_async_copy(amps, half_ref.at[:, :, pl.ds(start, width), :], out_sem.at[1]),
     ]
-    if group:
+    if group == 1:
         given_in.wait()
         at = pl.multiple_of((1 - me) * half, 16)
         outs.append(
-            pltpu.make_async_copy(given, whole_ref.at[:, :, pl.ds(at, width), :], out_sem.at[2])
+            pltpu.make_async_copy(
+                given, whole_ref.at[:, :, pl.ds(at, block_width), :], out_sem.at[2]
+            )
         )
-    else:
+    if group == 0:
         outs.append(pltpu.make_async_copy(kv, ket_all, out_sem.at[2]))
     for copy in outs:
         copy.start()
@@ -187,63 +203,68 @@
 
     for n in range(2):
         share = share_of(jnp.where(low, 2 + n, n))
-        for q in range(2):
-            far_ref[q][n] = share[q * batch : (q + 1) * batch]
-            send_ref[q][n] = share[q * batch : (q + 1) * batch].astype(jnp.bfloat16)
+        for p, rows in enumerate(parts_of(group, batch)):
+            far_ref[p][n] = share[rows]
+            send_ref[p][n] = share[rows].astype(jnp.bfloat16)
     for out, home in ((pair_ref, pair), (own_ref, here_col)):
         share = share_of(home)
-        for q in range(2):
-            out[q][...] = share[q * batch : (q + 1) * batch]
+        for p, rows in enumerate(parts_of(group, batch)):
+            out[p][...] = share[rows]
     for copy in outs:
         copy.wait()
 
 
 def run_group(group, ket, pieces, bras, energies, held):
-    _, _, batch, width = bras[0].shape
+    _, _, batch, block_width = bras[0].shape
+    _, _, width = place_of(group, block_width)
     span = ket[0].shape[1] // 2
-    half = width * GROUPS
+    half = block_width * BLOCKS
     total = 8 * batch
     flops = 2 * 2 * total * 2 * width * 2 * span
     any_space = pl.BlockSpec(memory_space=pl.ANY)
     in_vmem = pl.BlockSpec(memory_space=pltpu.VMEM)
     in_hbm = pl.BlockSpec(memory_space=pltpu.HBM)
     ahead = len(ket) + len(bras) + 2
-    block = jax.ShapeDtypeStruct((batch, 2 * width), jnp.float32)
-    far = jax.ShapeDtypeStruct((2, batch, 2 * width), jnp.float32)
-    send = jax.ShapeDtypeStruct((2, batch, 2 * width), jnp.bfloat16)
+    count = 1 + SPLIT[group]
+    rows = 2 * batch // count
+    block = jax.ShapeDtypeStruct((rows, 2 * width), jnp.float32)
+    far = jax.ShapeDtypeStruct((2, rows, 2 * width), jnp.float32)
+    send = jax.ShapeDtypeStruct((2, rows, 2 * width), jnp.bfloat16)
+    half_shape = (2, 2, block_width, span)
     results = pl.pallas_call(
         functools.partial(group_kernel, pieces, group),
         out_shape=(
             jax.ShapeDtypeStruct((2, 2, 2 * half, span), jnp.bfloat16),
-            jax.ShapeDtypeStruct((2, 2, width, span), jnp.bfloat16),
+            jax.ShapeDtypeStruct(half_shape, jnp.bfloat16),
         )
-        + (block,) * 4
-        + (far,) * 2
-        + (send,) * 2
+        + (block,) * (2 * count)
+        + (far,) * count
+        + (send,) * count
         + (() if group else (jax.ShapeDtypeStruct((total, 2 * span), jnp.bfloat16),)),
         in_specs=[in_hbm if group else any_space] * len(ket)
         + [any_space] * len(bras)
         + [pl.BlockSpec(memory_space=pltpu.SMEM), in_vmem]
         + [any_space] * len(held),
-        out_specs=(any_space, any_space) + (in_vmem,) * 8 + (() if group else (in_hbm,)),
+        out_specs=(any_space, any_space) + (in_vmem,) * (4 * count) + (() if group else (in_hbm,)),
         scratch_shapes=[
             pltpu.VMEM((total, 2 * span), jnp.bfloat16),
             pltpu.VMEM((4, 2 * batch, 2 * width), jnp.bfloat16),
             pltpu.VMEM((2 * width, total), jnp.bfloat16),
             pltpu.VMEM((2 * width, 2 * span), jnp.bfloat16),
             pltpu.VMEM((2, 2, width, span), jnp.bfloat16),
-            pltpu.VMEM((2, 2, width, span), jnp.bfloat16),
+            pltpu.VMEM(half_shape if group == 1 else (2, 2, 16, 128), jnp.bfloat16),
             pltpu.SemaphoreType.DMA((SLICES, 2 * len(pieces), 2)),
             pltpu.SemaphoreType.DMA((4, 2, 2)),
             pltpu.SemaphoreType.DMA((3,)),
         ],
-        input_output_aliases={ahead + 1: 0} if held else {},
+        input_output_aliases=({}, {ahead + 1: 0}, {ahead: 1, ahead + 1: 0})[group],
         compiler_params=pltpu.CompilerParams(vmem_limit_bytes=44 * 2**20),
         cost_estimate=pl.CostEstimate(
             flops=flops, bytes_accessed=total * 2 * span * 2, transcendentals=0
         ),
     )(*ket, *bras, *energies, *held)
-    return results[:2], *(results[n : n + 2] for n in (2, 4, 6, 8)), results[10:]
+    ends = [2 + n * count for n in range(5)]
+    return results[:2], *(results[n : n + count] for n in ends[:4]), results[ends[4] :]
 
 
 def pick_kernel(bra, kept_out, given_out):
@@ -251,7 +272,7 @@
     span = bra.shape[1] // 2
     me = lax.axis_index("occ")
     for side, out in ((1 - me, given_out), (me, kept_out)):
-        for g in range(GROUPS):
+        for g in range(BLOCKS):
             for i in range(2):
                 home = i * span + side * (span // 2) + g * width
                 out[g, i] = bra[:, pl.ds(pl.multiple_of(home, 128), width)]
@@ -259,7 +280,7 @@
 
 def pick(bra):
     batch, columns = bra.shape
-    part = jax.ShapeDtypeStruct((GROUPS, 2, batch, columns // 4 // GROUPS), bra.dtype)
+    part = jax.ShapeDtypeStruct((BLOCKS, 2, batch, columns // 4 // BLOCKS), bra.dtype)
     return pl.pallas_call(
         pick_kernel,
         out_shape=(part, part),
@@ -273,10 +294,11 @@
 def close_kernel(*refs):
     other, _, *totals = refs[: 2 + 2 * GROUPS]
     amps, gamma, amp_buffer, gamma_buffer, sems, gamma_sems = refs[2 + 2 * GROUPS :]
-    width = other.shape[2]
-    half = width * GROUPS
+    block_width = other.shape[2]
+    half = block_width * BLOCKS
+    batch = gamma.shape[0]
     me = lax.axis_index("occ")
-    at = pl.multiple_of((1 - me) * half + half - width, 16)
+    at = pl.multiple_of((1 - me) * half + half - block_width, 16)
     blocks = [(i, j) for i in range(2) for j in range(2)]
     reads = [
         pltpu.make_async_copy(other.at[i, j], amp_buffer.at[i, j], sems.at[0, i, j])
@@ -284,53 +306,58 @@
     ]
     writes = [
         pltpu.make_async_copy(
-            amp_buffer.at[i, j], amps.at[i, j, pl.ds(at, width), :], sems.at[1, i, j]
+            amp_buffer.at[i, j], amps.at[i, j, pl.ds(at, block_width), :], sems.at[1, i, j]
         )
         for i, j in blocks
     ]
     for copy in reads:
         copy.start()
     for n in range(2 * GROUPS):
-        side, g = divmod(n, GROUPS)
-        home = jnp.where(me == side, 0, half) + g * width
+        side, group = divmod(n, GROUPS)
+        number, start, width = place_of(group, block_width)
+        at = number * block_width + start
+        home = jnp.where(me == side, 0, half) + at
+        columns = pl.ds(side * half + at, width)
         for i in range(2):
-            gamma_buffer[n, :, i, :] = totals[n][:, i * width : (i + 1) * width]
+            gamma_buffer[:, i, columns] = totals[n][:batch, i * width : (i + 1) * width]
         writes.append(
             pltpu.make_async_copy(
-                gamma_buffer.at[n],
+                gamma_buffer.at[:, :, columns],
                 gamma.at[:, :, pl.ds(pl.multiple_of(home, 128), width)],
                 gamma_sems.at[n],
             )
         )
-        reads[n].wait()
-        writes[n].start()
+        if n < len(blocks):
+            reads[n].wait()
+            writes[n].start()
         writes[-1].start()
     for copy in writes:
         copy.wait()
 
 
 def close(other, whole, kept, received):
-    batch, double = received[0].shape
+    batch = received[0].shape[0]
+    columns = whole.shape[2]
     any_space = pl.BlockSpec(memory_space=pl.ANY)
     in_vmem = pl.BlockSpec(memory_space=pltpu.VMEM)
     return pl.pallas_call(
         close_kernel,
         out_shape=(
             jax.ShapeDtypeStruct(whole.shape, whole.dtype),
-            jax.ShapeDtypeStruct((batch, 2, GROUPS * double), jnp.float32),
+            jax.ShapeDtypeStruct((batch, 2, columns), jnp.float32),
         ),
         in_specs=[any_space, any_space] + [in_vmem] * (2 * GROUPS),
         out_specs=(any_space, any_space),
         scratch_shapes=[
             pltpu.VMEM(other.shape, other.dtype),
-            pltpu.VMEM((2 * GROUPS, batch, 2, double // 2), jnp.float32),
+            pltpu.VMEM((batch, 2, columns), jnp.float32),
             pltpu.SemaphoreType.DMA((2, 2, 2)),
             pltpu.SemaphoreType.DMA((2 * GROUPS,)),
         ],
         input_output_aliases={1: 0},
         compiler_params=pltpu.CompilerParams(vmem_limit_bytes=48 * 2**20),
         cost_estimate=pl.CostEstimate(
-            flops=0, bytes_accessed=4 * other.size + 16 * batch * double * GROUPS, transcendentals=0
+            flops=0, bytes_accessed=4 * other.size + 16 * batch * columns, transcendentals=0
         ),
     )(other, whole, *kept, *received)
 
@@ -419,40 +446,50 @@
         ours = lax.dynamic_index_in_dim(two, near, 0, keepdims=False)
         return own + up_cast(ours) + up_cast(three)
 
-    both = (1, 0)
+    def finish_all(group, own, two, three):
+        total = [finish(*part) for part in zip(own, two, three)]
+        if not SPLIT[group]:
+            total = [total[0][batch:], total[0][:batch]]
+        return total[1], swap(total[0])
+
     arrived = [bra[0], *ups[0], *downs[0]]
     (whole, mine), own0, pair0, far0, send0, (ket_all,) = run_group(
         0, ket, pieces, arrived, energies, ()
     )
-    one0 = {q: inward(send0[q]) for q in both}
-    own_first, up, down = tie(own0[0], ups[1][0], downs[1][0])
-    for hop in (1, 2):
-        ups[1].append(hop_up(ups[1][hop - 1] if hop > 1 else up, hop))
-        downs[1].append(hop_down(downs[1][hop - 1] if hop > 1 else down, hop))
-    other0 = swap(mine)
-    two0 = {1: cross(far0[1], one0[1])}
+    one0 = [inward(send) for send in send0]
+    own_last, up, down = tie(own0[1], ups[1][0], downs[1][0])
+    own0 = (own0[0], own_last)
+    ups[1] += [hop_up(up, 1)]
+    downs[1] += [hop_down(down, 1)]
+    ups[1] += [hop_up(ups[1][1], 2)]
+    downs[1] += [hop_down(downs[1][1], 2)]
+    other = swap(mine)
+    two0 = [cross(far0[0], one0[0])]
     arrived = [bra[1], *ups[1], *downs[1]]
-    two0[1], arrived[0] = tie(two0[1], arrived[0])
+    two0[0], arrived[0] = tie(two0[0], arrived[0])
     (whole, mine), own1, pair1, far1, send1, _ = run_group(
-        1, [ket_all], pieces, arrived, energies, (other0, whole)
-    )
-    one1 = {q: inward(send1[q]) for q in both}
-    other1 = swap(mine)
-    two0[0] = cross(far0[0], one0[0])
-    two1 = {q: cross(far1[q], one1[q]) for q in both}
-    one1[1], two0[0], two0[1] = tie(one1[1], two0[0], two0[1])
-    own0 = (own_first, own0[1])
-    three0 = {q: exchange(pair0[q], two0[q]) for q in both}
-    three1 = {q: exchange(pair1[q], two1[q]) for q in both}
-    received = [
-        swap(finish(own[1], two[1], three[1]))
-        for own, two, three in ((own0, two0, three0), (own1, two1, three1))
+        1, [ket_all], pieces, arrived, energies, (other, whole)
+    )
+    one1 = [inward(send) for send in send1]
+    arrived = list(arrived)
+    (whole, mine), own2, pair2, far2, send2, _ = run_group(
+        2, [ket_all], pieces, arrived, energies, (mine, whole)
+    )
+    one2 = [inward(send) for send in send2]
+    other = swap(mine)
+    two0.append(cross(far0[1], one0[1]))
+    two1 = [cross(*part) for part in zip(far1, one1)]
+    two2 = [cross(*part) for part in zip(far2, one2)]
+    one2[0], two0[1] = tie(one2[0], two0[1])
+    three0 = [exchange(*part) for part in zip(pair0, two0)]
+    three1 = [exchange(*part) for part in zip(pair1, two1)]
+    three2 = [exchange(*part) for part in zip(pair2, two2)]
+    ends = [
+        finish_all(0, own0, two0, three0),
+        finish_all(1, own1, two1, three1),
+        finish_all(2, own2, two2, three2),
     ]
-    kept = [
-        finish(own[0], two[0], three[0])
-        for own, two, three in ((own0, two0, three0), (own1, two1, three1))
-    ]
-    return close(other1, whole, kept, received)
+    return close(other, whole, [end[0] for end in ends], [end[1] for end in ends])
 
 
 def solution(mesh):
@@ -463,7 +500,7 @@
             sizes["occ"] == 2
             and sizes["row"] == 4
             and sizes["col"] == 4
-            and bra_factor.shape[2] % (256 * GROUPS) == 0
+            and bra_factor.shape[2] % 1024 == 0
             and ket_factor.shape[2] % 512 == 0
             and bra_factor.shape[0] % 128 == 0
         )

time: 244 us -> 239 us (0.980)
  waiting for transfers between devices: 121 us -> 87.9 us
  starting transfers between devices: 55.8 us -> 86.3 us
  other arithmetic: 12.1 us -> 7.96 us
  Pallas kernels: 46.1 us -> 48.9 us
    ppermute x4 -> x5, starting transfers between devices: 10.5 us -> 39.8 us  [pairs(): return lax.ppermute(x, 'col', [(0, 1), (1, 0), (2, 3), (3, 2)])]
    ppermute x6, waiting for transfers between devices: 39.6 us -> 24.9 us  [hop_down(): return lax.ppermute(x, 'col', [(3 - c, 2 - c) for c in range(first, 3)])]
    ppermute x4 -> x5, waiting for transfers between devices: 16.9 us -> 5.35 us  [pairs(): return lax.ppermute(x, 'col', [(0, 1), (1, 0), (2, 3), (3, 2)])]
    ppermute x4 -> x5, waiting for transfers between devices: 36.2 us -> 28.8 us  [inward(): return lax.ppermute(x, 'col', [(0, 1), (3, 2)])]
    pallas_call x2 -> x3, Pallas kernels: 43.1 us -> 45.8 us  [run_group(): pl.pallas_call(functools.partial(group_kernel, pieces, group), out_shape=...]
    convert_element_type x4 -> x5, other arithmetic: 3.9 us -> 1.43 us  [exchange(): return pairs((pair + up_cast(theirs)).astype(jnp.bfloat16))]
    unnamed x54 -> x46, local copies, waits for them, and re-layouts: 5.99 us -> 5.09 us
    convert_element_type x4 -> x5, other arithmetic: 5.5 us -> 4.86 us  [cross(): return across((far + up_cast(one)).astype(jnp.bfloat16))]
  transfers between devices with their start and end apart: 38 -> 42, of which waited for: 17 -> 17; matrix products, arithmetic and copies ran while one was open for 5% -> 4% of each run, Pallas kernels for 18% -> 19%
where the time goes in v2:
time: 239 us; the launch traced here: 238 us
  waiting for transfers between devices  87.9 us (37%)
  starting transfers between devices  86.3 us (36%)
  Pallas kernels  48.9 us (20%)
  other arithmetic  7.96 us (3%)
  local copies, waits for them, and re-layouts  5.28 us (2%)
    pallas_call x3, Pallas kernels, run_group(): pl.pallas_call(functools.partial(group_kernel, pieces, group), out_shape=...  45.8 us
    ppermute x5, starting transfers between devices, pairs(): return lax.ppermute(x, 'col', [(0, 1), (1, 0), (2, 3), (3, 2)])  39.8 us
    ppermute x5, waiting for transfers between devices, inward(): return lax.ppermute(x, 'col', [(0, 1), (3, 2)])  28.8 us
    ppermute x4, waiting for transfers between devices, planar(): return lax.ppermute(x, 'row', [(r, r ^ offset) for r in range(4)])  27.1 us
    ppermute x6, waiting for transfers between devices, hop_down(): return lax.ppermute(x, 'col', [(3 - c, 2 - c) for c in range(first, 3)])  24.9 us
    ppermute x5, starting transfers between devices, inward(): return lax.ppermute(x, 'col', [(0, 1), (3, 2)])  12.9 us
    ppermute x6, starting transfers between devices, hop_up(): return lax.ppermute(x, 'col', [(c, c + 1) for c in range(first, 3)])  12.4 us
    ppermute x6, starting transfers between devices, hop_down(): return lax.ppermute(x, 'col', [(3 - c, 2 - c) for c in range(first, 3)])  7.72 us
  transfers between devices with their start and end apart: 42, of which 17 were waited for; matrix products, arithmetic and copies ran while one was open for 4% of the time, Pallas kernels for 19%

profile of v2, /device:TPU:0, one launch (start us, length us, event | category | flops | bytes accessed | tf_op | source)
XLA Modules:
  0.0 237.8 jit_solution(17875863790159309851)
XLA Ops:
  0.6 1.8 copy.11
  2.7 0.5 collective-permute-start.2
  3.2 0.6 copy-done.11
  3.9 0.4 copy.10
  4.4 0.5 collective-permute-start.7
  4.9 2.6 %collective-permute-start.1 = (bf16[384,2048]{1,0:T(8,128)(2,1)S(1)}, bf16[384,2048]{1,0:T(8,128)(2,1)S(1)}, u32[]{:S(2)}, u32[]{:S(2)}) collective-permute-start(bf16[384,2048]{1,0:T(8,128)(2,1)S(1)} %bitcast.49), channel_id=1, source_target_pairs={{0,8},{4,12},{8,0},{12,4},{1,9},{5,13},{9,1},{13,5},{2,10},{6,14},... | collective-permute-start | bytes 4718600 | tf_op jit(solution)/shard_map/ppermute | solution.py:370
  7.6 1.3 collective-permute-start.5
  8.9 1.6 collective-permute-start
  10.5 4.6 %collective-permute-start.3 = (bf16[2,2,384,256]{3,2,1,0:T(8,128)(2,1)S(1)}, bf16[2,2,384,256]{3,2,1,0:T(8,128)(2,1)S(1)}, u32[]{:S(2)}, u32[]{:S(2)}) collective-permute-start(bf16[2,2,384,256]{3,2,1,0:T(8,128)(2,1)S(1)} %get-tuple-element.109.refs_10_), channel_id=1, source_target_pairs={{0,1},{1,2},{2,3},{4,5},{5,6},{6,7},{8,9},{9,10},{10,11},{12,13},{... | collective-permute-start | bytes 2359304 | tf_op jit(solution)/shard_map/ppermute | solution.py:374
  15.1 14.0 %collective-permute-done.5.refs_14_ = bf16[2,2,384,256]{3,2,1,0:T(8,128)(2,1)S(1)} collective-permute-done((bf16[2,2,384,256]{3,2,1,0:T(8,128)(2,1)S(1)}, bf16[2,2,384,256]{3,2,1,0:T(8,128)(2,1)S(1)}, u32[]{:S(2)}, u32[]{:S(2)}) %collective-permute-start.5) | collective-permute-done | bytes 786464 | tf_op jit(solution)/shard_map/ppermute | solution.py:378
  29.1 1.3 collective-permute-start.6
  30.4 1.2 collective-permute-done.3.refs_11_
  31.6 0.7 collective-permute-start.4
  32.3 10.1 %collective-permute-done.1.refs_2_ = bf16[384,2048]{1,0:T(8,128)(2,1)S(1)} collective-permute-done((bf16[384,2048]{1,0:T(8,128)(2,1)S(1)}, bf16[384,2048]{1,0:T(8,128)(2,1)S(1)}, u32[]{:S(2)}, u32[]{:S(2)}) %collective-permute-start.1) | collective-permute-done | bytes 1572896 | tf_op jit(solution)/shard_map/ppermute | solution.py:370
  42.5 3.0 %collective-permute-done.refs_1_ = bf16[384,2048]{1,0:T(8,128)(2,1)S(1)} collective-permute-done((bf16[384,2048]{1,0:T(8,128)(2,1)S(1)}, bf16[384,2048]{1,0:T(8,128)(2,1)S(1)}, u32[]{:S(2)}, u32[]{:S(2)}) %collective-permute-start) | collective-permute-done | bytes 1572896 | tf_op jit(solution)/shard_map/ppermute | solution.py:370
  45.5 4.3 %collective-permute-done.6.refs_15_ = bf16[2,2,384,256]{3,2,1,0:T(8,128)(2,1)S(1)} collective-permute-done((bf16[2,2,384,256]{3,2,1,0:T(8,128)(2,1)S(1)}, bf16[2,2,384,256]{3,2,1,0:T(8,128)(2,1)S(1)}, u32[]{:S(2)}, u32[]{:S(2)}) %collective-permute-start.6) | collective-permute-done | bytes 786464 | tf_op jit(solution)/shard_map/ppermute | solution.py:378
  50.0 0.6 collective-permute-start.10
  50.6 1.5 collective-permute-start.11
  52.0 0.7 collective-permute-start.8
  52.8 1.3 collective-permute-start.9
  54.1 13.7 %collective-permute-done.10.refs_3_ = bf16[192,2048]{1,0:T(8,128)(2,1)S(1)} collective-permute-done((bf16[192,2048]{1,0:T(8,128)(2,1)S(1)}, bf16[192,2048]{1,0:T(8,128)(2,1)S(1)}, u32[]{:S(2)}, u32[]{:S(2)}) %collective-permute-start.10) | collective-permute-done | bytes 786464 | tf_op jit(solution)/shard_map/ppermute | solution.py:370
  68.1 4.0 %collective-permute-done.9.refs_16_ = bf16[2,2,384,256]{3,2,1,0:T(8,128)(2,1)S(1)} collective-permute-done((bf16[2,2,384,256]{3,2,1,0:T(8,128)(2,1)S(1)}, bf16[2,2,384,256]{3,2,1,0:T(8,128)(2,1)S(1)}, u32[]{:S(2)}, u32[]{:S(2)}) %collective-permute-start.9) | collective-permute-done | bytes 786464 | tf_op jit(solution)/shard_map/ppermute | solution.py:378
  72.1 0.5 collective-permute-start.15
  72.6 1.3 collective-permute-start.19
  73.9 0.5 collective-permute-done.14.refs_8_
  74.4 4.1 %collective-permute-start.18 = (bf16[2,2,384,256]{3,2,1,0:T(8,128)(2,1)S(1)}, bf16[2,2,384,256]{3,2,1,0:T(8,128)(2,1)S(1)}, u32[]{:S(2)}, u32[]{:S(2)}) collective-permute-start(bf16[2,2,384,256]{3,2,1,0:T(8,128)(2,1)S(1)} %get-tuple-element.78.refs_1_), channel_id=1, source_target_pairs={{0,1},{1,2},{2,3},{4,5},{5,6},{6,7},{8,9},{9,10},{10,11},{12,13},{... | collective-permute-start | bytes 2359304 | tf_op jit(solution)/shard_map/ppermute | solution.py:374
  78.6 1.2 copy-done.17
  79.8 0.5 copy-done.16
  80.3 21.0 %shard_map.60 = (bf16[2,2,1024,1024]{3,2,1,0:T(8,128)(2,1)}, bf16[2,2,256,1024]{3,2,1,0:T(8,128)(2,1)}, f32[384,512]{1,0:T(8,128)S(1)}, f32[384,512]{1,0:T(8,128...) custom-call(bf16[384,2048]{1,0:T(8,128)(2,1)} %bitcast.51, ...), custom_call_target="tpu_custom_call" | custom-call | flops 12884901888 | bytes 12582912 | tf_op jit(solution)/shard_map/pallas_call | solution.py:234
  101.4 3.0 %collective-permute-start.16 = (bf16[2,384,512]{2,1,0:T(8,128)(2,1)S(1)}, bf16[2,384,512]{2,1,0:T(8,128)(2,1)S(1)}, u32[]{:S(2)}, u32[]{:S(2)}) collective-permute-start(bf16[2,384,512]{2,1,0:T(8,128)(2,1)S(1)} %get-tuple-element.76), channel_id=1, source_target_pairs={{0,1},{3,2},{4,5},{7,6},{8,9},{11,10},{12,13},{15,14},{16,17},{19,... | collective-permute-start | bytes 2359304 | tf_op jit(solution)/shard_map/ppermute | solution.py:394
  104.5 0.7 collective-permute-start.20
  105.2 1.3 collective-permute-start.22
  106.5 5.7 %collective-permute-start.27 = (bf16[2,384,512]{2,1,0:T(8,128)(2,1)}, bf16[2,384,512]{2,1,0:T(8,128)(2,1)}, u32[]{:S(2)}, u32[]{:S(2)}) collective-permute-start(bf16[2,384,512]{2,1,0:T(8,128)(2,1)} %get-tuple-element.91), channel_id=1, source_target_pairs={{0,1},{3,2},{4,5},{7,6},{8,9},{11,10},{12,13},{15,14},{16,17},{19,... | collective-permute-start | bytes 2359304 | tf_op jit(solution)/shard_map/ppermute | solution.py:394
  112.2 10.0 %collective-permute-done.16 = bf16[2,384,512]{2,1,0:T(8,128)(2,1)S(1)} collective-permute-done((bf16[2,384,512]{2,1,0:T(8,128)(2,1)S(1)}, bf16[2,384,512]{2,1,0:T(8,128)(2,1)S(1)}, u32[]{:S(2)}, u32[]{:S(2)}) %collective-permute-start.16) | collective-permute-done | bytes 786464 | tf_op jit(solution)/shard_map/ppermute | solution.py:394
  122.2 2.6 %add_convert_fusion.2 = bf16[2,384,512]{2,1,0:T(8,128)(2,1)} fusion(f32[2,384,512]{2,1,0:T(8,128)} %get-tuple-element.75, bf16[2,384,512]{2,1,0:T(8,128)(2,1)S(1)} %collective-permute-done.16), kind=kLoop, calls=%fused_computation.4 | loop fusion | flops 1179648 | bytes 3145728 | tf_op jit(solution)/shard_map/convert_element_type | solution.py:439
  124.8 1.6 collective-permute-start.17
  126.4 1.6 collective-permute-start.21
  128.0 1.3 collective-permute-start.23
  129.3 8.8 %collective-permute-done.27 = bf16[2,384,512]{2,1,0:T(8,128)(2,1)} collective-permute-done((bf16[2,384,512]{2,1,0:T(8,128)(2,1)}, bf16[2,384,512]{2,1,0:T(8,128)(2,1)}, u32[]{:S(2)}, u32[]{:S(2)}) %collective-permute-start.27) | collective-permute-done | bytes 786464 | tf_op jit(solution)/shard_map/ppermute | solution.py:394
  138.1 1.9 add_convert_fusion.1
  140.0 0.7 collective-permute-start.28
  140.8 1.1 fusion.3
  141.9 7.1 %collective-permute-start.36 = (bf16[384,512]{1,0:T(8,128)(2,1)S(1)}, bf16[384,512]{1,0:T(8,128)(2,1)S(1)}, u32[]{:S(2)}, u32[]{:S(2)}) collective-permute-start(bf16[384,512]{1,0:T(8,128)(2,1)S(1)} %fusion.3), channel_id=1, source_target_pairs={{0,1},{1,0},{2,3},{3,2},{4,5},{5,4},{6,7},{7,6},{8,9},{9,8},{10,11... | collective-permute-start | bytes 1179656 | tf_op jit(solution)/shard_map/ppermute | solution.py:382
  149.0 2.6 %collective-permute-done.23.refs_7_ = bf16[2,2,384,256]{3,2,1,0:T(8,128)(2,1)} collective-permute-done((bf16[2,2,384,256]{3,2,1,0:T(8,128)(2,1)}, bf16[2,2,384,256]{3,2,1,0:T(8,128)(2,1)}, u32[]{:S(2)}, u32[]{:S(2)}) %collective-permute-start.23) | collective-permute-done | bytes 786464 | tf_op jit(solution)/shard_map/ppermute | solution.py:378
  151.5 12.4 %shard_map.61 = (bf16[2,2,1024,1024]{3,2,1,0:T(8,128)(2,1)}, bf16[2,2,256,1024]{3,2,1,0:T(8,128)(2,1)}, f32[768,256]{1,0:T(8,128)S(1)}, f32[768,256]{1,0:T(8,128...) custom-call(bf16[3072,2048]{1,0:T(8,128)(2,1)} %get-tuple-element.74.refs_0_, ...), custom_call_target="tpu_custom_call", output_to_operand_aliasing={{0}: (11, {})} | custom-call | flops 6442450944 | bytes 12582912 | tf_op jit(solution)/shard_map/pallas_call | solution.py:234
  164.0 1.4 collective-permute-start.30
  165.4 12.3 %shard_map.62 = (bf16[2,2,1024,1024]{3,2,1,0:T(8,128)(2,1)}, bf16[2,2,256,1024]{3,2,1,0:T(8,128)(2,1)}, f32[384,256]{1,0:T(8,128)S(1)}, f32[384,256]{1,0:T(8,128...) custom-call(bf16[3072,2048]{1,0:T(8,128)(2,1)} %get-tuple-element.74, ...), custom_call_target="tpu_custom_call", output_to_operand_aliasing={{1}: (10, {}), {0}: (11, {})} | custom-call | flops 6442450944 | bytes 12582912 | tf_op jit(solution)/shard_map/pallas_call | solution.py:234
  177.7 1.4 collective-permute-start.26
  179.2 1.2 fusion.4
  180.5 1.3 collective-permute-start.33
  181.8 0.6 collective-permute-start.25
  182.5 5.9 %collective-permute-done.26 = bf16[2,384,256]{2,1,0:T(8,128)(2,1)S(1)} collective-permute-done((bf16[2,384,256]{2,1,0:T(8,128)(2,1)S(1)}, bf16[2,384,256]{2,1,0:T(8,128)(2,1)S(1)}, u32[]{:S(2)}, u32[]{:S(2)}) %collective-permute-start.26) | collective-permute-done | bytes 393248 | tf_op jit(solution)/shard_map/ppermute | solution.py:394
  188.5 0.7 collective-permute-start.31
  189.3 0.7 collective-permute-start.39
  190.1 4.0 %collective-permute-done.33 = bf16[2,384,256]{2,1,0:T(8,128)(2,1)S(1)} collective-permute-done((bf16[2,384,256]{2,1,0:T(8,128)(2,1)S(1)}, bf16[2,384,256]{2,1,0:T(8,128)(2,1)S(1)}, u32[]{:S(2)}, u32[]{:S(2)}) %collective-permute-start.33) | collective-permute-done | bytes 393248 | tf_op jit(solution)/shard_map/ppermute | solution.py:394
  194.1 3.0 %collective-permute-start.29 = (bf16[384,512]{1,0:T(8,128)(2,1)S(1)}, bf16[384,512]{1,0:T(8,128)(2,1)S(1)}, u32[]{:S(2)}, u32[]{:S(2)}) collective-permute-start(bf16[384,512]{1,0:T(8,128)(2,1)S(1)} %fusion.7), channel_id=1, source_target_pairs={{0,1},{1,0},{2,3},{3,2},{4,5},{5,4},{6,7},{7,6},{8,9},{9,8},{10,11... | collective-permute-start | bytes 1179656 | tf_op jit(solution)/shard_map/ppermute | solution.py:382
  197.2 0.7 collective-permute-start.34
  198.0 22.1 %collective-permute-start.40 = (bf16[384,256]{1,0:T(8,128)(2,1)S(1)}, bf16[384,256]{1,0:T(8,128)(2,1)S(1)}, u32[]{:S(2)}, u32[]{:S(2)}) collective-permute-start(bf16[384,256]{1,0:T(8,128)(2,1)S(1)} %fusion.9), channel_id=1, source_target_pairs={{0,1},{1,0},{2,3},{3,2},{4,5},{5,4},{6,7},{7,6},{8,9},{9,8},{10,11... | collective-permute-start | bytes 589832 | tf_op jit(solution)/shard_map/ppermute | solution.py:382
  220.1 6.6 %collective-permute-start.32 = (bf16[768,256]{1,0:T(8,128)(2,1)S(1)}, bf16[768,256]{1,0:T(8,128)(2,1)S(1)}, u32[]{:S(2)}, u32[]{:S(2)}) collective-permute-start(bf16[768,256]{1,0:T(8,128)(2,1)S(1)} %fusion.5), channel_id=1, source_target_pairs={{0,1},{1,0},{2,3},{3,2},{4,5},{5,4},{6,7},{7,6},{8,9},{9,8},{10,11... | collective-permute-start | bytes 1179656 | tf_op jit(solution)/shard_map/ppermute | solution.py:382
  226.8 1.1 collective-permute-start.35
  227.9 4.5 %collective-permute-done.32 = bf16[768,256]{1,0:T(8,128)(2,1)S(1)} collective-permute-done((bf16[768,256]{1,0:T(8,128)(2,1)S(1)}, bf16[768,256]{1,0:T(8,128)(2,1)S(1)}, u32[]{:S(2)}, u32[]{:S(2)}) %collective-permute-start.32) | collective-permute-done | bytes 393248 | tf_op jit(solution)/shard_map/ppermute | solution.py:382
  232.7 0.6 collective-permute-start.38
  233.8 0.8 collective-permute-done.35
  234.8 2.9 %shard_map.63 = (bf16[2,2,1024,1024]{3,2,1,0:T(8,128)(2,1)}, f32[384,2,1024]{2,1,0:T(2,128)}) custom-call(bf16[2,2,256,1024]{3,2,1,0:T(8,128)(2,1)S(1)} %collective-permute-done.25.refs_0_, bf16[2,2,1024,1024]{3,2,1,0:T(8,128)(2,1)} %get-tuple-element.87.refs_1_, f32[384,512]{1,0:T(8,128)S(1)} %fusion.8.refs_2_, ...), custom_call_target="tpu_custom_call", output_to_operand_aliasing={{0}: (1, {})} | custom-call | bytes 10485760 | tf_op jit(solution)/shard_map/pallas_call | solution.py:343
  (90 shorter events, 2.6 us)
Async XLA Ops:
  2.5 1.4 copy-start.11
  2.7 4.7 %collective-permute-start.2 = (bf16[2,2,384,256]{3,2,1,0:T(8,128)(2,1)S(1)}, bf16[2,2,384,256]{3,2,1,0:T(8,128)(2,1)S(1)}, u32[]{:S(2)}, u32[]{:S(2)}) collective-permute-start(bf16[2,2,384,256]{3,2,1,0:T(8,128)(2,1)S(1)} %get-tuple-element.56), channel_id=1, source_target_pairs={{0,16},{16,0},{1,17},{17,1},{2,18},{18,2},{3,19},{19,3},{4,20},{20... | collective-permute-start | bytes 2359304 | tf_op jit(solution)/shard_map/ppermute | solution.py:366
  4.3 4.6 %copy-start.12 = (bf16[48,8,2,1024]{3,1,2,0:T(8,128)(2,1)}, bf16[48,8,2,1024]{3,1,2,0:T(8,128)(2,1)S(1)}, u32[]{:S(2)}) copy-start(bf16[48,8,2,1024]{3,1,2,0:T(8,128)(2,1)S(1)} %copy.10) | copy-start | bytes 4718596
  4.4 28.0 %collective-permute-start.7 = (bf16[384,2048]{1,0:T(8,128)(2,1)S(1)}, bf16[384,2048]{1,0:T(8,128)(2,1)S(1)}, u32[]{:S(2)}, u32[]{:S(2)}) collective-permute-start(bf16[384,2048]{1,0:T(8,128)(2,1)S(1)} %bitcast.48), channel_id=1, source_target_pairs={{0,16},{16,0},{1,17},{17,1},{2,18},{18,2},{3,19},{19,3},{4,20},{20... | collective-permute-start | bytes 4718600 | tf_op jit(solution)/shard_map/ppermute | solution.py:366
  4.9 37.6 %collective-permute-start.1 = (bf16[384,2048]{1,0:T(8,128)(2,1)S(1)}, bf16[384,2048]{1,0:T(8,128)(2,1)S(1)}, u32[]{:S(2)}, u32[]{:S(2)}) collective-permute-start(bf16[384,2048]{1,0:T(8,128)(2,1)S(1)} %bitcast.49), channel_id=1, source_target_pairs={{0,8},{4,12},{8,0},{12,4},{1,9},{5,13},{9,1},{13,5},{2,10},{6,14},... | collective-permute-start | bytes 4718600 | tf_op jit(solution)/shard_map/ppermute | solution.py:370
  7.6 72.7 %copy-start.8 = (f32[4096]{0:T(1024)S(1)}, f32[4096]{0:T(1024)}, u32[]{:S(2)}) copy-start(f32[4096]{0:T(1024)} %param.7) | copy-start | bytes 49156
  7.6 72.7 %copy-start.9 = (f32[2]{0:T(128)S(1)}, f32[2]{0:T(128)}, u32[]{:S(2)}) copy-start(f32[2]{0:T(128)} %refs_8_.3) | copy-start | bytes 28
  7.6 21.5 %collective-permute-start.5 = (bf16[2,2,384,256]{3,2,1,0:T(8,128)(2,1)S(1)}, bf16[2,2,384,256]{3,2,1,0:T(8,128)(2,1)S(1)}, u32[]{:S(2)}, u32[]{:S(2)}) collective-permute-start(bf16[2,2,384,256]{3,2,1,0:T(8,128)(2,1)S(1)} %get-tuple-element.109.refs_10_), channel_id=1, source_target_pairs={{3,2},{2,1},{1,0},{7,6},{6,5},{5,4},{11,10},{10,9},{9,8},{15,14},{... | collective-permute-start | bytes 2359304 | tf_op jit(solution)/shard_map/ppermute | solution.py:378
  8.9 36.5 %collective-permute-start = (bf16[384,2048]{1,0:T(8,128)(2,1)S(1)}, bf16[384,2048]{1,0:T(8,128)(2,1)S(1)}, u32[]{:S(2)}, u32[]{:S(2)}) collective-permute-start(bf16[384,2048]{1,0:T(8,128)(2,1)S(1)} %bitcast.50), channel_id=1, source_target_pairs={{0,4},{4,0},{8,12},{12,8},{1,5},{5,1},{9,13},{13,9},{2,6},{6,2},{1... | collective-permute-start | bytes 4718600 | tf_op jit(solution)/shard_map/ppermute | solution.py:370
  10.5 21.1 %collective-permute-start.3 = (bf16[2,2,384,256]{3,2,1,0:T(8,128)(2,1)S(1)}, bf16[2,2,384,256]{3,2,1,0:T(8,128)(2,1)S(1)}, u32[]{:S(2)}, u32[]{:S(2)}) collective-permute-start(bf16[2,2,384,256]{3,2,1,0:T(8,128)(2,1)S(1)} %get-tuple-element.109.refs_10_), channel_id=1, source_target_pairs={{0,1},{1,2},{2,3},{4,5},{5,6},{6,7},{8,9},{9,10},{10,11},{12,13},{... | collective-permute-start | bytes 2359304 | tf_op jit(solution)/shard_map/ppermute | solution.py:374
  29.1 50.6 %copy-start.18 = (bf16[2,2,384,256]{3,2,1,0:T(8,128)(2,1)}, bf16[2,2,384,256]{3,2,1,0:T(8,128)(2,1)S(1)}, u32[]{:S(2)}) copy-start(bf16[2,2,384,256]{3,2,1,0:T(8,128)(2,1)S(1)} %collective-permute-done.5.refs_14_) | copy-start | bytes 2359300
  29.1 20.7 %collective-permute-start.6 = (bf16[2,2,384,256]{3,2,1,0:T(8,128)(2,1)S(1)}, bf16[2,2,384,256]{3,2,1,0:T(8,128)(2,1)S(1)}, u32[]{:S(2)}, u32[]{:S(2)}) collective-permute-start(bf16[2,2,384,256]{3,2,1,0:T(8,128)(2,1)S(1)} %collective-permute-done.5.refs_14_), channel_id=1, source_target_pairs={{2,1},{1,0},{6,5},{5,4},{10,9},{9,8},{14,13},{13,12},{18,17},{17,1... | collective-permute-start | bytes 2359304 | tf_op jit(solution)/shard_map/ppermute | solution.py:378
  31.6 18.2 %collective-permute-start.4 = (bf16[2,2,384,256]{3,2,1,0:T(8,128)(2,1)S(1)}, bf16[2,2,384,256]{3,2,1,0:T(8,128)(2,1)S(1)}, u32[]{:S(2)}, u32[]{:S(2)}) collective-permute-start(bf16[2,2,384,256]{3,2,1,0:T(8,128)(2,1)S(1)} %collective-permute-done.3.refs_11_), channel_id=1, source_target_pairs={{1,2},{2,3},{5,6},{6,7},{9,10},{10,11},{13,14},{14,15},{17,18},{18... | collective-permute-start | bytes 2359304 | tf_op jit(solution)/shard_map/ppermute | solution.py:374
  32.3 47.4 %copy-start.15 = (bf16[384,2048]{1,0:T(8,128)(2,1)}, bf16[384,2048]{1,0:T(8,128)(2,1)S(1)}, u32[]{:S(2)}) copy-start(bf16[384,2048]{1,0:T(8,128)(2,1)S(1)} %collective-permute-done.7.refs_5_) | copy-start | bytes 4718596
  42.5 25.4 %copy-start.13 = (bf16[384,2048]{1,0:T(8,128)(2,1)}, bf16[384,2048]{1,0:T(8,128)(2,1)S(1)}, u32[]{:S(2)}) copy-start(bf16[384,2048]{1,0:T(8,128)(2,1)S(1)} %collective-permute-done.1.refs_2_) | copy-start | bytes 4718596
  45.5 8.6 %copy-start.14 = (bf16[384,2048]{1,0:T(8,128)(2,1)}, bf16[384,2048]{1,0:T(8,128)(2,1)S(1)}, u32[]{:S(2)}) copy-start(bf16[384,2048]{1,0:T(8,128)(2,1)S(1)} %collective-permute-done.refs_1_) | copy-start | bytes 4718596
  49.8 29.9 %copy-start.19 = (bf16[2,2,384,256]{3,2,1,0:T(8,128)(2,1)}, bf16[2,2,384,256]{3,2,1,0:T(8,128)(2,1)S(1)}, u32[]{:S(2)}) copy-start(bf16[2,2,384,256]{3,2,1,0:T(8,128)(2,1)S(1)} %collective-permute-done.6.refs_15_) | copy-start | bytes 2359300
  50.0 17.9 %collective-permute-start.10 = (bf16[192,2048]{1,0:T(8,128)(2,1)S(1)}, bf16[192,2048]{1,0:T(8,128)(2,1)S(1)}, u32[]{:S(2)}, u32[]{:S(2)}) collective-permute-start(bf16[192,2048]{1,0:T(8,128)(2,1)S(1)} %slice.22), channel_id=1, source_target_pairs={{0,8},{4,12},{8,0},{12,4},{1,9},{5,13},{9,1},{13,5},{2,10},{6,14},... | collective-permute-start | bytes 2359304 | tf_op jit(solution)/shard_map/ppermute | solution.py:370
  50.6 17.6 %collective-permute-start.11 = (bf16[192,2048]{1,0:T(8,128)(2,1)S(1)}, bf16[192,2048]{1,0:T(8,128)(2,1)S(1)}, u32[]{:S(2)}, u32[]{:S(2)}) collective-permute-start(bf16[192,2048]{1,0:T(8,128)(2,1)S(1)} %slice.23), channel_id=1, source_target_pairs={{0,4},{4,0},{8,12},{12,8},{1,5},{5,1},{9,13},{13,9},{2,6},{6,2},{1... | collective-permute-start | bytes 2359304 | tf_op jit(solution)/shard_map/ppermute | solution.py:370
  52.0 16.1 %collective-permute-start.8 = (bf16[2,2,384,256]{3,2,1,0:T(8,128)(2,1)S(1)}, bf16[2,2,384,256]{3,2,1,0:T(8,128)(2,1)S(1)}, u32[]{:S(2)}, u32[]{:S(2)}) collective-permute-start(bf16[2,2,384,256]{3,2,1,0:T(8,128)(2,1)S(1)} %collective-permute-done.4.refs_12_), channel_id=1, source_target_pairs={{2,3},{6,7},{10,11},{14,15},{18,19},{22,23},{26,27},{30,31}} | collective-permute-start | bytes 2359304 | tf_op jit(solution)/shard_map/ppermute | solution.py:374
  52.8 19.3 %collective-permute-start.9 = (bf16[2,2,384,256]{3,2,1,0:T(8,128)(2,1)S(1)}, bf16[2,2,384,256]{3,2,1,0:T(8,128)(2,1)S(1)}, u32[]{:S(2)}, u32[]{:S(2)}) collective-permute-start(bf16[2,2,384,256]{3,2,1,0:T(8,128)(2,1)S(1)} %collective-permute-done.6.refs_15_), channel_id=1, source_target_pairs={{1,0},{5,4},{9,8},{13,12},{17,16},{21,20},{25,24},{29,28}} | collective-permute-start | bytes 2359304 | tf_op jit(solution)/shard_map/ppermute | solution.py:378
  54.1 24.5 %collective-permute-start.12 = (bf16[384,2048]{1,0:T(8,128)(2,1)S(1)}, bf16[384,2048]{1,0:T(8,128)(2,1)S(1)}, u32[]{:S(2)}, u32[]{:S(2)}) collective-permute-start(bf16[384,2048]{1,0:T(8,128)(2,1)S(1)} %collective-permute-done.refs_1_), channel_id=1, source_target_pairs={{0,16},{16,0},{1,17},{17,1},{2,18},{18,2},{3,19},{19,3},{4,20},{20... | collective-permute-start | bytes 4718600 | tf_op jit(solution)/shard_map/ppermute | solution.py:366
  67.9 10.7 %collective-permute-start.13 = (bf16[384,2048]{1,0:T(8,128)(2,1)S(1)}, bf16[384,2048]{1,0:T(8,128)(2,1)S(1)}, u32[]{:S(2)}, u32[]{:S(2)}) collective-permute-start(bf16[384,2048]{1,0:T(8,128)(2,1)S(1)} %collective-permute-done.1.refs_2_), channel_id=1, source_target_pairs={{0,16},{16,0},{1,17},{17,1},{2,18},{18,2},{3,19},{19,3},{4,20},{20... | collective-permute-start | bytes 4718600 | tf_op jit(solution)/shard_map/ppermute | solution.py:366
  68.1 4.5 %copy-start.20 = (bf16[2,2,384,256]{3,2,1,0:T(8,128)(2,1)}, bf16[2,2,384,256]{3,2,1,0:T(8,128)(2,1)S(1)}, u32[]{:S(2)}) copy-start(bf16[2,2,384,256]{3,2,1,0:T(8,128)(2,1)S(1)} %collective-permute-done.8.refs_13_) | copy-start | bytes 2359300
  72.1 1.8 copy-start.21
  72.1 2.3 collective-permute-start.14
  72.1 6.4 %collective-permute-start.15 = (bf16[192,2048]{1,0:T(8,128)(2,1)S(1)}, bf16[192,2048]{1,0:T(8,128)(2,1)S(1)}, u32[]{:S(2)}, u32[]{:S(2)}) collective-permute-start(bf16[192,2048]{1,0:T(8,128)(2,1)S(1)} %collective-permute-done.11.refs_4_), channel_id=1, source_target_pairs={{0,16},{16,0},{1,17},{17,1},{2,18},{18,2},{3,19},{19,3},{4,20},{20... | collective-permute-start | bytes 2359304 | tf_op jit(solution)/shard_map/ppermute | solution.py:366
  72.6 31.8 %collective-permute-start.19 = (bf16[2,2,384,256]{3,2,1,0:T(8,128)(2,1)S(1)}, bf16[2,2,384,256]{3,2,1,0:T(8,128)(2,1)S(1)}, u32[]{:S(2)}, u32[]{:S(2)}) collective-permute-start(bf16[2,2,384,256]{3,2,1,0:T(8,128)(2,1)S(1)} %get-tuple-element.78.refs_1_), channel_id=1, source_target_pairs={{3,2},{2,1},{1,0},{7,6},{6,5},{5,4},{11,10},{10,9},{9,8},{15,14},{... | collective-permute-start | bytes 2359304 | tf_op jit(solution)/shard_map/ppermute | solution.py:378
  74.4 30.1 %collective-permute-start.18 = (bf16[2,2,384,256]{3,2,1,0:T(8,128)(2,1)S(1)}, bf16[2,2,384,256]{3,2,1,0:T(8,128)(2,1)S(1)}, u32[]{:S(2)}, u32[]{:S(2)}) collective-permute-start(bf16[2,2,384,256]{3,2,1,0:T(8,128)(2,1)S(1)} %get-tuple-element.78.refs_1_), channel_id=1, source_target_pairs={{0,1},{1,2},{2,3},{4,5},{5,6},{6,7},{8,9},{9,10},{10,11},{12,13},{... | collective-permute-start | bytes 2359304 | tf_op jit(solution)/shard_map/ppermute | solution.py:374
  78.5 1.7 copy-start.16
  78.6 1.2 copy-start.17
  101.3 23.5 %copy-start = (f32[384,512]{1,0:T(8,128)}, f32[384,512]{1,0:T(8,128)S(1)}, u32[]{:S(2)}) copy-start(f32[384,512]{1,0:T(8,128)S(1)} %get-tuple-element.88) | copy-start | bytes 2359300
  101.3 23.5 %copy-start.2 = (f32[384,512]{1,0:T(8,128)}, f32[384,512]{1,0:T(8,128)S(1)}, u32[]{:S(2)}) copy-start(f32[384,512]{1,0:T(8,128)S(1)} %get-tuple-element.102) | copy-start | bytes 2359300
  101.4 23.5 %copy-start.4 = (f32[384,512]{1,0:T(8,128)}, f32[384,512]{1,0:T(8,128)S(1)}, u32[]{:S(2)}) copy-start(f32[384,512]{1,0:T(8,128)S(1)} %get-tuple-element.93) | copy-start | bytes 2359300
  101.4 23.5 %copy-start.6 = (f32[384,512]{1,0:T(8,128)}, f32[384,512]{1,0:T(8,128)S(1)}, u32[]{:S(2)}) copy-start(f32[384,512]{1,0:T(8,128)S(1)} %get-tuple-element.104) | copy-start | bytes 2359300
  101.4 20.9 %collective-permute-start.16 = (bf16[2,384,512]{2,1,0:T(8,128)(2,1)S(1)}, bf16[2,384,512]{2,1,0:T(8,128)(2,1)S(1)}, u32[]{:S(2)}, u32[]{:S(2)}) collective-permute-start(bf16[2,384,512]{2,1,0:T(8,128)(2,1)S(1)} %get-tuple-element.76), channel_id=1, source_target_pairs={{0,1},{3,2},{4,5},{7,6},{8,9},{11,10},{12,13},{15,14},{16,17},{19,... | collective-permute-start | bytes 2359304 | tf_op jit(solution)/shard_map/ppermute | solution.py:394
  104.4 47.2 %collective-permute-start.24 = (bf16[2,2,256,1024]{3,2,1,0:T(8,128)(2,1)}, bf16[2,2,256,1024]{3,2,1,0:T(8,128)(2,1)}, u32[]{:S(2)}, u32[]{:S(2)}) collective-permute-start(bf16[2,2,256,1024]{3,2,1,0:T(8,128)(2,1)} %get-tuple-element.82), channel_id=1, source_target_pairs={{0,16},{16,0},{1,17},{17,1},{2,18},{18,2},{3,19},{19,3},{4,20},{20... | collective-permute-start | bytes 6291464 | tf_op jit(solution)/shard_map/ppermute | solution.py:366
  104.5 22.0 %collective-permute-start.20 = (bf16[2,2,384,256]{3,2,1,0:T(8,128)(2,1)S(1)}, bf16[2,2,384,256]{3,2,1,0:T(8,128)(2,1)S(1)}, u32[]{:S(2)}, u32[]{:S(2)}) collective-permute-start(bf16[2,2,384,256]{3,2,1,0:T(8,128)(2,1)S(1)} %collective-permute-done.18.refs_2_), channel_id=1, source_target_pairs={{1,2},{2,3},{5,6},{6,7},{9,10},{10,11},{13,14},{14,15},{17,18},{18... | collective-permute-start | bytes 2359304 | tf_op jit(solution)/shard_map/ppermute | solution.py:374
  105.2 22.8 %collective-permute-start.22 = (bf16[2,2,384,256]{3,2,1,0:T(8,128)(2,1)S(1)}, bf16[2,2,384,256]{3,2,1,0:T(8,128)(2,1)}, u32[]{:S(2)}, u32[]{:S(2)}) collective-permute-start(bf16[2,2,384,256]{3,2,1,0:T(8,128)(2,1)S(1)} %collective-permute-done.19.refs_5_), channel_id=1, source_target_pairs={{2,1},{1,0},{6,5},{5,4},{10,9},{9,8},{14,13},{13,12},{18,17},{17,1... | collective-permute-start | bytes 2359304 | tf_op jit(solution)/shard_map/ppermute | solution.py:378
  106.5 31.6 %collective-permute-start.27 = (bf16[2,384,512]{2,1,0:T(8,128)(2,1)}, bf16[2,384,512]{2,1,0:T(8,128)(2,1)}, u32[]{:S(2)}, u32[]{:S(2)}) collective-permute-start(bf16[2,384,512]{2,1,0:T(8,128)(2,1)} %get-tuple-element.91), channel_id=1, source_target_pairs={{0,1},{3,2},{4,5},{7,6},{8,9},{11,10},{12,13},{15,14},{16,17},{19,... | collective-permute-start | bytes 2359304 | tf_op jit(solution)/shard_map/ppermute | solution.py:394
  124.8 15.9 %collective-permute-start.17 = (bf16[2,384,512]{2,1,0:T(8,128)(2,1)}, bf16[2,384,512]{2,1,0:T(8,128)(2,1)}, u32[]{:S(2)}, u32[]{:S(2)}) collective-permute-start(bf16[2,384,512]{2,1,0:T(8,128)(2,1)} %add_convert_fusion.2), channel_id=1, source_target_pairs={{1,2},{2,1},{5,6},{6,5},{9,10},{10,9},{13,14},{14,13},{17,18},{18,... | collective-permute-start | bytes 2359304 | tf_op jit(solution)/shard_map/ppermute | solution.py:386
  126.4 22.6 %collective-permute-start.21 = (bf16[2,2,384,256]{3,2,1,0:T(8,128)(2,1)S(1)}, bf16[2,2,384,256]{3,2,1,0:T(8,128)(2,1)}, u32[]{:S(2)}, u32[]{:S(2)}) collective-permute-start(bf16[2,2,384,256]{3,2,1,0:T(8,128)(2,1)S(1)} %collective-permute-done.20.refs_3_), channel_id=1, source_target_pairs={{2,3},{6,7},{10,11},{14,15},{18,19},{22,23},{26,27},{30,31}} | collective-permute-start | bytes 2359304 | tf_op jit(solution)/shard_map/ppermute | solution.py:374
  128.0 23.6 %collective-permute-start.23 = (bf16[2,2,384,256]{3,2,1,0:T(8,128)(2,1)}, bf16[2,2,384,256]{3,2,1,0:T(8,128)(2,1)}, u32[]{:S(2)}, u32[]{:S(2)}) collective-permute-start(bf16[2,2,384,256]{3,2,1,0:T(8,128)(2,1)} %collective-permute-done.22.refs_6_), channel_id=1, source_target_pairs={{1,0},{5,4},{9,8},{13,12},{17,16},{21,20},{25,24},{29,28}} | collective-permute-start | bytes 2359304 | tf_op jit(solution)/shard_map/ppermute | solution.py:378
  138.1 2.7 %copy-start.7 = (f32[384,512]{1,0:T(8,128)S(1)}, f32[384,512]{1,0:T(8,128)}, u32[]{:S(2)}) copy-start(f32[384,512]{1,0:T(8,128)} %copy-done.6) | copy-start | bytes 2359300
  140.0 49.2 %collective-permute-start.28 = (bf16[2,384,512]{2,1,0:T(8,128)(2,1)S(1)}, bf16[2,384,512]{2,1,0:T(8,128)(2,1)S(1)}, u32[]{:S(2)}, u32[]{:S(2)}) collective-permute-start(bf16[2,384,512]{2,1,0:T(8,128)(2,1)S(1)} %add_convert_fusion.1), channel_id=1, source_target_pairs={{1,2},{2,1},{5,6},{6,5},{9,10},{10,9},{13,14},{14,13},{17,18},{18,... | collective-permute-start | bytes 2359304 | tf_op jit(solution)/shard_map/ppermute | solution.py:386
  141.9 37.3 %collective-permute-start.36 = (bf16[384,512]{1,0:T(8,128)(2,1)S(1)}, bf16[384,512]{1,0:T(8,128)(2,1)S(1)}, u32[]{:S(2)}, u32[]{:S(2)}) collective-permute-start(bf16[384,512]{1,0:T(8,128)(2,1)S(1)} %fusion.3), channel_id=1, source_target_pairs={{0,1},{1,0},{2,3},{3,2},{4,5},{5,4},{6,7},{7,6},{8,9},{9,8},{10,11... | collective-permute-start | bytes 1179656 | tf_op jit(solution)/shard_map/ppermute | solution.py:382
  164.0 17.8 %collective-permute-start.30 = (bf16[2,768,256]{2,1,0:T(8,128)(2,1)S(1)}, bf16[2,768,256]{2,1,0:T(8,128)(2,1)S(1)}, u32[]{:S(2)}, u32[]{:S(2)}) collective-permute-start(bf16[2,768,256]{2,1,0:T(8,128)(2,1)S(1)} %get-tuple-element.96), channel_id=1, source_target_pairs={{0,1},{3,2},{4,5},{7,6},{8,9},{11,10},{12,13},{15,14},{16,17},{19,... | collective-permute-start | bytes 2359304 | tf_op jit(solution)/shard_map/ppermute | solution.py:394
  165.4 13.8 %copy-start.3 = (f32[384,512]{1,0:T(8,128)S(1)}, f32[384,512]{1,0:T(8,128)}, u32[]{:S(2)}) copy-start(f32[384,512]{1,0:T(8,128)} %copy-done.2) | copy-start | bytes 2359300
  177.7 4.1 %copy-start.10 = (bf16[2,2,256,1024]{3,2,1,0:T(8,128)(2,1)S(1)}, bf16[2,2,256,1024]{3,2,1,0:T(8,128)(2,1)}, u32[]{:S(2)}) copy-start(bf16[2,2,256,1024]{3,2,1,0:T(8,128)(2,1)} %get-tuple-element.86) | copy-start | bytes 6291460
  177.7 10.7 %collective-permute-start.26 = (bf16[2,384,256]{2,1,0:T(8,128)(2,1)S(1)}, bf16[2,384,256]{2,1,0:T(8,128)(2,1)S(1)}, u32[]{:S(2)}, u32[]{:S(2)}) collective-permute-start(bf16[2,384,256]{2,1,0:T(8,128)(2,1)S(1)} %get-tuple-element.89), channel_id=1, source_target_pairs={{0,1},{3,2},{4,5},{7,6},{8,9},{11,10},{12,13},{15,14},{16,17},{19,... | collective-permute-start | bytes 1179656 | tf_op jit(solution)/shard_map/ppermute | solution.py:394
  180.4 54.3 %collective-permute-start.37 = (f32[384,512]{1,0:T(8,128)S(1)}, f32[384,512]{1,0:T(8,128)S(1)}, u32[]{:S(2)}, u32[]{:S(2)}) collective-permute-start(f32[384,512]{1,0:T(8,128)S(1)} %fusion.4), channel_id=1, source_target_pairs={{0,16},{16,0},{1,17},{17,1},{2,18},{18,2},{3,19},{19,3},{4,20},{20... | collective-permute-start | bytes 2359304 | tf_op jit(solution)/shard_map/ppermute | solution.py:366
  180.5 13.7 %collective-permute-start.33 = (bf16[2,384,256]{2,1,0:T(8,128)(2,1)S(1)}, bf16[2,384,256]{2,1,0:T(8,128)(2,1)S(1)}, u32[]{:S(2)}, u32[]{:S(2)}) collective-permute-start(bf16[2,384,256]{2,1,0:T(8,128)(2,1)S(1)} %get-tuple-element.100), channel_id=1, source_target_pairs={{0,1},{3,2},{4,5},{7,6},{8,9},{11,10},{12,13},{15,14},{16,17},{19,... | collective-permute-start | bytes 1179656 | tf_op jit(solution)/shard_map/ppermute | solution.py:394
  181.8 52.9 %collective-permute-start.25 = (bf16[2,2,256,1024]{3,2,1,0:T(8,128)(2,1)S(1)}, bf16[2,2,256,1024]{3,2,1,0:T(8,128)(2,1)S(1)}, u32[]{:S(2)}, u32[]{:S(2)}) collective-permute-start(bf16[2,2,256,1024]{3,2,1,0:T(8,128)(2,1)S(1)} %copy-done.10), channel_id=1, source_target_pairs={{0,16},{16,0},{1,17},{17,1},{2,18},{18,2},{3,19},{19,3},{4,20},{20... | collective-permute-start | bytes 6291464 | tf_op jit(solution)/shard_map/ppermute | solution.py:366
  182.5 7.4 %copy-start.5 = (f32[384,512]{1,0:T(8,128)S(1)}, f32[384,512]{1,0:T(8,128)}, u32[]{:S(2)}) copy-start(f32[384,512]{1,0:T(8,128)} %copy-done.4) | copy-start | bytes 2359300
  188.5 9.5 %collective-permute-start.31 = (bf16[2,768,256]{2,1,0:T(8,128)(2,1)S(1)}, bf16[2,768,256]{2,1,0:T(8,128)(2,1)S(1)}, u32[]{:S(2)}, u32[]{:S(2)}) collective-permute-start(bf16[2,768,256]{2,1,0:T(8,128)(2,1)S(1)} %add_convert_fusion), channel_id=1, source_target_pairs={{1,2},{2,1},{5,6},{6,5},{9,10},{10,9},{13,14},{14,13},{17,18},{18,... | collective-permute-start | bytes 2359304 | tf_op jit(solution)/shard_map/ppermute | solution.py:386
  189.3 7.9 %collective-permute-start.39 = (bf16[2,384,256]{2,1,0:T(8,128)(2,1)S(1)}, bf16[2,384,256]{2,1,0:T(8,128)(2,1)S(1)}, u32[]{:S(2)}, u32[]{:S(2)}) collective-permute-start(bf16[2,384,256]{2,1,0:T(8,128)(2,1)S(1)} %add_convert_fusion.3), channel_id=1, source_target_pairs={{1,2},{2,1},{5,6},{6,5},{9,10},{10,9},{13,14},{14,13},{17,18},{18,... | collective-permute-start | bytes 1179656 | tf_op jit(solution)/shard_map/ppermute | solution.py:386
  194.1 38.6 %collective-permute-start.29 = (bf16[384,512]{1,0:T(8,128)(2,1)S(1)}, bf16[384,512]{1,0:T(8,128)(2,1)S(1)}, u32[]{:S(2)}, u32[]{:S(2)}) collective-permute-start(bf16[384,512]{1,0:T(8,128)(2,1)S(1)} %fusion.7), channel_id=1, source_target_pairs={{0,1},{1,0},{2,3},{3,2},{4,5},{5,4},{6,7},{7,6},{8,9},{9,8},{10,11... | collective-permute-start | bytes 1179656 | tf_op jit(solution)/shard_map/ppermute | solution.py:382
  197.2 22.9 %collective-permute-start.34 = (bf16[2,384,256]{2,1,0:T(8,128)(2,1)S(1)}, bf16[2,384,256]{2,1,0:T(8,128)(2,1)S(1)}, u32[]{:S(2)}, u32[]{:S(2)}) collective-permute-start(bf16[2,384,256]{2,1,0:T(8,128)(2,1)S(1)} %add_convert_fusion.4), channel_id=1, source_target_pairs={{1,2},{2,1},{5,6},{6,5},{9,10},{10,9},{13,14},{14,13},{17,18},{18,... | collective-permute-start | bytes 1179656 | tf_op jit(solution)/shard_map/ppermute | solution.py:386
  198.0 28.8 %collective-permute-start.40 = (bf16[384,256]{1,0:T(8,128)(2,1)S(1)}, bf16[384,256]{1,0:T(8,128)(2,1)S(1)}, u32[]{:S(2)}, u32[]{:S(2)}) collective-permute-start(bf16[384,256]{1,0:T(8,128)(2,1)S(1)} %fusion.9), channel_id=1, source_target_pairs={{0,1},{1,0},{2,3},{3,2},{4,5},{5,4},{6,7},{7,6},{8,9},{9,8},{10,11... | collective-permute-start | bytes 589832 | tf_op jit(solution)/shard_map/ppermute | solution.py:382
  220.1 12.3 %collective-permute-start.32 = (bf16[768,256]{1,0:T(8,128)(2,1)S(1)}, bf16[768,256]{1,0:T(8,128)(2,1)S(1)}, u32[]{:S(2)}, u32[]{:S(2)}) collective-permute-start(bf16[768,256]{1,0:T(8,128)(2,1)S(1)} %fusion.5), channel_id=1, source_target_pairs={{0,1},{1,0},{2,3},{3,2},{4,5},{5,4},{6,7},{7,6},{8,9},{9,8},{10,11... | collective-permute-start | bytes 1179656 | tf_op jit(solution)/shard_map/ppermute | solution.py:382
  226.8 7.8 %collective-permute-start.35 = (bf16[384,256]{1,0:T(8,128)(2,1)S(1)}, bf16[384,256]{1,0:T(8,128)(2,1)S(1)}, u32[]{:S(2)}, u32[]{:S(2)}) collective-permute-start(bf16[384,256]{1,0:T(8,128)(2,1)S(1)} %fusion.11), channel_id=1, source_target_pairs={{0,1},{1,0},{2,3},{3,2},{4,5},{5,4},{6,7},{7,6},{8,9},{9,8},{10,11... | collective-permute-start | bytes 589832 | tf_op jit(solution)/shard_map/ppermute | solution.py:382
  232.5 2.2 collective-permute-start.41
  232.5 1.1 copy-start.1
  232.7 2.1 collective-permute-start.38

commit v3 on v2

--- a/solution.py
+++ b/solution.py
@@ -76,7 +76,8 @@
     take = lambda count: [refs.pop(0) for _ in range(count)]
     ket = take(1 if group else 2 * len(pieces))
     (bra,) = take(1)
-    ups, downs = take(3), take(3)
+    (paired,) = take(1)
+    crossed, handed = take(2), take(2)
     occ_ref, virt_ref = take(2)
     aliased = take(2) if group else None
     whole_ref, half_ref = take(2)
@@ -92,6 +93,7 @@
     me = lax.axis_index("occ")
     pair = lax.bitwise_xor(here_col, 1)
     low = here_col < 2
+    middle = jnp.logical_or(here_col == 1, here_col == 2)
 
     def bra_copies(source, home, slot):
         return [
@@ -110,12 +112,12 @@
             for copy in bra_copies(source, home, slot):
                 copy.start()
 
-    for copy in bra_copies(bra, here_col, 0):
+    for copy in bra_copies(bra, here_col, 0) + bra_copies(paired, pair, 1):
         copy.start()
-    for d in range(1, 4):
-        home = lax.rem(here_col + 4 - d, 4)
-        fetch(here_col >= d, ups[d - 1], home, d)
-        fetch(here_col < d, downs[3 - d], home, d)
+    for n in range(2):
+        home = jnp.where(low, 2 + n, 1 - n)
+        fetch(middle, crossed[n], home, 2 + n)
+        fetch(jnp.logical_not(middle), handed[n], home, 2 + n)
 
     copies = [[] for _ in range(SLICES)]
     for n in range(SLICES):
@@ -370,14 +372,6 @@
     return lax.ppermute(x, "row", [(r, r ^ offset) for r in range(4)])
 
 
-def hop_up(x, first):
-    return lax.ppermute(x, "col", [(c, c + 1) for c in range(first, 3)])
-
-
-def hop_down(x, first):
-    return lax.ppermute(x, "col", [(3 - c, 2 - c) for c in range(first, 3)])
-
-
 def pairs(x):
     return lax.ppermute(x, "col", [(0, 1), (1, 0), (2, 3), (3, 2)])
 
@@ -410,24 +404,27 @@
     cut = batch // 2
     pieces = ((0, 0, batch), (1, 0, batch), (2, 0, batch), (3, 0, cut), (3, cut, batch - cut))
 
-    ups, downs = [[hop_up(bra[0], 0)], []], [[hop_down(bra[0], 0)], []]
+    block, later = bra[0], bra[1]
+    paired, crossed = pairs(block), [across(block)]
     ket_swapped = swap(ket_own)
-    ups[0].append(hop_up(ups[0][0], 1))
-    downs[0].append(hop_down(downs[0][0], 1))
-    ket_x, ket_y, ups[0][1], downs[0][1], ket_swapped = tie(
-        ket_x, ket_y, ups[0][1], downs[0][1], ket_swapped
+    crossed.append(across(paired))
+    handed = [outward(crossed[0])]
+    ket_x, ket_y, crossed[1], handed[0], ket_swapped = tie(
+        ket_x, ket_y, crossed[1], handed[0], ket_swapped
     )
     part_x, part_y, late_x, late_y = tie(ket_x[:cut], ket_y[cut:], ket_x, ket_y)
     far_y, far_x = planar(part_x, 2), planar(part_y, 1)
     late_y, far_y = tie(late_y, far_y)
-    ups[0].append(hop_up(ups[0][1], 2))
-    downs[0].append(hop_down(downs[0][1], 2))
+    handed.append(outward(crossed[1]))
+    crossed[1], early = tie(crossed[1], later)
+    later_crossed = [across(early)]
     straight = [swap(late_x), swap(late_y)]
-    ups[0][2], downs[0][2], far_y, far_x = tie(ups[0][2], downs[0][2], far_y, far_x)
+    handed[1], later_crossed[0], far_y, far_x = tie(handed[1], later_crossed[0], far_y, far_x)
     ket = [ket_own, ket_x, ket_y, far_y, far_x, ket_swapped, *straight, swap(far_y), swap(far_x)]
-    ups[0][2], downs[0][2], block = tie(ups[0][2], downs[0][2], bra[1])
-    ups[1].append(hop_up(block, 0))
-    downs[1].append(hop_down(block, 0))
+    handed[1], early, cross_first = tie(handed[1], later, later_crossed[0])
+    later_paired = pairs(early)
+    later_handed = [outward(cross_first)]
+    first = [block, paired, *crossed, *handed]
     energies = (occ_energy, virt_energy[None, :])
 
     def up_cast(x):
@@ -452,20 +449,18 @@
             total = [total[0][batch:], total[0][:batch]]
         return total[1], swap(total[0])
 
-    arrived = [bra[0], *ups[0], *downs[0]]
     (whole, mine), own0, pair0, far0, send0, (ket_all,) = run_group(
-        0, ket, pieces, arrived, energies, ()
-    )
-    one0 = [inward(send) for send in send0]
-    own_last, up, down = tie(own0[1], ups[1][0], downs[1][0])
+        0, ket, pieces, first, energies, ()
+    )
+    send_last, later_handed[0] = tie(send0[1], later_handed[0])
+    one0 = [inward(send0[0]), inward(send_last)]
+    own_last, later_paired = tie(own0[1], later_paired)
     own0 = (own0[0], own_last)
-    ups[1] += [hop_up(up, 1)]
-    downs[1] += [hop_down(down, 1)]
-    ups[1] += [hop_up(ups[1][1], 2)]
-    downs[1] += [hop_down(downs[1][1], 2)]
+    later_crossed.append(across(later_paired))
+    later_handed.append(outward(later_crossed[1]))
     other = swap(mine)
     two0 = [cross(far0[0], one0[0])]
-    arrived = [bra[1], *ups[1], *downs[1]]
+    arrived = [later, later_paired, *later_crossed, *later_handed]
     two0[0], arrived[0] = tie(two0[0], arrived[0])
     (whole, mine), own1, pair1, far1, send1, _ = run_group(
         1, [ket_all], pieces, arrived, energies, (other, whole)

time: 239 us -> 243 us (1.017)
  starting transfers between devices: 86.3 us -> 76.6 us
  Pallas kernels: 48.9 us -> 56.8 us
  waiting for transfers between devices: 87.9 us -> 93.8 us
    ppermute x5 -> x7, waiting for transfers between devices: 5.35 us -> 20.6 us  [pairs(): return lax.ppermute(x, 'col', [(0, 1), (1, 0), (2, 3), (3, 2)])]
    ppermute x12 -> x4, starting transfers between devices: 20.1 us -> 5.13 us  [outward(): return lax.ppermute(x, 'col', [(1, 0), (2, 3)])]
    ppermute x12 -> x4, waiting for transfers between devices: 26.1 us -> 12.6 us  [outward(): return lax.ppermute(x, 'col', [(1, 0), (2, 3)])]
    pallas_call x3, Pallas kernels: 45.8 us -> 53.7 us  [run_group(): pl.pallas_call(functools.partial(group_kernel, pieces, group), out_shape=...]
    ppermute x5 -> x9, starting transfers between devices: 4.36 us -> 8.01 us  [across(): return lax.ppermute(x, 'col', [(1, 2), (2, 1)])]
    ppermute x5 -> x7, starting transfers between devices: 39.8 us -> 43.5 us  [pairs(): return lax.ppermute(x, 'col', [(0, 1), (1, 0), (2, 3), (3, 2)])]
    ppermute x5, waiting for transfers between devices: 28.8 us -> 31.8 us  [inward(): return lax.ppermute(x, 'col', [(0, 1), (3, 2)])]
    unnamed x46 -> x44, local copies, waits for them, and re-layouts: 5.09 us -> 5.07 us
  transfers between devices with their start and end apart: 42 -> 40, of which waited for: 17 -> 16; matrix products, arithmetic and copies ran while one was open for 4% -> 4% of each run, Pallas kernels for 19% -> 22%
where the time goes in v3:
time: 243 us; the launch traced here: 242 us
  waiting for transfers between devices  93.8 us (39%)
  starting transfers between devices  76.6 us (32%)
  Pallas kernels  56.8 us (23%)
  other arithmetic  7.99 us (3%)
  local copies, waits for them, and re-layouts  5.26 us (2%)
    pallas_call x3, Pallas kernels, run_group(): pl.pallas_call(functools.partial(group_kernel, pieces, group), out_shape=...  53.7 us
    ppermute x7, starting transfers between devices, pairs(): return lax.ppermute(x, 'col', [(0, 1), (1, 0), (2, 3), (3, 2)])  43.5 us
    ppermute x5, waiting for transfers between devices, inward(): return lax.ppermute(x, 'col', [(0, 1), (3, 2)])  31.8 us
    ppermute x4, waiting for transfers between devices, planar(): return lax.ppermute(x, 'row', [(r, r ^ offset) for r in range(4)])  26.8 us
    ppermute x7, waiting for transfers between devices, pairs(): return lax.ppermute(x, 'col', [(0, 1), (1, 0), (2, 3), (3, 2)])  20.6 us
    ppermute x4, waiting for transfers between devices, outward(): return lax.ppermute(x, 'col', [(1, 0), (2, 3)])  12.6 us
    ppermute x5, starting transfers between devices, inward(): return lax.ppermute(x, 'col', [(0, 1), (3, 2)])  10.8 us
    ppermute x9, starting transfers between devices, across(): return lax.ppermute(x, 'col', [(1, 2), (2, 1)])  8.01 us
  transfers between devices with their start and end apart: 40, of which 16 were waited for; matrix products, arithmetic and copies ran while one was open for 4% of the time, Pallas kernels for 22%

profile of v3, /device:TPU:0, one launch (start us, length us, event | category | flops | bytes accessed | tf_op | source)
XLA Modules:
  0.0 241.9 jit_solution(5097337954689169323)
XLA Ops:
  0.6 1.8 copy.11
  2.5 0.2 shard_map.59
  2.7 0.5 collective-permute-start.2
  3.2 0.6 copy-done.11
  3.9 0.4 copy.10
  4.4 0.5 collective-permute-start.7
  4.9 2.6 %collective-permute-start.1 = (bf16[384,2048]{1,0:T(8,128)(2,1)S(1)}, bf16[384,2048]{1,0:T(8,128)(2,1)S(1)}, u32[]{:S(2)}, u32[]{:S(2)}) collective-permute-start(bf16[384,2048]{1,0:T(8,128)(2,1)S(1)} %bitcast.49), channel_id=1, source_target_pairs={{0,8},{4,12},{8,0},{12,4},{1,9},{5,13},{9,1},{13,5},{2,10},{6,14},... | collective-permute-start | bytes 4718600 | tf_op jit(solution)/shard_map/ppermute | solution.py:372
  7.6 0.7 collective-permute-start.5
  8.4 1.6 collective-permute-start
  9.9 4.3 %collective-permute-start.3 = (bf16[2,2,384,256]{3,2,1,0:T(8,128)(2,1)S(1)}, bf16[2,2,384,256]{3,2,1,0:T(8,128)(2,1)S(1)}, u32[]{:S(2)}, u32[]{:S(2)}) collective-permute-start(bf16[2,2,384,256]{3,2,1,0:T(8,128)(2,1)S(1)} %get-tuple-element.115.refs_10_), channel_id=1, source_target_pairs={{0,1},{1,0},{2,3},{3,2},{4,5},{5,4},{6,7},{7,6},{8,9},{9,8},{10,11... | collective-permute-start | bytes 2359304 | tf_op jit(solution)/shard_map/ppermute | solution.py:376
  14.3 1.3 collective-permute-start.6
  15.6 16.0 %collective-permute-done.3.refs_11_ = bf16[2,2,384,256]{3,2,1,0:T(8,128)(2,1)S(1)} collective-permute-done((bf16[2,2,384,256]{3,2,1,0:T(8,128)(2,1)S(1)}, bf16[2,2,384,256]{3,2,1,0:T(8,128)(2,1)S(1)}, u32[]{:S(2)}, u32[]{:S(2)}) %collective-permute-start.3) | collective-permute-done | bytes 786464 | tf_op jit(solution)/shard_map/ppermute | solution.py:376
  31.6 0.7 collective-permute-start.4
  32.3 10.1 %collective-permute-done.1.refs_2_ = bf16[384,2048]{1,0:T(8,128)(2,1)S(1)} collective-permute-done((bf16[384,2048]{1,0:T(8,128)(2,1)S(1)}, bf16[384,2048]{1,0:T(8,128)(2,1)S(1)}, u32[]{:S(2)}, u32[]{:S(2)}) %collective-permute-start.1) | collective-permute-done | bytes 1572896 | tf_op jit(solution)/shard_map/ppermute | solution.py:372
  42.5 2.4 %collective-permute-done.refs_1_ = bf16[384,2048]{1,0:T(8,128)(2,1)S(1)} collective-permute-done((bf16[384,2048]{1,0:T(8,128)(2,1)S(1)}, bf16[384,2048]{1,0:T(8,128)(2,1)S(1)}, u32[]{:S(2)}, u32[]{:S(2)}) %collective-permute-start) | collective-permute-done | bytes 1572896 | tf_op jit(solution)/shard_map/ppermute | solution.py:372
  44.9 4.1 %collective-permute-done.6.refs_14_ = bf16[2,2,384,256]{3,2,1,0:T(8,128)(2,1)S(1)} collective-permute-done((bf16[2,2,384,256]{3,2,1,0:T(8,128)(2,1)S(1)}, bf16[2,2,384,256]{3,2,1,0:T(8,128)(2,1)S(1)}, u32[]{:S(2)}, u32[]{:S(2)}) %collective-permute-start.6) | collective-permute-done | bytes 786464 | tf_op jit(solution)/shard_map/ppermute | solution.py:384
  49.2 0.6 collective-permute-start.10
  49.8 1.5 collective-permute-start.11
  51.3 0.7 collective-permute-start.9
  52.0 1.3 collective-permute-start.8
  53.4 14.0 %collective-permute-done.10.refs_3_ = bf16[192,2048]{1,0:T(8,128)(2,1)S(1)} collective-permute-done((bf16[192,2048]{1,0:T(8,128)(2,1)S(1)}, bf16[192,2048]{1,0:T(8,128)(2,1)S(1)}, u32[]{:S(2)}, u32[]{:S(2)}) %collective-permute-start.10) | collective-permute-done | bytes 786464 | tf_op jit(solution)/shard_map/ppermute | solution.py:372
  67.4 0.2 collective-permute-done.11.refs_4_
  67.6 7.4 %collective-permute-done.8.refs_15_ = bf16[2,2,384,256]{3,2,1,0:T(8,128)(2,1)S(1)} collective-permute-done((bf16[2,2,384,256]{3,2,1,0:T(8,128)(2,1)S(1)}, bf16[2,2,384,256]{3,2,1,0:T(8,128)(2,1)S(1)}, u32[]{:S(2)}, u32[]{:S(2)}) %collective-permute-start.8) | collective-permute-done | bytes 786464 | tf_op jit(solution)/shard_map/ppermute | solution.py:384
  75.0 0.5 collective-permute-start.15
  75.5 1.8 collective-permute-done.14.refs_8_
  77.3 1.3 collective-permute-start.20
  78.6 1.2 copy-done.17
  79.8 0.5 copy-done.16
  80.3 24.2 %shard_map.60 = (bf16[2,2,1024,1024]{3,2,1,0:T(8,128)(2,1)}, bf16[2,2,256,1024]{3,2,1,0:T(8,128)(2,1)}, f32[384,512]{1,0:T(8,128)S(1)}, f32[384,512]{1,0:T(8,128...) custom-call(bf16[384,2048]{1,0:T(8,128)(2,1)} %bitcast.51, ...), custom_call_target="tpu_custom_call" | custom-call | flops 12884901888 | bytes 12582912 | tf_op jit(solution)/shard_map/pallas_call | solution.py:236
  104.6 4.4 %collective-permute-start.16 = (bf16[2,384,512]{2,1,0:T(8,128)(2,1)S(1)}, bf16[2,384,512]{2,1,0:T(8,128)(2,1)S(1)}, u32[]{:S(2)}, u32[]{:S(2)}) collective-permute-start(bf16[2,384,512]{2,1,0:T(8,128)(2,1)S(1)} %get-tuple-element.80), channel_id=1, source_target_pairs={{0,1},{3,2},{4,5},{7,6},{8,9},{11,10},{12,13},{15,14},{16,17},{19,... | collective-permute-start | bytes 2359304 | tf_op jit(solution)/shard_map/ppermute | solution.py:388
  109.1 1.5 collective-permute-start.19
  110.6 1.2 collective-permute-done.20.refs_5_
  111.8 2.3 collective-permute-start.25
  114.1 12.8 %collective-permute-done.16 = bf16[2,384,512]{2,1,0:T(8,128)(2,1)S(1)} collective-permute-done((bf16[2,384,512]{2,1,0:T(8,128)(2,1)S(1)}, bf16[2,384,512]{2,1,0:T(8,128)(2,1)S(1)}, u32[]{:S(2)}, u32[]{:S(2)}) %collective-permute-start.16) | collective-permute-done | bytes 786464 | tf_op jit(solution)/shard_map/ppermute | solution.py:388
  126.9 2.6 %add_convert_fusion.2 = bf16[2,384,512]{2,1,0:T(8,128)(2,1)} fusion(f32[2,384,512]{2,1,0:T(8,128)} %get-tuple-element.79, bf16[2,384,512]{2,1,0:T(8,128)(2,1)S(1)} %collective-permute-done.16), kind=kLoop, calls=%fused_computation.4 | loop fusion | flops 1179648 | bytes 3145728 | tf_op jit(solution)/shard_map/convert_element_type | solution.py:436
  129.5 1.6 collective-permute-start.17
  131.1 1.3 collective-permute-start.21
  132.4 10.4 %collective-permute-done.25 = bf16[2,384,512]{2,1,0:T(8,128)(2,1)} collective-permute-done((bf16[2,384,512]{2,1,0:T(8,128)(2,1)}, bf16[2,384,512]{2,1,0:T(8,128)(2,1)}, u32[]{:S(2)}, u32[]{:S(2)}) %collective-permute-start.25) | collective-permute-done | bytes 786464 | tf_op jit(solution)/shard_map/ppermute | solution.py:388
  142.7 1.9 add_convert_fusion.1
  144.7 0.7 collective-permute-start.26
  145.4 1.1 fusion.3
  146.5 7.0 %collective-permute-start.34 = (bf16[384,512]{1,0:T(8,128)(2,1)S(1)}, bf16[384,512]{1,0:T(8,128)(2,1)S(1)}, u32[]{:S(2)}, u32[]{:S(2)}) collective-permute-start(bf16[384,512]{1,0:T(8,128)(2,1)S(1)} %fusion.3), channel_id=1, source_target_pairs={{0,1},{1,0},{2,3},{3,2},{4,5},{5,4},{6,7},{7,6},{8,9},{9,8},{10,11... | collective-permute-start | bytes 1179656 | tf_op jit(solution)/shard_map/ppermute | solution.py:376
  153.6 14.3 %shard_map.61 = (bf16[2,2,1024,1024]{3,2,1,0:T(8,128)(2,1)}, bf16[2,2,256,1024]{3,2,1,0:T(8,128)(2,1)}, f32[768,256]{1,0:T(8,128)S(1)}, f32[768,256]{1,0:T(8,128...) custom-call(bf16[3072,2048]{1,0:T(8,128)(2,1)} %get-tuple-element.78.refs_0_, ...), custom_call_target="tpu_custom_call", output_to_operand_aliasing={{0}: (10, {})} | custom-call | flops 6442450944 | bytes 12582912 | tf_op jit(solution)/shard_map/pallas_call | solution.py:236
  167.9 1.3 collective-permute-start.28
  169.2 15.2 %shard_map.62 = (bf16[2,2,1024,1024]{3,2,1,0:T(8,128)(2,1)}, bf16[2,2,256,1024]{3,2,1,0:T(8,128)(2,1)}, f32[384,256]{1,0:T(8,128)S(1)}, f32[384,256]{1,0:T(8,128...) custom-call(bf16[3072,2048]{1,0:T(8,128)(2,1)} %get-tuple-element.78, ...), custom_call_target="tpu_custom_call", output_to_operand_aliasing={{1}: (9, {}), {0}: (10, {})} | custom-call | flops 6442450944 | bytes 12582912 | tf_op jit(solution)/shard_map/pallas_call | solution.py:236
  184.5 1.4 collective-permute-start.24
  186.0 1.2 fusion.4
  187.2 1.3 collective-permute-start.31
  188.5 0.6 collective-permute-start.23
  189.1 0.2 add_convert_fusion
  189.3 3.7 %collective-permute-done.24 = bf16[2,384,256]{2,1,0:T(8,128)(2,1)S(1)} collective-permute-done((bf16[2,384,256]{2,1,0:T(8,128)(2,1)S(1)}, bf16[2,384,256]{2,1,0:T(8,128)(2,1)S(1)}, u32[]{:S(2)}, u32[]{:S(2)}) %collective-permute-start.24) | collective-permute-done | bytes 393248 | tf_op jit(solution)/shard_map/ppermute | solution.py:388
  192.9 0.7 collective-permute-start.29
  193.8 0.7 collective-permute-start.37
  194.6 5.0 %collective-permute-done.31 = bf16[2,384,256]{2,1,0:T(8,128)(2,1)S(1)} collective-permute-done((bf16[2,384,256]{2,1,0:T(8,128)(2,1)S(1)}, bf16[2,384,256]{2,1,0:T(8,128)(2,1)S(1)}, u32[]{:S(2)}, u32[]{:S(2)}) %collective-permute-start.31) | collective-permute-done | bytes 393248 | tf_op jit(solution)/shard_map/ppermute | solution.py:388
  199.6 2.5 %collective-permute-start.27 = (bf16[384,512]{1,0:T(8,128)(2,1)S(1)}, bf16[384,512]{1,0:T(8,128)(2,1)S(1)}, u32[]{:S(2)}, u32[]{:S(2)}) collective-permute-start(bf16[384,512]{1,0:T(8,128)(2,1)S(1)} %fusion.7), channel_id=1, source_target_pairs={{0,1},{1,0},{2,3},{3,2},{4,5},{5,4},{6,7},{7,6},{8,9},{9,8},{10,11... | collective-permute-start | bytes 1179656 | tf_op jit(solution)/shard_map/ppermute | solution.py:376
  202.2 0.7 collective-permute-start.32
  203.0 22.0 %collective-permute-start.38 = (bf16[384,256]{1,0:T(8,128)(2,1)S(1)}, bf16[384,256]{1,0:T(8,128)(2,1)S(1)}, u32[]{:S(2)}, u32[]{:S(2)}) collective-permute-start(bf16[384,256]{1,0:T(8,128)(2,1)S(1)} %fusion.9), channel_id=1, source_target_pairs={{0,1},{1,0},{2,3},{3,2},{4,5},{5,4},{6,7},{7,6},{8,9},{9,8},{10,11... | collective-permute-start | bytes 589832 | tf_op jit(solution)/shard_map/ppermute | solution.py:376
  225.0 5.8 %collective-permute-start.30 = (bf16[768,256]{1,0:T(8,128)(2,1)S(1)}, bf16[768,256]{1,0:T(8,128)(2,1)S(1)}, u32[]{:S(2)}, u32[]{:S(2)}) collective-permute-start(bf16[768,256]{1,0:T(8,128)(2,1)S(1)} %fusion.5), channel_id=1, source_target_pairs={{0,1},{1,0},{2,3},{3,2},{4,5},{5,4},{6,7},{7,6},{8,9},{9,8},{10,11... | collective-permute-start | bytes 1179656 | tf_op jit(solution)/shard_map/ppermute | solution.py:376
  230.9 1.9 collective-permute-start.33
  232.8 3.7 %collective-permute-done.30 = bf16[768,256]{1,0:T(8,128)(2,1)S(1)} collective-permute-done((bf16[768,256]{1,0:T(8,128)(2,1)S(1)}, bf16[768,256]{1,0:T(8,128)(2,1)S(1)}, u32[]{:S(2)}, u32[]{:S(2)}) %collective-permute-start.30) | collective-permute-done | bytes 393248 | tf_op jit(solution)/shard_map/ppermute | solution.py:376
  236.8 0.6 collective-permute-start.36
  237.3 0.4 copy-done.1
  237.9 0.8 collective-permute-done.33
  238.9 2.9 %shard_map.63 = (bf16[2,2,1024,1024]{3,2,1,0:T(8,128)(2,1)}, f32[384,2,1024]{2,1,0:T(2,128)}) custom-call(bf16[2,2,256,1024]{3,2,1,0:T(8,128)(2,1)S(1)} %collective-permute-done.23.refs_0_, bf16[2,2,1024,1024]{3,2,1,0:T(8,128)(2,1)} %get-tuple-element.93.refs_1_, f32[384,512]{1,0:T(8,128)S(1)} %fusion.8.refs_2_, ...), custom_call_target="tpu_custom_call", output_to_operand_aliasing={{0}: (1, {})} | custom-call | bytes 10485760 | tf_op jit(solution)/shard_map/pallas_call | solution.py:345
  (84 shorter events, 1.7 us)
Async XLA Ops:
  2.5 1.4 copy-start.11
  2.7 4.7 %collective-permute-start.2 = (bf16[2,2,384,256]{3,2,1,0:T(8,128)(2,1)S(1)}, bf16[2,2,384,256]{3,2,1,0:T(8,128)(2,1)S(1)}, u32[]{:S(2)}, u32[]{:S(2)}) collective-permute-start(bf16[2,2,384,256]{3,2,1,0:T(8,128)(2,1)S(1)} %get-tuple-element.59), channel_id=1, source_target_pairs={{0,16},{16,0},{1,17},{17,1},{2,18},{18,2},{3,19},{19,3},{4,20},{20... | collective-permute-start | bytes 2359304 | tf_op jit(solution)/shard_map/ppermute | solution.py:368
  4.3 4.0 %copy-start.12 = (bf16[48,8,2,1024]{3,1,2,0:T(8,128)(2,1)}, bf16[48,8,2,1024]{3,1,2,0:T(8,128)(2,1)S(1)}, u32[]{:S(2)}) copy-start(bf16[48,8,2,1024]{3,1,2,0:T(8,128)(2,1)S(1)} %copy.10) | copy-start | bytes 4718596
  4.4 27.9 %collective-permute-start.7 = (bf16[384,2048]{1,0:T(8,128)(2,1)S(1)}, bf16[384,2048]{1,0:T(8,128)(2,1)S(1)}, u32[]{:S(2)}, u32[]{:S(2)}) collective-permute-start(bf16[384,2048]{1,0:T(8,128)(2,1)S(1)} %bitcast.48), channel_id=1, source_target_pairs={{0,16},{16,0},{1,17},{17,1},{2,18},{18,2},{3,19},{19,3},{4,20},{20... | collective-permute-start | bytes 4718600 | tf_op jit(solution)/shard_map/ppermute | solution.py:368
  4.9 37.6 %collective-permute-start.1 = (bf16[384,2048]{1,0:T(8,128)(2,1)S(1)}, bf16[384,2048]{1,0:T(8,128)(2,1)S(1)}, u32[]{:S(2)}, u32[]{:S(2)}) collective-permute-start(bf16[384,2048]{1,0:T(8,128)(2,1)S(1)} %bitcast.49), channel_id=1, source_target_pairs={{0,8},{4,12},{8,0},{12,4},{1,9},{5,13},{9,1},{13,5},{2,10},{6,14},... | collective-permute-start | bytes 4718600 | tf_op jit(solution)/shard_map/ppermute | solution.py:372
  7.6 72.7 %copy-start.8 = (f32[4096]{0:T(1024)S(1)}, f32[4096]{0:T(1024)}, u32[]{:S(2)}) copy-start(f32[4096]{0:T(1024)} %param.7) | copy-start | bytes 49156
  7.6 72.7 %copy-start.9 = (f32[2]{0:T(128)S(1)}, f32[2]{0:T(128)}, u32[]{:S(2)}) copy-start(f32[2]{0:T(128)} %refs_7_.3) | copy-start | bytes 28
  7.6 6.6 %collective-permute-start.5 = (bf16[2,2,384,256]{3,2,1,0:T(8,128)(2,1)S(1)}, bf16[2,2,384,256]{3,2,1,0:T(8,128)(2,1)S(1)}, u32[]{:S(2)}, u32[]{:S(2)}) collective-permute-start(bf16[2,2,384,256]{3,2,1,0:T(8,128)(2,1)S(1)} %get-tuple-element.115.refs_10_), channel_id=1, source_target_pairs={{1,2},{2,1},{5,6},{6,5},{9,10},{10,9},{13,14},{14,13},{17,18},{18,... | collective-permute-start | bytes 2359304 | tf_op jit(solution)/shard_map/ppermute | solution.py:380
  8.4 36.5 %collective-permute-start = (bf16[384,2048]{1,0:T(8,128)(2,1)S(1)}, bf16[384,2048]{1,0:T(8,128)(2,1)S(1)}, u32[]{:S(2)}, u32[]{:S(2)}) collective-permute-start(bf16[384,2048]{1,0:T(8,128)(2,1)S(1)} %bitcast.50), channel_id=1, source_target_pairs={{0,4},{4,0},{8,12},{12,8},{1,5},{5,1},{9,13},{13,9},{2,6},{6,2},{1... | collective-permute-start | bytes 4718600 | tf_op jit(solution)/shard_map/ppermute | solution.py:372
  9.9 21.7 %collective-permute-start.3 = (bf16[2,2,384,256]{3,2,1,0:T(8,128)(2,1)S(1)}, bf16[2,2,384,256]{3,2,1,0:T(8,128)(2,1)S(1)}, u32[]{:S(2)}, u32[]{:S(2)}) collective-permute-start(bf16[2,2,384,256]{3,2,1,0:T(8,128)(2,1)S(1)} %get-tuple-element.115.refs_10_), channel_id=1, source_target_pairs={{0,1},{1,0},{2,3},{3,2},{4,5},{5,4},{6,7},{7,6},{8,9},{9,8},{10,11... | collective-permute-start | bytes 2359304 | tf_op jit(solution)/shard_map/ppermute | solution.py:376
  14.3 34.7 %collective-permute-start.6 = (bf16[2,2,384,256]{3,2,1,0:T(8,128)(2,1)S(1)}, bf16[2,2,384,256]{3,2,1,0:T(8,128)(2,1)S(1)}, u32[]{:S(2)}, u32[]{:S(2)}) collective-permute-start(bf16[2,2,384,256]{3,2,1,0:T(8,128)(2,1)S(1)} %collective-permute-done.5.refs_12_), channel_id=1, source_target_pairs={{1,0},{2,3},{5,4},{6,7},{9,8},{10,11},{13,12},{14,15},{17,16},{18,... | collective-permute-start | bytes 2359304 | tf_op jit(solution)/shard_map/ppermute | solution.py:384
  31.6 17.4 %collective-permute-start.4 = (bf16[2,2,384,256]{3,2,1,0:T(8,128)(2,1)S(1)}, bf16[2,2,384,256]{3,2,1,0:T(8,128)(2,1)S(1)}, u32[]{:S(2)}, u32[]{:S(2)}) collective-permute-start(bf16[2,2,384,256]{3,2,1,0:T(8,128)(2,1)S(1)} %collective-permute-done.3.refs_11_), channel_id=1, source_target_pairs={{1,2},{2,1},{5,6},{6,5},{9,10},{10,9},{13,14},{14,13},{17,18},{18,... | collective-permute-start | bytes 2359304 | tf_op jit(solution)/shard_map/ppermute | solution.py:380
  32.3 47.5 %copy-start.15 = (bf16[384,2048]{1,0:T(8,128)(2,1)}, bf16[384,2048]{1,0:T(8,128)(2,1)S(1)}, u32[]{:S(2)}) copy-start(bf16[384,2048]{1,0:T(8,128)(2,1)S(1)} %collective-permute-done.7.refs_5_) | copy-start | bytes 4718596
  42.5 25.0 %copy-start.13 = (bf16[384,2048]{1,0:T(8,128)(2,1)}, bf16[384,2048]{1,0:T(8,128)(2,1)S(1)}, u32[]{:S(2)}) copy-start(bf16[384,2048]{1,0:T(8,128)(2,1)S(1)} %collective-permute-done.1.refs_2_) | copy-start | bytes 4718596
  44.9 8.4 %copy-start.14 = (bf16[384,2048]{1,0:T(8,128)(2,1)}, bf16[384,2048]{1,0:T(8,128)(2,1)S(1)}, u32[]{:S(2)}) copy-start(bf16[384,2048]{1,0:T(8,128)(2,1)S(1)} %collective-permute-done.refs_1_) | copy-start | bytes 4718596
  49.0 30.8 %copy-start.18 = (bf16[2,2,384,256]{3,2,1,0:T(8,128)(2,1)}, bf16[2,2,384,256]{3,2,1,0:T(8,128)(2,1)S(1)}, u32[]{:S(2)}) copy-start(bf16[2,2,384,256]{3,2,1,0:T(8,128)(2,1)S(1)} %collective-permute-done.6.refs_14_) | copy-start | bytes 2359300
  49.0 29.6 %copy-start.19 = (bf16[2,2,384,256]{3,2,1,0:T(8,128)(2,1)}, bf16[2,2,384,256]{3,2,1,0:T(8,128)(2,1)S(1)}, u32[]{:S(2)}) copy-start(bf16[2,2,384,256]{3,2,1,0:T(8,128)(2,1)S(1)} %collective-permute-done.4.refs_13_) | copy-start | bytes 2359300
  49.2 18.2 %collective-permute-start.10 = (bf16[192,2048]{1,0:T(8,128)(2,1)S(1)}, bf16[192,2048]{1,0:T(8,128)(2,1)S(1)}, u32[]{:S(2)}, u32[]{:S(2)}) collective-permute-start(bf16[192,2048]{1,0:T(8,128)(2,1)S(1)} %slice.20), channel_id=1, source_target_pairs={{0,8},{4,12},{8,0},{12,4},{1,9},{5,13},{9,1},{13,5},{2,10},{6,14},... | collective-permute-start | bytes 2359304 | tf_op jit(solution)/shard_map/ppermute | solution.py:372
  49.8 17.9 %collective-permute-start.11 = (bf16[192,2048]{1,0:T(8,128)(2,1)S(1)}, bf16[192,2048]{1,0:T(8,128)(2,1)S(1)}, u32[]{:S(2)}, u32[]{:S(2)}) collective-permute-start(bf16[192,2048]{1,0:T(8,128)(2,1)S(1)} %slice.21), channel_id=1, source_target_pairs={{0,4},{4,0},{8,12},{12,8},{1,5},{5,1},{9,13},{13,9},{2,6},{6,2},{1... | collective-permute-start | bytes 2359304 | tf_op jit(solution)/shard_map/ppermute | solution.py:372
  51.3 16.4 %collective-permute-start.9 = (bf16[2,2,384,256]{3,2,1,0:T(8,128)(2,1)S(1)}, bf16[2,2,384,256]{3,2,1,0:T(8,128)(2,1)S(1)}, u32[]{:S(2)}, u32[]{:S(2)}) collective-permute-start(bf16[2,2,384,256]{3,2,1,0:T(8,128)(2,1)S(1)} %get-tuple-element.83.refs_1_), channel_id=1, source_target_pairs={{1,2},{2,1},{5,6},{6,5},{9,10},{10,9},{13,14},{14,13},{17,18},{18,... | collective-permute-start | bytes 2359304 | tf_op jit(solution)/shard_map/ppermute | solution.py:380
  52.0 23.0 %collective-permute-start.8 = (bf16[2,2,384,256]{3,2,1,0:T(8,128)(2,1)S(1)}, bf16[2,2,384,256]{3,2,1,0:T(8,128)(2,1)S(1)}, u32[]{:S(2)}, u32[]{:S(2)}) collective-permute-start(bf16[2,2,384,256]{3,2,1,0:T(8,128)(2,1)S(1)} %collective-permute-done.4.refs_13_), channel_id=1, source_target_pairs={{1,0},{2,3},{5,4},{6,7},{9,8},{10,11},{13,12},{14,15},{17,16},{18,... | collective-permute-start | bytes 2359304 | tf_op jit(solution)/shard_map/ppermute | solution.py:384
  53.3 25.3 %collective-permute-start.12 = (bf16[384,2048]{1,0:T(8,128)(2,1)S(1)}, bf16[384,2048]{1,0:T(8,128)(2,1)S(1)}, u32[]{:S(2)}, u32[]{:S(2)}) collective-permute-start(bf16[384,2048]{1,0:T(8,128)(2,1)S(1)} %collective-permute-done.refs_1_), channel_id=1, source_target_pairs={{0,16},{16,0},{1,17},{17,1},{2,18},{18,2},{3,19},{19,3},{4,20},{20... | collective-permute-start | bytes 4718600 | tf_op jit(solution)/shard_map/ppermute | solution.py:368
  67.4 11.2 %collective-permute-start.13 = (bf16[384,2048]{1,0:T(8,128)(2,1)S(1)}, bf16[384,2048]{1,0:T(8,128)(2,1)S(1)}, u32[]{:S(2)}, u32[]{:S(2)}) collective-permute-start(bf16[384,2048]{1,0:T(8,128)(2,1)S(1)} %collective-permute-done.1.refs_2_), channel_id=1, source_target_pairs={{0,16},{16,0},{1,17},{17,1},{2,18},{18,2},{3,19},{19,3},{4,20},{20... | collective-permute-start | bytes 4718600 | tf_op jit(solution)/shard_map/ppermute | solution.py:368
  75.0 3.6 %copy-start.20 = (bf16[2,2,384,256]{3,2,1,0:T(8,128)(2,1)}, bf16[2,2,384,256]{3,2,1,0:T(8,128)(2,1)S(1)}, u32[]{:S(2)}) copy-start(bf16[2,2,384,256]{3,2,1,0:T(8,128)(2,1)S(1)} %collective-permute-done.8.refs_15_) | copy-start | bytes 2359300
  75.0 2.3 collective-permute-start.14
  75.0 3.6 %collective-permute-start.15 = (bf16[192,2048]{1,0:T(8,128)(2,1)S(1)}, bf16[192,2048]{1,0:T(8,128)(2,1)S(1)}, u32[]{:S(2)}, u32[]{:S(2)}) collective-permute-start(bf16[192,2048]{1,0:T(8,128)(2,1)S(1)} %collective-permute-done.11.refs_4_), channel_id=1, source_target_pairs={{0,16},{16,0},{1,17},{17,1},{2,18},{18,2},{3,19},{19,3},{4,20},{20... | collective-permute-start | bytes 2359304 | tf_op jit(solution)/shard_map/ppermute | solution.py:368
  75.5 33.6 %collective-permute-start.18 = (bf16[2,2,384,256]{3,2,1,0:T(8,128)(2,1)S(1)}, bf16[2,2,384,256]{3,2,1,0:T(8,128)(2,1)S(1)}, u32[]{:S(2)}, u32[]{:S(2)}) collective-permute-start(bf16[2,2,384,256]{3,2,1,0:T(8,128)(2,1)S(1)} %get-tuple-element.83.refs_1_), channel_id=1, source_target_pairs={{0,1},{1,0},{2,3},{3,2},{4,5},{5,4},{6,7},{7,6},{8,9},{9,8},{10,11... | collective-permute-start | bytes 2359304 | tf_op jit(solution)/shard_map/ppermute | solution.py:376
  77.3 34.5 %collective-permute-start.20 = (bf16[2,2,384,256]{3,2,1,0:T(8,128)(2,1)S(1)}, bf16[2,2,384,256]{3,2,1,0:T(8,128)(2,1)S(1)}, u32[]{:S(2)}, u32[]{:S(2)}) collective-permute-start(bf16[2,2,384,256]{3,2,1,0:T(8,128)(2,1)S(1)} %collective-permute-done.9.refs_3_), channel_id=1, source_target_pairs={{1,0},{2,3},{5,4},{6,7},{9,8},{10,11},{13,12},{14,15},{17,16},{18,... | collective-permute-start | bytes 2359304 | tf_op jit(solution)/shard_map/ppermute | solution.py:384
  78.6 1.7 copy-start.16
  78.6 1.2 copy-start.17
  104.5 24.9 %copy-start = (f32[384,512]{1,0:T(8,128)}, f32[384,512]{1,0:T(8,128)S(1)}, u32[]{:S(2)}) copy-start(f32[384,512]{1,0:T(8,128)S(1)} %get-tuple-element.94) | copy-start | bytes 2359300
  104.6 24.9 %copy-start.2 = (f32[384,512]{1,0:T(8,128)}, f32[384,512]{1,0:T(8,128)S(1)}, u32[]{:S(2)}) copy-start(f32[384,512]{1,0:T(8,128)S(1)} %get-tuple-element.108) | copy-start | bytes 2359300
  104.6 24.9 %copy-start.4 = (f32[384,512]{1,0:T(8,128)}, f32[384,512]{1,0:T(8,128)S(1)}, u32[]{:S(2)}) copy-start(f32[384,512]{1,0:T(8,128)S(1)} %get-tuple-element.99) | copy-start | bytes 2359300
  104.6 24.9 %copy-start.6 = (f32[384,512]{1,0:T(8,128)}, f32[384,512]{1,0:T(8,128)S(1)}, u32[]{:S(2)}) copy-start(f32[384,512]{1,0:T(8,128)S(1)} %get-tuple-element.110) | copy-start | bytes 2359300
  104.6 22.3 %collective-permute-start.16 = (bf16[2,384,512]{2,1,0:T(8,128)(2,1)S(1)}, bf16[2,384,512]{2,1,0:T(8,128)(2,1)S(1)}, u32[]{:S(2)}, u32[]{:S(2)}) collective-permute-start(bf16[2,384,512]{2,1,0:T(8,128)(2,1)S(1)} %get-tuple-element.80), channel_id=1, source_target_pairs={{0,1},{3,2},{4,5},{7,6},{8,9},{11,10},{12,13},{15,14},{16,17},{19,... | collective-permute-start | bytes 2359304 | tf_op jit(solution)/shard_map/ppermute | solution.py:388
  109.0 44.6 %collective-permute-start.22 = (bf16[2,2,256,1024]{3,2,1,0:T(8,128)(2,1)}, bf16[2,2,256,1024]{3,2,1,0:T(8,128)(2,1)}, u32[]{:S(2)}, u32[]{:S(2)}) collective-permute-start(bf16[2,2,256,1024]{3,2,1,0:T(8,128)(2,1)} %get-tuple-element.88), channel_id=1, source_target_pairs={{0,16},{16,0},{1,17},{17,1},{2,18},{18,2},{3,19},{19,3},{4,20},{20... | collective-permute-start | bytes 6291464 | tf_op jit(solution)/shard_map/ppermute | solution.py:368
  109.1 22.0 %collective-permute-start.19 = (bf16[2,2,384,256]{3,2,1,0:T(8,128)(2,1)S(1)}, bf16[2,2,384,256]{3,2,1,0:T(8,128)(2,1)}, u32[]{:S(2)}, u32[]{:S(2)}) collective-permute-start(bf16[2,2,384,256]{3,2,1,0:T(8,128)(2,1)S(1)} %collective-permute-done.18.refs_2_), channel_id=1, source_target_pairs={{1,2},{2,1},{5,6},{6,5},{9,10},{10,9},{13,14},{14,13},{17,18},{18,... | collective-permute-start | bytes 2359304 | tf_op jit(solution)/shard_map/ppermute | solution.py:380
  111.8 30.9 %collective-permute-start.25 = (bf16[2,384,512]{2,1,0:T(8,128)(2,1)}, bf16[2,384,512]{2,1,0:T(8,128)(2,1)}, u32[]{:S(2)}, u32[]{:S(2)}) collective-permute-start(bf16[2,384,512]{2,1,0:T(8,128)(2,1)} %get-tuple-element.97), channel_id=1, source_target_pairs={{0,1},{3,2},{4,5},{7,6},{8,9},{11,10},{12,13},{15,14},{16,17},{19,... | collective-permute-start | bytes 2359304 | tf_op jit(solution)/shard_map/ppermute | solution.py:388
  129.5 15.9 %collective-permute-start.17 = (bf16[2,384,512]{2,1,0:T(8,128)(2,1)}, bf16[2,384,512]{2,1,0:T(8,128)(2,1)}, u32[]{:S(2)}, u32[]{:S(2)}) collective-permute-start(bf16[2,384,512]{2,1,0:T(8,128)(2,1)} %add_convert_fusion.2), channel_id=1, source_target_pairs={{1,2},{2,1},{5,6},{6,5},{9,10},{10,9},{13,14},{14,13},{17,18},{18,... | collective-permute-start | bytes 2359304 | tf_op jit(solution)/shard_map/ppermute | solution.py:380
  131.1 22.5 %collective-permute-start.21 = (bf16[2,2,384,256]{3,2,1,0:T(8,128)(2,1)}, bf16[2,2,384,256]{3,2,1,0:T(8,128)(2,1)}, u32[]{:S(2)}, u32[]{:S(2)}) collective-permute-start(bf16[2,2,384,256]{3,2,1,0:T(8,128)(2,1)} %collective-permute-done.19.refs_4_), channel_id=1, source_target_pairs={{1,0},{2,3},{5,4},{6,7},{9,8},{10,11},{13,12},{14,15},{17,16},{18,... | collective-permute-start | bytes 2359304 | tf_op jit(solution)/shard_map/ppermute | solution.py:384
  142.7 2.7 %copy-start.7 = (f32[384,512]{1,0:T(8,128)S(1)}, f32[384,512]{1,0:T(8,128)}, u32[]{:S(2)}) copy-start(f32[384,512]{1,0:T(8,128)} %copy-done.6) | copy-start | bytes 2359300
  144.7 49.1 %collective-permute-start.26 = (bf16[2,384,512]{2,1,0:T(8,128)(2,1)S(1)}, bf16[2,384,512]{2,1,0:T(8,128)(2,1)S(1)}, u32[]{:S(2)}, u32[]{:S(2)}) collective-permute-start(bf16[2,384,512]{2,1,0:T(8,128)(2,1)S(1)} %add_convert_fusion.1), channel_id=1, source_target_pairs={{1,2},{2,1},{5,6},{6,5},{9,10},{10,9},{13,14},{14,13},{17,18},{18,... | collective-permute-start | bytes 2359304 | tf_op jit(solution)/shard_map/ppermute | solution.py:380
  146.5 39.4 %collective-permute-start.34 = (bf16[384,512]{1,0:T(8,128)(2,1)S(1)}, bf16[384,512]{1,0:T(8,128)(2,1)S(1)}, u32[]{:S(2)}, u32[]{:S(2)}) collective-permute-start(bf16[384,512]{1,0:T(8,128)(2,1)S(1)} %fusion.3), channel_id=1, source_target_pairs={{0,1},{1,0},{2,3},{3,2},{4,5},{5,4},{6,7},{7,6},{8,9},{9,8},{10,11... | collective-permute-start | bytes 1179656 | tf_op jit(solution)/shard_map/ppermute | solution.py:376
  167.9 20.6 %collective-permute-start.28 = (bf16[2,768,256]{2,1,0:T(8,128)(2,1)S(1)}, bf16[2,768,256]{2,1,0:T(8,128)(2,1)S(1)}, u32[]{:S(2)}, u32[]{:S(2)}) collective-permute-start(bf16[2,768,256]{2,1,0:T(8,128)(2,1)S(1)} %get-tuple-element.102), channel_id=1, source_target_pairs={{0,1},{3,2},{4,5},{7,6},{8,9},{11,10},{12,13},{15,14},{16,17},{19,... | collective-permute-start | bytes 2359304 | tf_op jit(solution)/shard_map/ppermute | solution.py:388
  169.2 16.7 %copy-start.3 = (f32[384,512]{1,0:T(8,128)S(1)}, f32[384,512]{1,0:T(8,128)}, u32[]{:S(2)}) copy-start(f32[384,512]{1,0:T(8,128)} %copy-done.2) | copy-start | bytes 2359300
  184.5 4.1 %copy-start.10 = (bf16[2,2,256,1024]{3,2,1,0:T(8,128)(2,1)S(1)}, bf16[2,2,256,1024]{3,2,1,0:T(8,128)(2,1)}, u32[]{:S(2)}) copy-start(bf16[2,2,256,1024]{3,2,1,0:T(8,128)(2,1)} %get-tuple-element.92) | copy-start | bytes 6291460
  184.5 8.5 %collective-permute-start.24 = (bf16[2,384,256]{2,1,0:T(8,128)(2,1)S(1)}, bf16[2,384,256]{2,1,0:T(8,128)(2,1)S(1)}, u32[]{:S(2)}, u32[]{:S(2)}) collective-permute-start(bf16[2,384,256]{2,1,0:T(8,128)(2,1)S(1)} %get-tuple-element.95), channel_id=1, source_target_pairs={{0,1},{3,2},{4,5},{7,6},{8,9},{11,10},{12,13},{15,14},{16,17},{19,... | collective-permute-start | bytes 1179656 | tf_op jit(solution)/shard_map/ppermute | solution.py:388
  187.1 51.6 %collective-permute-start.35 = (f32[384,512]{1,0:T(8,128)S(1)}, f32[384,512]{1,0:T(8,128)S(1)}, u32[]{:S(2)}, u32[]{:S(2)}) collective-permute-start(f32[384,512]{1,0:T(8,128)S(1)} %fusion.4), channel_id=1, source_target_pairs={{0,16},{16,0},{1,17},{17,1},{2,18},{18,2},{3,19},{19,3},{4,20},{20... | collective-permute-start | bytes 2359304 | tf_op jit(solution)/shard_map/ppermute | solution.py:368
  187.2 12.4 %collective-permute-start.31 = (bf16[2,384,256]{2,1,0:T(8,128)(2,1)S(1)}, bf16[2,384,256]{2,1,0:T(8,128)(2,1)S(1)}, u32[]{:S(2)}, u32[]{:S(2)}) collective-permute-start(bf16[2,384,256]{2,1,0:T(8,128)(2,1)S(1)} %get-tuple-element.106), channel_id=1, source_target_pairs={{0,1},{3,2},{4,5},{7,6},{8,9},{11,10},{12,13},{15,14},{16,17},{19,... | collective-permute-start | bytes 1179656 | tf_op jit(solution)/shard_map/ppermute | solution.py:388
  188.5 50.2 %collective-permute-start.23 = (bf16[2,2,256,1024]{3,2,1,0:T(8,128)(2,1)S(1)}, bf16[2,2,256,1024]{3,2,1,0:T(8,128)(2,1)S(1)}, u32[]{:S(2)}, u32[]{:S(2)}) collective-permute-start(bf16[2,2,256,1024]{3,2,1,0:T(8,128)(2,1)S(1)} %copy-done.10), channel_id=1, source_target_pairs={{0,16},{16,0},{1,17},{17,1},{2,18},{18,2},{3,19},{19,3},{4,20},{20... | collective-permute-start | bytes 6291464 | tf_op jit(solution)/shard_map/ppermute | solution.py:368
  189.3 5.2 %copy-start.5 = (f32[384,512]{1,0:T(8,128)S(1)}, f32[384,512]{1,0:T(8,128)}, u32[]{:S(2)}) copy-start(f32[384,512]{1,0:T(8,128)} %copy-done.4) | copy-start | bytes 2359300
  192.9 10.0 %collective-permute-start.29 = (bf16[2,768,256]{2,1,0:T(8,128)(2,1)S(1)}, bf16[2,768,256]{2,1,0:T(8,128)(2,1)S(1)}, u32[]{:S(2)}, u32[]{:S(2)}) collective-permute-start(bf16[2,768,256]{2,1,0:T(8,128)(2,1)S(1)} %add_convert_fusion), channel_id=1, source_target_pairs={{1,2},{2,1},{5,6},{6,5},{9,10},{10,9},{13,14},{14,13},{17,18},{18,... | collective-permute-start | bytes 2359304 | tf_op jit(solution)/shard_map/ppermute | solution.py:380
  193.8 8.4 %collective-permute-start.37 = (bf16[2,384,256]{2,1,0:T(8,128)(2,1)S(1)}, bf16[2,384,256]{2,1,0:T(8,128)(2,1)S(1)}, u32[]{:S(2)}, u32[]{:S(2)}) collective-permute-start(bf16[2,384,256]{2,1,0:T(8,128)(2,1)S(1)} %add_convert_fusion.3), channel_id=1, source_target_pairs={{1,2},{2,1},{5,6},{6,5},{9,10},{10,9},{13,14},{14,13},{17,18},{18,... | collective-permute-start | bytes 1179656 | tf_op jit(solution)/shard_map/ppermute | solution.py:380
  199.6 37.1 %collective-permute-start.27 = (bf16[384,512]{1,0:T(8,128)(2,1)S(1)}, bf16[384,512]{1,0:T(8,128)(2,1)S(1)}, u32[]{:S(2)}, u32[]{:S(2)}) collective-permute-start(bf16[384,512]{1,0:T(8,128)(2,1)S(1)} %fusion.7), channel_id=1, source_target_pairs={{0,1},{1,0},{2,3},{3,2},{4,5},{5,4},{6,7},{7,6},{8,9},{9,8},{10,11... | collective-permute-start | bytes 1179656 | tf_op jit(solution)/shard_map/ppermute | solution.py:376
  202.2 22.8 %collective-permute-start.32 = (bf16[2,384,256]{2,1,0:T(8,128)(2,1)S(1)}, bf16[2,384,256]{2,1,0:T(8,128)(2,1)S(1)}, u32[]{:S(2)}, u32[]{:S(2)}) collective-permute-start(bf16[2,384,256]{2,1,0:T(8,128)(2,1)S(1)} %add_convert_fusion.4), channel_id=1, source_target_pairs={{1,2},{2,1},{5,6},{6,5},{9,10},{10,9},{13,14},{14,13},{17,18},{18,... | collective-permute-start | bytes 1179656 | tf_op jit(solution)/shard_map/ppermute | solution.py:380
  203.0 27.9 %collective-permute-start.38 = (bf16[384,256]{1,0:T(8,128)(2,1)S(1)}, bf16[384,256]{1,0:T(8,128)(2,1)S(1)}, u32[]{:S(2)}, u32[]{:S(2)}) collective-permute-start(bf16[384,256]{1,0:T(8,128)(2,1)S(1)} %fusion.9), channel_id=1, source_target_pairs={{0,1},{1,0},{2,3},{3,2},{4,5},{5,4},{6,7},{7,6},{8,9},{9,8},{10,11... | collective-permute-start | bytes 589832 | tf_op jit(solution)/shard_map/ppermute | solution.py:376
  225.0 11.5 %collective-permute-start.30 = (bf16[768,256]{1,0:T(8,128)(2,1)S(1)}, bf16[768,256]{1,0:T(8,128)(2,1)S(1)}, u32[]{:S(2)}, u32[]{:S(2)}) collective-permute-start(bf16[768,256]{1,0:T(8,128)(2,1)S(1)} %fusion.5), channel_id=1, source_target_pairs={{0,1},{1,0},{2,3},{3,2},{4,5},{5,4},{6,7},{7,6},{8,9},{9,8},{10,11... | collective-permute-start | bytes 1179656 | tf_op jit(solution)/shard_map/ppermute | solution.py:376
  230.9 7.8 %collective-permute-start.33 = (bf16[384,256]{1,0:T(8,128)(2,1)S(1)}, bf16[384,256]{1,0:T(8,128)(2,1)S(1)}, u32[]{:S(2)}, u32[]{:S(2)}) collective-permute-start(bf16[384,256]{1,0:T(8,128)(2,1)S(1)} %fusion.11), channel_id=1, source_target_pairs={{0,1},{1,0},{2,3},{3,2},{4,5},{5,4},{6,7},{7,6},{8,9},{9,8},{10,11... | collective-permute-start | bytes 589832 | tf_op jit(solution)/shard_map/ppermute | solution.py:376
  236.6 2.2 collective-permute-start.39
  236.6 1.1 copy-start.1
  236.8 2.1 collective-permute-start.36

commit v4 on v2

--- a/solution.py
+++ b/solution.py
@@ -82,8 +82,8 @@
     whole_ref, half_ref = take(2)
     own_ref, pair_ref, far_ref, send_ref = (take(1 + SPLIT[group]) for _ in range(4))
     (ket_all,) = (None,) if group else take(1)
-    kv, bv, bt, t2, amps, given, ket_sem, bra_sem, out_sem = refs
-    batch, block_width = bra.shape[2:]
+    kv, bt, t2, amps, given, *tiles, ket_sem, bra_sem, out_sem = refs
+    block_width, batch = bra.shape[2:]
     number, start, width = place_of(group, block_width)
     span = ket[0].shape[1] // 2
     half = whole_ref.shape[2] // 2
@@ -96,8 +96,11 @@
     def bra_copies(source, home, slot):
         return [
             pltpu.make_async_copy(
-                source.at[q, i, :, pl.ds(start, width)],
-                bv.at[home, pl.ds(q * batch, batch), pl.ds(i * width, width)],
+                source.at[q, i, pl.ds(start, width), :],
+                bt.at[
+                    pl.ds(i * width, width),
+                    pl.ds(pl.multiple_of((2 * home + q) * batch, 128), batch),
+                ],
                 bra_sem.at[slot, q, i],
             )
             for q in range(2)
@@ -148,32 +151,37 @@
     first_at = here_row * (2 * half) + me * half + row_at
     first = virt_ref[:, pl.ds(pl.multiple_of(first_at, 128), width)]
     first = jnp.broadcast_to(first, (width, width)).T[:, :1]
-    for d in range(4):
-        bt[:, d * 2 * batch : (d + 1) * 2 * batch] = bv[d].T
+
+    def amplitudes_of(n):
+        tile = tiles[n % 2]
+        columns = slice(n * part, (n + 1) * part)
+        second_at = pl.multiple_of(here_col * span + n * part, 128)
+        second = virt_ref[:, pl.ds(second_at, part)]
+        for i in range(2):
+            for j in range(i, 2):
+                inverse = 1.0 / (((occ_ref[i] + occ_ref[j]) - first) - second)
+                for one, two in ((i, j), (j, i))[: 1 + (i != j)]:
+                    direct = tile[two, one * width : (one + 1) * width, :]
+                    exchange = tile[one, two * width : (two + 1) * width, :]
+                    block = ((2.0 * direct - exchange) * inverse).astype(jnp.bfloat16)
+                    amps[one, two, :, columns] = block
+                    t2[
+                        one * width : (one + 1) * width,
+                        two * span + n * part : two * span + (n + 1) * part,
+                    ] = block
+
     for n in range(SLICES):
         for copy in copies[n]:
             copy.wait()
-        tile = [
-            jnp.dot(
+        if n:
+            amplitudes_of(n - 1)
+        for j in range(2):
+            tiles[n % 2][j] = jnp.dot(
                 bt[...],
                 kv[:, j * span + n * part : j * span + (n + 1) * part],
                 preferred_element_type=jnp.float32,
             )
-            for j in range(2)
-        ]
-        second_at = pl.multiple_of(here_col * span + n * part, 128)
-        second = virt_ref[:, pl.ds(second_at, part)]
-        for i in range(2):
-            for j in range(2):
-                direct = tile[j][i * width : (i + 1) * width, :]
-                exchange = tile[i][j * width : (j + 1) * width, :]
-                denominator = ((occ_ref[i] + occ_ref[j]) - first) - second
-                block = ((2.0 * direct - exchange) / denominator).astype(jnp.bfloat16)
-                amps[i, j, :, n * part : (n + 1) * part] = block
-                t2[
-                    i * width : (i + 1) * width,
-                    j * span + n * part : j * span + (n + 1) * part,
-                ] = block
+    amplitudes_of(SLICES - 1)
     at = pl.multiple_of(me * half + row_at, 16)
     outs = [
         pltpu.make_async_copy(amps, whole_ref.at[:, :, pl.ds(at, width), :], out_sem.at[0]),
@@ -215,7 +223,7 @@
 
 
 def run_group(group, ket, pieces, bras, energies, held):
-    _, _, batch, block_width = bras[0].shape
+    _, _, block_width, batch = bras[0].shape
     _, _, width = place_of(group, block_width)
     span = ket[0].shape[1] // 2
     half = block_width * BLOCKS
@@ -248,11 +256,12 @@
         out_specs=(any_space, any_space) + (in_vmem,) * (4 * count) + (() if group else (in_hbm,)),
         scratch_shapes=[
             pltpu.VMEM((total, 2 * span), jnp.bfloat16),
-            pltpu.VMEM((4, 2 * batch, 2 * width), jnp.bfloat16),
             pltpu.VMEM((2 * width, total), jnp.bfloat16),
             pltpu.VMEM((2 * width, 2 * span), jnp.bfloat16),
             pltpu.VMEM((2, 2, width, span), jnp.bfloat16),
             pltpu.VMEM(half_shape if group == 1 else (2, 2, 16, 128), jnp.bfloat16),
+            pltpu.VMEM((2, 2 * width, span // SLICES), jnp.float32),
+            pltpu.VMEM((2, 2 * width, span // SLICES), jnp.float32),
             pltpu.SemaphoreType.DMA((SLICES, 2 * len(pieces), 2)),
             pltpu.SemaphoreType.DMA((4, 2, 2)),
             pltpu.SemaphoreType.DMA((3,)),
@@ -268,19 +277,19 @@
 
 
 def pick_kernel(bra, kept_out, given_out):
-    width = kept_out.shape[3]
+    width = kept_out.shape[2]
     span = bra.shape[1] // 2
     me = lax.axis_index("occ")
     for side, out in ((1 - me, given_out), (me, kept_out)):
         for g in range(BLOCKS):
             for i in range(2):
                 home = i * span + side * (span // 2) + g * width
-                out[g, i] = bra[:, pl.ds(pl.multiple_of(home, 128), width)]
+                out[g, i] = bra[:, pl.ds(pl.multiple_of(home, 128), width)].T
 
 
 def pick(bra):
     batch, columns = bra.shape
-    part = jax.ShapeDtypeStruct((BLOCKS, 2, batch, columns // 4 // BLOCKS), bra.dtype)
+    part = jax.ShapeDtypeStruct((BLOCKS, 2, columns // 4 // BLOCKS, batch), bra.dtype)
     return pl.pallas_call(
         pick_kernel,
         out_shape=(part, part),

time: 239 us -> 238 us (level)
  no operation moved by 1% of the time
where the time goes in v4:
time: 238 us; the launch traced here: 237 us
  waiting for transfers between devices  88.3 us (37%)
  starting transfers between devices  86.6 us (36%)
  Pallas kernels  48 us (20%)
  other arithmetic  8.01 us (3%)
  local copies, waits for them, and re-layouts  5.04 us (2%)
    pallas_call x3, Pallas kernels, run_group(): pl.pallas_call(functools.partial(group_kernel, pieces, group), out_shape=...  44.6 us
    ppermute x5, starting transfers between devices, pairs(): return lax.ppermute(x, 'col', [(0, 1), (1, 0), (2, 3), (3, 2)])  39.6 us
    ppermute x5, waiting for transfers between devices, inward(): return lax.ppermute(x, 'col', [(0, 1), (3, 2)])  29 us
    ppermute x4, waiting for transfers between devices, planar(): return lax.ppermute(x, 'row', [(r, r ^ offset) for r in range(4)])  27.1 us
    ppermute x6, waiting for transfers between devices, hop_down(): return lax.ppermute(x, 'col', [(3 - c, 2 - c) for c in range(first, 3)])  25.1 us
    ppermute x5, starting transfers between devices, inward(): return lax.ppermute(x, 'col', [(0, 1), (3, 2)])  13 us
    ppermute x6, starting transfers between devices, hop_up(): return lax.ppermute(x, 'col', [(c, c + 1) for c in range(first, 3)])  12.4 us
    ppermute x6, starting transfers between devices, hop_down(): return lax.ppermute(x, 'col', [(3 - c, 2 - c) for c in range(first, 3)])  7.72 us
  transfers between devices with their start and end apart: 42, of which 17 were waited for; matrix products, arithmetic and copies ran while one was open for 4% of the time, Pallas kernels for 19%

profile of v4, /device:TPU:0, one launch (start us, length us, event | category | flops | bytes accessed | tf_op | source)
XLA Modules:
  0.0 237.5 jit_solution(6177060884430328061)
XLA Ops:
  0.6 1.8 copy.11
  2.5 0.5 shard_map.59
  3.0 0.5 collective-permute-start.2
  4.4 0.5 collective-permute-start.7
  4.9 2.6 %collective-permute-start.1 = (bf16[384,2048]{1,0:T(8,128)(2,1)S(1)}, bf16[384,2048]{1,0:T(8,128)(2,1)S(1)}, u32[]{:S(2)}, u32[]{:S(2)}) collective-permute-start(bf16[384,2048]{1,0:T(8,128)(2,1)S(1)} %bitcast.49), channel_id=1, source_target_pairs={{0,8},{4,12},{8,0},{12,4},{1,9},{5,13},{9,1},{13,5},{2,10},{6,14},... | collective-permute-start | bytes 4718600 | tf_op jit(solution)/shard_map/ppermute | solution.py:379
  7.7 1.3 collective-permute-start.5
  9.0 1.6 collective-permute-start
  10.5 4.6 %collective-permute-start.3 = (bf16[2,2,256,384]{3,2,1,0:T(8,128)(2,1)S(1)}, bf16[2,2,256,384]{3,2,1,0:T(8,128)(2,1)S(1)}, u32[]{:S(2)}, u32[]{:S(2)}) collective-permute-start(bf16[2,2,256,384]{3,2,1,0:T(8,128)(2,1)S(1)} %get-tuple-element.109.refs_10_), channel_id=1, source_target_pairs={{0,1},{1,2},{2,3},{4,5},{5,6},{6,7},{8,9},{9,10},{10,11},{12,13},{... | collective-permute-start | bytes 2359304 | tf_op jit(solution)/shard_map/ppermute | solution.py:383
  15.1 14.0 %collective-permute-done.5.refs_14_ = bf16[2,2,256,384]{3,2,1,0:T(8,128)(2,1)S(1)} collective-permute-done((bf16[2,2,256,384]{3,2,1,0:T(8,128)(2,1)S(1)}, bf16[2,2,256,384]{3,2,1,0:T(8,128)(2,1)S(1)}, u32[]{:S(2)}, u32[]{:S(2)}) %collective-permute-start.5) | collective-permute-done | bytes 786464 | tf_op jit(solution)/shard_map/ppermute | solution.py:387
  29.2 1.3 collective-permute-start.6
  30.5 1.2 collective-permute-done.3.refs_11_
  31.6 0.7 collective-permute-start.4
  32.4 10.1 %collective-permute-done.1.refs_2_ = bf16[384,2048]{1,0:T(8,128)(2,1)S(1)} collective-permute-done((bf16[384,2048]{1,0:T(8,128)(2,1)S(1)}, bf16[384,2048]{1,0:T(8,128)(2,1)S(1)}, u32[]{:S(2)}, u32[]{:S(2)}) %collective-permute-start.1) | collective-permute-done | bytes 1572896 | tf_op jit(solution)/shard_map/ppermute | solution.py:379
  42.5 3.1 %collective-permute-done.refs_1_ = bf16[384,2048]{1,0:T(8,128)(2,1)S(1)} collective-permute-done((bf16[384,2048]{1,0:T(8,128)(2,1)S(1)}, bf16[384,2048]{1,0:T(8,128)(2,1)S(1)}, u32[]{:S(2)}, u32[]{:S(2)}) %collective-permute-start) | collective-permute-done | bytes 1572896 | tf_op jit(solution)/shard_map/ppermute | solution.py:379
  45.5 4.3 %collective-permute-done.6.refs_15_ = bf16[2,2,256,384]{3,2,1,0:T(8,128)(2,1)S(1)} collective-permute-done((bf16[2,2,256,384]{3,2,1,0:T(8,128)(2,1)S(1)}, bf16[2,2,256,384]{3,2,1,0:T(8,128)(2,1)S(1)}, u32[]{:S(2)}, u32[]{:S(2)}) %collective-permute-start.6) | collective-permute-done | bytes 786464 | tf_op jit(solution)/shard_map/ppermute | solution.py:387
  50.0 0.8 collective-permute-start.10
  50.8 1.5 collective-permute-start.11
  52.3 0.7 collective-permute-start.8
  53.0 1.3 collective-permute-start.9
  54.4 13.5 %collective-permute-done.10.refs_3_ = bf16[192,2048]{1,0:T(8,128)(2,1)S(1)} collective-permute-done((bf16[192,2048]{1,0:T(8,128)(2,1)S(1)}, bf16[192,2048]{1,0:T(8,128)(2,1)S(1)}, u32[]{:S(2)}, u32[]{:S(2)}) %collective-permute-start.10) | collective-permute-done | bytes 786464 | tf_op jit(solution)/shard_map/ppermute | solution.py:379
  67.9 0.5 collective-permute-done.11.refs_4_
  68.4 4.0 %collective-permute-done.9.refs_16_ = bf16[2,2,256,384]{3,2,1,0:T(8,128)(2,1)S(1)} collective-permute-done((bf16[2,2,256,384]{3,2,1,0:T(8,128)(2,1)S(1)}, bf16[2,2,256,384]{3,2,1,0:T(8,128)(2,1)S(1)}, u32[]{:S(2)}, u32[]{:S(2)}) %collective-permute-start.9) | collective-permute-done | bytes 786464 | tf_op jit(solution)/shard_map/ppermute | solution.py:387
  72.4 0.5 collective-permute-start.15
  72.9 1.3 collective-permute-start.19
  74.2 0.5 collective-permute-done.14.refs_8_
  74.7 4.1 %collective-permute-start.18 = (bf16[2,2,256,384]{3,2,1,0:T(8,128)(2,1)S(1)}, bf16[2,2,256,384]{3,2,1,0:T(8,128)(2,1)S(1)}, u32[]{:S(2)}, u32[]{:S(2)}) collective-permute-start(bf16[2,2,256,384]{3,2,1,0:T(8,128)(2,1)S(1)} %get-tuple-element.78.refs_1_), channel_id=1, source_target_pairs={{0,1},{1,2},{2,3},{4,5},{5,6},{6,7},{8,9},{9,10},{10,11},{12,13},{... | collective-permute-start | bytes 2359304 | tf_op jit(solution)/shard_map/ppermute | solution.py:383
  78.9 1.2 copy-done.17
  80.0 0.5 copy-done.16
  80.6 20.7 %shard_map.60 = (bf16[2,2,1024,1024]{3,2,1,0:T(8,128)(2,1)}, bf16[2,2,256,1024]{3,2,1,0:T(8,128)(2,1)}, f32[384,512]{1,0:T(8,128)S(1)}, f32[384,512]{1,0:T(8,128...) custom-call(bf16[384,2048]{1,0:T(8,128)(2,1)} %bitcast.51, ...), custom_call_target="tpu_custom_call" | custom-call | flops 12884901888 | bytes 12582912 | tf_op jit(solution)/shard_map/pallas_call | solution.py:242
  101.4 2.8 %collective-permute-start.16 = (bf16[2,384,512]{2,1,0:T(8,128)(2,1)S(1)}, bf16[2,384,512]{2,1,0:T(8,128)(2,1)S(1)}, u32[]{:S(2)}, u32[]{:S(2)}) collective-permute-start(bf16[2,384,512]{2,1,0:T(8,128)(2,1)S(1)} %get-tuple-element.76), channel_id=1, source_target_pairs={{0,1},{3,2},{4,5},{7,6},{8,9},{11,10},{12,13},{15,14},{16,17},{19,... | collective-permute-start | bytes 2359304 | tf_op jit(solution)/shard_map/ppermute | solution.py:403
  104.3 0.7 collective-permute-start.20
  105.0 1.3 collective-permute-start.22
  106.3 6.0 %collective-permute-start.27 = (bf16[2,384,512]{2,1,0:T(8,128)(2,1)}, bf16[2,384,512]{2,1,0:T(8,128)(2,1)}, u32[]{:S(2)}, u32[]{:S(2)}) collective-permute-start(bf16[2,384,512]{2,1,0:T(8,128)(2,1)} %get-tuple-element.91), channel_id=1, source_target_pairs={{0,1},{3,2},{4,5},{7,6},{8,9},{11,10},{12,13},{15,14},{16,17},{19,... | collective-permute-start | bytes 2359304 | tf_op jit(solution)/shard_map/ppermute | solution.py:403
  112.3 9.7 %collective-permute-done.16 = bf16[2,384,512]{2,1,0:T(8,128)(2,1)S(1)} collective-permute-done((bf16[2,384,512]{2,1,0:T(8,128)(2,1)S(1)}, bf16[2,384,512]{2,1,0:T(8,128)(2,1)S(1)}, u32[]{:S(2)}, u32[]{:S(2)}) %collective-permute-start.16) | collective-permute-done | bytes 786464 | tf_op jit(solution)/shard_map/ppermute | solution.py:403
  122.1 2.6 %add_convert_fusion.2 = bf16[2,384,512]{2,1,0:T(8,128)(2,1)} fusion(f32[2,384,512]{2,1,0:T(8,128)} %get-tuple-element.75, bf16[2,384,512]{2,1,0:T(8,128)(2,1)S(1)} %collective-permute-done.16), kind=kLoop, calls=%fused_computation.4 | loop fusion | flops 1179648 | bytes 3145728 | tf_op jit(solution)/shard_map/convert_element_type | solution.py:448
  124.7 1.6 collective-permute-start.17
  126.3 1.6 collective-permute-start.21
  127.8 1.3 collective-permute-start.23
  129.1 8.8 %collective-permute-done.27 = bf16[2,384,512]{2,1,0:T(8,128)(2,1)} collective-permute-done((bf16[2,384,512]{2,1,0:T(8,128)(2,1)}, bf16[2,384,512]{2,1,0:T(8,128)(2,1)}, u32[]{:S(2)}, u32[]{:S(2)}) %collective-permute-start.27) | collective-permute-done | bytes 786464 | tf_op jit(solution)/shard_map/ppermute | solution.py:403
  137.9 1.9 add_convert_fusion.1
  139.8 0.9 collective-permute-start.28
  140.8 1.1 fusion.3
  141.9 6.8 %collective-permute-start.36 = (bf16[384,512]{1,0:T(8,128)(2,1)S(1)}, bf16[384,512]{1,0:T(8,128)(2,1)S(1)}, u32[]{:S(2)}, u32[]{:S(2)}) collective-permute-start(bf16[384,512]{1,0:T(8,128)(2,1)S(1)} %fusion.3), channel_id=1, source_target_pairs={{0,1},{1,0},{2,3},{3,2},{4,5},{5,4},{6,7},{7,6},{8,9},{9,8},{10,11... | collective-permute-start | bytes 1179656 | tf_op jit(solution)/shard_map/ppermute | solution.py:391
  148.7 2.7 %collective-permute-done.23.refs_7_ = bf16[2,2,256,384]{3,2,1,0:T(8,128)(2,1)} collective-permute-done((bf16[2,2,256,384]{3,2,1,0:T(8,128)(2,1)}, bf16[2,2,256,384]{3,2,1,0:T(8,128)(2,1)}, u32[]{:S(2)}, u32[]{:S(2)}) %collective-permute-start.23) | collective-permute-done | bytes 786464 | tf_op jit(solution)/shard_map/ppermute | solution.py:387
  151.5 11.6 %shard_map.61 = (bf16[2,2,1024,1024]{3,2,1,0:T(8,128)(2,1)}, bf16[2,2,256,1024]{3,2,1,0:T(8,128)(2,1)}, f32[768,256]{1,0:T(8,128)S(1)}, f32[768,256]{1,0:T(8,128...) custom-call(bf16[3072,2048]{1,0:T(8,128)(2,1)} %get-tuple-element.74.refs_0_, ...), custom_call_target="tpu_custom_call", output_to_operand_aliasing={{0}: (11, {})} | custom-call | flops 6442450944 | bytes 12582912 | tf_op jit(solution)/shard_map/pallas_call | solution.py:242
  163.1 1.4 collective-permute-start.30
  164.5 12.3 %shard_map.62 = (bf16[2,2,1024,1024]{3,2,1,0:T(8,128)(2,1)}, bf16[2,2,256,1024]{3,2,1,0:T(8,128)(2,1)}, f32[384,256]{1,0:T(8,128)S(1)}, f32[384,256]{1,0:T(8,128...) custom-call(bf16[3072,2048]{1,0:T(8,128)(2,1)} %get-tuple-element.74, ...), custom_call_target="tpu_custom_call", output_to_operand_aliasing={{1}: (10, {}), {0}: (11, {})} | custom-call | flops 6442450944 | bytes 12582912 | tf_op jit(solution)/shard_map/pallas_call | solution.py:242
  176.8 1.4 collective-permute-start.26
  178.3 1.2 fusion.4
  179.5 1.3 collective-permute-start.33
  180.9 0.6 collective-permute-start.25
  181.6 6.5 %collective-permute-done.26 = bf16[2,384,256]{2,1,0:T(8,128)(2,1)S(1)} collective-permute-done((bf16[2,384,256]{2,1,0:T(8,128)(2,1)S(1)}, bf16[2,384,256]{2,1,0:T(8,128)(2,1)S(1)}, u32[]{:S(2)}, u32[]{:S(2)}) %collective-permute-start.26) | collective-permute-done | bytes 393248 | tf_op jit(solution)/shard_map/ppermute | solution.py:403
  188.1 0.7 collective-permute-start.31
  188.9 0.7 collective-permute-start.39
  189.7 4.0 %collective-permute-done.33 = bf16[2,384,256]{2,1,0:T(8,128)(2,1)S(1)} collective-permute-done((bf16[2,384,256]{2,1,0:T(8,128)(2,1)S(1)}, bf16[2,384,256]{2,1,0:T(8,128)(2,1)S(1)}, u32[]{:S(2)}, u32[]{:S(2)}) %collective-permute-start.33) | collective-permute-done | bytes 393248 | tf_op jit(solution)/shard_map/ppermute | solution.py:403
  193.7 3.0 %collective-permute-start.29 = (bf16[384,512]{1,0:T(8,128)(2,1)S(1)}, bf16[384,512]{1,0:T(8,128)(2,1)S(1)}, u32[]{:S(2)}, u32[]{:S(2)}) collective-permute-start(bf16[384,512]{1,0:T(8,128)(2,1)S(1)} %fusion.7), channel_id=1, source_target_pairs={{0,1},{1,0},{2,3},{3,2},{4,5},{5,4},{6,7},{7,6},{8,9},{9,8},{10,11... | collective-permute-start | bytes 1179656 | tf_op jit(solution)/shard_map/ppermute | solution.py:391
  196.8 0.7 collective-permute-start.34
  197.6 22.1 %collective-permute-start.40 = (bf16[384,256]{1,0:T(8,128)(2,1)S(1)}, bf16[384,256]{1,0:T(8,128)(2,1)S(1)}, u32[]{:S(2)}, u32[]{:S(2)}) collective-permute-start(bf16[384,256]{1,0:T(8,128)(2,1)S(1)} %fusion.9), channel_id=1, source_target_pairs={{0,1},{1,0},{2,3},{3,2},{4,5},{5,4},{6,7},{7,6},{8,9},{9,8},{10,11... | collective-permute-start | bytes 589832 | tf_op jit(solution)/shard_map/ppermute | solution.py:391
  219.8 6.6 %collective-permute-start.32 = (bf16[768,256]{1,0:T(8,128)(2,1)S(1)}, bf16[768,256]{1,0:T(8,128)(2,1)S(1)}, u32[]{:S(2)}, u32[]{:S(2)}) collective-permute-start(bf16[768,256]{1,0:T(8,128)(2,1)S(1)} %fusion.5), channel_id=1, source_target_pairs={{0,1},{1,0},{2,3},{3,2},{4,5},{5,4},{6,7},{7,6},{8,9},{9,8},{10,11... | collective-permute-start | bytes 1179656 | tf_op jit(solution)/shard_map/ppermute | solution.py:391
  226.4 1.1 collective-permute-start.35
  227.6 4.5 %collective-permute-done.32 = bf16[768,256]{1,0:T(8,128)(2,1)S(1)} collective-permute-done((bf16[768,256]{1,0:T(8,128)(2,1)S(1)}, bf16[768,256]{1,0:T(8,128)(2,1)S(1)}, u32[]{:S(2)}, u32[]{:S(2)}) %collective-permute-start.32) | collective-permute-done | bytes 393248 | tf_op jit(solution)/shard_map/ppermute | solution.py:391
  232.3 0.6 collective-permute-start.38
  233.4 0.8 collective-permute-done.35
  234.4 2.9 %shard_map.63 = (bf16[2,2,1024,1024]{3,2,1,0:T(8,128)(2,1)}, f32[384,2,1024]{2,1,0:T(2,128)}) custom-call(bf16[2,2,256,1024]{3,2,1,0:T(8,128)(2,1)S(1)} %collective-permute-done.25.refs_0_, bf16[2,2,1024,1024]{3,2,1,0:T(8,128)(2,1)} %get-tuple-element.87.refs_1_, f32[384,512]{1,0:T(8,128)S(1)} %fusion.8.refs_2_, ...), custom_call_target="tpu_custom_call", output_to_operand_aliasing={{0}: (1, {})} | custom-call | bytes 10485760 | tf_op jit(solution)/shard_map/pallas_call | solution.py:352
  (90 shorter events, 3.1 us)
Async XLA Ops:
  2.5 1.4 copy-start.11
  3.0 4.5 %collective-permute-start.2 = (bf16[2,2,256,384]{3,2,1,0:T(8,128)(2,1)S(1)}, bf16[2,2,256,384]{3,2,1,0:T(8,128)(2,1)S(1)}, u32[]{:S(2)}, u32[]{:S(2)}) collective-permute-start(bf16[2,2,256,384]{3,2,1,0:T(8,128)(2,1)S(1)} %get-tuple-element.56), channel_id=1, source_target_pairs={{0,16},{16,0},{1,17},{17,1},{2,18},{18,2},{3,19},{19,3},{4,20},{20... | collective-permute-start | bytes 2359304 | tf_op jit(solution)/shard_map/ppermute | solution.py:375
  4.3 4.6 %copy-start.12 = (bf16[48,8,2,1024]{3,1,2,0:T(8,128)(2,1)}, bf16[48,8,2,1024]{3,1,2,0:T(8,128)(2,1)S(1)}, u32[]{:S(2)}) copy-start(bf16[48,8,2,1024]{3,1,2,0:T(8,128)(2,1)S(1)} %copy.10) | copy-start | bytes 4718596
  4.4 28.0 %collective-permute-start.7 = (bf16[384,2048]{1,0:T(8,128)(2,1)S(1)}, bf16[384,2048]{1,0:T(8,128)(2,1)S(1)}, u32[]{:S(2)}, u32[]{:S(2)}) collective-permute-start(bf16[384,2048]{1,0:T(8,128)(2,1)S(1)} %bitcast.48), channel_id=1, source_target_pairs={{0,16},{16,0},{1,17},{17,1},{2,18},{18,2},{3,19},{19,3},{4,20},{20... | collective-permute-start | bytes 4718600 | tf_op jit(solution)/shard_map/ppermute | solution.py:375
  4.9 37.6 %collective-permute-start.1 = (bf16[384,2048]{1,0:T(8,128)(2,1)S(1)}, bf16[384,2048]{1,0:T(8,128)(2,1)S(1)}, u32[]{:S(2)}, u32[]{:S(2)}) collective-permute-start(bf16[384,2048]{1,0:T(8,128)(2,1)S(1)} %bitcast.49), channel_id=1, source_target_pairs={{0,8},{4,12},{8,0},{12,4},{1,9},{5,13},{9,1},{13,5},{2,10},{6,14},... | collective-permute-start | bytes 4718600 | tf_op jit(solution)/shard_map/ppermute | solution.py:379
  7.7 72.9 %copy-start.8 = (f32[4096]{0:T(1024)S(1)}, f32[4096]{0:T(1024)}, u32[]{:S(2)}) copy-start(f32[4096]{0:T(1024)} %param.7) | copy-start | bytes 49156
  7.7 72.9 %copy-start.9 = (f32[2]{0:T(128)S(1)}, f32[2]{0:T(128)}, u32[]{:S(2)}) copy-start(f32[2]{0:T(128)} %refs_8_.3) | copy-start | bytes 28
  7.7 21.5 %collective-permute-start.5 = (bf16[2,2,256,384]{3,2,1,0:T(8,128)(2,1)S(1)}, bf16[2,2,256,384]{3,2,1,0:T(8,128)(2,1)S(1)}, u32[]{:S(2)}, u32[]{:S(2)}) collective-permute-start(bf16[2,2,256,384]{3,2,1,0:T(8,128)(2,1)S(1)} %get-tuple-element.109.refs_10_), channel_id=1, source_target_pairs={{3,2},{2,1},{1,0},{7,6},{6,5},{5,4},{11,10},{10,9},{9,8},{15,14},{... | collective-permute-start | bytes 2359304 | tf_op jit(solution)/shard_map/ppermute | solution.py:387
  9.0 36.5 %collective-permute-start = (bf16[384,2048]{1,0:T(8,128)(2,1)S(1)}, bf16[384,2048]{1,0:T(8,128)(2,1)S(1)}, u32[]{:S(2)}, u32[]{:S(2)}) collective-permute-start(bf16[384,2048]{1,0:T(8,128)(2,1)S(1)} %bitcast.50), channel_id=1, source_target_pairs={{0,4},{4,0},{8,12},{12,8},{1,5},{5,1},{9,13},{13,9},{2,6},{6,2},{1... | collective-permute-start | bytes 4718600 | tf_op jit(solution)/shard_map/ppermute | solution.py:379
  10.5 21.1 %collective-permute-start.3 = (bf16[2,2,256,384]{3,2,1,0:T(8,128)(2,1)S(1)}, bf16[2,2,256,384]{3,2,1,0:T(8,128)(2,1)S(1)}, u32[]{:S(2)}, u32[]{:S(2)}) collective-permute-start(bf16[2,2,256,384]{3,2,1,0:T(8,128)(2,1)S(1)} %get-tuple-element.109.refs_10_), channel_id=1, source_target_pairs={{0,1},{1,2},{2,3},{4,5},{5,6},{6,7},{8,9},{9,10},{10,11},{12,13},{... | collective-permute-start | bytes 2359304 | tf_op jit(solution)/shard_map/ppermute | solution.py:383
  29.2 50.9 %copy-start.18 = (bf16[2,2,256,384]{3,2,1,0:T(8,128)(2,1)}, bf16[2,2,256,384]{3,2,1,0:T(8,128)(2,1)S(1)}, u32[]{:S(2)}) copy-start(bf16[2,2,256,384]{3,2,1,0:T(8,128)(2,1)S(1)} %collective-permute-done.5.refs_14_) | copy-start | bytes 2359300
  29.2 20.7 %collective-permute-start.6 = (bf16[2,2,256,384]{3,2,1,0:T(8,128)(2,1)S(1)}, bf16[2,2,256,384]{3,2,1,0:T(8,128)(2,1)S(1)}, u32[]{:S(2)}, u32[]{:S(2)}) collective-permute-start(bf16[2,2,256,384]{3,2,1,0:T(8,128)(2,1)S(1)} %collective-permute-done.5.refs_14_), channel_id=1, source_target_pairs={{2,1},{1,0},{6,5},{5,4},{10,9},{9,8},{14,13},{13,12},{18,17},{17,1... | collective-permute-start | bytes 2359304 | tf_op jit(solution)/shard_map/ppermute | solution.py:387
  31.6 18.2 %collective-permute-start.4 = (bf16[2,2,256,384]{3,2,1,0:T(8,128)(2,1)S(1)}, bf16[2,2,256,384]{3,2,1,0:T(8,128)(2,1)S(1)}, u32[]{:S(2)}, u32[]{:S(2)}) collective-permute-start(bf16[2,2,256,384]{3,2,1,0:T(8,128)(2,1)S(1)} %collective-permute-done.3.refs_11_), channel_id=1, source_target_pairs={{1,2},{2,3},{5,6},{6,7},{9,10},{10,11},{13,14},{14,15},{17,18},{18... | collective-permute-start | bytes 2359304 | tf_op jit(solution)/shard_map/ppermute | solution.py:383
  32.4 47.7 %copy-start.15 = (bf16[384,2048]{1,0:T(8,128)(2,1)}, bf16[384,2048]{1,0:T(8,128)(2,1)S(1)}, u32[]{:S(2)}) copy-start(bf16[384,2048]{1,0:T(8,128)(2,1)S(1)} %collective-permute-done.7.refs_5_) | copy-start | bytes 4718596
  42.5 25.5 %copy-start.13 = (bf16[384,2048]{1,0:T(8,128)(2,1)}, bf16[384,2048]{1,0:T(8,128)(2,1)S(1)}, u32[]{:S(2)}) copy-start(bf16[384,2048]{1,0:T(8,128)(2,1)S(1)} %collective-permute-done.1.refs_2_) | copy-start | bytes 4718596
  45.5 8.8 %copy-start.14 = (bf16[384,2048]{1,0:T(8,128)(2,1)}, bf16[384,2048]{1,0:T(8,128)(2,1)S(1)}, u32[]{:S(2)}) copy-start(bf16[384,2048]{1,0:T(8,128)(2,1)S(1)} %collective-permute-done.refs_1_) | copy-start | bytes 4718596
  49.8 30.2 %copy-start.19 = (bf16[2,2,256,384]{3,2,1,0:T(8,128)(2,1)}, bf16[2,2,256,384]{3,2,1,0:T(8,128)(2,1)S(1)}, u32[]{:S(2)}) copy-start(bf16[2,2,256,384]{3,2,1,0:T(8,128)(2,1)S(1)} %collective-permute-done.6.refs_15_) | copy-start | bytes 2359300
  50.0 17.9 %collective-permute-start.10 = (bf16[192,2048]{1,0:T(8,128)(2,1)S(1)}, bf16[192,2048]{1,0:T(8,128)(2,1)S(1)}, u32[]{:S(2)}, u32[]{:S(2)}) collective-permute-start(bf16[192,2048]{1,0:T(8,128)(2,1)S(1)} %slice.22), channel_id=1, source_target_pairs={{0,8},{4,12},{8,0},{12,4},{1,9},{5,13},{9,1},{13,5},{2,10},{6,14},... | collective-permute-start | bytes 2359304 | tf_op jit(solution)/shard_map/ppermute | solution.py:379
  50.8 17.6 %collective-permute-start.11 = (bf16[192,2048]{1,0:T(8,128)(2,1)S(1)}, bf16[192,2048]{1,0:T(8,128)(2,1)S(1)}, u32[]{:S(2)}, u32[]{:S(2)}) collective-permute-start(bf16[192,2048]{1,0:T(8,128)(2,1)S(1)} %slice.23), channel_id=1, source_target_pairs={{0,4},{4,0},{8,12},{12,8},{1,5},{5,1},{9,13},{13,9},{2,6},{6,2},{1... | collective-permute-start | bytes 2359304 | tf_op jit(solution)/shard_map/ppermute | solution.py:379
  52.3 16.1 %collective-permute-start.8 = (bf16[2,2,256,384]{3,2,1,0:T(8,128)(2,1)S(1)}, bf16[2,2,256,384]{3,2,1,0:T(8,128)(2,1)S(1)}, u32[]{:S(2)}, u32[]{:S(2)}) collective-permute-start(bf16[2,2,256,384]{3,2,1,0:T(8,128)(2,1)S(1)} %collective-permute-done.4.refs_12_), channel_id=1, source_target_pairs={{2,3},{6,7},{10,11},{14,15},{18,19},{22,23},{26,27},{30,31}} | collective-permute-start | bytes 2359304 | tf_op jit(solution)/shard_map/ppermute | solution.py:383
  53.0 19.3 %collective-permute-start.9 = (bf16[2,2,256,384]{3,2,1,0:T(8,128)(2,1)S(1)}, bf16[2,2,256,384]{3,2,1,0:T(8,128)(2,1)S(1)}, u32[]{:S(2)}, u32[]{:S(2)}) collective-permute-start(bf16[2,2,256,384]{3,2,1,0:T(8,128)(2,1)S(1)} %collective-permute-done.6.refs_15_), channel_id=1, source_target_pairs={{1,0},{5,4},{9,8},{13,12},{17,16},{21,20},{25,24},{29,28}} | collective-permute-start | bytes 2359304 | tf_op jit(solution)/shard_map/ppermute | solution.py:387
  54.3 24.5 %collective-permute-start.12 = (bf16[384,2048]{1,0:T(8,128)(2,1)S(1)}, bf16[384,2048]{1,0:T(8,128)(2,1)S(1)}, u32[]{:S(2)}, u32[]{:S(2)}) collective-permute-start(bf16[384,2048]{1,0:T(8,128)(2,1)S(1)} %collective-permute-done.refs_1_), channel_id=1, source_target_pairs={{0,16},{16,0},{1,17},{17,1},{2,18},{18,2},{3,19},{19,3},{4,20},{20... | collective-permute-start | bytes 4718600 | tf_op jit(solution)/shard_map/ppermute | solution.py:375
  67.9 10.9 %collective-permute-start.13 = (bf16[384,2048]{1,0:T(8,128)(2,1)S(1)}, bf16[384,2048]{1,0:T(8,128)(2,1)S(1)}, u32[]{:S(2)}, u32[]{:S(2)}) collective-permute-start(bf16[384,2048]{1,0:T(8,128)(2,1)S(1)} %collective-permute-done.1.refs_2_), channel_id=1, source_target_pairs={{0,16},{16,0},{1,17},{17,1},{2,18},{18,2},{3,19},{19,3},{4,20},{20... | collective-permute-start | bytes 4718600 | tf_op jit(solution)/shard_map/ppermute | solution.py:375
  68.4 4.5 %copy-start.20 = (bf16[2,2,256,384]{3,2,1,0:T(8,128)(2,1)}, bf16[2,2,256,384]{3,2,1,0:T(8,128)(2,1)S(1)}, u32[]{:S(2)}) copy-start(bf16[2,2,256,384]{3,2,1,0:T(8,128)(2,1)S(1)} %collective-permute-done.8.refs_13_) | copy-start | bytes 2359300
  72.4 1.8 copy-start.21
  72.4 2.3 collective-permute-start.14
  72.4 6.4 %collective-permute-start.15 = (bf16[192,2048]{1,0:T(8,128)(2,1)S(1)}, bf16[192,2048]{1,0:T(8,128)(2,1)S(1)}, u32[]{:S(2)}, u32[]{:S(2)}) collective-permute-start(bf16[192,2048]{1,0:T(8,128)(2,1)S(1)} %collective-permute-done.11.refs_4_), channel_id=1, source_target_pairs={{0,16},{16,0},{1,17},{17,1},{2,18},{18,2},{3,19},{19,3},{4,20},{20... | collective-permute-start | bytes 2359304 | tf_op jit(solution)/shard_map/ppermute | solution.py:375
  72.9 31.4 %collective-permute-start.19 = (bf16[2,2,256,384]{3,2,1,0:T(8,128)(2,1)S(1)}, bf16[2,2,256,384]{3,2,1,0:T(8,128)(2,1)S(1)}, u32[]{:S(2)}, u32[]{:S(2)}) collective-permute-start(bf16[2,2,256,384]{3,2,1,0:T(8,128)(2,1)S(1)} %get-tuple-element.78.refs_1_), channel_id=1, source_target_pairs={{3,2},{2,1},{1,0},{7,6},{6,5},{5,4},{11,10},{10,9},{9,8},{15,14},{... | collective-permute-start | bytes 2359304 | tf_op jit(solution)/shard_map/ppermute | solution.py:387
  74.7 29.6 %collective-permute-start.18 = (bf16[2,2,256,384]{3,2,1,0:T(8,128)(2,1)S(1)}, bf16[2,2,256,384]{3,2,1,0:T(8,128)(2,1)S(1)}, u32[]{:S(2)}, u32[]{:S(2)}) collective-permute-start(bf16[2,2,256,384]{3,2,1,0:T(8,128)(2,1)S(1)} %get-tuple-element.78.refs_1_), channel_id=1, source_target_pairs={{0,1},{1,2},{2,3},{4,5},{5,6},{6,7},{8,9},{9,10},{10,11},{12,13},{... | collective-permute-start | bytes 2359304 | tf_op jit(solution)/shard_map/ppermute | solution.py:383
  78.8 1.7 copy-start.16
  78.8 1.2 copy-start.17
  101.3 23.3 %copy-start = (f32[384,512]{1,0:T(8,128)}, f32[384,512]{1,0:T(8,128)S(1)}, u32[]{:S(2)}) copy-start(f32[384,512]{1,0:T(8,128)S(1)} %get-tuple-element.88) | copy-start | bytes 2359300
  101.3 23.3 %copy-start.2 = (f32[384,512]{1,0:T(8,128)}, f32[384,512]{1,0:T(8,128)S(1)}, u32[]{:S(2)}) copy-start(f32[384,512]{1,0:T(8,128)S(1)} %get-tuple-element.102) | copy-start | bytes 2359300
  101.3 23.3 %copy-start.4 = (f32[384,512]{1,0:T(8,128)}, f32[384,512]{1,0:T(8,128)S(1)}, u32[]{:S(2)}) copy-start(f32[384,512]{1,0:T(8,128)S(1)} %get-tuple-element.93) | copy-start | bytes 2359300
  101.3 23.3 %copy-start.6 = (f32[384,512]{1,0:T(8,128)}, f32[384,512]{1,0:T(8,128)S(1)}, u32[]{:S(2)}) copy-start(f32[384,512]{1,0:T(8,128)S(1)} %get-tuple-element.104) | copy-start | bytes 2359300
  101.4 20.7 %collective-permute-start.16 = (bf16[2,384,512]{2,1,0:T(8,128)(2,1)S(1)}, bf16[2,384,512]{2,1,0:T(8,128)(2,1)S(1)}, u32[]{:S(2)}, u32[]{:S(2)}) collective-permute-start(bf16[2,384,512]{2,1,0:T(8,128)(2,1)S(1)} %get-tuple-element.76), channel_id=1, source_target_pairs={{0,1},{3,2},{4,5},{7,6},{8,9},{11,10},{12,13},{15,14},{16,17},{19,... | collective-permute-start | bytes 2359304 | tf_op jit(solution)/shard_map/ppermute | solution.py:403
  104.2 47.3 %collective-permute-start.24 = (bf16[2,2,256,1024]{3,2,1,0:T(8,128)(2,1)}, bf16[2,2,256,1024]{3,2,1,0:T(8,128)(2,1)}, u32[]{:S(2)}, u32[]{:S(2)}) collective-permute-start(bf16[2,2,256,1024]{3,2,1,0:T(8,128)(2,1)} %get-tuple-element.82), channel_id=1, source_target_pairs={{0,16},{16,0},{1,17},{17,1},{2,18},{18,2},{3,19},{19,3},{4,20},{20... | collective-permute-start | bytes 6291464 | tf_op jit(solution)/shard_map/ppermute | solution.py:375
  104.3 22.0 %collective-permute-start.20 = (bf16[2,2,256,384]{3,2,1,0:T(8,128)(2,1)S(1)}, bf16[2,2,256,384]{3,2,1,0:T(8,128)(2,1)S(1)}, u32[]{:S(2)}, u32[]{:S(2)}) collective-permute-start(bf16[2,2,256,384]{3,2,1,0:T(8,128)(2,1)S(1)} %collective-permute-done.18.refs_2_), channel_id=1, source_target_pairs={{1,2},{2,3},{5,6},{6,7},{9,10},{10,11},{13,14},{14,15},{17,18},{18... | collective-permute-start | bytes 2359304 | tf_op jit(solution)/shard_map/ppermute | solution.py:383
  105.0 22.8 %collective-permute-start.22 = (bf16[2,2,256,384]{3,2,1,0:T(8,128)(2,1)S(1)}, bf16[2,2,256,384]{3,2,1,0:T(8,128)(2,1)}, u32[]{:S(2)}, u32[]{:S(2)}) collective-permute-start(bf16[2,2,256,384]{3,2,1,0:T(8,128)(2,1)S(1)} %collective-permute-done.19.refs_5_), channel_id=1, source_target_pairs={{2,1},{1,0},{6,5},{5,4},{10,9},{9,8},{14,13},{13,12},{18,17},{17,1... | collective-permute-start | bytes 2359304 | tf_op jit(solution)/shard_map/ppermute | solution.py:387
  106.3 31.6 %collective-permute-start.27 = (bf16[2,384,512]{2,1,0:T(8,128)(2,1)}, bf16[2,384,512]{2,1,0:T(8,128)(2,1)}, u32[]{:S(2)}, u32[]{:S(2)}) collective-permute-start(bf16[2,384,512]{2,1,0:T(8,128)(2,1)} %get-tuple-element.91), channel_id=1, source_target_pairs={{0,1},{3,2},{4,5},{7,6},{8,9},{11,10},{12,13},{15,14},{16,17},{19,... | collective-permute-start | bytes 2359304 | tf_op jit(solution)/shard_map/ppermute | solution.py:403
  124.7 16.1 %collective-permute-start.17 = (bf16[2,384,512]{2,1,0:T(8,128)(2,1)}, bf16[2,384,512]{2,1,0:T(8,128)(2,1)}, u32[]{:S(2)}, u32[]{:S(2)}) collective-permute-start(bf16[2,384,512]{2,1,0:T(8,128)(2,1)} %add_convert_fusion.2), channel_id=1, source_target_pairs={{1,2},{2,1},{5,6},{6,5},{9,10},{10,9},{13,14},{14,13},{17,18},{18,... | collective-permute-start | bytes 2359304 | tf_op jit(solution)/shard_map/ppermute | solution.py:395
  126.3 22.5 %collective-permute-start.21 = (bf16[2,2,256,384]{3,2,1,0:T(8,128)(2,1)S(1)}, bf16[2,2,256,384]{3,2,1,0:T(8,128)(2,1)}, u32[]{:S(2)}, u32[]{:S(2)}) collective-permute-start(bf16[2,2,256,384]{3,2,1,0:T(8,128)(2,1)S(1)} %collective-permute-done.20.refs_3_), channel_id=1, source_target_pairs={{2,3},{6,7},{10,11},{14,15},{18,19},{22,23},{26,27},{30,31}} | collective-permute-start | bytes 2359304 | tf_op jit(solution)/shard_map/ppermute | solution.py:383
  127.8 23.6 %collective-permute-start.23 = (bf16[2,2,256,384]{3,2,1,0:T(8,128)(2,1)}, bf16[2,2,256,384]{3,2,1,0:T(8,128)(2,1)}, u32[]{:S(2)}, u32[]{:S(2)}) collective-permute-start(bf16[2,2,256,384]{3,2,1,0:T(8,128)(2,1)} %collective-permute-done.22.refs_6_), channel_id=1, source_target_pairs={{1,0},{5,4},{9,8},{13,12},{17,16},{21,20},{25,24},{29,28}} | collective-permute-start | bytes 2359304 | tf_op jit(solution)/shard_map/ppermute | solution.py:387
  137.9 2.9 %copy-start.7 = (f32[384,512]{1,0:T(8,128)S(1)}, f32[384,512]{1,0:T(8,128)}, u32[]{:S(2)}) copy-start(f32[384,512]{1,0:T(8,128)} %copy-done.6) | copy-start | bytes 2359300
  139.8 49.0 %collective-permute-start.28 = (bf16[2,384,512]{2,1,0:T(8,128)(2,1)S(1)}, bf16[2,384,512]{2,1,0:T(8,128)(2,1)S(1)}, u32[]{:S(2)}, u32[]{:S(2)}) collective-permute-start(bf16[2,384,512]{2,1,0:T(8,128)(2,1)S(1)} %add_convert_fusion.1), channel_id=1, source_target_pairs={{1,2},{2,1},{5,6},{6,5},{9,10},{10,9},{13,14},{14,13},{17,18},{18,... | collective-permute-start | bytes 2359304 | tf_op jit(solution)/shard_map/ppermute | solution.py:395
  141.9 36.3 %collective-permute-start.36 = (bf16[384,512]{1,0:T(8,128)(2,1)S(1)}, bf16[384,512]{1,0:T(8,128)(2,1)S(1)}, u32[]{:S(2)}, u32[]{:S(2)}) collective-permute-start(bf16[384,512]{1,0:T(8,128)(2,1)S(1)} %fusion.3), channel_id=1, source_target_pairs={{0,1},{1,0},{2,3},{3,2},{4,5},{5,4},{6,7},{7,6},{8,9},{9,8},{10,11... | collective-permute-start | bytes 1179656 | tf_op jit(solution)/shard_map/ppermute | solution.py:391
  163.1 17.8 %collective-permute-start.30 = (bf16[2,768,256]{2,1,0:T(8,128)(2,1)S(1)}, bf16[2,768,256]{2,1,0:T(8,128)(2,1)S(1)}, u32[]{:S(2)}, u32[]{:S(2)}) collective-permute-start(bf16[2,768,256]{2,1,0:T(8,128)(2,1)S(1)} %get-tuple-element.96), channel_id=1, source_target_pairs={{0,1},{3,2},{4,5},{7,6},{8,9},{11,10},{12,13},{15,14},{16,17},{19,... | collective-permute-start | bytes 2359304 | tf_op jit(solution)/shard_map/ppermute | solution.py:403
  164.5 13.8 %copy-start.3 = (f32[384,512]{1,0:T(8,128)S(1)}, f32[384,512]{1,0:T(8,128)}, u32[]{:S(2)}) copy-start(f32[384,512]{1,0:T(8,128)} %copy-done.2) | copy-start | bytes 2359300
  176.8 4.1 %copy-start.10 = (bf16[2,2,256,1024]{3,2,1,0:T(8,128)(2,1)S(1)}, bf16[2,2,256,1024]{3,2,1,0:T(8,128)(2,1)}, u32[]{:S(2)}) copy-start(bf16[2,2,256,1024]{3,2,1,0:T(8,128)(2,1)} %get-tuple-element.86) | copy-start | bytes 6291460
  176.8 11.3 %collective-permute-start.26 = (bf16[2,384,256]{2,1,0:T(8,128)(2,1)S(1)}, bf16[2,384,256]{2,1,0:T(8,128)(2,1)S(1)}, u32[]{:S(2)}, u32[]{:S(2)}) collective-permute-start(bf16[2,384,256]{2,1,0:T(8,128)(2,1)S(1)} %get-tuple-element.89), channel_id=1, source_target_pairs={{0,1},{3,2},{4,5},{7,6},{8,9},{11,10},{12,13},{15,14},{16,17},{19,... | collective-permute-start | bytes 1179656 | tf_op jit(solution)/shard_map/ppermute | solution.py:403
  179.5 54.8 %collective-permute-start.37 = (f32[384,512]{1,0:T(8,128)S(1)}, f32[384,512]{1,0:T(8,128)S(1)}, u32[]{:S(2)}, u32[]{:S(2)}) collective-permute-start(f32[384,512]{1,0:T(8,128)S(1)} %fusion.4), channel_id=1, source_target_pairs={{0,16},{16,0},{1,17},{17,1},{2,18},{18,2},{3,19},{19,3},{4,20},{20... | collective-permute-start | bytes 2359304 | tf_op jit(solution)/shard_map/ppermute | solution.py:375
  179.5 14.2 %collective-permute-start.33 = (bf16[2,384,256]{2,1,0:T(8,128)(2,1)S(1)}, bf16[2,384,256]{2,1,0:T(8,128)(2,1)S(1)}, u32[]{:S(2)}, u32[]{:S(2)}) collective-permute-start(bf16[2,384,256]{2,1,0:T(8,128)(2,1)S(1)} %get-tuple-element.100), channel_id=1, source_target_pairs={{0,1},{3,2},{4,5},{7,6},{8,9},{11,10},{12,13},{15,14},{16,17},{19,... | collective-permute-start | bytes 1179656 | tf_op jit(solution)/shard_map/ppermute | solution.py:403
  180.9 53.4 %collective-permute-start.25 = (bf16[2,2,256,1024]{3,2,1,0:T(8,128)(2,1)S(1)}, bf16[2,2,256,1024]{3,2,1,0:T(8,128)(2,1)S(1)}, u32[]{:S(2)}, u32[]{:S(2)}) collective-permute-start(bf16[2,2,256,1024]{3,2,1,0:T(8,128)(2,1)S(1)} %copy-done.10), channel_id=1, source_target_pairs={{0,16},{16,0},{1,17},{17,1},{2,18},{18,2},{3,19},{19,3},{4,20},{20... | collective-permute-start | bytes 6291464 | tf_op jit(solution)/shard_map/ppermute | solution.py:375
  181.6 8.0 %copy-start.5 = (f32[384,512]{1,0:T(8,128)S(1)}, f32[384,512]{1,0:T(8,128)}, u32[]{:S(2)}) copy-start(f32[384,512]{1,0:T(8,128)} %copy-done.4) | copy-start | bytes 2359300
  188.1 9.5 %collective-permute-start.31 = (bf16[2,768,256]{2,1,0:T(8,128)(2,1)S(1)}, bf16[2,768,256]{2,1,0:T(8,128)(2,1)S(1)}, u32[]{:S(2)}, u32[]{:S(2)}) collective-permute-start(bf16[2,768,256]{2,1,0:T(8,128)(2,1)S(1)} %add_convert_fusion), channel_id=1, source_target_pairs={{1,2},{2,1},{5,6},{6,5},{9,10},{10,9},{13,14},{14,13},{17,18},{18,... | collective-permute-start | bytes 2359304 | tf_op jit(solution)/shard_map/ppermute | solution.py:395
  188.9 7.9 %collective-permute-start.39 = (bf16[2,384,256]{2,1,0:T(8,128)(2,1)S(1)}, bf16[2,384,256]{2,1,0:T(8,128)(2,1)S(1)}, u32[]{:S(2)}, u32[]{:S(2)}) collective-permute-start(bf16[2,384,256]{2,1,0:T(8,128)(2,1)S(1)} %add_convert_fusion.3), channel_id=1, source_target_pairs={{1,2},{2,1},{5,6},{6,5},{9,10},{10,9},{13,14},{14,13},{17,18},{18,... | collective-permute-start | bytes 1179656 | tf_op jit(solution)/shard_map/ppermute | solution.py:395
  193.7 38.6 %collective-permute-start.29 = (bf16[384,512]{1,0:T(8,128)(2,1)S(1)}, bf16[384,512]{1,0:T(8,128)(2,1)S(1)}, u32[]{:S(2)}, u32[]{:S(2)}) collective-permute-start(bf16[384,512]{1,0:T(8,128)(2,1)S(1)} %fusion.7), channel_id=1, source_target_pairs={{0,1},{1,0},{2,3},{3,2},{4,5},{5,4},{6,7},{7,6},{8,9},{9,8},{10,11... | collective-permute-start | bytes 1179656 | tf_op jit(solution)/shard_map/ppermute | solution.py:391
  196.8 23.0 %collective-permute-start.34 = (bf16[2,384,256]{2,1,0:T(8,128)(2,1)S(1)}, bf16[2,384,256]{2,1,0:T(8,128)(2,1)S(1)}, u32[]{:S(2)}, u32[]{:S(2)}) collective-permute-start(bf16[2,384,256]{2,1,0:T(8,128)(2,1)S(1)} %add_convert_fusion.4), channel_id=1, source_target_pairs={{1,2},{2,1},{5,6},{6,5},{9,10},{10,9},{13,14},{14,13},{17,18},{18,... | collective-permute-start | bytes 1179656 | tf_op jit(solution)/shard_map/ppermute | solution.py:395
  197.6 28.8 %collective-permute-start.40 = (bf16[384,256]{1,0:T(8,128)(2,1)S(1)}, bf16[384,256]{1,0:T(8,128)(2,1)S(1)}, u32[]{:S(2)}, u32[]{:S(2)}) collective-permute-start(bf16[384,256]{1,0:T(8,128)(2,1)S(1)} %fusion.9), channel_id=1, source_target_pairs={{0,1},{1,0},{2,3},{3,2},{4,5},{5,4},{6,7},{7,6},{8,9},{9,8},{10,11... | collective-permute-start | bytes 589832 | tf_op jit(solution)/shard_map/ppermute | solution.py:391
  219.8 12.3 %collective-permute-start.32 = (bf16[768,256]{1,0:T(8,128)(2,1)S(1)}, bf16[768,256]{1,0:T(8,128)(2,1)S(1)}, u32[]{:S(2)}, u32[]{:S(2)}) collective-permute-start(bf16[768,256]{1,0:T(8,128)(2,1)S(1)} %fusion.5), channel_id=1, source_target_pairs={{0,1},{1,0},{2,3},{3,2},{4,5},{5,4},{6,7},{7,6},{8,9},{9,8},{10,11... | collective-permute-start | bytes 1179656 | tf_op jit(solution)/shard_map/ppermute | solution.py:391
  226.4 7.8 %collective-permute-start.35 = (bf16[384,256]{1,0:T(8,128)(2,1)S(1)}, bf16[384,256]{1,0:T(8,128)(2,1)S(1)}, u32[]{:S(2)}, u32[]{:S(2)}) collective-permute-start(bf16[384,256]{1,0:T(8,128)(2,1)S(1)} %fusion.11), channel_id=1, source_target_pairs={{0,1},{1,0},{2,3},{3,2},{4,5},{5,4},{6,7},{7,6},{8,9},{9,8},{10,11... | collective-permute-start | bytes 589832 | tf_op jit(solution)/shard_map/ppermute | solution.py:391
  232.1 2.2 collective-permute-start.41
  232.1 1.1 copy-start.1
  232.3 2.1 collective-permute-start.38

commit v5 on v4

--- a/solution.py
+++ b/solution.py
@@ -485,13 +485,15 @@
         2, [ket_all], pieces, arrived, energies, (mine, whole)
     )
     one2 = [inward(send) for send in send2]
-    other = swap(mine)
     two0.append(cross(far0[1], one0[1]))
     two1 = [cross(*part) for part in zip(far1, one1)]
     two2 = [cross(*part) for part in zip(far2, one2)]
+    one2[1], mine = tie(one2[1], mine)
+    other = swap(mine)
     one2[0], two0[1] = tie(one2[0], two0[1])
     three0 = [exchange(*part) for part in zip(pair0, two0)]
     three1 = [exchange(*part) for part in zip(pair1, two1)]
+    three1[0], two2[0] = tie(three1[0], two2[0])
     three2 = [exchange(*part) for part in zip(pair2, two2)]
     ends = [
         finish_all(0, own0, two0, three0),

time: 238 us -> 242 us (1.017)
  waiting for transfers between devices: 88.3 us -> 114 us
  starting transfers between devices: 86.6 us -> 65.1 us
    ppermute x5, starting transfers between devices: 39.6 us -> 15.6 us  [pairs(): return lax.ppermute(x, 'col', [(0, 1), (1, 0), (2, 3), (3, 2)])]
    ppermute x5, waiting for transfers between devices: 5.33 us -> 21 us  [pairs(): return lax.ppermute(x, 'col', [(0, 1), (1, 0), (2, 3), (3, 2)])]
    ppermute x6, waiting for transfers between devices: 25.1 us -> 31.8 us  [hop_down(): return lax.ppermute(x, 'col', [(3 - c, 2 - c) for c in range(first, 3)])]
    ppermute x5, starting transfers between devices: 13 us -> 15.5 us  [inward(): return lax.ppermute(x, 'col', [(0, 1), (3, 2)])]
    ppermute x5, waiting for transfers between devices: 29 us -> 31.5 us  [inward(): return lax.ppermute(x, 'col', [(0, 1), (3, 2)])]
  transfers between devices with their start and end apart: 42 -> 42, of which waited for: 17 -> 18; matrix products, arithmetic and copies ran while one was open for 4% -> 3% of each run, Pallas kernels for 19% -> 18%
where the time goes in v5:
time: 242 us
  waiting for transfers between devices  114 us (47%)
  starting transfers between devices  65.1 us (27%)
  Pallas kernels  48 us (20%)
  other arithmetic  7.9 us (3%)
  local copies, waits for them, and re-layouts  4.67 us (2%)
    pallas_call x3, Pallas kernels, run_group(): pl.pallas_call(functools.partial(group_kernel, pieces, group), out_shape=...  44.6 us
    ppermute x6, waiting for transfers between devices, hop_down(): return lax.ppermute(x, 'col', [(3 - c, 2 - c) for c in range(first, 3)])  31.8 us
    ppermute x5, waiting for transfers between devices, inward(): return lax.ppermute(x, 'col', [(0, 1), (3, 2)])  31.5 us
    ppermute x4, waiting for transfers between devices, planar(): return lax.ppermute(x, 'row', [(r, r ^ offset) for r in range(4)])  27.1 us
    ppermute x5, waiting for transfers between devices, pairs(): return lax.ppermute(x, 'col', [(0, 1), (1, 0), (2, 3), (3, 2)])  21 us
    ppermute x5, starting transfers between devices, pairs(): return lax.ppermute(x, 'col', [(0, 1), (1, 0), (2, 3), (3, 2)])  15.6 us
    ppermute x5, starting transfers between devices, inward(): return lax.ppermute(x, 'col', [(0, 1), (3, 2)])  15.5 us
    ppermute x6, starting transfers between devices, hop_up(): return lax.ppermute(x, 'col', [(c, c + 1) for c in range(first, 3)])  12.4 us
  transfers between devices with their start and end apart: 42, of which 18 were waited for; matrix products, arithmetic and copies ran while one was open for 3% of the time, Pallas kernels for 18%

profile of v5, /device:TPU:0, one launch (start us, length us, event | category | flops | bytes accessed | tf_op | source)
XLA Modules:
  0.0 241.6 jit_solution(3921084726762175895)
XLA Ops:
  0.6 1.8 copy.11
  2.5 0.5 shard_map.59
  3.0 0.5 collective-permute-start.2
  4.4 0.5 collective-permute-start.7
  4.9 2.6 %collective-permute-start.1 = (bf16[384,2048]{1,0:T(8,128)(2,1)S(1)}, bf16[384,2048]{1,0:T(8,128)(2,1)S(1)}, u32[]{:S(2)}, u32[]{:S(2)}) collective-permute-start(bf16[384,2048]{1,0:T(8,128)(2,1)S(1)} %bitcast.49), channel_id=1, source_target_pairs={{0,8},{4,12},{8,0},{12,4},{1,9},{5,13},{9,1},{13,5},{2,10},{6,14},... | collective-permute-start | bytes 4718600 | tf_op jit(solution)/shard_map/ppermute | solution.py:379
  7.7 1.3 collective-permute-start.5
  9.0 1.6 collective-permute-start
  10.5 4.6 %collective-permute-start.3 = (bf16[2,2,256,384]{3,2,1,0:T(8,128)(2,1)S(1)}, bf16[2,2,256,384]{3,2,1,0:T(8,128)(2,1)S(1)}, u32[]{:S(2)}, u32[]{:S(2)}) collective-permute-start(bf16[2,2,256,384]{3,2,1,0:T(8,128)(2,1)S(1)} %get-tuple-element.115.refs_10_), channel_id=1, source_target_pairs={{0,1},{1,2},{2,3},{4,5},{5,6},{6,7},{8,9},{9,10},{10,11},{12,13},{... | collective-permute-start | bytes 2359304 | tf_op jit(solution)/shard_map/ppermute | solution.py:383
  15.1 14.0 %collective-permute-done.5.refs_14_ = bf16[2,2,256,384]{3,2,1,0:T(8,128)(2,1)S(1)} collective-permute-done((bf16[2,2,256,384]{3,2,1,0:T(8,128)(2,1)S(1)}, bf16[2,2,256,384]{3,2,1,0:T(8,128)(2,1)S(1)}, u32[]{:S(2)}, u32[]{:S(2)}) %collective-permute-start.5) | collective-permute-done | bytes 786464 | tf_op jit(solution)/shard_map/ppermute | solution.py:387
  29.2 1.3 collective-permute-start.6
  30.5 1.2 collective-permute-done.3.refs_11_
  31.6 0.7 collective-permute-start.4
  32.4 10.1 %collective-permute-done.1.refs_2_ = bf16[384,2048]{1,0:T(8,128)(2,1)S(1)} collective-permute-done((bf16[384,2048]{1,0:T(8,128)(2,1)S(1)}, bf16[384,2048]{1,0:T(8,128)(2,1)S(1)}, u32[]{:S(2)}, u32[]{:S(2)}) %collective-permute-start.1) | collective-permute-done | bytes 1572896 | tf_op jit(solution)/shard_map/ppermute | solution.py:379
  42.5 3.1 %collective-permute-done.refs_1_ = bf16[384,2048]{1,0:T(8,128)(2,1)S(1)} collective-permute-done((bf16[384,2048]{1,0:T(8,128)(2,1)S(1)}, bf16[384,2048]{1,0:T(8,128)(2,1)S(1)}, u32[]{:S(2)}, u32[]{:S(2)}) %collective-permute-start) | collective-permute-done | bytes 1572896 | tf_op jit(solution)/shard_map/ppermute | solution.py:379
  45.5 4.3 %collective-permute-done.6.refs_15_ = bf16[2,2,256,384]{3,2,1,0:T(8,128)(2,1)S(1)} collective-permute-done((bf16[2,2,256,384]{3,2,1,0:T(8,128)(2,1)S(1)}, bf16[2,2,256,384]{3,2,1,0:T(8,128)(2,1)S(1)}, u32[]{:S(2)}, u32[]{:S(2)}) %collective-permute-start.6) | collective-permute-done | bytes 786464 | tf_op jit(solution)/shard_map/ppermute | solution.py:387
  50.0 0.8 collective-permute-start.10
  50.8 1.5 collective-permute-start.11
  52.3 0.7 collective-permute-start.8
  53.0 1.3 collective-permute-start.9
  54.4 13.5 %collective-permute-done.10.refs_3_ = bf16[192,2048]{1,0:T(8,128)(2,1)S(1)} collective-permute-done((bf16[192,2048]{1,0:T(8,128)(2,1)S(1)}, bf16[192,2048]{1,0:T(8,128)(2,1)S(1)}, u32[]{:S(2)}, u32[]{:S(2)}) %collective-permute-start.10) | collective-permute-done | bytes 786464 | tf_op jit(solution)/shard_map/ppermute | solution.py:379
  67.9 0.5 collective-permute-done.11.refs_4_
  68.4 4.0 %collective-permute-done.9.refs_16_ = bf16[2,2,256,384]{3,2,1,0:T(8,128)(2,1)S(1)} collective-permute-done((bf16[2,2,256,384]{3,2,1,0:T(8,128)(2,1)S(1)}, bf16[2,2,256,384]{3,2,1,0:T(8,128)(2,1)S(1)}, u32[]{:S(2)}, u32[]{:S(2)}) %collective-permute-start.9) | collective-permute-done | bytes 786464 | tf_op jit(solution)/shard_map/ppermute | solution.py:387
  72.4 0.5 collective-permute-start.15
  72.9 1.3 collective-permute-start.19
  74.2 0.5 collective-permute-done.14.refs_8_
  74.7 4.1 %collective-permute-start.18 = (bf16[2,2,256,384]{3,2,1,0:T(8,128)(2,1)S(1)}, bf16[2,2,256,384]{3,2,1,0:T(8,128)(2,1)S(1)}, u32[]{:S(2)}, u32[]{:S(2)}) collective-permute-start(bf16[2,2,256,384]{3,2,1,0:T(8,128)(2,1)S(1)} %get-tuple-element.81.refs_1_), channel_id=1, source_target_pairs={{0,1},{1,2},{2,3},{4,5},{5,6},{6,7},{8,9},{9,10},{10,11},{12,13},{... | collective-permute-start | bytes 2359304 | tf_op jit(solution)/shard_map/ppermute | solution.py:383
  78.9 1.2 copy-done.17
  80.0 0.5 copy-done.16
  80.6 20.7 %shard_map.60 = (bf16[2,2,1024,1024]{3,2,1,0:T(8,128)(2,1)}, bf16[2,2,256,1024]{3,2,1,0:T(8,128)(2,1)}, f32[384,512]{1,0:T(8,128)S(1)}, f32[384,512]{1,0:T(8,128...) custom-call(bf16[384,2048]{1,0:T(8,128)(2,1)} %bitcast.51, ...), custom_call_target="tpu_custom_call" | custom-call | flops 12884901888 | bytes 12582912 | tf_op jit(solution)/shard_map/pallas_call | solution.py:242
  101.4 2.8 %collective-permute-start.16 = (bf16[2,384,512]{2,1,0:T(8,128)(2,1)S(1)}, bf16[2,384,512]{2,1,0:T(8,128)(2,1)S(1)}, u32[]{:S(2)}, u32[]{:S(2)}) collective-permute-start(bf16[2,384,512]{2,1,0:T(8,128)(2,1)S(1)} %get-tuple-element.79), channel_id=1, source_target_pairs={{0,1},{3,2},{4,5},{7,6},{8,9},{11,10},{12,13},{15,14},{16,17},{19,... | collective-permute-start | bytes 2359304 | tf_op jit(solution)/shard_map/ppermute | solution.py:403
  104.3 0.7 collective-permute-start.20
  105.0 1.3 collective-permute-start.22
  106.3 6.0 %collective-permute-start.28 = (bf16[2,384,512]{2,1,0:T(8,128)(2,1)}, bf16[2,384,512]{2,1,0:T(8,128)(2,1)}, u32[]{:S(2)}, u32[]{:S(2)}) collective-permute-start(bf16[2,384,512]{2,1,0:T(8,128)(2,1)} %get-tuple-element.96), channel_id=1, source_target_pairs={{0,1},{3,2},{4,5},{7,6},{8,9},{11,10},{12,13},{15,14},{16,17},{19,... | collective-permute-start | bytes 2359304 | tf_op jit(solution)/shard_map/ppermute | solution.py:403
  112.3 9.7 %collective-permute-done.16 = bf16[2,384,512]{2,1,0:T(8,128)(2,1)S(1)} collective-permute-done((bf16[2,384,512]{2,1,0:T(8,128)(2,1)S(1)}, bf16[2,384,512]{2,1,0:T(8,128)(2,1)S(1)}, u32[]{:S(2)}, u32[]{:S(2)}) %collective-permute-start.16) | collective-permute-done | bytes 786464 | tf_op jit(solution)/shard_map/ppermute | solution.py:403
  122.1 2.6 %add_convert_fusion.2 = bf16[2,384,512]{2,1,0:T(8,128)(2,1)} fusion(f32[2,384,512]{2,1,0:T(8,128)} %get-tuple-element.78, bf16[2,384,512]{2,1,0:T(8,128)(2,1)S(1)} %collective-permute-done.16), kind=kLoop, calls=%fused_computation.4 | loop fusion | flops 1179648 | bytes 3145728 | tf_op jit(solution)/shard_map/convert_element_type | solution.py:448
  124.7 1.6 collective-permute-start.17
  126.2 1.6 collective-permute-start.21
  127.8 1.3 collective-permute-start.23
  129.1 9.5 %collective-permute-done.28 = bf16[2,384,512]{2,1,0:T(8,128)(2,1)} collective-permute-done((bf16[2,384,512]{2,1,0:T(8,128)(2,1)}, bf16[2,384,512]{2,1,0:T(8,128)(2,1)}, u32[]{:S(2)}, u32[]{:S(2)}) %collective-permute-start.28) | collective-permute-done | bytes 786464 | tf_op jit(solution)/shard_map/ppermute | solution.py:403
  138.6 1.9 add_convert_fusion.1
  140.5 0.9 collective-permute-start.29
  141.4 9.5 %collective-permute-done.23.refs_7_ = bf16[2,2,256,384]{3,2,1,0:T(8,128)(2,1)} collective-permute-done((bf16[2,2,256,384]{3,2,1,0:T(8,128)(2,1)}, bf16[2,2,256,384]{3,2,1,0:T(8,128)(2,1)}, u32[]{:S(2)}, u32[]{:S(2)}) %collective-permute-start.23) | collective-permute-done | bytes 786464 | tf_op jit(solution)/shard_map/ppermute | solution.py:387
  150.9 11.6 %shard_map.61 = (bf16[2,2,1024,1024]{3,2,1,0:T(8,128)(2,1)}, bf16[2,2,256,1024]{3,2,1,0:T(8,128)(2,1)}, f32[768,256]{1,0:T(8,128)S(1)}, f32[768,256]{1,0:T(8,128...) custom-call(bf16[3072,2048]{1,0:T(8,128)(2,1)} %get-tuple-element.77.refs_0_, ...), custom_call_target="tpu_custom_call", output_to_operand_aliasing={{0}: (11, {})} | custom-call | flops 6442450944 | bytes 12582912 | tf_op jit(solution)/shard_map/pallas_call | solution.py:242
  162.6 1.4 collective-permute-start.31
  164.0 1.1 fusion.3
  165.2 12.3 %shard_map.62 = (bf16[2,2,1024,1024]{3,2,1,0:T(8,128)(2,1)}, bf16[2,2,256,1024]{3,2,1,0:T(8,128)(2,1)}, f32[384,256]{1,0:T(8,128)S(1)}, f32[384,256]{1,0:T(8,128...) custom-call(bf16[3072,2048]{1,0:T(8,128)(2,1)} %get-tuple-element.77, ...), custom_call_target="tpu_custom_call", output_to_operand_aliasing={{1}: (10, {}), {0}: (11, {})} | custom-call | flops 6442450944 | bytes 12582912 | tf_op jit(solution)/shard_map/pallas_call | solution.py:242
  177.5 3.9 %collective-permute-start.25 = (bf16[2,384,256]{2,1,0:T(8,128)(2,1)S(1)}, bf16[2,384,256]{2,1,0:T(8,128)(2,1)S(1)}, u32[]{:S(2)}, u32[]{:S(2)}) collective-permute-start(bf16[2,384,256]{2,1,0:T(8,128)(2,1)S(1)} %get-tuple-element.89), channel_id=1, source_target_pairs={{0,1},{3,2},{4,5},{7,6},{8,9},{11,10},{12,13},{15,14},{16,17},{19,... | collective-permute-start | bytes 1179656 | tf_op jit(solution)/shard_map/ppermute | solution.py:403
  181.4 1.3 collective-permute-start.27
  183.0 0.8 collective-permute-start.32
  183.8 6.5 %collective-permute-done.37 = bf16[384,512]{1,0:T(8,128)(2,1)S(1)} collective-permute-done((bf16[384,512]{1,0:T(8,128)(2,1)S(1)}, bf16[384,512]{1,0:T(8,128)(2,1)S(1)}, u32[]{:S(2)}, u32[]{:S(2)}) %collective-permute-start.37) | collective-permute-done | bytes 393248 | tf_op jit(solution)/shard_map/ppermute | solution.py:391
  190.3 1.1 fusion.4
  191.6 7.2 %collective-permute-done.25 = bf16[2,384,256]{2,1,0:T(8,128)(2,1)S(1)} collective-permute-done((bf16[2,384,256]{2,1,0:T(8,128)(2,1)S(1)}, bf16[2,384,256]{2,1,0:T(8,128)(2,1)S(1)}, u32[]{:S(2)}, u32[]{:S(2)}) %collective-permute-start.25) | collective-permute-done | bytes 393248 | tf_op jit(solution)/shard_map/ppermute | solution.py:403
  198.8 0.8 collective-permute-start.35
  199.7 5.0 %collective-permute-done.27 = bf16[2,384,256]{2,1,0:T(8,128)(2,1)S(1)} collective-permute-done((bf16[2,384,256]{2,1,0:T(8,128)(2,1)S(1)}, bf16[2,384,256]{2,1,0:T(8,128)(2,1)S(1)}, u32[]{:S(2)}, u32[]{:S(2)}) %collective-permute-start.27) | collective-permute-done | bytes 393248 | tf_op jit(solution)/shard_map/ppermute | solution.py:403
  204.8 0.8 collective-permute-start.34
  205.8 3.8 %collective-permute-start.33 = (bf16[768,256]{1,0:T(8,128)(2,1)S(1)}, bf16[768,256]{1,0:T(8,128)(2,1)S(1)}, u32[]{:S(2)}, u32[]{:S(2)}) collective-permute-start(bf16[768,256]{1,0:T(8,128)(2,1)S(1)} %fusion.5), channel_id=1, source_target_pairs={{0,1},{1,0},{2,3},{3,2},{4,5},{5,4},{6,7},{7,6},{8,9},{9,8},{10,11... | collective-permute-start | bytes 1179656 | tf_op jit(solution)/shard_map/ppermute | solution.py:391
  209.8 2.9 %collective-permute-start.30 = (bf16[384,512]{1,0:T(8,128)(2,1)S(1)}, bf16[384,512]{1,0:T(8,128)(2,1)S(1)}, u32[]{:S(2)}, u32[]{:S(2)}) collective-permute-start(bf16[384,512]{1,0:T(8,128)(2,1)S(1)} %fusion.7), channel_id=1, source_target_pairs={{0,1},{1,0},{2,3},{3,2},{4,5},{5,4},{6,7},{7,6},{8,9},{9,8},{10,11... | collective-permute-start | bytes 1179656 | tf_op jit(solution)/shard_map/ppermute | solution.py:391
  212.7 6.9 %collective-permute-start.36 = (bf16[384,256]{1,0:T(8,128)(2,1)S(1)}, bf16[384,256]{1,0:T(8,128)(2,1)S(1)}, u32[]{:S(2)}, u32[]{:S(2)}) collective-permute-start(bf16[384,256]{1,0:T(8,128)(2,1)S(1)} %fusion.11), channel_id=1, source_target_pairs={{0,1},{1,0},{2,3},{3,2},{4,5},{5,4},{6,7},{7,6},{8,9},{9,8},{10,11... | collective-permute-start | bytes 589832 | tf_op jit(solution)/shard_map/ppermute | solution.py:391
  219.6 2.0 collective-permute-start.40
  221.8 14.4 %collective-permute-done.40 = bf16[384,256]{1,0:T(8,128)(2,1)S(1)} collective-permute-done((bf16[384,256]{1,0:T(8,128)(2,1)S(1)}, bf16[384,256]{1,0:T(8,128)(2,1)S(1)}, u32[]{:S(2)}, u32[]{:S(2)}) %collective-permute-start.40) | collective-permute-done | bytes 196640 | tf_op jit(solution)/shard_map/ppermute | solution.py:391
  236.3 0.6 collective-permute-start.41
  237.1 0.8 collective-permute-done.39.refs_6_
  238.0 0.6 collective-permute-done.41.refs_7_
  238.5 2.9 %shard_map.63 = (bf16[2,2,1024,1024]{3,2,1,0:T(8,128)(2,1)}, f32[384,2,1024]{2,1,0:T(2,128)}) custom-call(bf16[2,2,256,1024]{3,2,1,0:T(8,128)(2,1)S(1)} %collective-permute-done.26.refs_0_, bf16[2,2,1024,1024]{3,2,1,0:T(8,128)(2,1)} %get-tuple-element.92.refs_1_, f32[384,512]{1,0:T(8,128)S(1)} %fusion.8.refs_2_, ...), custom_call_target="tpu_custom_call", output_to_operand_aliasing={{0}: (1, {})} | custom-call | bytes 10485760 | tf_op jit(solution)/shard_map/pallas_call | solution.py:352
  (90 shorter events, 2.8 us)
Async XLA Ops:
  2.5 1.4 copy-start.11
  3.0 4.5 %collective-permute-start.2 = (bf16[2,2,256,384]{3,2,1,0:T(8,128)(2,1)S(1)}, bf16[2,2,256,384]{3,2,1,0:T(8,128)(2,1)S(1)}, u32[]{:S(2)}, u32[]{:S(2)}) collective-permute-start(bf16[2,2,256,384]{3,2,1,0:T(8,128)(2,1)S(1)} %get-tuple-element.59), channel_id=1, source_target_pairs={{0,16},{16,0},{1,17},{17,1},{2,18},{18,2},{3,19},{19,3},{4,20},{20... | collective-permute-start | bytes 2359304 | tf_op jit(solution)/shard_map/ppermute | solution.py:375
  4.3 4.6 %copy-start.12 = (bf16[48,8,2,1024]{3,1,2,0:T(8,128)(2,1)}, bf16[48,8,2,1024]{3,1,2,0:T(8,128)(2,1)S(1)}, u32[]{:S(2)}) copy-start(bf16[48,8,2,1024]{3,1,2,0:T(8,128)(2,1)S(1)} %copy.10) | copy-start | bytes 4718596
  4.4 28.0 %collective-permute-start.7 = (bf16[384,2048]{1,0:T(8,128)(2,1)S(1)}, bf16[384,2048]{1,0:T(8,128)(2,1)S(1)}, u32[]{:S(2)}, u32[]{:S(2)}) collective-permute-start(bf16[384,2048]{1,0:T(8,128)(2,1)S(1)} %bitcast.48), channel_id=1, source_target_pairs={{0,16},{16,0},{1,17},{17,1},{2,18},{18,2},{3,19},{19,3},{4,20},{20... | collective-permute-start | bytes 4718600 | tf_op jit(solution)/shard_map/ppermute | solution.py:375
  4.9 37.6 %collective-permute-start.1 = (bf16[384,2048]{1,0:T(8,128)(2,1)S(1)}, bf16[384,2048]{1,0:T(8,128)(2,1)S(1)}, u32[]{:S(2)}, u32[]{:S(2)}) collective-permute-start(bf16[384,2048]{1,0:T(8,128)(2,1)S(1)} %bitcast.49), channel_id=1, source_target_pairs={{0,8},{4,12},{8,0},{12,4},{1,9},{5,13},{9,1},{13,5},{2,10},{6,14},... | collective-permute-start | bytes 4718600 | tf_op jit(solution)/shard_map/ppermute | solution.py:379
  7.7 72.9 %copy-start.8 = (f32[4096]{0:T(1024)S(1)}, f32[4096]{0:T(1024)}, u32[]{:S(2)}) copy-start(f32[4096]{0:T(1024)} %param.7) | copy-start | bytes 49156
  7.7 72.9 %copy-start.9 = (f32[2]{0:T(128)S(1)}, f32[2]{0:T(128)}, u32[]{:S(2)}) copy-start(f32[2]{0:T(128)} %refs_8_.3) | copy-start | bytes 28
  7.7 21.5 %collective-permute-start.5 = (bf16[2,2,256,384]{3,2,1,0:T(8,128)(2,1)S(1)}, bf16[2,2,256,384]{3,2,1,0:T(8,128)(2,1)S(1)}, u32[]{:S(2)}, u32[]{:S(2)}) collective-permute-start(bf16[2,2,256,384]{3,2,1,0:T(8,128)(2,1)S(1)} %get-tuple-element.115.refs_10_), channel_id=1, source_target_pairs={{3,2},{2,1},{1,0},{7,6},{6,5},{5,4},{11,10},{10,9},{9,8},{15,14},{... | collective-permute-start | bytes 2359304 | tf_op jit(solution)/shard_map/ppermute | solution.py:387
  9.0 36.5 %collective-permute-start = (bf16[384,2048]{1,0:T(8,128)(2,1)S(1)}, bf16[384,2048]{1,0:T(8,128)(2,1)S(1)}, u32[]{:S(2)}, u32[]{:S(2)}) collective-permute-start(bf16[384,2048]{1,0:T(8,128)(2,1)S(1)} %bitcast.50), channel_id=1, source_target_pairs={{0,4},{4,0},{8,12},{12,8},{1,5},{5,1},{9,13},{13,9},{2,6},{6,2},{1... | collective-permute-start | bytes 4718600 | tf_op jit(solution)/shard_map/ppermute | solution.py:379
  10.5 21.1 %collective-permute-start.3 = (bf16[2,2,256,384]{3,2,1,0:T(8,128)(2,1)S(1)}, bf16[2,2,256,384]{3,2,1,0:T(8,128)(2,1)S(1)}, u32[]{:S(2)}, u32[]{:S(2)}) collective-permute-start(bf16[2,2,256,384]{3,2,1,0:T(8,128)(2,1)S(1)} %get-tuple-element.115.refs_10_), channel_id=1, source_target_pairs={{0,1},{1,2},{2,3},{4,5},{5,6},{6,7},{8,9},{9,10},{10,11},{12,13},{... | collective-permute-start | bytes 2359304 | tf_op jit(solution)/shard_map/ppermute | solution.py:383
  29.2 50.9 %copy-start.18 = (bf16[2,2,256,384]{3,2,1,0:T(8,128)(2,1)}, bf16[2,2,256,384]{3,2,1,0:T(8,128)(2,1)S(1)}, u32[]{:S(2)}) copy-start(bf16[2,2,256,384]{3,2,1,0:T(8,128)(2,1)S(1)} %collective-permute-done.5.refs_14_) | copy-start | bytes 2359300
  29.2 20.7 %collective-permute-start.6 = (bf16[2,2,256,384]{3,2,1,0:T(8,128)(2,1)S(1)}, bf16[2,2,256,384]{3,2,1,0:T(8,128)(2,1)S(1)}, u32[]{:S(2)}, u32[]{:S(2)}) collective-permute-start(bf16[2,2,256,384]{3,2,1,0:T(8,128)(2,1)S(1)} %collective-permute-done.5.refs_14_), channel_id=1, source_target_pairs={{2,1},{1,0},{6,5},{5,4},{10,9},{9,8},{14,13},{13,12},{18,17},{17,1... | collective-permute-start | bytes 2359304 | tf_op jit(solution)/shard_map/ppermute | solution.py:387
  31.6 18.2 %collective-permute-start.4 = (bf16[2,2,256,384]{3,2,1,0:T(8,128)(2,1)S(1)}, bf16[2,2,256,384]{3,2,1,0:T(8,128)(2,1)S(1)}, u32[]{:S(2)}, u32[]{:S(2)}) collective-permute-start(bf16[2,2,256,384]{3,2,1,0:T(8,128)(2,1)S(1)} %collective-permute-done.3.refs_11_), channel_id=1, source_target_pairs={{1,2},{2,3},{5,6},{6,7},{9,10},{10,11},{13,14},{14,15},{17,18},{18... | collective-permute-start | bytes 2359304 | tf_op jit(solution)/shard_map/ppermute | solution.py:383
  32.4 47.7 %copy-start.15 = (bf16[384,2048]{1,0:T(8,128)(2,1)}, bf16[384,2048]{1,0:T(8,128)(2,1)S(1)}, u32[]{:S(2)}) copy-start(bf16[384,2048]{1,0:T(8,128)(2,1)S(1)} %collective-permute-done.7.refs_5_) | copy-start | bytes 4718596
  42.5 25.5 %copy-start.13 = (bf16[384,2048]{1,0:T(8,128)(2,1)}, bf16[384,2048]{1,0:T(8,128)(2,1)S(1)}, u32[]{:S(2)}) copy-start(bf16[384,2048]{1,0:T(8,128)(2,1)S(1)} %collective-permute-done.1.refs_2_) | copy-start | bytes 4718596
  45.5 8.8 %copy-start.14 = (bf16[384,2048]{1,0:T(8,128)(2,1)}, bf16[384,2048]{1,0:T(8,128)(2,1)S(1)}, u32[]{:S(2)}) copy-start(bf16[384,2048]{1,0:T(8,128)(2,1)S(1)} %collective-permute-done.refs_1_) | copy-start | bytes 4718596
  49.8 30.2 %copy-start.19 = (bf16[2,2,256,384]{3,2,1,0:T(8,128)(2,1)}, bf16[2,2,256,384]{3,2,1,0:T(8,128)(2,1)S(1)}, u32[]{:S(2)}) copy-start(bf16[2,2,256,384]{3,2,1,0:T(8,128)(2,1)S(1)} %collective-permute-done.6.refs_15_) | copy-start | bytes 2359300
  50.0 17.9 %collective-permute-start.10 = (bf16[192,2048]{1,0:T(8,128)(2,1)S(1)}, bf16[192,2048]{1,0:T(8,128)(2,1)S(1)}, u32[]{:S(2)}, u32[]{:S(2)}) collective-permute-start(bf16[192,2048]{1,0:T(8,128)(2,1)S(1)} %slice.22), channel_id=1, source_target_pairs={{0,8},{4,12},{8,0},{12,4},{1,9},{5,13},{9,1},{13,5},{2,10},{6,14},... | collective-permute-start | bytes 2359304 | tf_op jit(solution)/shard_map/ppermute | solution.py:379
  50.8 17.6 %collective-permute-start.11 = (bf16[192,2048]{1,0:T(8,128)(2,1)S(1)}, bf16[192,2048]{1,0:T(8,128)(2,1)S(1)}, u32[]{:S(2)}, u32[]{:S(2)}) collective-permute-start(bf16[192,2048]{1,0:T(8,128)(2,1)S(1)} %slice.23), channel_id=1, source_target_pairs={{0,4},{4,0},{8,12},{12,8},{1,5},{5,1},{9,13},{13,9},{2,6},{6,2},{1... | collective-permute-start | bytes 2359304 | tf_op jit(solution)/shard_map/ppermute | solution.py:379
  52.3 16.1 %collective-permute-start.8 = (bf16[2,2,256,384]{3,2,1,0:T(8,128)(2,1)S(1)}, bf16[2,2,256,384]{3,2,1,0:T(8,128)(2,1)S(1)}, u32[]{:S(2)}, u32[]{:S(2)}) collective-permute-start(bf16[2,2,256,384]{3,2,1,0:T(8,128)(2,1)S(1)} %collective-permute-done.4.refs_12_), channel_id=1, source_target_pairs={{2,3},{6,7},{10,11},{14,15},{18,19},{22,23},{26,27},{30,31}} | collective-permute-start | bytes 2359304 | tf_op jit(solution)/shard_map/ppermute | solution.py:383
  53.0 19.3 %collective-permute-start.9 = (bf16[2,2,256,384]{3,2,1,0:T(8,128)(2,1)S(1)}, bf16[2,2,256,384]{3,2,1,0:T(8,128)(2,1)S(1)}, u32[]{:S(2)}, u32[]{:S(2)}) collective-permute-start(bf16[2,2,256,384]{3,2,1,0:T(8,128)(2,1)S(1)} %collective-permute-done.6.refs_15_), channel_id=1, source_target_pairs={{1,0},{5,4},{9,8},{13,12},{17,16},{21,20},{25,24},{29,28}} | collective-permute-start | bytes 2359304 | tf_op jit(solution)/shard_map/ppermute | solution.py:387
  54.3 24.5 %collective-permute-start.12 = (bf16[384,2048]{1,0:T(8,128)(2,1)S(1)}, bf16[384,2048]{1,0:T(8,128)(2,1)S(1)}, u32[]{:S(2)}, u32[]{:S(2)}) collective-permute-start(bf16[384,2048]{1,0:T(8,128)(2,1)S(1)} %collective-permute-done.refs_1_), channel_id=1, source_target_pairs={{0,16},{16,0},{1,17},{17,1},{2,18},{18,2},{3,19},{19,3},{4,20},{20... | collective-permute-start | bytes 4718600 | tf_op jit(solution)/shard_map/ppermute | solution.py:375
  67.9 10.9 %collective-permute-start.13 = (bf16[384,2048]{1,0:T(8,128)(2,1)S(1)}, bf16[384,2048]{1,0:T(8,128)(2,1)S(1)}, u32[]{:S(2)}, u32[]{:S(2)}) collective-permute-start(bf16[384,2048]{1,0:T(8,128)(2,1)S(1)} %collective-permute-done.1.refs_2_), channel_id=1, source_target_pairs={{0,16},{16,0},{1,17},{17,1},{2,18},{18,2},{3,19},{19,3},{4,20},{20... | collective-permute-start | bytes 4718600 | tf_op jit(solution)/shard_map/ppermute | solution.py:375
  68.4 4.5 %copy-start.20 = (bf16[2,2,256,384]{3,2,1,0:T(8,128)(2,1)}, bf16[2,2,256,384]{3,2,1,0:T(8,128)(2,1)S(1)}, u32[]{:S(2)}) copy-start(bf16[2,2,256,384]{3,2,1,0:T(8,128)(2,1)S(1)} %collective-permute-done.8.refs_13_) | copy-start | bytes 2359300
  72.4 1.8 copy-start.21
  72.4 2.3 collective-permute-start.14
  72.4 6.4 %collective-permute-start.15 = (bf16[192,2048]{1,0:T(8,128)(2,1)S(1)}, bf16[192,2048]{1,0:T(8,128)(2,1)S(1)}, u32[]{:S(2)}, u32[]{:S(2)}) collective-permute-start(bf16[192,2048]{1,0:T(8,128)(2,1)S(1)} %collective-permute-done.11.refs_4_), channel_id=1, source_target_pairs={{0,16},{16,0},{1,17},{17,1},{2,18},{18,2},{3,19},{19,3},{4,20},{20... | collective-permute-start | bytes 2359304 | tf_op jit(solution)/shard_map/ppermute | solution.py:375
  72.9 31.4 %collective-permute-start.19 = (bf16[2,2,256,384]{3,2,1,0:T(8,128)(2,1)S(1)}, bf16[2,2,256,384]{3,2,1,0:T(8,128)(2,1)S(1)}, u32[]{:S(2)}, u32[]{:S(2)}) collective-permute-start(bf16[2,2,256,384]{3,2,1,0:T(8,128)(2,1)S(1)} %get-tuple-element.81.refs_1_), channel_id=1, source_target_pairs={{3,2},{2,1},{1,0},{7,6},{6,5},{5,4},{11,10},{10,9},{9,8},{15,14},{... | collective-permute-start | bytes 2359304 | tf_op jit(solution)/shard_map/ppermute | solution.py:387
  74.7 29.6 %collective-permute-start.18 = (bf16[2,2,256,384]{3,2,1,0:T(8,128)(2,1)S(1)}, bf16[2,2,256,384]{3,2,1,0:T(8,128)(2,1)S(1)}, u32[]{:S(2)}, u32[]{:S(2)}) collective-permute-start(bf16[2,2,256,384]{3,2,1,0:T(8,128)(2,1)S(1)} %get-tuple-element.81.refs_1_), channel_id=1, source_target_pairs={{0,1},{1,2},{2,3},{4,5},{5,6},{6,7},{8,9},{9,10},{10,11},{12,13},{... | collective-permute-start | bytes 2359304 | tf_op jit(solution)/shard_map/ppermute | solution.py:383
  78.8 1.7 copy-start.16
  78.8 1.2 copy-start.17
  101.3 23.3 %copy-start = (f32[384,512]{1,0:T(8,128)}, f32[384,512]{1,0:T(8,128)S(1)}, u32[]{:S(2)}) copy-start(f32[384,512]{1,0:T(8,128)S(1)} %get-tuple-element.93) | copy-start | bytes 2359300
  101.3 23.3 %copy-start.2 = (f32[384,512]{1,0:T(8,128)}, f32[384,512]{1,0:T(8,128)S(1)}, u32[]{:S(2)}) copy-start(f32[384,512]{1,0:T(8,128)S(1)} %get-tuple-element.108) | copy-start | bytes 2359300
  101.3 23.3 %copy-start.4 = (f32[384,512]{1,0:T(8,128)}, f32[384,512]{1,0:T(8,128)S(1)}, u32[]{:S(2)}) copy-start(f32[384,512]{1,0:T(8,128)S(1)} %get-tuple-element.98) | copy-start | bytes 2359300
  101.3 23.3 %copy-start.6 = (f32[384,512]{1,0:T(8,128)}, f32[384,512]{1,0:T(8,128)S(1)}, u32[]{:S(2)}) copy-start(f32[384,512]{1,0:T(8,128)S(1)} %get-tuple-element.110) | copy-start | bytes 2359300
  101.4 49.6 %collective-permute-start.24 = (bf16[2,2,256,1024]{3,2,1,0:T(8,128)(2,1)}, bf16[2,2,256,1024]{3,2,1,0:T(8,128)(2,1)}, u32[]{:S(2)}, u32[]{:S(2)}) collective-permute-start(bf16[2,2,256,1024]{3,2,1,0:T(8,128)(2,1)} %get-tuple-element.85), channel_id=1, source_target_pairs={{0,16},{16,0},{1,17},{17,1},{2,18},{18,2},{3,19},{19,3},{4,20},{20... | collective-permute-start | bytes 6291464 | tf_op jit(solution)/shard_map/ppermute | solution.py:375
  101.4 20.6 %collective-permute-start.16 = (bf16[2,384,512]{2,1,0:T(8,128)(2,1)S(1)}, bf16[2,384,512]{2,1,0:T(8,128)(2,1)S(1)}, u32[]{:S(2)}, u32[]{:S(2)}) collective-permute-start(bf16[2,384,512]{2,1,0:T(8,128)(2,1)S(1)} %get-tuple-element.79), channel_id=1, source_target_pairs={{0,1},{3,2},{4,5},{7,6},{8,9},{11,10},{12,13},{15,14},{16,17},{19,... | collective-permute-start | bytes 2359304 | tf_op jit(solution)/shard_map/ppermute | solution.py:403
  104.3 22.0 %collective-permute-start.20 = (bf16[2,2,256,384]{3,2,1,0:T(8,128)(2,1)S(1)}, bf16[2,2,256,384]{3,2,1,0:T(8,128)(2,1)S(1)}, u32[]{:S(2)}, u32[]{:S(2)}) collective-permute-start(bf16[2,2,256,384]{3,2,1,0:T(8,128)(2,1)S(1)} %collective-permute-done.18.refs_2_), channel_id=1, source_target_pairs={{1,2},{2,3},{5,6},{6,7},{9,10},{10,11},{13,14},{14,15},{17,18},{18... | collective-permute-start | bytes 2359304 | tf_op jit(solution)/shard_map/ppermute | solution.py:383
  105.0 22.8 %collective-permute-start.22 = (bf16[2,2,256,384]{3,2,1,0:T(8,128)(2,1)S(1)}, bf16[2,2,256,384]{3,2,1,0:T(8,128)(2,1)}, u32[]{:S(2)}, u32[]{:S(2)}) collective-permute-start(bf16[2,2,256,384]{3,2,1,0:T(8,128)(2,1)S(1)} %collective-permute-done.19.refs_5_), channel_id=1, source_target_pairs={{2,1},{1,0},{6,5},{5,4},{10,9},{9,8},{14,13},{13,12},{18,17},{17,1... | collective-permute-start | bytes 2359304 | tf_op jit(solution)/shard_map/ppermute | solution.py:387
  106.3 32.3 %collective-permute-start.28 = (bf16[2,384,512]{2,1,0:T(8,128)(2,1)}, bf16[2,384,512]{2,1,0:T(8,128)(2,1)}, u32[]{:S(2)}, u32[]{:S(2)}) collective-permute-start(bf16[2,384,512]{2,1,0:T(8,128)(2,1)} %get-tuple-element.96), channel_id=1, source_target_pairs={{0,1},{3,2},{4,5},{7,6},{8,9},{11,10},{12,13},{15,14},{16,17},{19,... | collective-permute-start | bytes 2359304 | tf_op jit(solution)/shard_map/ppermute | solution.py:403
  124.7 16.7 %collective-permute-start.17 = (bf16[2,384,512]{2,1,0:T(8,128)(2,1)}, bf16[2,384,512]{2,1,0:T(8,128)(2,1)}, u32[]{:S(2)}, u32[]{:S(2)}) collective-permute-start(bf16[2,384,512]{2,1,0:T(8,128)(2,1)} %add_convert_fusion.2), channel_id=1, source_target_pairs={{1,2},{2,1},{5,6},{6,5},{9,10},{10,9},{13,14},{14,13},{17,18},{18,... | collective-permute-start | bytes 2359304 | tf_op jit(solution)/shard_map/ppermute | solution.py:395
  126.2 15.2 %collective-permute-start.21 = (bf16[2,2,256,384]{3,2,1,0:T(8,128)(2,1)S(1)}, bf16[2,2,256,384]{3,2,1,0:T(8,128)(2,1)}, u32[]{:S(2)}, u32[]{:S(2)}) collective-permute-start(bf16[2,2,256,384]{3,2,1,0:T(8,128)(2,1)S(1)} %collective-permute-done.20.refs_3_), channel_id=1, source_target_pairs={{2,3},{6,7},{10,11},{14,15},{18,19},{22,23},{26,27},{30,31}} | collective-permute-start | bytes 2359304 | tf_op jit(solution)/shard_map/ppermute | solution.py:383
  127.8 23.1 %collective-permute-start.23 = (bf16[2,2,256,384]{3,2,1,0:T(8,128)(2,1)}, bf16[2,2,256,384]{3,2,1,0:T(8,128)(2,1)}, u32[]{:S(2)}, u32[]{:S(2)}) collective-permute-start(bf16[2,2,256,384]{3,2,1,0:T(8,128)(2,1)} %collective-permute-done.22.refs_6_), channel_id=1, source_target_pairs={{1,0},{5,4},{9,8},{13,12},{17,16},{21,20},{25,24},{29,28}} | collective-permute-start | bytes 2359304 | tf_op jit(solution)/shard_map/ppermute | solution.py:387
  140.5 59.2 %collective-permute-start.29 = (bf16[2,384,512]{2,1,0:T(8,128)(2,1)S(1)}, bf16[2,384,512]{2,1,0:T(8,128)(2,1)S(1)}, u32[]{:S(2)}, u32[]{:S(2)}) collective-permute-start(bf16[2,384,512]{2,1,0:T(8,128)(2,1)S(1)} %add_convert_fusion.1), channel_id=1, source_target_pairs={{1,2},{2,1},{5,6},{6,5},{9,10},{10,9},{13,14},{14,13},{17,18},{18,... | collective-permute-start | bytes 2359304 | tf_op jit(solution)/shard_map/ppermute | solution.py:395
  150.9 13.0 %copy-start.7 = (f32[384,512]{1,0:T(8,128)S(1)}, f32[384,512]{1,0:T(8,128)}, u32[]{:S(2)}) copy-start(f32[384,512]{1,0:T(8,128)} %copy-done.6) | copy-start | bytes 2359300
  162.6 20.2 %collective-permute-start.31 = (bf16[2,768,256]{2,1,0:T(8,128)(2,1)S(1)}, bf16[2,768,256]{2,1,0:T(8,128)(2,1)S(1)}, u32[]{:S(2)}, u32[]{:S(2)}) collective-permute-start(bf16[2,768,256]{2,1,0:T(8,128)(2,1)S(1)} %get-tuple-element.101), channel_id=1, source_target_pairs={{0,1},{3,2},{4,5},{7,6},{8,9},{11,10},{12,13},{15,14},{16,17},{19,... | collective-permute-start | bytes 2359304 | tf_op jit(solution)/shard_map/ppermute | solution.py:403
  165.1 25.2 %collective-permute-start.37 = (bf16[384,512]{1,0:T(8,128)(2,1)S(1)}, bf16[384,512]{1,0:T(8,128)(2,1)S(1)}, u32[]{:S(2)}, u32[]{:S(2)}) collective-permute-start(bf16[384,512]{1,0:T(8,128)(2,1)S(1)} %fusion.3), channel_id=1, source_target_pairs={{0,1},{1,0},{2,3},{3,2},{4,5},{5,4},{6,7},{7,6},{8,9},{9,8},{10,11... | collective-permute-start | bytes 1179656 | tf_op jit(solution)/shard_map/ppermute | solution.py:391
  177.5 21.3 %collective-permute-start.25 = (bf16[2,384,256]{2,1,0:T(8,128)(2,1)S(1)}, bf16[2,384,256]{2,1,0:T(8,128)(2,1)S(1)}, u32[]{:S(2)}, u32[]{:S(2)}) collective-permute-start(bf16[2,384,256]{2,1,0:T(8,128)(2,1)S(1)} %get-tuple-element.89), channel_id=1, source_target_pairs={{0,1},{3,2},{4,5},{7,6},{8,9},{11,10},{12,13},{15,14},{16,17},{19,... | collective-permute-start | bytes 1179656 | tf_op jit(solution)/shard_map/ppermute | solution.py:403
  181.4 23.3 %collective-permute-start.27 = (bf16[2,384,256]{2,1,0:T(8,128)(2,1)S(1)}, bf16[2,384,256]{2,1,0:T(8,128)(2,1)S(1)}, u32[]{:S(2)}, u32[]{:S(2)}) collective-permute-start(bf16[2,384,256]{2,1,0:T(8,128)(2,1)S(1)} %get-tuple-element.94), channel_id=1, source_target_pairs={{0,1},{3,2},{4,5},{7,6},{8,9},{11,10},{12,13},{15,14},{16,17},{19,... | collective-permute-start | bytes 1179656 | tf_op jit(solution)/shard_map/ppermute | solution.py:403
  182.8 7.6 %copy-start.3 = (f32[384,512]{1,0:T(8,128)S(1)}, f32[384,512]{1,0:T(8,128)}, u32[]{:S(2)}) copy-start(f32[384,512]{1,0:T(8,128)} %copy-done.2) | copy-start | bytes 2359300
  183.0 22.8 %collective-permute-start.32 = (bf16[2,768,256]{2,1,0:T(8,128)(2,1)S(1)}, bf16[2,768,256]{2,1,0:T(8,128)(2,1)S(1)}, u32[]{:S(2)}, u32[]{:S(2)}) collective-permute-start(bf16[2,768,256]{2,1,0:T(8,128)(2,1)S(1)} %add_convert_fusion), channel_id=1, source_target_pairs={{1,2},{2,1},{5,6},{6,5},{9,10},{10,9},{13,14},{14,13},{17,18},{18,... | collective-permute-start | bytes 2359304 | tf_op jit(solution)/shard_map/ppermute | solution.py:395
  191.5 45.6 %collective-permute-start.38 = (f32[384,512]{1,0:T(8,128)S(1)}, f32[384,512]{1,0:T(8,128)S(1)}, u32[]{:S(2)}, u32[]{:S(2)}) collective-permute-start(f32[384,512]{1,0:T(8,128)S(1)} %fusion.4), channel_id=1, source_target_pairs={{0,16},{16,0},{1,17},{17,1},{2,18},{18,2},{3,19},{19,3},{4,20},{20... | collective-permute-start | bytes 2359304 | tf_op jit(solution)/shard_map/ppermute | solution.py:375
  198.8 6.9 %copy-start.10 = (bf16[2,2,256,1024]{3,2,1,0:T(8,128)(2,1)S(1)}, bf16[2,2,256,1024]{3,2,1,0:T(8,128)(2,1)}, u32[]{:S(2)}) copy-start(bf16[2,2,256,1024]{3,2,1,0:T(8,128)(2,1)} %get-tuple-element.91) | copy-start | bytes 6291460
  198.8 10.9 %collective-permute-start.35 = (bf16[2,384,256]{2,1,0:T(8,128)(2,1)S(1)}, bf16[2,384,256]{2,1,0:T(8,128)(2,1)S(1)}, u32[]{:S(2)}, u32[]{:S(2)}) collective-permute-start(bf16[2,384,256]{2,1,0:T(8,128)(2,1)S(1)} %add_convert_fusion.3), channel_id=1, source_target_pairs={{1,2},{2,1},{5,6},{6,5},{9,10},{10,9},{13,14},{14,13},{17,18},{18,... | collective-permute-start | bytes 1179656 | tf_op jit(solution)/shard_map/ppermute | solution.py:395
  204.7 4.9 %copy-start.5 = (f32[384,512]{1,0:T(8,128)S(1)}, f32[384,512]{1,0:T(8,128)}, u32[]{:S(2)}) copy-start(f32[384,512]{1,0:T(8,128)} %copy-done.4) | copy-start | bytes 2359300
  204.8 7.8 %collective-permute-start.34 = (bf16[2,384,256]{2,1,0:T(8,128)(2,1)S(1)}, bf16[2,384,256]{2,1,0:T(8,128)(2,1)S(1)}, u32[]{:S(2)}, u32[]{:S(2)}) collective-permute-start(bf16[2,384,256]{2,1,0:T(8,128)(2,1)S(1)} %add_convert_fusion.4), channel_id=1, source_target_pairs={{1,2},{2,1},{5,6},{6,5},{9,10},{10,9},{13,14},{14,13},{17,18},{18,... | collective-permute-start | bytes 1179656 | tf_op jit(solution)/shard_map/ppermute | solution.py:395
  205.7 32.3 %collective-permute-start.26 = (bf16[2,2,256,1024]{3,2,1,0:T(8,128)(2,1)S(1)}, bf16[2,2,256,1024]{3,2,1,0:T(8,128)(2,1)S(1)}, u32[]{:S(2)}, u32[]{:S(2)}) collective-permute-start(bf16[2,2,256,1024]{3,2,1,0:T(8,128)(2,1)S(1)} %copy-done.10), channel_id=1, source_target_pairs={{0,16},{16,0},{1,17},{17,1},{2,18},{18,2},{3,19},{19,3},{4,20},{20... | collective-permute-start | bytes 6291464 | tf_op jit(solution)/shard_map/ppermute | solution.py:375
  205.8 13.7 %collective-permute-start.33 = (bf16[768,256]{1,0:T(8,128)(2,1)S(1)}, bf16[768,256]{1,0:T(8,128)(2,1)S(1)}, u32[]{:S(2)}, u32[]{:S(2)}) collective-permute-start(bf16[768,256]{1,0:T(8,128)(2,1)S(1)} %fusion.5), channel_id=1, source_target_pairs={{0,1},{1,0},{2,3},{3,2},{4,5},{5,4},{6,7},{7,6},{8,9},{9,8},{10,11... | collective-permute-start | bytes 1179656 | tf_op jit(solution)/shard_map/ppermute | solution.py:391
  209.8 26.5 %collective-permute-start.30 = (bf16[384,512]{1,0:T(8,128)(2,1)S(1)}, bf16[384,512]{1,0:T(8,128)(2,1)S(1)}, u32[]{:S(2)}, u32[]{:S(2)}) collective-permute-start(bf16[384,512]{1,0:T(8,128)(2,1)S(1)} %fusion.7), channel_id=1, source_target_pairs={{0,1},{1,0},{2,3},{3,2},{4,5},{5,4},{6,7},{7,6},{8,9},{9,8},{10,11... | collective-permute-start | bytes 1179656 | tf_op jit(solution)/shard_map/ppermute | solution.py:391
  212.7 24.4 %collective-permute-start.36 = (bf16[384,256]{1,0:T(8,128)(2,1)S(1)}, bf16[384,256]{1,0:T(8,128)(2,1)S(1)}, u32[]{:S(2)}, u32[]{:S(2)}) collective-permute-start(bf16[384,256]{1,0:T(8,128)(2,1)S(1)} %fusion.11), channel_id=1, source_target_pairs={{0,1},{1,0},{2,3},{3,2},{4,5},{5,4},{6,7},{7,6},{8,9},{9,8},{10,11... | collective-permute-start | bytes 589832 | tf_op jit(solution)/shard_map/ppermute | solution.py:391
  219.6 16.6 %collective-permute-start.40 = (bf16[384,256]{1,0:T(8,128)(2,1)S(1)}, bf16[384,256]{1,0:T(8,128)(2,1)S(1)}, u32[]{:S(2)}, u32[]{:S(2)}) collective-permute-start(bf16[384,256]{1,0:T(8,128)(2,1)S(1)} %fusion.9), channel_id=1, source_target_pairs={{0,1},{1,0},{2,3},{3,2},{4,5},{5,4},{6,7},{7,6},{8,9},{9,8},{10,11... | collective-permute-start | bytes 589832 | tf_op jit(solution)/shard_map/ppermute | solution.py:391
  221.8 15.1 %copy-start.1 = (f32[384,512]{1,0:T(8,128)S(1)}, f32[384,512]{1,0:T(8,128)}, u32[]{:S(2)}) copy-start(f32[384,512]{1,0:T(8,128)} %copy-done) | copy-start | bytes 2359300
  236.2 1.7 collective-permute-start.39
  236.3 2.2 collective-permute-start.41

commit v6 on v5

--- a/solution.py
+++ b/solution.py
@@ -493,7 +493,6 @@
     one2[0], two0[1] = tie(one2[0], two0[1])
     three0 = [exchange(*part) for part in zip(pair0, two0)]
     three1 = [exchange(*part) for part in zip(pair1, two1)]
-    three1[0], two2[0] = tie(three1[0], two2[0])
     three2 = [exchange(*part) for part in zip(pair2, two2)]
     ends = [
         finish_all(0, own0, two0, three0),

time: 242 us -> 238 us (0.983)
  waiting for transfers between devices: 114 us -> 95.9 us
  starting transfers between devices: 65.1 us -> 78.7 us
    ppermute x5, starting transfers between devices: 15.6 us -> 32.2 us  [pairs(): return lax.ppermute(x, 'col', [(0, 1), (1, 0), (2, 3), (3, 2)])]
    ppermute x5, waiting for transfers between devices: 21 us -> 11.6 us  [pairs(): return lax.ppermute(x, 'col', [(0, 1), (1, 0), (2, 3), (3, 2)])]
    ppermute x6, waiting for transfers between devices: 31.8 us -> 25.1 us  [hop_down(): return lax.ppermute(x, 'col', [(3 - c, 2 - c) for c in range(first, 3)])]
    ppermute x5, starting transfers between devices: 15.5 us -> 12.9 us  [inward(): return lax.ppermute(x, 'col', [(0, 1), (3, 2)])]
  transfers between devices with their start and end apart: 42 -> 42, of which waited for: 18 -> 18; matrix products, arithmetic and copies ran while one was open for 3% -> 4% of each run, Pallas kernels for 18% -> 19%
where the time goes in v6:
time: 238 us; the launch traced here: 237 us
  waiting for transfers between devices  95.9 us (40%)
  starting transfers between devices  78.7 us (33%)
  Pallas kernels  48 us (20%)
  other arithmetic  8.01 us (3%)
  local copies, waits for them, and re-layouts  5.04 us (2%)
    pallas_call x3, Pallas kernels, run_group(): pl.pallas_call(functools.partial(group_kernel, pieces, group), out_shape=...  44.6 us
    ppermute x5, starting transfers between devices, pairs(): return lax.ppermute(x, 'col', [(0, 1), (1, 0), (2, 3), (3, 2)])  32.2 us
    ppermute x5, waiting for transfers between devices, inward(): return lax.ppermute(x, 'col', [(0, 1), (3, 2)])  30.3 us
    ppermute x4, waiting for transfers between devices, planar(): return lax.ppermute(x, 'row', [(r, r ^ offset) for r in range(4)])  27.1 us
    ppermute x6, waiting for transfers between devices, hop_down(): return lax.ppermute(x, 'col', [(3 - c, 2 - c) for c in range(first, 3)])  25.1 us
    ppermute x5, starting transfers between devices, inward(): return lax.ppermute(x, 'col', [(0, 1), (3, 2)])  12.9 us
    ppermute x6, starting transfers between devices, hop_up(): return lax.ppermute(x, 'col', [(c, c + 1) for c in range(first, 3)])  12.4 us
    ppermute x5, waiting for transfers between devices, pairs(): return lax.ppermute(x, 'col', [(0, 1), (1, 0), (2, 3), (3, 2)])  11.6 us
  transfers between devices with their start and end apart: 42, of which 18 were waited for; matrix products, arithmetic and copies ran while one was open for 4% of the time, Pallas kernels for 19%

profile of v6, /device:TPU:0, one launch (start us, length us, event | category | flops | bytes accessed | tf_op | source)
XLA Modules:
  0.0 237.2 jit_solution(9020572198018240547)
XLA Ops:
  0.6 1.8 copy.11
  2.5 0.5 shard_map.59
  3.0 0.5 collective-permute-start.2
  3.9 0.4 copy.10
  4.4 0.5 collective-permute-start.7
  4.9 2.6 %collective-permute-start.1 = (bf16[384,2048]{1,0:T(8,128)(2,1)S(1)}, bf16[384,2048]{1,0:T(8,128)(2,1)S(1)}, u32[]{:S(2)}, u32[]{:S(2)}) collective-permute-start(bf16[384,2048]{1,0:T(8,128)(2,1)S(1)} %bitcast.49), channel_id=1, source_target_pairs={{0,8},{4,12},{8,0},{12,4},{1,9},{5,13},{9,1},{13,5},{2,10},{6,14},... | collective-permute-start | bytes 4718600 | tf_op jit(solution)/shard_map/ppermute | solution.py:379
  7.7 1.3 collective-permute-start.5
  9.0 1.6 collective-permute-start
  10.5 4.6 %collective-permute-start.3 = (bf16[2,2,256,384]{3,2,1,0:T(8,128)(2,1)S(1)}, bf16[2,2,256,384]{3,2,1,0:T(8,128)(2,1)S(1)}, u32[]{:S(2)}, u32[]{:S(2)}) collective-permute-start(bf16[2,2,256,384]{3,2,1,0:T(8,128)(2,1)S(1)} %get-tuple-element.111.refs_10_), channel_id=1, source_target_pairs={{0,1},{1,2},{2,3},{4,5},{5,6},{6,7},{8,9},{9,10},{10,11},{12,13},{... | collective-permute-start | bytes 2359304 | tf_op jit(solution)/shard_map/ppermute | solution.py:383
  15.1 14.0 %collective-permute-done.5.refs_14_ = bf16[2,2,256,384]{3,2,1,0:T(8,128)(2,1)S(1)} collective-permute-done((bf16[2,2,256,384]{3,2,1,0:T(8,128)(2,1)S(1)}, bf16[2,2,256,384]{3,2,1,0:T(8,128)(2,1)S(1)}, u32[]{:S(2)}, u32[]{:S(2)}) %collective-permute-start.5) | collective-permute-done | bytes 786464 | tf_op jit(solution)/shard_map/ppermute | solution.py:387
  29.2 1.3 collective-permute-start.6
  30.5 1.2 collective-permute-done.3.refs_11_
  31.6 0.7 collective-permute-start.4
  32.4 10.1 %collective-permute-done.1.refs_2_ = bf16[384,2048]{1,0:T(8,128)(2,1)S(1)} collective-permute-done((bf16[384,2048]{1,0:T(8,128)(2,1)S(1)}, bf16[384,2048]{1,0:T(8,128)(2,1)S(1)}, u32[]{:S(2)}, u32[]{:S(2)}) %collective-permute-start.1) | collective-permute-done | bytes 1572896 | tf_op jit(solution)/shard_map/ppermute | solution.py:379
  42.5 3.1 %collective-permute-done.refs_1_ = bf16[384,2048]{1,0:T(8,128)(2,1)S(1)} collective-permute-done((bf16[384,2048]{1,0:T(8,128)(2,1)S(1)}, bf16[384,2048]{1,0:T(8,128)(2,1)S(1)}, u32[]{:S(2)}, u32[]{:S(2)}) %collective-permute-start) | collective-permute-done | bytes 1572896 | tf_op jit(solution)/shard_map/ppermute | solution.py:379
  45.5 4.3 %collective-permute-done.6.refs_15_ = bf16[2,2,256,384]{3,2,1,0:T(8,128)(2,1)S(1)} collective-permute-done((bf16[2,2,256,384]{3,2,1,0:T(8,128)(2,1)S(1)}, bf16[2,2,256,384]{3,2,1,0:T(8,128)(2,1)S(1)}, u32[]{:S(2)}, u32[]{:S(2)}) %collective-permute-start.6) | collective-permute-done | bytes 786464 | tf_op jit(solution)/shard_map/ppermute | solution.py:387
  50.0 0.8 collective-permute-start.10
  50.8 1.5 collective-permute-start.11
  52.3 0.7 collective-permute-start.8
  53.0 1.3 collective-permute-start.9
  54.4 13.5 %collective-permute-done.10.refs_3_ = bf16[192,2048]{1,0:T(8,128)(2,1)S(1)} collective-permute-done((bf16[192,2048]{1,0:T(8,128)(2,1)S(1)}, bf16[192,2048]{1,0:T(8,128)(2,1)S(1)}, u32[]{:S(2)}, u32[]{:S(2)}) %collective-permute-start.10) | collective-permute-done | bytes 786464 | tf_op jit(solution)/shard_map/ppermute | solution.py:379
  67.9 0.5 collective-permute-done.11.refs_4_
  68.4 4.0 %collective-permute-done.9.refs_16_ = bf16[2,2,256,384]{3,2,1,0:T(8,128)(2,1)S(1)} collective-permute-done((bf16[2,2,256,384]{3,2,1,0:T(8,128)(2,1)S(1)}, bf16[2,2,256,384]{3,2,1,0:T(8,128)(2,1)S(1)}, u32[]{:S(2)}, u32[]{:S(2)}) %collective-permute-start.9) | collective-permute-done | bytes 786464 | tf_op jit(solution)/shard_map/ppermute | solution.py:387
  72.4 0.5 collective-permute-start.15
  72.9 1.3 collective-permute-start.19
  74.2 0.5 collective-permute-done.14.refs_8_
  74.7 4.1 %collective-permute-start.18 = (bf16[2,2,256,384]{3,2,1,0:T(8,128)(2,1)S(1)}, bf16[2,2,256,384]{3,2,1,0:T(8,128)(2,1)S(1)}, u32[]{:S(2)}, u32[]{:S(2)}) collective-permute-start(bf16[2,2,256,384]{3,2,1,0:T(8,128)(2,1)S(1)} %get-tuple-element.79.refs_1_), channel_id=1, source_target_pairs={{0,1},{1,2},{2,3},{4,5},{5,6},{6,7},{8,9},{9,10},{10,11},{12,13},{... | collective-permute-start | bytes 2359304 | tf_op jit(solution)/shard_map/ppermute | solution.py:383
  78.9 1.2 copy-done.17
  80.0 0.5 copy-done.16
  80.6 20.7 %shard_map.60 = (bf16[2,2,1024,1024]{3,2,1,0:T(8,128)(2,1)}, bf16[2,2,256,1024]{3,2,1,0:T(8,128)(2,1)}, f32[384,512]{1,0:T(8,128)S(1)}, f32[384,512]{1,0:T(8,128...) custom-call(bf16[384,2048]{1,0:T(8,128)(2,1)} %bitcast.51, ...), custom_call_target="tpu_custom_call" | custom-call | flops 12884901888 | bytes 12582912 | tf_op jit(solution)/shard_map/pallas_call | solution.py:242
  101.4 2.8 %collective-permute-start.16 = (bf16[2,384,512]{2,1,0:T(8,128)(2,1)S(1)}, bf16[2,384,512]{2,1,0:T(8,128)(2,1)S(1)}, u32[]{:S(2)}, u32[]{:S(2)}) collective-permute-start(bf16[2,384,512]{2,1,0:T(8,128)(2,1)S(1)} %get-tuple-element.77), channel_id=1, source_target_pairs={{0,1},{3,2},{4,5},{7,6},{8,9},{11,10},{12,13},{15,14},{16,17},{19,... | collective-permute-start | bytes 2359304 | tf_op jit(solution)/shard_map/ppermute | solution.py:403
  104.3 0.7 collective-permute-start.20
  105.0 1.3 collective-permute-start.22
  106.3 6.0 %collective-permute-start.28 = (bf16[2,384,512]{2,1,0:T(8,128)(2,1)}, bf16[2,384,512]{2,1,0:T(8,128)(2,1)}, u32[]{:S(2)}, u32[]{:S(2)}) collective-permute-start(bf16[2,384,512]{2,1,0:T(8,128)(2,1)} %get-tuple-element.94), channel_id=1, source_target_pairs={{0,1},{3,2},{4,5},{7,6},{8,9},{11,10},{12,13},{15,14},{16,17},{19,... | collective-permute-start | bytes 2359304 | tf_op jit(solution)/shard_map/ppermute | solution.py:403
  112.3 9.7 %collective-permute-done.16 = bf16[2,384,512]{2,1,0:T(8,128)(2,1)S(1)} collective-permute-done((bf16[2,384,512]{2,1,0:T(8,128)(2,1)S(1)}, bf16[2,384,512]{2,1,0:T(8,128)(2,1)S(1)}, u32[]{:S(2)}, u32[]{:S(2)}) %collective-permute-start.16) | collective-permute-done | bytes 786464 | tf_op jit(solution)/shard_map/ppermute | solution.py:403
  122.1 2.6 %add_convert_fusion.2 = bf16[2,384,512]{2,1,0:T(8,128)(2,1)} fusion(f32[2,384,512]{2,1,0:T(8,128)} %get-tuple-element.76, bf16[2,384,512]{2,1,0:T(8,128)(2,1)S(1)} %collective-permute-done.16), kind=kLoop, calls=%fused_computation.4 | loop fusion | flops 1179648 | bytes 3145728 | tf_op jit(solution)/shard_map/convert_element_type | solution.py:448
  124.7 1.6 collective-permute-start.17
  126.3 1.6 collective-permute-start.21
  127.8 1.3 collective-permute-start.23
  129.1 8.8 %collective-permute-done.28 = bf16[2,384,512]{2,1,0:T(8,128)(2,1)} collective-permute-done((bf16[2,384,512]{2,1,0:T(8,128)(2,1)}, bf16[2,384,512]{2,1,0:T(8,128)(2,1)}, u32[]{:S(2)}, u32[]{:S(2)}) %collective-permute-start.28) | collective-permute-done | bytes 786464 | tf_op jit(solution)/shard_map/ppermute | solution.py:403
  137.9 1.9 add_convert_fusion.1
  139.8 0.9 collective-permute-start.29
  140.8 1.1 fusion.3
  141.9 6.8 %collective-permute-start.36 = (bf16[384,512]{1,0:T(8,128)(2,1)S(1)}, bf16[384,512]{1,0:T(8,128)(2,1)S(1)}, u32[]{:S(2)}, u32[]{:S(2)}) collective-permute-start(bf16[384,512]{1,0:T(8,128)(2,1)S(1)} %fusion.3), channel_id=1, source_target_pairs={{0,1},{1,0},{2,3},{3,2},{4,5},{5,4},{6,7},{7,6},{8,9},{9,8},{10,11... | collective-permute-start | bytes 1179656 | tf_op jit(solution)/shard_map/ppermute | solution.py:391
  148.7 2.7 %collective-permute-done.23.refs_7_ = bf16[2,2,256,384]{3,2,1,0:T(8,128)(2,1)} collective-permute-done((bf16[2,2,256,384]{3,2,1,0:T(8,128)(2,1)}, bf16[2,2,256,384]{3,2,1,0:T(8,128)(2,1)}, u32[]{:S(2)}, u32[]{:S(2)}) %collective-permute-start.23) | collective-permute-done | bytes 786464 | tf_op jit(solution)/shard_map/ppermute | solution.py:387
  151.5 11.6 %shard_map.61 = (bf16[2,2,1024,1024]{3,2,1,0:T(8,128)(2,1)}, bf16[2,2,256,1024]{3,2,1,0:T(8,128)(2,1)}, f32[768,256]{1,0:T(8,128)S(1)}, f32[768,256]{1,0:T(8,128...) custom-call(bf16[3072,2048]{1,0:T(8,128)(2,1)} %get-tuple-element.75.refs_0_, ...), custom_call_target="tpu_custom_call", output_to_operand_aliasing={{0}: (11, {})} | custom-call | flops 6442450944 | bytes 12582912 | tf_op jit(solution)/shard_map/pallas_call | solution.py:242
  163.1 1.4 collective-permute-start.31
  164.5 12.3 %shard_map.62 = (bf16[2,2,1024,1024]{3,2,1,0:T(8,128)(2,1)}, bf16[2,2,256,1024]{3,2,1,0:T(8,128)(2,1)}, f32[384,256]{1,0:T(8,128)S(1)}, f32[384,256]{1,0:T(8,128...) custom-call(bf16[3072,2048]{1,0:T(8,128)(2,1)} %get-tuple-element.75, ...), custom_call_target="tpu_custom_call", output_to_operand_aliasing={{1}: (10, {}), {0}: (11, {})} | custom-call | flops 6442450944 | bytes 12582912 | tf_op jit(solution)/shard_map/pallas_call | solution.py:242
  176.8 1.3 collective-permute-start.27
  178.2 1.2 fusion.4
  179.4 1.3 collective-permute-start.25
  180.9 0.7 collective-permute-start.32
  181.6 6.6 %collective-permute-done.27 = bf16[2,384,256]{2,1,0:T(8,128)(2,1)S(1)} collective-permute-done((bf16[2,384,256]{2,1,0:T(8,128)(2,1)S(1)}, bf16[2,384,256]{2,1,0:T(8,128)(2,1)S(1)}, u32[]{:S(2)}, u32[]{:S(2)}) %collective-permute-start.27) | collective-permute-done | bytes 393248 | tf_op jit(solution)/shard_map/ppermute | solution.py:403
  188.3 5.2 %collective-permute-done.25 = bf16[2,384,256]{2,1,0:T(8,128)(2,1)S(1)} collective-permute-done((bf16[2,384,256]{2,1,0:T(8,128)(2,1)S(1)}, bf16[2,384,256]{2,1,0:T(8,128)(2,1)S(1)}, u32[]{:S(2)}, u32[]{:S(2)}) %collective-permute-start.25) | collective-permute-done | bytes 393248 | tf_op jit(solution)/shard_map/ppermute | solution.py:403
  193.5 0.7 collective-permute-start.39
  194.3 0.7 collective-permute-start.34
  195.2 18.0 %collective-permute-start.30 = (bf16[384,512]{1,0:T(8,128)(2,1)S(1)}, bf16[384,512]{1,0:T(8,128)(2,1)S(1)}, u32[]{:S(2)}, u32[]{:S(2)}) collective-permute-start(bf16[384,512]{1,0:T(8,128)(2,1)S(1)} %fusion.7), channel_id=1, source_target_pairs={{0,1},{1,0},{2,3},{3,2},{4,5},{5,4},{6,7},{7,6},{8,9},{9,8},{10,11... | collective-permute-start | bytes 1179656 | tf_op jit(solution)/shard_map/ppermute | solution.py:391
  213.5 5.4 %collective-permute-start.33 = (bf16[768,256]{1,0:T(8,128)(2,1)S(1)}, bf16[768,256]{1,0:T(8,128)(2,1)S(1)}, u32[]{:S(2)}, u32[]{:S(2)}) collective-permute-start(bf16[768,256]{1,0:T(8,128)(2,1)S(1)} %fusion.5), channel_id=1, source_target_pairs={{0,1},{1,0},{2,3},{3,2},{4,5},{5,4},{6,7},{7,6},{8,9},{9,8},{10,11... | collective-permute-start | bytes 1179656 | tf_op jit(solution)/shard_map/ppermute | solution.py:391
  218.9 6.5 %collective-permute-done.40 = bf16[384,256]{1,0:T(8,128)(2,1)S(1)} collective-permute-done((bf16[384,256]{1,0:T(8,128)(2,1)S(1)}, bf16[384,256]{1,0:T(8,128)(2,1)S(1)}, u32[]{:S(2)}, u32[]{:S(2)}) %collective-permute-start.40) | collective-permute-done | bytes 196640 | tf_op jit(solution)/shard_map/ppermute | solution.py:391
  225.4 2.0 collective-permute-start.35
  227.5 4.3 %collective-permute-done.33 = bf16[768,256]{1,0:T(8,128)(2,1)S(1)} collective-permute-done((bf16[768,256]{1,0:T(8,128)(2,1)S(1)}, bf16[768,256]{1,0:T(8,128)(2,1)S(1)}, u32[]{:S(2)}, u32[]{:S(2)}) %collective-permute-start.33) | collective-permute-done | bytes 393248 | tf_op jit(solution)/shard_map/ppermute | solution.py:391
  232.0 0.6 collective-permute-start.38
  233.1 0.8 collective-permute-done.35
  234.1 2.9 %shard_map.63 = (bf16[2,2,1024,1024]{3,2,1,0:T(8,128)(2,1)}, f32[384,2,1024]{2,1,0:T(2,128)}) custom-call(bf16[2,2,256,1024]{3,2,1,0:T(8,128)(2,1)S(1)} %collective-permute-done.26.refs_0_, bf16[2,2,1024,1024]{3,2,1,0:T(8,128)(2,1)} %get-tuple-element.90.refs_1_, f32[384,512]{1,0:T(8,128)S(1)} %fusion.8.refs_2_, ...), custom_call_target="tpu_custom_call", output_to_operand_aliasing={{0}: (1, {})} | custom-call | bytes 10485760 | tf_op jit(solution)/shard_map/pallas_call | solution.py:352
  (90 shorter events, 2.8 us)
Async XLA Ops:
  2.5 1.4 copy-start.11
  3.0 4.5 %collective-permute-start.2 = (bf16[2,2,256,384]{3,2,1,0:T(8,128)(2,1)S(1)}, bf16[2,2,256,384]{3,2,1,0:T(8,128)(2,1)S(1)}, u32[]{:S(2)}, u32[]{:S(2)}) collective-permute-start(bf16[2,2,256,384]{3,2,1,0:T(8,128)(2,1)S(1)} %get-tuple-element.57), channel_id=1, source_target_pairs={{0,16},{16,0},{1,17},{17,1},{2,18},{18,2},{3,19},{19,3},{4,20},{20... | collective-permute-start | bytes 2359304 | tf_op jit(solution)/shard_map/ppermute | solution.py:375
  4.3 4.6 %copy-start.12 = (bf16[48,8,2,1024]{3,1,2,0:T(8,128)(2,1)}, bf16[48,8,2,1024]{3,1,2,0:T(8,128)(2,1)S(1)}, u32[]{:S(2)}) copy-start(bf16[48,8,2,1024]{3,1,2,0:T(8,128)(2,1)S(1)} %copy.10) | copy-start | bytes 4718596
  4.4 28.0 %collective-permute-start.7 = (bf16[384,2048]{1,0:T(8,128)(2,1)S(1)}, bf16[384,2048]{1,0:T(8,128)(2,1)S(1)}, u32[]{:S(2)}, u32[]{:S(2)}) collective-permute-start(bf16[384,2048]{1,0:T(8,128)(2,1)S(1)} %bitcast.48), channel_id=1, source_target_pairs={{0,16},{16,0},{1,17},{17,1},{2,18},{18,2},{3,19},{19,3},{4,20},{20... | collective-permute-start | bytes 4718600 | tf_op jit(solution)/shard_map/ppermute | solution.py:375
  4.9 37.6 %collective-permute-start.1 = (bf16[384,2048]{1,0:T(8,128)(2,1)S(1)}, bf16[384,2048]{1,0:T(8,128)(2,1)S(1)}, u32[]{:S(2)}, u32[]{:S(2)}) collective-permute-start(bf16[384,2048]{1,0:T(8,128)(2,1)S(1)} %bitcast.49), channel_id=1, source_target_pairs={{0,8},{4,12},{8,0},{12,4},{1,9},{5,13},{9,1},{13,5},{2,10},{6,14},... | collective-permute-start | bytes 4718600 | tf_op jit(solution)/shard_map/ppermute | solution.py:379
  7.7 72.9 %copy-start.8 = (f32[4096]{0:T(1024)S(1)}, f32[4096]{0:T(1024)}, u32[]{:S(2)}) copy-start(f32[4096]{0:T(1024)} %param.7) | copy-start | bytes 49156
  7.7 72.9 %copy-start.9 = (f32[2]{0:T(128)S(1)}, f32[2]{0:T(128)}, u32[]{:S(2)}) copy-start(f32[2]{0:T(128)} %refs_8_.3) | copy-start | bytes 28
  7.7 21.5 %collective-permute-start.5 = (bf16[2,2,256,384]{3,2,1,0:T(8,128)(2,1)S(1)}, bf16[2,2,256,384]{3,2,1,0:T(8,128)(2,1)S(1)}, u32[]{:S(2)}, u32[]{:S(2)}) collective-permute-start(bf16[2,2,256,384]{3,2,1,0:T(8,128)(2,1)S(1)} %get-tuple-element.111.refs_10_), channel_id=1, source_target_pairs={{3,2},{2,1},{1,0},{7,6},{6,5},{5,4},{11,10},{10,9},{9,8},{15,14},{... | collective-permute-start | bytes 2359304 | tf_op jit(solution)/shard_map/ppermute | solution.py:387
  9.0 36.5 %collective-permute-start = (bf16[384,2048]{1,0:T(8,128)(2,1)S(1)}, bf16[384,2048]{1,0:T(8,128)(2,1)S(1)}, u32[]{:S(2)}, u32[]{:S(2)}) collective-permute-start(bf16[384,2048]{1,0:T(8,128)(2,1)S(1)} %bitcast.50), channel_id=1, source_target_pairs={{0,4},{4,0},{8,12},{12,8},{1,5},{5,1},{9,13},{13,9},{2,6},{6,2},{1... | collective-permute-start | bytes 4718600 | tf_op jit(solution)/shard_map/ppermute | solution.py:379
  10.5 21.1 %collective-permute-start.3 = (bf16[2,2,256,384]{3,2,1,0:T(8,128)(2,1)S(1)}, bf16[2,2,256,384]{3,2,1,0:T(8,128)(2,1)S(1)}, u32[]{:S(2)}, u32[]{:S(2)}) collective-permute-start(bf16[2,2,256,384]{3,2,1,0:T(8,128)(2,1)S(1)} %get-tuple-element.111.refs_10_), channel_id=1, source_target_pairs={{0,1},{1,2},{2,3},{4,5},{5,6},{6,7},{8,9},{9,10},{10,11},{12,13},{... | collective-permute-start | bytes 2359304 | tf_op jit(solution)/shard_map/ppermute | solution.py:383
  29.2 50.9 %copy-start.18 = (bf16[2,2,256,384]{3,2,1,0:T(8,128)(2,1)}, bf16[2,2,256,384]{3,2,1,0:T(8,128)(2,1)S(1)}, u32[]{:S(2)}) copy-start(bf16[2,2,256,384]{3,2,1,0:T(8,128)(2,1)S(1)} %collective-permute-done.5.refs_14_) | copy-start | bytes 2359300
  29.2 20.7 %collective-permute-start.6 = (bf16[2,2,256,384]{3,2,1,0:T(8,128)(2,1)S(1)}, bf16[2,2,256,384]{3,2,1,0:T(8,128)(2,1)S(1)}, u32[]{:S(2)}, u32[]{:S(2)}) collective-permute-start(bf16[2,2,256,384]{3,2,1,0:T(8,128)(2,1)S(1)} %collective-permute-done.5.refs_14_), channel_id=1, source_target_pairs={{2,1},{1,0},{6,5},{5,4},{10,9},{9,8},{14,13},{13,12},{18,17},{17,1... | collective-permute-start | bytes 2359304 | tf_op jit(solution)/shard_map/ppermute | solution.py:387
  31.6 18.2 %collective-permute-start.4 = (bf16[2,2,256,384]{3,2,1,0:T(8,128)(2,1)S(1)}, bf16[2,2,256,384]{3,2,1,0:T(8,128)(2,1)S(1)}, u32[]{:S(2)}, u32[]{:S(2)}) collective-permute-start(bf16[2,2,256,384]{3,2,1,0:T(8,128)(2,1)S(1)} %collective-permute-done.3.refs_11_), channel_id=1, source_target_pairs={{1,2},{2,3},{5,6},{6,7},{9,10},{10,11},{13,14},{14,15},{17,18},{18... | collective-permute-start | bytes 2359304 | tf_op jit(solution)/shard_map/ppermute | solution.py:383
  32.4 47.7 %copy-start.15 = (bf16[384,2048]{1,0:T(8,128)(2,1)}, bf16[384,2048]{1,0:T(8,128)(2,1)S(1)}, u32[]{:S(2)}) copy-start(bf16[384,2048]{1,0:T(8,128)(2,1)S(1)} %collective-permute-done.7.refs_5_) | copy-start | bytes 4718596
  42.5 25.5 %copy-start.13 = (bf16[384,2048]{1,0:T(8,128)(2,1)}, bf16[384,2048]{1,0:T(8,128)(2,1)S(1)}, u32[]{:S(2)}) copy-start(bf16[384,2048]{1,0:T(8,128)(2,1)S(1)} %collective-permute-done.1.refs_2_) | copy-start | bytes 4718596
  45.5 8.8 %copy-start.14 = (bf16[384,2048]{1,0:T(8,128)(2,1)}, bf16[384,2048]{1,0:T(8,128)(2,1)S(1)}, u32[]{:S(2)}) copy-start(bf16[384,2048]{1,0:T(8,128)(2,1)S(1)} %collective-permute-done.refs_1_) | copy-start | bytes 4718596
  49.8 30.2 %copy-start.19 = (bf16[2,2,256,384]{3,2,1,0:T(8,128)(2,1)}, bf16[2,2,256,384]{3,2,1,0:T(8,128)(2,1)S(1)}, u32[]{:S(2)}) copy-start(bf16[2,2,256,384]{3,2,1,0:T(8,128)(2,1)S(1)} %collective-permute-done.6.refs_15_) | copy-start | bytes 2359300
  50.0 17.9 %collective-permute-start.10 = (bf16[192,2048]{1,0:T(8,128)(2,1)S(1)}, bf16[192,2048]{1,0:T(8,128)(2,1)S(1)}, u32[]{:S(2)}, u32[]{:S(2)}) collective-permute-start(bf16[192,2048]{1,0:T(8,128)(2,1)S(1)} %slice.22), channel_id=1, source_target_pairs={{0,8},{4,12},{8,0},{12,4},{1,9},{5,13},{9,1},{13,5},{2,10},{6,14},... | collective-permute-start | bytes 2359304 | tf_op jit(solution)/shard_map/ppermute | solution.py:379
  50.8 17.6 %collective-permute-start.11 = (bf16[192,2048]{1,0:T(8,128)(2,1)S(1)}, bf16[192,2048]{1,0:T(8,128)(2,1)S(1)}, u32[]{:S(2)}, u32[]{:S(2)}) collective-permute-start(bf16[192,2048]{1,0:T(8,128)(2,1)S(1)} %slice.23), channel_id=1, source_target_pairs={{0,4},{4,0},{8,12},{12,8},{1,5},{5,1},{9,13},{13,9},{2,6},{6,2},{1... | collective-permute-start | bytes 2359304 | tf_op jit(solution)/shard_map/ppermute | solution.py:379
  52.3 16.1 %collective-permute-start.8 = (bf16[2,2,256,384]{3,2,1,0:T(8,128)(2,1)S(1)}, bf16[2,2,256,384]{3,2,1,0:T(8,128)(2,1)S(1)}, u32[]{:S(2)}, u32[]{:S(2)}) collective-permute-start(bf16[2,2,256,384]{3,2,1,0:T(8,128)(2,1)S(1)} %collective-permute-done.4.refs_12_), channel_id=1, source_target_pairs={{2,3},{6,7},{10,11},{14,15},{18,19},{22,23},{26,27},{30,31}} | collective-permute-start | bytes 2359304 | tf_op jit(solution)/shard_map/ppermute | solution.py:383
  53.0 19.3 %collective-permute-start.9 = (bf16[2,2,256,384]{3,2,1,0:T(8,128)(2,1)S(1)}, bf16[2,2,256,384]{3,2,1,0:T(8,128)(2,1)S(1)}, u32[]{:S(2)}, u32[]{:S(2)}) collective-permute-start(bf16[2,2,256,384]{3,2,1,0:T(8,128)(2,1)S(1)} %collective-permute-done.6.refs_15_), channel_id=1, source_target_pairs={{1,0},{5,4},{9,8},{13,12},{17,16},{21,20},{25,24},{29,28}} | collective-permute-start | bytes 2359304 | tf_op jit(solution)/shard_map/ppermute | solution.py:387
  54.3 24.5 %collective-permute-start.12 = (bf16[384,2048]{1,0:T(8,128)(2,1)S(1)}, bf16[384,2048]{1,0:T(8,128)(2,1)S(1)}, u32[]{:S(2)}, u32[]{:S(2)}) collective-permute-start(bf16[384,2048]{1,0:T(8,128)(2,1)S(1)} %collective-permute-done.refs_1_), channel_id=1, source_target_pairs={{0,16},{16,0},{1,17},{17,1},{2,18},{18,2},{3,19},{19,3},{4,20},{20... | collective-permute-start | bytes 4718600 | tf_op jit(solution)/shard_map/ppermute | solution.py:375
  67.9 10.9 %collective-permute-start.13 = (bf16[384,2048]{1,0:T(8,128)(2,1)S(1)}, bf16[384,2048]{1,0:T(8,128)(2,1)S(1)}, u32[]{:S(2)}, u32[]{:S(2)}) collective-permute-start(bf16[384,2048]{1,0:T(8,128)(2,1)S(1)} %collective-permute-done.1.refs_2_), channel_id=1, source_target_pairs={{0,16},{16,0},{1,17},{17,1},{2,18},{18,2},{3,19},{19,3},{4,20},{20... | collective-permute-start | bytes 4718600 | tf_op jit(solution)/shard_map/ppermute | solution.py:375
  68.4 4.5 %copy-start.20 = (bf16[2,2,256,384]{3,2,1,0:T(8,128)(2,1)}, bf16[2,2,256,384]{3,2,1,0:T(8,128)(2,1)S(1)}, u32[]{:S(2)}) copy-start(bf16[2,2,256,384]{3,2,1,0:T(8,128)(2,1)S(1)} %collective-permute-done.8.refs_13_) | copy-start | bytes 2359300
  72.4 1.8 copy-start.21
  72.4 2.3 collective-permute-start.14
  72.4 6.4 %collective-permute-start.15 = (bf16[192,2048]{1,0:T(8,128)(2,1)S(1)}, bf16[192,2048]{1,0:T(8,128)(2,1)S(1)}, u32[]{:S(2)}, u32[]{:S(2)}) collective-permute-start(bf16[192,2048]{1,0:T(8,128)(2,1)S(1)} %collective-permute-done.11.refs_4_), channel_id=1, source_target_pairs={{0,16},{16,0},{1,17},{17,1},{2,18},{18,2},{3,19},{19,3},{4,20},{20... | collective-permute-start | bytes 2359304 | tf_op jit(solution)/shard_map/ppermute | solution.py:375
  72.9 31.4 %collective-permute-start.19 = (bf16[2,2,256,384]{3,2,1,0:T(8,128)(2,1)S(1)}, bf16[2,2,256,384]{3,2,1,0:T(8,128)(2,1)S(1)}, u32[]{:S(2)}, u32[]{:S(2)}) collective-permute-start(bf16[2,2,256,384]{3,2,1,0:T(8,128)(2,1)S(1)} %get-tuple-element.79.refs_1_), channel_id=1, source_target_pairs={{3,2},{2,1},{1,0},{7,6},{6,5},{5,4},{11,10},{10,9},{9,8},{15,14},{... | collective-permute-start | bytes 2359304 | tf_op jit(solution)/shard_map/ppermute | solution.py:387
  74.7 29.6 %collective-permute-start.18 = (bf16[2,2,256,384]{3,2,1,0:T(8,128)(2,1)S(1)}, bf16[2,2,256,384]{3,2,1,0:T(8,128)(2,1)S(1)}, u32[]{:S(2)}, u32[]{:S(2)}) collective-permute-start(bf16[2,2,256,384]{3,2,1,0:T(8,128)(2,1)S(1)} %get-tuple-element.79.refs_1_), channel_id=1, source_target_pairs={{0,1},{1,2},{2,3},{4,5},{5,6},{6,7},{8,9},{9,10},{10,11},{12,13},{... | collective-permute-start | bytes 2359304 | tf_op jit(solution)/shard_map/ppermute | solution.py:383
  78.8 1.7 copy-start.16
  78.8 1.2 copy-start.17
  101.3 23.3 %copy-start = (f32[384,512]{1,0:T(8,128)}, f32[384,512]{1,0:T(8,128)S(1)}, u32[]{:S(2)}) copy-start(f32[384,512]{1,0:T(8,128)S(1)} %get-tuple-element.91) | copy-start | bytes 2359300
  101.3 23.3 %copy-start.2 = (f32[384,512]{1,0:T(8,128)}, f32[384,512]{1,0:T(8,128)S(1)}, u32[]{:S(2)}) copy-start(f32[384,512]{1,0:T(8,128)S(1)} %get-tuple-element.104) | copy-start | bytes 2359300
  101.3 23.3 %copy-start.4 = (f32[384,512]{1,0:T(8,128)}, f32[384,512]{1,0:T(8,128)S(1)}, u32[]{:S(2)}) copy-start(f32[384,512]{1,0:T(8,128)S(1)} %get-tuple-element.96) | copy-start | bytes 2359300
  101.3 23.3 %copy-start.6 = (f32[384,512]{1,0:T(8,128)}, f32[384,512]{1,0:T(8,128)S(1)}, u32[]{:S(2)}) copy-start(f32[384,512]{1,0:T(8,128)S(1)} %get-tuple-element.106) | copy-start | bytes 2359300
  101.4 20.7 %collective-permute-start.16 = (bf16[2,384,512]{2,1,0:T(8,128)(2,1)S(1)}, bf16[2,384,512]{2,1,0:T(8,128)(2,1)S(1)}, u32[]{:S(2)}, u32[]{:S(2)}) collective-permute-start(bf16[2,384,512]{2,1,0:T(8,128)(2,1)S(1)} %get-tuple-element.77), channel_id=1, source_target_pairs={{0,1},{3,2},{4,5},{7,6},{8,9},{11,10},{12,13},{15,14},{16,17},{19,... | collective-permute-start | bytes 2359304 | tf_op jit(solution)/shard_map/ppermute | solution.py:403
  104.2 47.3 %collective-permute-start.24 = (bf16[2,2,256,1024]{3,2,1,0:T(8,128)(2,1)}, bf16[2,2,256,1024]{3,2,1,0:T(8,128)(2,1)}, u32[]{:S(2)}, u32[]{:S(2)}) collective-permute-start(bf16[2,2,256,1024]{3,2,1,0:T(8,128)(2,1)} %get-tuple-element.83), channel_id=1, source_target_pairs={{0,16},{16,0},{1,17},{17,1},{2,18},{18,2},{3,19},{19,3},{4,20},{20... | collective-permute-start | bytes 6291464 | tf_op jit(solution)/shard_map/ppermute | solution.py:375
  104.3 22.0 %collective-permute-start.20 = (bf16[2,2,256,384]{3,2,1,0:T(8,128)(2,1)S(1)}, bf16[2,2,256,384]{3,2,1,0:T(8,128)(2,1)S(1)}, u32[]{:S(2)}, u32[]{:S(2)}) collective-permute-start(bf16[2,2,256,384]{3,2,1,0:T(8,128)(2,1)S(1)} %collective-permute-done.18.refs_2_), channel_id=1, source_target_pairs={{1,2},{2,3},{5,6},{6,7},{9,10},{10,11},{13,14},{14,15},{17,18},{18... | collective-permute-start | bytes 2359304 | tf_op jit(solution)/shard_map/ppermute | solution.py:383
  105.0 22.8 %collective-permute-start.22 = (bf16[2,2,256,384]{3,2,1,0:T(8,128)(2,1)S(1)}, bf16[2,2,256,384]{3,2,1,0:T(8,128)(2,1)}, u32[]{:S(2)}, u32[]{:S(2)}) collective-permute-start(bf16[2,2,256,384]{3,2,1,0:T(8,128)(2,1)S(1)} %collective-permute-done.19.refs_5_), channel_id=1, source_target_pairs={{2,1},{1,0},{6,5},{5,4},{10,9},{9,8},{14,13},{13,12},{18,17},{17,1... | collective-permute-start | bytes 2359304 | tf_op jit(solution)/shard_map/ppermute | solution.py:387
  106.3 31.6 %collective-permute-start.28 = (bf16[2,384,512]{2,1,0:T(8,128)(2,1)}, bf16[2,384,512]{2,1,0:T(8,128)(2,1)}, u32[]{:S(2)}, u32[]{:S(2)}) collective-permute-start(bf16[2,384,512]{2,1,0:T(8,128)(2,1)} %get-tuple-element.94), channel_id=1, source_target_pairs={{0,1},{3,2},{4,5},{7,6},{8,9},{11,10},{12,13},{15,14},{16,17},{19,... | collective-permute-start | bytes 2359304 | tf_op jit(solution)/shard_map/ppermute | solution.py:403
  124.7 16.1 %collective-permute-start.17 = (bf16[2,384,512]{2,1,0:T(8,128)(2,1)}, bf16[2,384,512]{2,1,0:T(8,128)(2,1)}, u32[]{:S(2)}, u32[]{:S(2)}) collective-permute-start(bf16[2,384,512]{2,1,0:T(8,128)(2,1)} %add_convert_fusion.2), channel_id=1, source_target_pairs={{1,2},{2,1},{5,6},{6,5},{9,10},{10,9},{13,14},{14,13},{17,18},{18,... | collective-permute-start | bytes 2359304 | tf_op jit(solution)/shard_map/ppermute | solution.py:395
  126.3 22.5 %collective-permute-start.21 = (bf16[2,2,256,384]{3,2,1,0:T(8,128)(2,1)S(1)}, bf16[2,2,256,384]{3,2,1,0:T(8,128)(2,1)}, u32[]{:S(2)}, u32[]{:S(2)}) collective-permute-start(bf16[2,2,256,384]{3,2,1,0:T(8,128)(2,1)S(1)} %collective-permute-done.20.refs_3_), channel_id=1, source_target_pairs={{2,3},{6,7},{10,11},{14,15},{18,19},{22,23},{26,27},{30,31}} | collective-permute-start | bytes 2359304 | tf_op jit(solution)/shard_map/ppermute | solution.py:383
  127.8 23.6 %collective-permute-start.23 = (bf16[2,2,256,384]{3,2,1,0:T(8,128)(2,1)}, bf16[2,2,256,384]{3,2,1,0:T(8,128)(2,1)}, u32[]{:S(2)}, u32[]{:S(2)}) collective-permute-start(bf16[2,2,256,384]{3,2,1,0:T(8,128)(2,1)} %collective-permute-done.22.refs_6_), channel_id=1, source_target_pairs={{1,0},{5,4},{9,8},{13,12},{17,16},{21,20},{25,24},{29,28}} | collective-permute-start | bytes 2359304 | tf_op jit(solution)/shard_map/ppermute | solution.py:387
  137.9 2.9 %copy-start.7 = (f32[384,512]{1,0:T(8,128)S(1)}, f32[384,512]{1,0:T(8,128)}, u32[]{:S(2)}) copy-start(f32[384,512]{1,0:T(8,128)} %copy-done.6) | copy-start | bytes 2359300
  139.8 55.2 %collective-permute-start.29 = (bf16[2,384,512]{2,1,0:T(8,128)(2,1)S(1)}, bf16[2,384,512]{2,1,0:T(8,128)(2,1)S(1)}, u32[]{:S(2)}, u32[]{:S(2)}) collective-permute-start(bf16[2,384,512]{2,1,0:T(8,128)(2,1)S(1)} %add_convert_fusion.1), channel_id=1, source_target_pairs={{1,2},{2,1},{5,6},{6,5},{9,10},{10,9},{13,14},{14,13},{17,18},{18,... | collective-permute-start | bytes 2359304 | tf_op jit(solution)/shard_map/ppermute | solution.py:395
  141.9 36.2 %collective-permute-start.36 = (bf16[384,512]{1,0:T(8,128)(2,1)S(1)}, bf16[384,512]{1,0:T(8,128)(2,1)S(1)}, u32[]{:S(2)}, u32[]{:S(2)}) collective-permute-start(bf16[384,512]{1,0:T(8,128)(2,1)S(1)} %fusion.3), channel_id=1, source_target_pairs={{0,1},{1,0},{2,3},{3,2},{4,5},{5,4},{6,7},{7,6},{8,9},{9,8},{10,11... | collective-permute-start | bytes 1179656 | tf_op jit(solution)/shard_map/ppermute | solution.py:391
  163.1 17.6 %collective-permute-start.31 = (bf16[2,768,256]{2,1,0:T(8,128)(2,1)S(1)}, bf16[2,768,256]{2,1,0:T(8,128)(2,1)S(1)}, u32[]{:S(2)}, u32[]{:S(2)}) collective-permute-start(bf16[2,768,256]{2,1,0:T(8,128)(2,1)S(1)} %get-tuple-element.99), channel_id=1, source_target_pairs={{0,1},{3,2},{4,5},{7,6},{8,9},{11,10},{12,13},{15,14},{16,17},{19,... | collective-permute-start | bytes 2359304 | tf_op jit(solution)/shard_map/ppermute | solution.py:403
  164.5 13.6 %copy-start.3 = (f32[384,512]{1,0:T(8,128)S(1)}, f32[384,512]{1,0:T(8,128)}, u32[]{:S(2)}) copy-start(f32[384,512]{1,0:T(8,128)} %copy-done.2) | copy-start | bytes 2359300
  176.8 11.4 %collective-permute-start.27 = (bf16[2,384,256]{2,1,0:T(8,128)(2,1)S(1)}, bf16[2,384,256]{2,1,0:T(8,128)(2,1)S(1)}, u32[]{:S(2)}, u32[]{:S(2)}) collective-permute-start(bf16[2,384,256]{2,1,0:T(8,128)(2,1)S(1)} %get-tuple-element.92), channel_id=1, source_target_pairs={{0,1},{3,2},{4,5},{7,6},{8,9},{11,10},{12,13},{15,14},{16,17},{19,... | collective-permute-start | bytes 1179656 | tf_op jit(solution)/shard_map/ppermute | solution.py:403
  179.3 54.7 %collective-permute-start.37 = (f32[384,512]{1,0:T(8,128)S(1)}, f32[384,512]{1,0:T(8,128)S(1)}, u32[]{:S(2)}, u32[]{:S(2)}) collective-permute-start(f32[384,512]{1,0:T(8,128)S(1)} %fusion.4), channel_id=1, source_target_pairs={{0,16},{16,0},{1,17},{17,1},{2,18},{18,2},{3,19},{19,3},{4,20},{20... | collective-permute-start | bytes 2359304 | tf_op jit(solution)/shard_map/ppermute | solution.py:375
  179.4 14.1 %collective-permute-start.25 = (bf16[2,384,256]{2,1,0:T(8,128)(2,1)S(1)}, bf16[2,384,256]{2,1,0:T(8,128)(2,1)S(1)}, u32[]{:S(2)}, u32[]{:S(2)}) collective-permute-start(bf16[2,384,256]{2,1,0:T(8,128)(2,1)S(1)} %get-tuple-element.87), channel_id=1, source_target_pairs={{0,1},{3,2},{4,5},{7,6},{8,9},{11,10},{12,13},{15,14},{16,17},{19,... | collective-permute-start | bytes 1179656 | tf_op jit(solution)/shard_map/ppermute | solution.py:403
  180.9 32.4 %collective-permute-start.32 = (bf16[2,768,256]{2,1,0:T(8,128)(2,1)S(1)}, bf16[2,768,256]{2,1,0:T(8,128)(2,1)S(1)}, u32[]{:S(2)}, u32[]{:S(2)}) collective-permute-start(bf16[2,768,256]{2,1,0:T(8,128)(2,1)S(1)} %add_convert_fusion), channel_id=1, source_target_pairs={{1,2},{2,1},{5,6},{6,5},{9,10},{10,9},{13,14},{14,13},{17,18},{18,... | collective-permute-start | bytes 2359304 | tf_op jit(solution)/shard_map/ppermute | solution.py:395
  188.2 6.8 %copy-start.10 = (bf16[2,2,256,1024]{3,2,1,0:T(8,128)(2,1)S(1)}, bf16[2,2,256,1024]{3,2,1,0:T(8,128)(2,1)}, u32[]{:S(2)}) copy-start(bf16[2,2,256,1024]{3,2,1,0:T(8,128)(2,1)} %get-tuple-element.89) | copy-start | bytes 6291460
  188.2 6.9 %copy-start.5 = (f32[384,512]{1,0:T(8,128)S(1)}, f32[384,512]{1,0:T(8,128)}, u32[]{:S(2)}) copy-start(f32[384,512]{1,0:T(8,128)} %copy-done.4) | copy-start | bytes 2359300
  193.5 1.7 collective-permute-start.39
  194.3 19.2 %collective-permute-start.34 = (bf16[2,384,256]{2,1,0:T(8,128)(2,1)S(1)}, bf16[2,384,256]{2,1,0:T(8,128)(2,1)S(1)}, u32[]{:S(2)}, u32[]{:S(2)}) collective-permute-start(bf16[2,384,256]{2,1,0:T(8,128)(2,1)S(1)} %add_convert_fusion.4), channel_id=1, source_target_pairs={{1,2},{2,1},{5,6},{6,5},{9,10},{10,9},{13,14},{14,13},{17,18},{18,... | collective-permute-start | bytes 1179656 | tf_op jit(solution)/shard_map/ppermute | solution.py:395
  195.0 39.1 %collective-permute-start.26 = (bf16[2,2,256,1024]{3,2,1,0:T(8,128)(2,1)S(1)}, bf16[2,2,256,1024]{3,2,1,0:T(8,128)(2,1)S(1)}, u32[]{:S(2)}, u32[]{:S(2)}) collective-permute-start(bf16[2,2,256,1024]{3,2,1,0:T(8,128)(2,1)S(1)} %copy-done.10), channel_id=1, source_target_pairs={{0,16},{16,0},{1,17},{17,1},{2,18},{18,2},{3,19},{19,3},{4,20},{20... | collective-permute-start | bytes 6291464 | tf_op jit(solution)/shard_map/ppermute | solution.py:375
  195.2 36.7 %collective-permute-start.30 = (bf16[384,512]{1,0:T(8,128)(2,1)S(1)}, bf16[384,512]{1,0:T(8,128)(2,1)S(1)}, u32[]{:S(2)}, u32[]{:S(2)}) collective-permute-start(bf16[384,512]{1,0:T(8,128)(2,1)S(1)} %fusion.7), channel_id=1, source_target_pairs={{0,1},{1,0},{2,3},{3,2},{4,5},{5,4},{6,7},{7,6},{8,9},{9,8},{10,11... | collective-permute-start | bytes 1179656 | tf_op jit(solution)/shard_map/ppermute | solution.py:391
  213.3 12.1 %collective-permute-start.40 = (bf16[384,256]{1,0:T(8,128)(2,1)S(1)}, bf16[384,256]{1,0:T(8,128)(2,1)S(1)}, u32[]{:S(2)}, u32[]{:S(2)}) collective-permute-start(bf16[384,256]{1,0:T(8,128)(2,1)S(1)} %fusion.9), channel_id=1, source_target_pairs={{0,1},{1,0},{2,3},{3,2},{4,5},{5,4},{6,7},{7,6},{8,9},{9,8},{10,11... | collective-permute-start | bytes 589832 | tf_op jit(solution)/shard_map/ppermute | solution.py:391
  213.5 18.3 %collective-permute-start.33 = (bf16[768,256]{1,0:T(8,128)(2,1)S(1)}, bf16[768,256]{1,0:T(8,128)(2,1)S(1)}, u32[]{:S(2)}, u32[]{:S(2)}) collective-permute-start(bf16[768,256]{1,0:T(8,128)(2,1)S(1)} %fusion.5), channel_id=1, source_target_pairs={{0,1},{1,0},{2,3},{3,2},{4,5},{5,4},{6,7},{7,6},{8,9},{9,8},{10,11... | collective-permute-start | bytes 1179656 | tf_op jit(solution)/shard_map/ppermute | solution.py:391
  225.4 8.5 %collective-permute-start.35 = (bf16[384,256]{1,0:T(8,128)(2,1)S(1)}, bf16[384,256]{1,0:T(8,128)(2,1)S(1)}, u32[]{:S(2)}, u32[]{:S(2)}) collective-permute-start(bf16[384,256]{1,0:T(8,128)(2,1)S(1)} %fusion.11), channel_id=1, source_target_pairs={{0,1},{1,0},{2,3},{3,2},{4,5},{5,4},{6,7},{7,6},{8,9},{9,8},{10,11... | collective-permute-start | bytes 589832 | tf_op jit(solution)/shard_map/ppermute | solution.py:391
  231.8 2.2 collective-permute-start.41
  231.8 1.1 copy-start.1
  232.0 2.1 collective-permute-start.38

commit v7 on v5

--- a/solution.py
+++ b/solution.py
@@ -490,7 +490,6 @@
     two2 = [cross(*part) for part in zip(far2, one2)]
     one2[1], mine = tie(one2[1], mine)
     other = swap(mine)
-    one2[0], two0[1] = tie(one2[0], two0[1])
     three0 = [exchange(*part) for part in zip(pair0, two0)]
     three1 = [exchange(*part) for part in zip(pair1, two1)]
     three1[0], two2[0] = tie(three1[0], two2[0])

time: 242 us -> 239 us (0.988)
  waiting for transfers between devices: 114 us -> 111 us
    ppermute x5, waiting for transfers between devices: 21 us -> 10.5 us  [pairs(): return lax.ppermute(x, 'col', [(0, 1), (1, 0), (2, 3), (3, 2)])]
    ppermute x6, waiting for transfers between devices: 31.8 us -> 36.1 us  [hop_down(): return lax.ppermute(x, 'col', [(3 - c, 2 - c) for c in range(first, 3)])]
  transfers between devices with their start and end apart: 42 -> 42, of which waited for: 18 -> 17; matrix products, arithmetic and copies ran while one was open for 3% -> 3% of each run, Pallas kernels for 18% -> 19%
where the time goes in v7:
time: 239 us; the launch traced here: 238 us
  waiting for transfers between devices  111 us (46%)
  starting transfers between devices  65.5 us (27%)
  Pallas kernels  48 us (20%)
  other arithmetic  7.67 us (3%)
  local copies, waits for them, and re-layouts  4.64 us (2%)
    pallas_call x3, Pallas kernels, run_group(): pl.pallas_call(functools.partial(group_kernel, pieces, group), out_shape=...  44.7 us
    ppermute x6, waiting for transfers between devices, hop_down(): return lax.ppermute(x, 'col', [(3 - c, 2 - c) for c in range(first, 3)])  36.1 us
    ppermute x5, waiting for transfers between devices, inward(): return lax.ppermute(x, 'col', [(0, 1), (3, 2)])  33.7 us
    ppermute x4, waiting for transfers between devices, planar(): return lax.ppermute(x, 'row', [(r, r ^ offset) for r in range(4)])  27.1 us
    ppermute x5, starting transfers between devices, inward(): return lax.ppermute(x, 'col', [(0, 1), (3, 2)])  17.1 us
    ppermute x5, starting transfers between devices, pairs(): return lax.ppermute(x, 'col', [(0, 1), (1, 0), (2, 3), (3, 2)])  14.4 us
    ppermute x6, starting transfers between devices, hop_up(): return lax.ppermute(x, 'col', [(c, c + 1) for c in range(first, 3)])  12.4 us
    ppermute x5, waiting for transfers between devices, pairs(): return lax.ppermute(x, 'col', [(0, 1), (1, 0), (2, 3), (3, 2)])  10.5 us
  transfers between devices with their start and end apart: 42, of which 17 were waited for; matrix products, arithmetic and copies ran while one was open for 3% of the time, Pallas kernels for 19%

profile of v7, /device:TPU:0, one launch (start us, length us, event | category | flops | bytes accessed | tf_op | source)
XLA Modules:
  0.0 237.8 jit_solution(7429221066863302792)
XLA Ops:
  0.6 1.8 copy.11
  2.5 0.5 shard_map.59
  3.0 0.5 collective-permute-start.2
  3.5 0.4 copy-done.11
  3.9 0.4 copy.10
  4.3 0.5 collective-permute-start.7
  4.9 2.6 %collective-permute-start.1 = (bf16[384,2048]{1,0:T(8,128)(2,1)S(1)}, bf16[384,2048]{1,0:T(8,128)(2,1)S(1)}, u32[]{:S(2)}, u32[]{:S(2)}) collective-permute-start(bf16[384,2048]{1,0:T(8,128)(2,1)S(1)} %bitcast.49), channel_id=1, source_target_pairs={{0,8},{4,12},{8,0},{12,4},{1,9},{5,13},{9,1},{13,5},{2,10},{6,14},... | collective-permute-start | bytes 4718600 | tf_op jit(solution)/shard_map/ppermute | solution.py:379
  7.7 1.3 collective-permute-start.5
  9.0 1.6 collective-permute-start
  10.5 4.6 %collective-permute-start.3 = (bf16[2,2,256,384]{3,2,1,0:T(8,128)(2,1)S(1)}, bf16[2,2,256,384]{3,2,1,0:T(8,128)(2,1)S(1)}, u32[]{:S(2)}, u32[]{:S(2)}) collective-permute-start(bf16[2,2,256,384]{3,2,1,0:T(8,128)(2,1)S(1)} %get-tuple-element.113.refs_10_), channel_id=1, source_target_pairs={{0,1},{1,2},{2,3},{4,5},{5,6},{6,7},{8,9},{9,10},{10,11},{12,13},{... | collective-permute-start | bytes 2359304 | tf_op jit(solution)/shard_map/ppermute | solution.py:383
  15.1 14.0 %collective-permute-done.5.refs_14_ = bf16[2,2,256,384]{3,2,1,0:T(8,128)(2,1)S(1)} collective-permute-done((bf16[2,2,256,384]{3,2,1,0:T(8,128)(2,1)S(1)}, bf16[2,2,256,384]{3,2,1,0:T(8,128)(2,1)S(1)}, u32[]{:S(2)}, u32[]{:S(2)}) %collective-permute-start.5) | collective-permute-done | bytes 786464 | tf_op jit(solution)/shard_map/ppermute | solution.py:387
  29.2 1.3 collective-permute-start.6
  30.5 1.2 collective-permute-done.3.refs_11_
  31.6 0.7 collective-permute-start.4
  32.4 10.1 %collective-permute-done.1.refs_2_ = bf16[384,2048]{1,0:T(8,128)(2,1)S(1)} collective-permute-done((bf16[384,2048]{1,0:T(8,128)(2,1)S(1)}, bf16[384,2048]{1,0:T(8,128)(2,1)S(1)}, u32[]{:S(2)}, u32[]{:S(2)}) %collective-permute-start.1) | collective-permute-done | bytes 1572896 | tf_op jit(solution)/shard_map/ppermute | solution.py:379
  42.5 3.1 %collective-permute-done.refs_1_ = bf16[384,2048]{1,0:T(8,128)(2,1)S(1)} collective-permute-done((bf16[384,2048]{1,0:T(8,128)(2,1)S(1)}, bf16[384,2048]{1,0:T(8,128)(2,1)S(1)}, u32[]{:S(2)}, u32[]{:S(2)}) %collective-permute-start) | collective-permute-done | bytes 1572896 | tf_op jit(solution)/shard_map/ppermute | solution.py:379
  45.5 4.3 %collective-permute-done.6.refs_15_ = bf16[2,2,256,384]{3,2,1,0:T(8,128)(2,1)S(1)} collective-permute-done((bf16[2,2,256,384]{3,2,1,0:T(8,128)(2,1)S(1)}, bf16[2,2,256,384]{3,2,1,0:T(8,128)(2,1)S(1)}, u32[]{:S(2)}, u32[]{:S(2)}) %collective-permute-start.6) | collective-permute-done | bytes 786464 | tf_op jit(solution)/shard_map/ppermute | solution.py:387
  50.0 0.8 collective-permute-start.10
  50.8 1.5 collective-permute-start.11
  52.3 0.7 collective-permute-start.8
  53.0 1.3 collective-permute-start.9
  54.4 13.5 %collective-permute-done.10.refs_3_ = bf16[192,2048]{1,0:T(8,128)(2,1)S(1)} collective-permute-done((bf16[192,2048]{1,0:T(8,128)(2,1)S(1)}, bf16[192,2048]{1,0:T(8,128)(2,1)S(1)}, u32[]{:S(2)}, u32[]{:S(2)}) %collective-permute-start.10) | collective-permute-done | bytes 786464 | tf_op jit(solution)/shard_map/ppermute | solution.py:379
  67.9 0.5 collective-permute-done.11.refs_4_
  68.4 4.1 %collective-permute-done.9.refs_16_ = bf16[2,2,256,384]{3,2,1,0:T(8,128)(2,1)} collective-permute-done((bf16[2,2,256,384]{3,2,1,0:T(8,128)(2,1)S(1)}, bf16[2,2,256,384]{3,2,1,0:T(8,128)(2,1)}, u32[]{:S(2)}, u32[]{:S(2)}) %collective-permute-start.9) | collective-permute-done | bytes 786464 | tf_op jit(solution)/shard_map/ppermute | solution.py:387
  72.5 0.5 collective-permute-start.15
  73.0 1.3 collective-permute-start.19
  74.3 0.5 collective-permute-done.14.refs_8_
  74.8 4.1 %collective-permute-start.18 = (bf16[2,2,256,384]{3,2,1,0:T(8,128)(2,1)S(1)}, bf16[2,2,256,384]{3,2,1,0:T(8,128)(2,1)S(1)}, u32[]{:S(2)}, u32[]{:S(2)}) collective-permute-start(bf16[2,2,256,384]{3,2,1,0:T(8,128)(2,1)S(1)} %get-tuple-element.80.refs_1_), channel_id=1, source_target_pairs={{0,1},{1,2},{2,3},{4,5},{5,6},{6,7},{8,9},{9,10},{10,11},{12,13},{... | collective-permute-start | bytes 2359304 | tf_op jit(solution)/shard_map/ppermute | solution.py:383
  79.0 1.2 copy-done.18
  80.6 20.8 %shard_map.60 = (bf16[2,2,1024,1024]{3,2,1,0:T(8,128)(2,1)}, bf16[2,2,256,1024]{3,2,1,0:T(8,128)(2,1)}, f32[384,512]{1,0:T(8,128)S(1)}, f32[384,512]{1,0:T(8,128...) custom-call(bf16[384,2048]{1,0:T(8,128)(2,1)} %bitcast.51, ...), custom_call_target="tpu_custom_call" | custom-call | flops 12884901888 | bytes 12582912 | tf_op jit(solution)/shard_map/pallas_call | solution.py:242
  101.5 2.7 %collective-permute-start.16 = (bf16[2,384,512]{2,1,0:T(8,128)(2,1)S(1)}, bf16[2,384,512]{2,1,0:T(8,128)(2,1)S(1)}, u32[]{:S(2)}, u32[]{:S(2)}) collective-permute-start(bf16[2,384,512]{2,1,0:T(8,128)(2,1)S(1)} %get-tuple-element.78), channel_id=1, source_target_pairs={{0,1},{3,2},{4,5},{7,6},{8,9},{11,10},{12,13},{15,14},{16,17},{19,... | collective-permute-start | bytes 2359304 | tf_op jit(solution)/shard_map/ppermute | solution.py:403
  104.3 0.7 collective-permute-start.20
  105.0 1.3 collective-permute-start.22
  106.3 15.3 %collective-permute-done.16 = bf16[2,384,512]{2,1,0:T(8,128)(2,1)S(1)} collective-permute-done((bf16[2,384,512]{2,1,0:T(8,128)(2,1)S(1)}, bf16[2,384,512]{2,1,0:T(8,128)(2,1)S(1)}, u32[]{:S(2)}, u32[]{:S(2)}) %collective-permute-start.16) | collective-permute-done | bytes 786464 | tf_op jit(solution)/shard_map/ppermute | solution.py:403
  121.6 2.6 %add_convert_fusion.2 = bf16[2,384,512]{2,1,0:T(8,128)(2,1)} fusion(f32[2,384,512]{2,1,0:T(8,128)} %get-tuple-element.77, bf16[2,384,512]{2,1,0:T(8,128)(2,1)S(1)} %collective-permute-done.16), kind=kLoop, calls=%fused_computation.4 | loop fusion | flops 1179648 | bytes 3145728 | tf_op jit(solution)/shard_map/convert_element_type | solution.py:448
  124.2 1.6 collective-permute-start.17
  125.8 1.5 collective-permute-start.21
  127.3 1.3 collective-permute-start.23
  128.6 8.4 %collective-permute-start.27 = (bf16[2,384,512]{2,1,0:T(8,128)(2,1)}, bf16[2,384,512]{2,1,0:T(8,128)(2,1)}, u32[]{:S(2)}, u32[]{:S(2)}) collective-permute-start(bf16[2,384,512]{2,1,0:T(8,128)(2,1)} %get-tuple-element.94), channel_id=1, source_target_pairs={{0,1},{3,2},{4,5},{7,6},{8,9},{11,10},{12,13},{15,14},{16,17},{19,... | collective-permute-start | bytes 2359304 | tf_op jit(solution)/shard_map/ppermute | solution.py:403
  137.1 13.7 %collective-permute-done.23.refs_7_ = bf16[2,2,256,384]{3,2,1,0:T(8,128)(2,1)} collective-permute-done((bf16[2,2,256,384]{3,2,1,0:T(8,128)(2,1)}, bf16[2,2,256,384]{3,2,1,0:T(8,128)(2,1)}, u32[]{:S(2)}, u32[]{:S(2)}) %collective-permute-start.23) | collective-permute-done | bytes 786464 | tf_op jit(solution)/shard_map/ppermute | solution.py:387
  150.8 11.7 %shard_map.61 = (bf16[2,2,1024,1024]{3,2,1,0:T(8,128)(2,1)}, bf16[2,2,256,1024]{3,2,1,0:T(8,128)(2,1)}, f32[768,256]{1,0:T(8,128)S(1)}, f32[768,256]{1,0:T(8,128...) custom-call(bf16[3072,2048]{1,0:T(8,128)(2,1)} %get-tuple-element.76.refs_0_, ...), custom_call_target="tpu_custom_call", output_to_operand_aliasing={{0}: (11, {})} | custom-call | flops 6442450944 | bytes 12582912 | tf_op jit(solution)/shard_map/pallas_call | solution.py:242
  162.4 1.5 collective-permute-start.30
  163.9 1.5 add_convert_fusion.1
  165.4 0.7 collective-permute-start.28
  166.1 12.3 %shard_map.62 = (bf16[2,2,1024,1024]{3,2,1,0:T(8,128)(2,1)}, bf16[2,2,256,1024]{3,2,1,0:T(8,128)(2,1)}, f32[384,256]{1,0:T(8,128)S(1)}, f32[384,256]{1,0:T(8,128...) custom-call(bf16[3072,2048]{1,0:T(8,128)(2,1)} %get-tuple-element.76, ...), custom_call_target="tpu_custom_call", output_to_operand_aliasing={{1}: (10, {}), {0}: (11, {})} | custom-call | flops 6442450944 | bytes 12582912 | tf_op jit(solution)/shard_map/pallas_call | solution.py:242
  178.4 2.5 %collective-permute-start.25 = (bf16[2,384,256]{2,1,0:T(8,128)(2,1)S(1)}, bf16[2,384,256]{2,1,0:T(8,128)(2,1)S(1)}, u32[]{:S(2)}, u32[]{:S(2)}) collective-permute-start(bf16[2,384,256]{2,1,0:T(8,128)(2,1)S(1)} %get-tuple-element.88), channel_id=1, source_target_pairs={{0,1},{3,2},{4,5},{7,6},{8,9},{11,10},{12,13},{15,14},{16,17},{19,... | collective-permute-start | bytes 1179656 | tf_op jit(solution)/shard_map/ppermute | solution.py:403
  181.2 0.8 collective-permute-start.31
  182.1 1.1 fusion.3
  183.2 2.6 %collective-permute-start.37 = (bf16[384,512]{1,0:T(8,128)(2,1)S(1)}, bf16[384,512]{1,0:T(8,128)(2,1)S(1)}, u32[]{:S(2)}, u32[]{:S(2)}) collective-permute-start(bf16[384,512]{1,0:T(8,128)(2,1)S(1)} %fusion.3), channel_id=1, source_target_pairs={{0,1},{1,0},{2,3},{3,2},{4,5},{5,4},{6,7},{7,6},{8,9},{9,8},{10,11... | collective-permute-start | bytes 1179656 | tf_op jit(solution)/shard_map/ppermute | solution.py:391
  185.8 1.9 collective-permute-start.33
  188.0 2.4 %collective-permute-done.25 = bf16[2,384,256]{2,1,0:T(8,128)(2,1)S(1)} collective-permute-done((bf16[2,384,256]{2,1,0:T(8,128)(2,1)S(1)}, bf16[2,384,256]{2,1,0:T(8,128)(2,1)S(1)}, u32[]{:S(2)}, u32[]{:S(2)}) %collective-permute-start.25) | collective-permute-done | bytes 393248 | tf_op jit(solution)/shard_map/ppermute | solution.py:403
  190.6 0.8 collective-permute-start.35
  191.4 15.9 %collective-permute-done.33 = bf16[2,384,256]{2,1,0:T(8,128)(2,1)S(1)} collective-permute-done((bf16[2,384,256]{2,1,0:T(8,128)(2,1)S(1)}, bf16[2,384,256]{2,1,0:T(8,128)(2,1)S(1)}, u32[]{:S(2)}, u32[]{:S(2)}) %collective-permute-start.33) | collective-permute-done | bytes 393248 | tf_op jit(solution)/shard_map/ppermute | solution.py:403
  207.4 0.8 collective-permute-start.34
  208.5 5.8 %collective-permute-start.32 = (bf16[768,256]{1,0:T(8,128)(2,1)S(1)}, bf16[768,256]{1,0:T(8,128)(2,1)S(1)}, u32[]{:S(2)}, u32[]{:S(2)}) collective-permute-start(bf16[768,256]{1,0:T(8,128)(2,1)S(1)} %fusion.5), channel_id=1, source_target_pairs={{0,1},{1,0},{2,3},{3,2},{4,5},{5,4},{6,7},{7,6},{8,9},{9,8},{10,11... | collective-permute-start | bytes 1179656 | tf_op jit(solution)/shard_map/ppermute | solution.py:391
  214.2 1.2 fusion.4
  215.8 3.9 %collective-permute-start.36 = (bf16[384,256]{1,0:T(8,128)(2,1)S(1)}, bf16[384,256]{1,0:T(8,128)(2,1)S(1)}, u32[]{:S(2)}, u32[]{:S(2)}) collective-permute-start(bf16[384,256]{1,0:T(8,128)(2,1)S(1)} %fusion.11), channel_id=1, source_target_pairs={{0,1},{1,0},{2,3},{3,2},{4,5},{5,4},{6,7},{7,6},{8,9},{9,8},{10,11... | collective-permute-start | bytes 589832 | tf_op jit(solution)/shard_map/ppermute | solution.py:391
  219.7 4.5 %collective-permute-done.32 = bf16[768,256]{1,0:T(8,128)(2,1)S(1)} collective-permute-done((bf16[768,256]{1,0:T(8,128)(2,1)S(1)}, bf16[768,256]{1,0:T(8,128)(2,1)S(1)}, u32[]{:S(2)}, u32[]{:S(2)}) %collective-permute-start.32) | collective-permute-done | bytes 393248 | tf_op jit(solution)/shard_map/ppermute | solution.py:391
  224.3 2.0 collective-permute-start.40
  226.5 6.0 %collective-permute-done.40 = bf16[384,256]{1,0:T(8,128)(2,1)S(1)} collective-permute-done((bf16[384,256]{1,0:T(8,128)(2,1)S(1)}, bf16[384,256]{1,0:T(8,128)(2,1)S(1)}, u32[]{:S(2)}, u32[]{:S(2)}) %collective-permute-start.40) | collective-permute-done | bytes 196640 | tf_op jit(solution)/shard_map/ppermute | solution.py:391
  232.5 0.6 collective-permute-start.41
  233.4 0.8 collective-permute-done.39.refs_6_
  234.2 0.6 collective-permute-done.41.refs_7_
  234.7 2.9 %shard_map.63 = (bf16[2,2,1024,1024]{3,2,1,0:T(8,128)(2,1)}, f32[384,2,1024]{2,1,0:T(2,128)}) custom-call(bf16[2,2,256,1024]{3,2,1,0:T(8,128)(2,1)S(1)} %collective-permute-done.26.refs_0_, bf16[2,2,1024,1024]{3,2,1,0:T(8,128)(2,1)} %get-tuple-element.91.refs_1_, f32[384,512]{1,0:T(8,128)S(1)} %fusion.8.refs_2_, ...), custom_call_target="tpu_custom_call", output_to_operand_aliasing={{0}: (1, {})} | custom-call | bytes 10485760 | tf_op jit(solution)/shard_map/pallas_call | solution.py:352
  (90 shorter events, 2.7 us)
Async XLA Ops:
  2.5 1.4 copy-start.11
  3.0 4.5 %collective-permute-start.2 = (bf16[2,2,256,384]{3,2,1,0:T(8,128)(2,1)S(1)}, bf16[2,2,256,384]{3,2,1,0:T(8,128)(2,1)S(1)}, u32[]{:S(2)}, u32[]{:S(2)}) collective-permute-start(bf16[2,2,256,384]{3,2,1,0:T(8,128)(2,1)S(1)} %get-tuple-element.58), channel_id=1, source_target_pairs={{0,16},{16,0},{1,17},{17,1},{2,18},{18,2},{3,19},{19,3},{4,20},{20... | collective-permute-start | bytes 2359304 | tf_op jit(solution)/shard_map/ppermute | solution.py:375
  4.3 4.6 %copy-start.12 = (bf16[48,8,2,1024]{3,1,2,0:T(8,128)(2,1)}, bf16[48,8,2,1024]{3,1,2,0:T(8,128)(2,1)S(1)}, u32[]{:S(2)}) copy-start(bf16[48,8,2,1024]{3,1,2,0:T(8,128)(2,1)S(1)} %copy.10) | copy-start | bytes 4718596
  4.3 28.0 %collective-permute-start.7 = (bf16[384,2048]{1,0:T(8,128)(2,1)S(1)}, bf16[384,2048]{1,0:T(8,128)(2,1)S(1)}, u32[]{:S(2)}, u32[]{:S(2)}) collective-permute-start(bf16[384,2048]{1,0:T(8,128)(2,1)S(1)} %bitcast.48), channel_id=1, source_target_pairs={{0,16},{16,0},{1,17},{17,1},{2,18},{18,2},{3,19},{19,3},{4,20},{20... | collective-permute-start | bytes 4718600 | tf_op jit(solution)/shard_map/ppermute | solution.py:375
  4.9 37.6 %collective-permute-start.1 = (bf16[384,2048]{1,0:T(8,128)(2,1)S(1)}, bf16[384,2048]{1,0:T(8,128)(2,1)S(1)}, u32[]{:S(2)}, u32[]{:S(2)}) collective-permute-start(bf16[384,2048]{1,0:T(8,128)(2,1)S(1)} %bitcast.49), channel_id=1, source_target_pairs={{0,8},{4,12},{8,0},{12,4},{1,9},{5,13},{9,1},{13,5},{2,10},{6,14},... | collective-permute-start | bytes 4718600 | tf_op jit(solution)/shard_map/ppermute | solution.py:379
  7.6 73.0 %copy-start.8 = (f32[4096]{0:T(1024)S(1)}, f32[4096]{0:T(1024)}, u32[]{:S(2)}) copy-start(f32[4096]{0:T(1024)} %param.7) | copy-start | bytes 49156
  7.7 72.9 %copy-start.9 = (f32[2]{0:T(128)S(1)}, f32[2]{0:T(128)}, u32[]{:S(2)}) copy-start(f32[2]{0:T(128)} %refs_8_.3) | copy-start | bytes 28
  7.7 21.5 %collective-permute-start.5 = (bf16[2,2,256,384]{3,2,1,0:T(8,128)(2,1)S(1)}, bf16[2,2,256,384]{3,2,1,0:T(8,128)(2,1)S(1)}, u32[]{:S(2)}, u32[]{:S(2)}) collective-permute-start(bf16[2,2,256,384]{3,2,1,0:T(8,128)(2,1)S(1)} %get-tuple-element.113.refs_10_), channel_id=1, source_target_pairs={{3,2},{2,1},{1,0},{7,6},{6,5},{5,4},{11,10},{10,9},{9,8},{15,14},{... | collective-permute-start | bytes 2359304 | tf_op jit(solution)/shard_map/ppermute | solution.py:387
  9.0 36.5 %collective-permute-start = (bf16[384,2048]{1,0:T(8,128)(2,1)S(1)}, bf16[384,2048]{1,0:T(8,128)(2,1)S(1)}, u32[]{:S(2)}, u32[]{:S(2)}) collective-permute-start(bf16[384,2048]{1,0:T(8,128)(2,1)S(1)} %bitcast.50), channel_id=1, source_target_pairs={{0,4},{4,0},{8,12},{12,8},{1,5},{5,1},{9,13},{13,9},{2,6},{6,2},{1... | collective-permute-start | bytes 4718600 | tf_op jit(solution)/shard_map/ppermute | solution.py:379
  10.5 21.1 %collective-permute-start.3 = (bf16[2,2,256,384]{3,2,1,0:T(8,128)(2,1)S(1)}, bf16[2,2,256,384]{3,2,1,0:T(8,128)(2,1)S(1)}, u32[]{:S(2)}, u32[]{:S(2)}) collective-permute-start(bf16[2,2,256,384]{3,2,1,0:T(8,128)(2,1)S(1)} %get-tuple-element.113.refs_10_), channel_id=1, source_target_pairs={{0,1},{1,2},{2,3},{4,5},{5,6},{6,7},{8,9},{9,10},{10,11},{12,13},{... | collective-permute-start | bytes 2359304 | tf_op jit(solution)/shard_map/ppermute | solution.py:383
  29.2 51.0 %copy-start.19 = (bf16[2,2,256,384]{3,2,1,0:T(8,128)(2,1)}, bf16[2,2,256,384]{3,2,1,0:T(8,128)(2,1)S(1)}, u32[]{:S(2)}) copy-start(bf16[2,2,256,384]{3,2,1,0:T(8,128)(2,1)S(1)} %collective-permute-done.5.refs_14_) | copy-start | bytes 2359300
  29.2 20.7 %collective-permute-start.6 = (bf16[2,2,256,384]{3,2,1,0:T(8,128)(2,1)S(1)}, bf16[2,2,256,384]{3,2,1,0:T(8,128)(2,1)S(1)}, u32[]{:S(2)}, u32[]{:S(2)}) collective-permute-start(bf16[2,2,256,384]{3,2,1,0:T(8,128)(2,1)S(1)} %collective-permute-done.5.refs_14_), channel_id=1, source_target_pairs={{2,1},{1,0},{6,5},{5,4},{10,9},{9,8},{14,13},{13,12},{18,17},{17,1... | collective-permute-start | bytes 2359304 | tf_op jit(solution)/shard_map/ppermute | solution.py:387
  31.6 18.2 %collective-permute-start.4 = (bf16[2,2,256,384]{3,2,1,0:T(8,128)(2,1)S(1)}, bf16[2,2,256,384]{3,2,1,0:T(8,128)(2,1)S(1)}, u32[]{:S(2)}, u32[]{:S(2)}) collective-permute-start(bf16[2,2,256,384]{3,2,1,0:T(8,128)(2,1)S(1)} %collective-permute-done.3.refs_11_), channel_id=1, source_target_pairs={{1,2},{2,3},{5,6},{6,7},{9,10},{10,11},{13,14},{14,15},{17,18},{18... | collective-permute-start | bytes 2359304 | tf_op jit(solution)/shard_map/ppermute | solution.py:383
  32.4 46.6 %copy-start.16 = (bf16[384,2048]{1,0:T(8,128)(2,1)}, bf16[384,2048]{1,0:T(8,128)(2,1)S(1)}, u32[]{:S(2)}) copy-start(bf16[384,2048]{1,0:T(8,128)(2,1)S(1)} %collective-permute-done.7.refs_5_) | copy-start | bytes 4718596
  42.4 25.5 %copy-start.14 = (bf16[384,2048]{1,0:T(8,128)(2,1)}, bf16[384,2048]{1,0:T(8,128)(2,1)S(1)}, u32[]{:S(2)}) copy-start(bf16[384,2048]{1,0:T(8,128)(2,1)S(1)} %collective-permute-done.1.refs_2_) | copy-start | bytes 4718596
  45.5 8.8 %copy-start.15 = (bf16[384,2048]{1,0:T(8,128)(2,1)}, bf16[384,2048]{1,0:T(8,128)(2,1)S(1)}, u32[]{:S(2)}) copy-start(bf16[384,2048]{1,0:T(8,128)(2,1)S(1)} %collective-permute-done.refs_1_) | copy-start | bytes 4718596
  49.8 30.4 %copy-start.20 = (bf16[2,2,256,384]{3,2,1,0:T(8,128)(2,1)}, bf16[2,2,256,384]{3,2,1,0:T(8,128)(2,1)S(1)}, u32[]{:S(2)}) copy-start(bf16[2,2,256,384]{3,2,1,0:T(8,128)(2,1)S(1)} %collective-permute-done.6.refs_15_) | copy-start | bytes 2359300
  50.0 17.9 %collective-permute-start.10 = (bf16[192,2048]{1,0:T(8,128)(2,1)S(1)}, bf16[192,2048]{1,0:T(8,128)(2,1)S(1)}, u32[]{:S(2)}, u32[]{:S(2)}) collective-permute-start(bf16[192,2048]{1,0:T(8,128)(2,1)S(1)} %slice.22), channel_id=1, source_target_pairs={{0,8},{4,12},{8,0},{12,4},{1,9},{5,13},{9,1},{13,5},{2,10},{6,14},... | collective-permute-start | bytes 2359304 | tf_op jit(solution)/shard_map/ppermute | solution.py:379
  50.8 17.6 %collective-permute-start.11 = (bf16[192,2048]{1,0:T(8,128)(2,1)S(1)}, bf16[192,2048]{1,0:T(8,128)(2,1)S(1)}, u32[]{:S(2)}, u32[]{:S(2)}) collective-permute-start(bf16[192,2048]{1,0:T(8,128)(2,1)S(1)} %slice.23), channel_id=1, source_target_pairs={{0,4},{4,0},{8,12},{12,8},{1,5},{5,1},{9,13},{13,9},{2,6},{6,2},{1... | collective-permute-start | bytes 2359304 | tf_op jit(solution)/shard_map/ppermute | solution.py:379
  52.3 16.1 %collective-permute-start.8 = (bf16[2,2,256,384]{3,2,1,0:T(8,128)(2,1)S(1)}, bf16[2,2,256,384]{3,2,1,0:T(8,128)(2,1)S(1)}, u32[]{:S(2)}, u32[]{:S(2)}) collective-permute-start(bf16[2,2,256,384]{3,2,1,0:T(8,128)(2,1)S(1)} %collective-permute-done.4.refs_12_), channel_id=1, source_target_pairs={{2,3},{6,7},{10,11},{14,15},{18,19},{22,23},{26,27},{30,31}} | collective-permute-start | bytes 2359304 | tf_op jit(solution)/shard_map/ppermute | solution.py:383
  53.0 19.4 %collective-permute-start.9 = (bf16[2,2,256,384]{3,2,1,0:T(8,128)(2,1)S(1)}, bf16[2,2,256,384]{3,2,1,0:T(8,128)(2,1)}, u32[]{:S(2)}, u32[]{:S(2)}) collective-permute-start(bf16[2,2,256,384]{3,2,1,0:T(8,128)(2,1)S(1)} %collective-permute-done.6.refs_15_), channel_id=1, source_target_pairs={{1,0},{5,4},{9,8},{13,12},{17,16},{21,20},{25,24},{29,28}} | collective-permute-start | bytes 2359304 | tf_op jit(solution)/shard_map/ppermute | solution.py:387
  54.3 24.6 %collective-permute-start.12 = (bf16[384,2048]{1,0:T(8,128)(2,1)S(1)}, bf16[384,2048]{1,0:T(8,128)(2,1)S(1)}, u32[]{:S(2)}, u32[]{:S(2)}) collective-permute-start(bf16[384,2048]{1,0:T(8,128)(2,1)S(1)} %collective-permute-done.refs_1_), channel_id=1, source_target_pairs={{0,16},{16,0},{1,17},{17,1},{2,18},{18,2},{3,19},{19,3},{4,20},{20... | collective-permute-start | bytes 4718600 | tf_op jit(solution)/shard_map/ppermute | solution.py:375
  67.9 11.0 %collective-permute-start.13 = (bf16[384,2048]{1,0:T(8,128)(2,1)S(1)}, bf16[384,2048]{1,0:T(8,128)(2,1)S(1)}, u32[]{:S(2)}, u32[]{:S(2)}) collective-permute-start(bf16[384,2048]{1,0:T(8,128)(2,1)S(1)} %collective-permute-done.1.refs_2_), channel_id=1, source_target_pairs={{0,16},{16,0},{1,17},{17,1},{2,18},{18,2},{3,19},{19,3},{4,20},{20... | collective-permute-start | bytes 4718600 | tf_op jit(solution)/shard_map/ppermute | solution.py:375
  68.4 11.8 %copy-start.21 = (bf16[2,2,256,384]{3,2,1,0:T(8,128)(2,1)}, bf16[2,2,256,384]{3,2,1,0:T(8,128)(2,1)S(1)}, u32[]{:S(2)}) copy-start(bf16[2,2,256,384]{3,2,1,0:T(8,128)(2,1)S(1)} %collective-permute-done.8.refs_13_) | copy-start | bytes 2359300
  72.5 2.3 collective-permute-start.14
  72.5 6.4 %collective-permute-start.15 = (bf16[192,2048]{1,0:T(8,128)(2,1)S(1)}, bf16[192,2048]{1,0:T(8,128)(2,1)S(1)}, u32[]{:S(2)}, u32[]{:S(2)}) collective-permute-start(bf16[192,2048]{1,0:T(8,128)(2,1)S(1)} %collective-permute-done.11.refs_4_), channel_id=1, source_target_pairs={{0,16},{16,0},{1,17},{17,1},{2,18},{18,2},{3,19},{19,3},{4,20},{20... | collective-permute-start | bytes 2359304 | tf_op jit(solution)/shard_map/ppermute | solution.py:375
  73.0 31.3 %collective-permute-start.19 = (bf16[2,2,256,384]{3,2,1,0:T(8,128)(2,1)S(1)}, bf16[2,2,256,384]{3,2,1,0:T(8,128)(2,1)S(1)}, u32[]{:S(2)}, u32[]{:S(2)}) collective-permute-start(bf16[2,2,256,384]{3,2,1,0:T(8,128)(2,1)S(1)} %get-tuple-element.80.refs_1_), channel_id=1, source_target_pairs={{3,2},{2,1},{1,0},{7,6},{6,5},{5,4},{11,10},{10,9},{9,8},{15,14},{... | collective-permute-start | bytes 2359304 | tf_op jit(solution)/shard_map/ppermute | solution.py:387
  74.8 29.5 %collective-permute-start.18 = (bf16[2,2,256,384]{3,2,1,0:T(8,128)(2,1)S(1)}, bf16[2,2,256,384]{3,2,1,0:T(8,128)(2,1)S(1)}, u32[]{:S(2)}, u32[]{:S(2)}) collective-permute-start(bf16[2,2,256,384]{3,2,1,0:T(8,128)(2,1)S(1)} %get-tuple-element.80.refs_1_), channel_id=1, source_target_pairs={{0,1},{1,2},{2,3},{4,5},{5,6},{6,7},{8,9},{9,10},{10,11},{12,13},{... | collective-permute-start | bytes 2359304 | tf_op jit(solution)/shard_map/ppermute | solution.py:383
  78.9 1.7 copy-start.17
  78.9 1.2 copy-start.18
  101.4 22.8 %copy-start = (f32[384,512]{1,0:T(8,128)}, f32[384,512]{1,0:T(8,128)S(1)}, u32[]{:S(2)}) copy-start(f32[384,512]{1,0:T(8,128)S(1)} %get-tuple-element.92) | copy-start | bytes 2359300
  101.4 22.8 %copy-start.2 = (f32[384,512]{1,0:T(8,128)}, f32[384,512]{1,0:T(8,128)S(1)}, u32[]{:S(2)}) copy-start(f32[384,512]{1,0:T(8,128)S(1)} %get-tuple-element.106) | copy-start | bytes 2359300
  101.4 22.8 %copy-start.4 = (f32[384,512]{1,0:T(8,128)}, f32[384,512]{1,0:T(8,128)S(1)}, u32[]{:S(2)}) copy-start(f32[384,512]{1,0:T(8,128)S(1)} %get-tuple-element.95) | copy-start | bytes 2359300
  101.4 22.8 %copy-start.6 = (f32[384,512]{1,0:T(8,128)}, f32[384,512]{1,0:T(8,128)S(1)}, u32[]{:S(2)}) copy-start(f32[384,512]{1,0:T(8,128)S(1)} %get-tuple-element.108) | copy-start | bytes 2359300
  101.4 49.3 %collective-permute-start.24 = (bf16[2,2,256,1024]{3,2,1,0:T(8,128)(2,1)}, bf16[2,2,256,1024]{3,2,1,0:T(8,128)(2,1)}, u32[]{:S(2)}, u32[]{:S(2)}) collective-permute-start(bf16[2,2,256,1024]{3,2,1,0:T(8,128)(2,1)} %get-tuple-element.84), channel_id=1, source_target_pairs={{0,16},{16,0},{1,17},{17,1},{2,18},{18,2},{3,19},{19,3},{4,20},{20... | collective-permute-start | bytes 6291464 | tf_op jit(solution)/shard_map/ppermute | solution.py:375
  101.5 20.1 %collective-permute-start.16 = (bf16[2,384,512]{2,1,0:T(8,128)(2,1)S(1)}, bf16[2,384,512]{2,1,0:T(8,128)(2,1)S(1)}, u32[]{:S(2)}, u32[]{:S(2)}) collective-permute-start(bf16[2,384,512]{2,1,0:T(8,128)(2,1)S(1)} %get-tuple-element.78), channel_id=1, source_target_pairs={{0,1},{3,2},{4,5},{7,6},{8,9},{11,10},{12,13},{15,14},{16,17},{19,... | collective-permute-start | bytes 2359304 | tf_op jit(solution)/shard_map/ppermute | solution.py:403
  104.3 21.5 %collective-permute-start.20 = (bf16[2,2,256,384]{3,2,1,0:T(8,128)(2,1)S(1)}, bf16[2,2,256,384]{3,2,1,0:T(8,128)(2,1)S(1)}, u32[]{:S(2)}, u32[]{:S(2)}) collective-permute-start(bf16[2,2,256,384]{3,2,1,0:T(8,128)(2,1)S(1)} %collective-permute-done.18.refs_2_), channel_id=1, source_target_pairs={{1,2},{2,3},{5,6},{6,7},{9,10},{10,11},{13,14},{14,15},{17,18},{18... | collective-permute-start | bytes 2359304 | tf_op jit(solution)/shard_map/ppermute | solution.py:383
  105.0 22.4 %collective-permute-start.22 = (bf16[2,2,256,384]{3,2,1,0:T(8,128)(2,1)S(1)}, bf16[2,2,256,384]{3,2,1,0:T(8,128)(2,1)}, u32[]{:S(2)}, u32[]{:S(2)}) collective-permute-start(bf16[2,2,256,384]{3,2,1,0:T(8,128)(2,1)S(1)} %collective-permute-done.19.refs_5_), channel_id=1, source_target_pairs={{2,1},{1,0},{6,5},{5,4},{10,9},{9,8},{14,13},{13,12},{18,17},{17,1... | collective-permute-start | bytes 2359304 | tf_op jit(solution)/shard_map/ppermute | solution.py:387
  124.2 12.8 %collective-permute-start.17 = (bf16[2,384,512]{2,1,0:T(8,128)(2,1)}, bf16[2,384,512]{2,1,0:T(8,128)(2,1)}, u32[]{:S(2)}, u32[]{:S(2)}) collective-permute-start(bf16[2,384,512]{2,1,0:T(8,128)(2,1)} %add_convert_fusion.2), channel_id=1, source_target_pairs={{1,2},{2,1},{5,6},{6,5},{9,10},{10,9},{13,14},{14,13},{17,18},{18,... | collective-permute-start | bytes 2359304 | tf_op jit(solution)/shard_map/ppermute | solution.py:395
  125.8 11.3 %collective-permute-start.21 = (bf16[2,2,256,384]{3,2,1,0:T(8,128)(2,1)S(1)}, bf16[2,2,256,384]{3,2,1,0:T(8,128)(2,1)}, u32[]{:S(2)}, u32[]{:S(2)}) collective-permute-start(bf16[2,2,256,384]{3,2,1,0:T(8,128)(2,1)S(1)} %collective-permute-done.20.refs_3_), channel_id=1, source_target_pairs={{2,3},{6,7},{10,11},{14,15},{18,19},{22,23},{26,27},{30,31}} | collective-permute-start | bytes 2359304 | tf_op jit(solution)/shard_map/ppermute | solution.py:383
  127.3 23.4 %collective-permute-start.23 = (bf16[2,2,256,384]{3,2,1,0:T(8,128)(2,1)}, bf16[2,2,256,384]{3,2,1,0:T(8,128)(2,1)}, u32[]{:S(2)}, u32[]{:S(2)}) collective-permute-start(bf16[2,2,256,384]{3,2,1,0:T(8,128)(2,1)} %collective-permute-done.22.refs_6_), channel_id=1, source_target_pairs={{1,0},{5,4},{9,8},{13,12},{17,16},{21,20},{25,24},{29,28}} | collective-permute-start | bytes 2359304 | tf_op jit(solution)/shard_map/ppermute | solution.py:387
  128.6 35.3 %collective-permute-start.27 = (bf16[2,384,512]{2,1,0:T(8,128)(2,1)}, bf16[2,384,512]{2,1,0:T(8,128)(2,1)}, u32[]{:S(2)}, u32[]{:S(2)}) collective-permute-start(bf16[2,384,512]{2,1,0:T(8,128)(2,1)} %get-tuple-element.94), channel_id=1, source_target_pairs={{0,1},{3,2},{4,5},{7,6},{8,9},{11,10},{12,13},{15,14},{16,17},{19,... | collective-permute-start | bytes 2359304 | tf_op jit(solution)/shard_map/ppermute | solution.py:403
  150.8 13.2 %copy-start.13 = (f32[2,384,512]{2,1,0:T(8,128)S(1)}, f32[2,384,512]{2,1,0:T(8,128)}, u32[]{:S(2)}) copy-start(f32[2,384,512]{2,1,0:T(8,128)} %get-tuple-element.93) | copy-start | bytes 4718596
  162.4 18.5 %collective-permute-start.30 = (bf16[2,768,256]{2,1,0:T(8,128)(2,1)S(1)}, bf16[2,768,256]{2,1,0:T(8,128)(2,1)S(1)}, u32[]{:S(2)}, u32[]{:S(2)}) collective-permute-start(bf16[2,768,256]{2,1,0:T(8,128)(2,1)S(1)} %get-tuple-element.98), channel_id=1, source_target_pairs={{0,1},{3,2},{4,5},{7,6},{8,9},{11,10},{12,13},{15,14},{16,17},{19,... | collective-permute-start | bytes 2359304 | tf_op jit(solution)/shard_map/ppermute | solution.py:403
  165.4 22.4 %collective-permute-start.28 = (bf16[2,384,512]{2,1,0:T(8,128)(2,1)S(1)}, bf16[2,384,512]{2,1,0:T(8,128)(2,1)S(1)}, u32[]{:S(2)}, u32[]{:S(2)}) collective-permute-start(bf16[2,384,512]{2,1,0:T(8,128)(2,1)S(1)} %add_convert_fusion.1), channel_id=1, source_target_pairs={{1,2},{2,1},{5,6},{6,5},{9,10},{10,9},{13,14},{14,13},{17,18},{18,... | collective-permute-start | bytes 2359304 | tf_op jit(solution)/shard_map/ppermute | solution.py:395
  178.4 12.1 %collective-permute-start.25 = (bf16[2,384,256]{2,1,0:T(8,128)(2,1)S(1)}, bf16[2,384,256]{2,1,0:T(8,128)(2,1)S(1)}, u32[]{:S(2)}, u32[]{:S(2)}) collective-permute-start(bf16[2,384,256]{2,1,0:T(8,128)(2,1)S(1)} %get-tuple-element.88), channel_id=1, source_target_pairs={{0,1},{3,2},{4,5},{7,6},{8,9},{11,10},{12,13},{15,14},{16,17},{19,... | collective-permute-start | bytes 1179656 | tf_op jit(solution)/shard_map/ppermute | solution.py:403
  180.9 1.1 copy-start.7
  181.2 6.6 %copy-start.5 = (f32[384,512]{1,0:T(8,128)S(1)}, f32[384,512]{1,0:T(8,128)}, u32[]{:S(2)}) copy-start(f32[384,512]{1,0:T(8,128)} %copy-done.4) | copy-start | bytes 2359300
  181.2 27.0 %collective-permute-start.31 = (bf16[2,768,256]{2,1,0:T(8,128)(2,1)S(1)}, bf16[2,768,256]{2,1,0:T(8,128)(2,1)S(1)}, u32[]{:S(2)}, u32[]{:S(2)}) collective-permute-start(bf16[2,768,256]{2,1,0:T(8,128)(2,1)S(1)} %add_convert_fusion), channel_id=1, source_target_pairs={{1,2},{2,1},{5,6},{6,5},{9,10},{10,9},{13,14},{14,13},{17,18},{18,... | collective-permute-start | bytes 2359304 | tf_op jit(solution)/shard_map/ppermute | solution.py:395
  183.2 25.2 %collective-permute-start.37 = (bf16[384,512]{1,0:T(8,128)(2,1)S(1)}, bf16[384,512]{1,0:T(8,128)(2,1)S(1)}, u32[]{:S(2)}, u32[]{:S(2)}) collective-permute-start(bf16[384,512]{1,0:T(8,128)(2,1)S(1)} %fusion.3), channel_id=1, source_target_pairs={{0,1},{1,0},{2,3},{3,2},{4,5},{5,4},{6,7},{7,6},{8,9},{9,8},{10,11... | collective-permute-start | bytes 1179656 | tf_op jit(solution)/shard_map/ppermute | solution.py:391
  185.8 21.5 %collective-permute-start.33 = (bf16[2,384,256]{2,1,0:T(8,128)(2,1)S(1)}, bf16[2,384,256]{2,1,0:T(8,128)(2,1)S(1)}, u32[]{:S(2)}, u32[]{:S(2)}) collective-permute-start(bf16[2,384,256]{2,1,0:T(8,128)(2,1)S(1)} %get-tuple-element.101), channel_id=1, source_target_pairs={{0,1},{3,2},{4,5},{7,6},{8,9},{11,10},{12,13},{15,14},{16,17},{19,... | collective-permute-start | bytes 1179656 | tf_op jit(solution)/shard_map/ppermute | solution.py:403
  187.9 44.6 %collective-permute-start.29 = (bf16[384,512]{1,0:T(8,128)(2,1)S(1)}, bf16[384,512]{1,0:T(8,128)(2,1)S(1)}, u32[]{:S(2)}, u32[]{:S(2)}) collective-permute-start(bf16[384,512]{1,0:T(8,128)(2,1)S(1)} %fusion.7), channel_id=1, source_target_pairs={{0,1},{1,0},{2,3},{3,2},{4,5},{5,4},{6,7},{7,6},{8,9},{9,8},{10,11... | collective-permute-start | bytes 1179656 | tf_op jit(solution)/shard_map/ppermute | solution.py:391
  190.5 17.8 %copy-start.10 = (bf16[2,2,256,1024]{3,2,1,0:T(8,128)(2,1)S(1)}, bf16[2,2,256,1024]{3,2,1,0:T(8,128)(2,1)}, u32[]{:S(2)}) copy-start(bf16[2,2,256,1024]{3,2,1,0:T(8,128)(2,1)} %get-tuple-element.90) | copy-start | bytes 6291460
  190.6 24.8 %collective-permute-start.35 = (bf16[2,384,256]{2,1,0:T(8,128)(2,1)S(1)}, bf16[2,384,256]{2,1,0:T(8,128)(2,1)S(1)}, u32[]{:S(2)}, u32[]{:S(2)}) collective-permute-start(bf16[2,384,256]{2,1,0:T(8,128)(2,1)S(1)} %add_convert_fusion.3), channel_id=1, source_target_pairs={{1,2},{2,1},{5,6},{6,5},{9,10},{10,9},{13,14},{14,13},{17,18},{18,... | collective-permute-start | bytes 1179656 | tf_op jit(solution)/shard_map/ppermute | solution.py:395
  207.3 6.9 %copy-start.3 = (f32[384,512]{1,0:T(8,128)S(1)}, f32[384,512]{1,0:T(8,128)}, u32[]{:S(2)}) copy-start(f32[384,512]{1,0:T(8,128)} %copy-done.2) | copy-start | bytes 2359300
  207.4 8.3 %collective-permute-start.34 = (bf16[2,384,256]{2,1,0:T(8,128)(2,1)S(1)}, bf16[2,384,256]{2,1,0:T(8,128)(2,1)S(1)}, u32[]{:S(2)}, u32[]{:S(2)}) collective-permute-start(bf16[2,384,256]{2,1,0:T(8,128)(2,1)S(1)} %add_convert_fusion.4), channel_id=1, source_target_pairs={{1,2},{2,1},{5,6},{6,5},{9,10},{10,9},{13,14},{14,13},{17,18},{18,... | collective-permute-start | bytes 1179656 | tf_op jit(solution)/shard_map/ppermute | solution.py:395
  208.3 25.9 %collective-permute-start.26 = (bf16[2,2,256,1024]{3,2,1,0:T(8,128)(2,1)S(1)}, bf16[2,2,256,1024]{3,2,1,0:T(8,128)(2,1)S(1)}, u32[]{:S(2)}, u32[]{:S(2)}) collective-permute-start(bf16[2,2,256,1024]{3,2,1,0:T(8,128)(2,1)S(1)} %copy-done.10), channel_id=1, source_target_pairs={{0,16},{16,0},{1,17},{17,1},{2,18},{18,2},{3,19},{19,3},{4,20},{20... | collective-permute-start | bytes 6291464 | tf_op jit(solution)/shard_map/ppermute | solution.py:375
  208.5 15.7 %collective-permute-start.32 = (bf16[768,256]{1,0:T(8,128)(2,1)S(1)}, bf16[768,256]{1,0:T(8,128)(2,1)S(1)}, u32[]{:S(2)}, u32[]{:S(2)}) collective-permute-start(bf16[768,256]{1,0:T(8,128)(2,1)S(1)} %fusion.5), channel_id=1, source_target_pairs={{0,1},{1,0},{2,3},{3,2},{4,5},{5,4},{6,7},{7,6},{8,9},{9,8},{10,11... | collective-permute-start | bytes 1179656 | tf_op jit(solution)/shard_map/ppermute | solution.py:391
  215.4 17.9 %collective-permute-start.38 = (f32[384,512]{1,0:T(8,128)S(1)}, f32[384,512]{1,0:T(8,128)S(1)}, u32[]{:S(2)}, u32[]{:S(2)}) collective-permute-start(f32[384,512]{1,0:T(8,128)S(1)} %fusion.4), channel_id=1, source_target_pairs={{0,16},{16,0},{1,17},{17,1},{2,18},{18,2},{3,19},{19,3},{4,20},{20... | collective-permute-start | bytes 2359304 | tf_op jit(solution)/shard_map/ppermute | solution.py:375
  215.8 17.5 %collective-permute-start.36 = (bf16[384,256]{1,0:T(8,128)(2,1)S(1)}, bf16[384,256]{1,0:T(8,128)(2,1)S(1)}, u32[]{:S(2)}, u32[]{:S(2)}) collective-permute-start(bf16[384,256]{1,0:T(8,128)(2,1)S(1)} %fusion.11), channel_id=1, source_target_pairs={{0,1},{1,0},{2,3},{3,2},{4,5},{5,4},{6,7},{7,6},{8,9},{9,8},{10,11... | collective-permute-start | bytes 589832 | tf_op jit(solution)/shard_map/ppermute | solution.py:391
  224.3 8.2 %collective-permute-start.40 = (bf16[384,256]{1,0:T(8,128)(2,1)S(1)}, bf16[384,256]{1,0:T(8,128)(2,1)S(1)}, u32[]{:S(2)}, u32[]{:S(2)}) collective-permute-start(bf16[384,256]{1,0:T(8,128)(2,1)S(1)} %fusion.9), channel_id=1, source_target_pairs={{0,1},{1,0},{2,3},{3,2},{4,5},{5,4},{6,7},{7,6},{8,9},{9,8},{10,11... | collective-permute-start | bytes 589832 | tf_op jit(solution)/shard_map/ppermute | solution.py:391
  226.4 6.7 %copy-start.1 = (f32[384,512]{1,0:T(8,128)S(1)}, f32[384,512]{1,0:T(8,128)}, u32[]{:S(2)}) copy-start(f32[384,512]{1,0:T(8,128)} %copy-done) | copy-start | bytes 2359300
  232.4 1.7 collective-permute-start.39
  232.5 2.2 collective-permute-start.41
